TPU v7x, 32 devices: a whole 2x2x4 slice. The times are simulated.
32 devices in a mesh: dp: 4 (over z), seq: 4 (over y, x), mp: 2 (over core).
Axes of the slice: x: 2, y: 2, z: 4, core: 2. Of those that a mesh axis runs over, the one named last changes fastest.
Arguments:
- features: bfloat16 [4, 2048, 1408], P('dp', ('seq', 'mp')), may hold values from -6 to 6
- conv_weight: bfloat16 [5, 1408, 1536], P(None, ('seq', 'mp')), may hold values from -0.0625 to 0.0625
- norm_gain: float32 [1536], replicated, may hold values from 0.25 to 1.75
- query_weight: bfloat16 [1536, 1024], replicated, may hold values from -0.15625 to 0.15625
- keyval_weight: bfloat16 [1536, 320], replicated, may hold values from -0.15625 to 0.15625
- head_scale: float32 [8], replicated, may hold values from 0.5 to 24
- output_weight: bfloat16 [1536, 1536], replicated, may hold values from -0.15625 to 0.15625
- pair_weight: bfloat16 [1536, 256], replicated, may hold values from -0.625 to 0.625
- pair_input: bfloat16 [4, 64, 64, 128], P('dp', ('seq', 'mp')), may hold values from -6 to 6
- flip_weight: bfloat16 [128, 128], replicated, may hold values from -0.5 to 0.5
- pair_cotangent: bfloat16 [4, 64, 64, 128], P('dp', ('seq', 'mp')), may hold values from -0.09375 to 0.09375
Outputs:
- block_out: bfloat16 [4, 1024, 1536], P('dp', ('seq', 'mp'))
- pair_out: bfloat16 [4, 64, 64, 128], P('dp', ('seq', 'mp'))
- grad_flip: float32 [128, 128], replicated
All inputs are finite; a program needn't handle non-finite values.
Results may differ from a plain program's by a relative error of at most 0.011.
Values may be sent and summed in bfloat16 or wider, within the bound.
No kernel may reach another device: no remote copies, remote signals or barrier semaphores. Data moves between devices by JAX's collectives and lax.ppermute only.
A program may use at most 192 MiB of HBM per device.

v0:
```python
import math

import jax
import jax.numpy as jnp
from jax import lax
from jax.sharding import PartitionSpec as P

PAIR_POOL = 16


norm_eps = 1e-06
logit_cap = 50.0


def padded_2(shard, sides, width):
    for axis, dim in sides:
        devices, length = (lax.axis_size(axis), shard.shape[dim])
        up = [(i, (i + 1) % devices) for i in range(devices - 1)]
        down = [(j, i) for i, j in up]
        last = lax.slice_in_dim(shard, length - width, length, axis=dim)
        initial = lax.slice_in_dim(shard, 0, width, axis=dim)
        before = lax.ppermute(last, axis, up)
        after = lax.ppermute(initial, axis, down)
        shard = jnp.concatenate([before, shard, after], axis=dim)
    return shard


def root_norm(values_in):
    return values_in * lax.rsqrt(jnp.mean(values_in * values_in, axis=-1, keepdims=True) + norm_eps)


def prepare(raw):
    return jax.nn.gelu(root_norm(raw.astype(jnp.float32)), approximate=False).astype(jnp.bfloat16)


def tap_sum(source, out_rows, tap_count, running, filter_rows):
    for lag_index in range(tap_count):
        running = running + jnp.dot(
            source[lag_index : lag_index + out_rows],
            filter_rows[lag_index],
            preferred_element_type=jnp.float32,
        )
    return running


def per_device(
    features,
    conv_weight,
    norm_gain,
    query_weight,
    keyval_weight,
    head_scale,
    output_weight,
    pair_weight,
    pair_input,
    flip_weight,
    pair_cotangent,
):
    fine_rows = features.shape[1]
    coarse_rows = fine_rows // 2
    in_channels = features.shape[2]
    model_dim = output_weight.shape[1]
    head_count = head_scale.shape[0]
    key_dim = query_weight.shape[1] // head_count
    pair_dim = flip_weight.shape[0]
    tap_count = conv_weight.shape[0]
    margin = tap_count // 2
    padded = padded_2(features, ((("seq", "mp"), 1),), margin)
    prepared = prepare(padded[0])
    starting = jnp.zeros((fine_rows, model_dim), jnp.float32)
    conv_sum = tap_sum(
        prepared,
        fine_rows,
        tap_count,
        starting,
        lax.all_gather(conv_weight, ("seq", "mp"), axis=1, tiled=True),
    )
    skipped = jnp.pad(features[0].astype(jnp.float32), ((0, 0), (0, model_dim - in_channels)))
    encoded = jnp.max((conv_sum + skipped).reshape(coarse_rows, 2, model_dim), axis=1).astype(
        jnp.bfloat16
    )
    widened = encoded.astype(jnp.float32)
    normed = (root_norm(widened) * norm_gain).astype(jnp.bfloat16)
    scale_row = jnp.repeat(head_scale, key_dim) / math.sqrt(key_dim)
    queries = (
        jnp.dot(normed, query_weight, preferred_element_type=jnp.float32) * scale_row
    ).astype(jnp.bfloat16)
    keyvals = jnp.dot(normed, keyval_weight, preferred_element_type=jnp.float32).astype(
        jnp.bfloat16
    )
    pooled = jnp.mean(
        widened.reshape(coarse_rows // PAIR_POOL, PAIR_POOL, model_dim), axis=1
    ).astype(jnp.bfloat16)
    pair_feats = jnp.dot(pooled, pair_weight, preferred_element_type=jnp.float32).astype(
        jnp.bfloat16
    )
    pair_q = pair_feats[:, :pair_dim]
    pair_k = pair_feats[:, pair_dim:]
    keys_all, pairk_all = (
        lax.all_gather(keyvals[None], ("seq", "mp"), axis=1, tiled=True),
        lax.all_gather(pair_k[None], ("seq", "mp"), axis=1, tiled=True),
    )
    summed = (
        pair_input[0].astype(jnp.float32)
        + pair_q[:, None, :].astype(jnp.float32) * pairk_all[0][None, :, :].astype(jnp.float32)
    ).astype(jnp.bfloat16)
    flipped = lax.all_to_all(summed[None], ("seq", "mp"), split_axis=2, concat_axis=1, tiled=True)[
        0
    ]
    turned = jnp.einsum("bac,cd->abd", flipped, flip_weight, preferred_element_type=jnp.float32)
    pair_out = (summed.astype(jnp.float32) + turned).astype(jnp.bfloat16)
    grad_term = jnp.einsum(
        "bac,abd->cd", flipped, pair_cotangent[0], preferred_element_type=jnp.float32
    )
    grad_flip = lax.psum(grad_term, ("dp", "seq", "mp"))
    key_rows = keys_all[0][:, :key_dim]
    value_rows = keys_all[0][:, key_dim:]
    query_rows = queries.reshape(coarse_rows * head_count, key_dim)
    scores = jnp.dot(query_rows, key_rows.T, preferred_element_type=jnp.float32)
    weights = jnp.exp(logit_cap * jnp.tanh(scores / logit_cap))
    totals = jnp.sum(weights, axis=-1, keepdims=True)
    mixed = (
        jnp.dot(weights.astype(jnp.bfloat16), value_rows, preferred_element_type=jnp.float32)
        / totals
    )
    heads_out = mixed.astype(jnp.bfloat16).reshape(coarse_rows, head_count * value_rows.shape[1])
    block_out = (
        widened + jnp.dot(heads_out, output_weight, preferred_element_type=jnp.float32)
    ).astype(jnp.bfloat16)
    return (block_out[None], pair_out[None], grad_flip)


def solution(mesh):
    placed = (
        P("dp", ("seq", "mp"), None),
        P(None, ("seq", "mp"), None),
        P(),
        P(),
        P(),
        P(),
        P(),
        P(),
        P("dp", ("seq", "mp"), None, None),
        P(),
        P("dp", ("seq", "mp"), None, None),
    )
    return jax.shard_map(
        per_device,
        mesh=mesh,
        in_specs=placed,
        out_specs=(P("dp", ("seq", "mp"), None), P("dp", ("seq", "mp"), None, None), P()),
        check_vma=False,
    )
```

profile of v0, /device:TPU:0, one launch (start us, length us, event | category | flops | bytes accessed | tf_op | source)
XLA Modules:
  0.0 324.1 jit_solution(10863281127152504339)
XLA Ops:
  8.8 2.4 collective-permute-start
  12.6 3.8 %collective-permute-done.1 = bf16[1,2,1408]{2,1,0:T(2,128)(2,1)S(1)} collective-permute-done((bf16[1,2,1408]{2,1,0:T(2,128)(2,1)S(1)}, bf16[1,2,1408]{2,1,0:T(2,128)(2,1)S(1)}, u32[]{:S(2)}, u32[]{:S(2)}) %collective-permute-start.1) | collective-permute-done | bytes 5664 | tf_op jit(solution)/shard_map/ppermute | solution.py:23
  17.8 6.0 %fusion.19 = bf16[260,1408]{1,0:T(8,128)(2,1)} fusion(f32[260]{0:T(512)S(1)} %add_rsqrt_fusion, bf16[1,2,1408]{2,1,0:T(2,128)(2,1)S(1)} %collective-permute-done.1, bf16[1,256,1408]{2,1,0:T(8,128)(2,1)} %param.11, bf16[1,2,1408]{2,1,0:T(2,128)(2,1)S(1)} %collective-permute-done), kind=kLoop, calls=%fused_computation.28 | loop fusion | flops 26723840 | bytes 1465360 | tf_op jit(solution)/shard_map/convert_element_type | solution.py:33
  23.8 99.2 %all-gather.4.cloned.1.call-done = bf16[5,1408,1536]{2,1,0:T(8,128)(2,1)} async-done(((bf16[5,176,1536]{2,1,0:T(8,128)(2,1)}), bf16[5,1408,1536]{2,1,0:T(8,128)(2,1)}) %all-gather.4.cloned.1.call-update) | async-done | bytes 21626896 | tf_op jit(solution)/shard_map/all_gather | solution.py:76
  123.0 3.9 %fusion.3 = f32[256,1536]{1,0:T(8,128)S(1)} fusion(bf16[5,1408,1536]{2,1,0:T(8,128)(2,1)} %all-gather.4.cloned.1.call-done, bf16[260,1408]{1,0:T(8,128)(2,1)} %fusion.19), kind=kOutput, calls=%fused_computation.7 | convolution fusion | flops 1107296256 | bytes 6619136 | tf_op jit(solution)/shard_map/dot_general | solution.py:38
  126.9 3.7 %fusion.7 = f32[256,1536]{1,0:T(8,128)S(1)} fusion(f32[256,1536]{1,0:T(8,128)S(1)} %fusion.3, bf16[5,1408,1536]{2,1,0:T(8,128)(2,1)} %all-gather.4.cloned.1.call-done, bf16[260,1408]{1,0:T(8,128)(2,1)S(1)} %copy-done.2), kind=kOutput, calls=%fused_computation.13 | convolution fusion | flops 1107689472 | bytes 8192000 | tf_op jit(solution)/shard_map/dot_general | solution.py:38
  130.6 3.6 %fusion.8 = f32[256,1536]{1,0:T(8,128)S(1)} fusion(f32[256,1536]{1,0:T(8,128)S(1)} %fusion.7, bf16[5,1408,1536]{2,1,0:T(8,128)(2,1)} %all-gather.4.cloned.1.call-done, bf16[260,1408]{1,0:T(8,128)(2,1)S(1)} %copy-done.2), kind=kOutput, calls=%fused_computation.14 | convolution fusion | flops 1107689472 | bytes 8192000 | tf_op jit(solution)/shard_map/dot_general | solution.py:38
  134.3 3.7 %fusion.9 = f32[256,1536]{1,0:T(8,128)S(1)} fusion(f32[256,1536]{1,0:T(8,128)S(1)} %fusion.8, bf16[5,1408,1536]{2,1,0:T(8,128)(2,1)} %all-gather.4.cloned.1.call-done, bf16[260,1408]{1,0:T(8,128)(2,1)S(1)} %copy-done.2), kind=kOutput, calls=%fused_computation.15 | convolution fusion | flops 1107689472 | bytes 8192000 | tf_op jit(solution)/shard_map/dot_general | solution.py:38
  138.0 4.6 %fusion.11 = bf16[256,1536]{1,0:T(8,128)(2,1)} fusion(f32[256,1536]{1,0:T(8,128)S(1)} %fusion.9, bf16[5,1408,1536]{2,1,0:T(8,128)(2,1)} %all-gather.4.cloned.1.call-done, bf16[256,1408]{1,0:T(8,128)(2,1)S(1)} %bitcast.77, bf16[260,1408]{1,0:T(8,128)(2,1)S(1)} %copy-done.2), kind=kOutput, calls=%fused_computation.17 | convolution fusion | flops 1108869120 | bytes 8126464 | tf_op jit(solution)/shard_map/dot_general | solution.py:38
  142.6 2.8 reshape.58
  145.5 3.0 reduce_max.9
  150.7 8.9 %all-gather.1 = bf16[64,128]{1,0:T(8,128)(2,1)S(1)} all-gather(bf16[8,128]{1,0:T(8,128)(2,1)S(1)} %get-tuple-element.15), channel_id=3, replica_groups=mesh['dp'=4,'seq'=4,'mp'=2] {'seq','mp'}, dimensions={0}, use_global_device_ids=true | all-gather | bytes 18432 | tf_op jit(solution)/shard_map/all_gather | solution.py:101
  160.9 4.0 %all-to-all-start = ((bf16[1,8,64,128]{3,1,0,2:T(8,128)(2,1)}), bf16[1,8,64,128]{3,1,0,2:T(8,128)(2,1)}, u32[]{:S(2)}, u32[]{:S(2)}) async-start(bf16[1,8,64,128]{3,1,0,2:T(8,128)(2,1)} %fusion.69), calls=%async_computation | async-start | bytes 262144 | tf_op jit(solution)/shard_map/all_to_all | solution.py:107
  165.7 1.7 convolution_convert_fusion
  167.4 11.9 %all-gather = bf16[1024,320]{0,1:T(8,128)(2,1)} all-gather(bf16[128,320]{0,1:T(8,128)(2,1)S(1)} %convolution_convert_fusion), channel_id=2, replica_groups=mesh['dp'=4,'seq'=4,'mp'=2] {'seq','mp'}, dimensions={0}, use_global_device_ids=true | all-gather | bytes 737280 | tf_op jit(solution)/shard_map/all_gather | solution.py:100
  180.6 1.8 reshape.59
  182.4 2.4 fusion.5
  184.8 2.2 fusion.55
  187.0 2.0 copy.23
  189.0 2.3 reshape.60
  191.2 4.0 %fusion.13 = bf16[1,128,1536]{2,1,0:T(8,128)(2,1)} fusion(bf16[128,1536]{1,0:T(8,128)(2,1)} %reshape.60, bf16[1536,1536]{1,0:T(8,128)(2,1)} %param.17, bf16[128,1536]{1,0:T(8,128)(2,1)S(1)} %reduce_max.9), kind=kOutput, calls=%fused_computation.20 | convolution fusion | flops 604569600 | bytes 5898240 | tf_op jit(solution)/shard_map/dot_general | solution.py:128
  196.2 1.8 convolution_bitcast_fusion.1
  198.9 116.8 %all-reduce.3.cloned.1.call-done = f32[128,128]{1,0:T(8,128)} async-done(((f32[128,128]{1,0:T(8,128)}), f32[128,128]{1,0:T(8,128)}) %all-reduce.3.cloned.1.call-update) | async-done | bytes 65552 | tf_op jit(solution)/shard_map/psum | solution.py:115
  315.8 1.5 copy.34
  (45 shorter events, 11.9 us)
Async XLA Ops:
  7.2 172.1 %copy-start = (bf16[1536,1024]{1,0:T(8,128)(2,1)S(1)}, bf16[1536,1024]{1,0:T(8,128)(2,1)}, u32[]{:S(2)}) copy-start(bf16[1536,1024]{1,0:T(8,128)(2,1)} %param.14) | copy-start | bytes 9437188
  7.2 5.3 %copy-start.10 = (f32[8]{0:T(128)S(1)}, f32[8]{0:T(128)}, u32[]{:S(2)}) copy-start(f32[8]{0:T(128)} %param.16) | copy-start | bytes 100
  7.2 115.8 %all-gather.4.cloned.1.call-start = ((), (), s32[]{:S(2)}) async-start(), calls=%async_computation.1 | async-start | bytes 24330240 | tf_op jit(solution)/shard_map/all_gather | solution.py:76
  8.8 3.8 %collective-permute-start = (bf16[1,2,1408]{2,1,0:T(2,128)(2,1)S(1)}, bf16[1,2,1408]{2,1,0:T(2,128)(2,1)S(1)}, u32[]{:S(2)}, u32[]{:S(2)}) collective-permute-start(bf16[1,2,1408]{2,1,0:T(2,128)(2,1)S(1)} %get-tuple-element.12), channel_id=1, source_target_pairs={{0,1},{1,2},{2,3},{3,4},{4,5},{5,6},{6,7},{8,9},{9,10},{10,11},{11... | collective-permute-start | bytes 16904 | tf_op jit(solution)/shard_map/ppermute | solution.py:22
  11.2 5.2 %collective-permute-start.1 = (bf16[1,2,1408]{2,1,0:T(2,128)(2,1)S(1)}, bf16[1,2,1408]{2,1,0:T(2,128)(2,1)S(1)}, u32[]{:S(2)}, u32[]{:S(2)}) collective-permute-start(bf16[1,2,1408]{2,1,0:T(2,128)(2,1)S(1)} %get-tuple-element.13), channel_id=1, source_target_pairs={{1,0},{2,1},{3,2},{4,3},{5,4},{6,5},{7,6},{9,8},{10,9},{11,10},{12... | collective-permute-start | bytes 16904 | tf_op jit(solution)/shard_map/ppermute | solution.py:23
  123.0 3.9 %copy-start.2 = (bf16[260,1408]{1,0:T(8,128)(2,1)S(1)}, bf16[260,1408]{1,0:T(8,128)(2,1)}, u32[]{:S(2)}) copy-start(bf16[260,1408]{1,0:T(8,128)(2,1)} %fusion.19) | copy-start | bytes 2196484
  134.3 3.7 %copy-start.1 = (bf16[1,256,1408]{2,1,0:T(8,128)(2,1)S(1)}, bf16[1,256,1408]{2,1,0:T(8,128)(2,1)}, u32[]{:S(2)}) copy-start(bf16[1,256,1408]{2,1,0:T(8,128)(2,1)} %param.11) | copy-start | bytes 2162692
  145.5 20.2 %copy-start.9 = (f32[1536]{0:T(1024)S(1)}, f32[1536]{0:T(1024)}, u32[]{:S(2)}) copy-start(f32[1536]{0:T(1024)} %param.13) | copy-start | bytes 18436
  148.5 11.7 %copy-start.4 = (bf16[1,8,64,128]{3,2,1,0:T(8,128)(2,1)S(1)}, bf16[1,8,64,128]{3,2,1,0:T(8,128)(2,1)}, u32[]{:S(2)}) copy-start(bf16[1,8,64,128]{3,2,1,0:T(8,128)(2,1)} %param.19) | copy-start | bytes 393220
  159.6 0.6 copy-start.6
  160.9 34.3 %all-to-all-start = ((bf16[1,8,64,128]{3,1,0,2:T(8,128)(2,1)}), bf16[1,8,64,128]{3,1,0,2:T(8,128)(2,1)}, u32[]{:S(2)}, u32[]{:S(2)}) async-start(bf16[1,8,64,128]{3,1,0,2:T(8,128)(2,1)} %fusion.69), calls=%async_computation | async-start | bytes 262144 | tf_op jit(solution)/shard_map/all_to_all | solution.py:107
  165.0 150.8 %all-reduce.3.cloned.1.call-start = ((), (), s32[]{:S(2)}) async-start(), calls=%async_computation.2 | async-start | bytes 131072 | tf_op jit(solution)/shard_map/psum | solution.py:115
  182.4 2.4 copy-start.3
  195.2 2.8 copy-start.5
  195.2 2.8 copy-start.7
  195.3 2.8 copy-start.8
Sparse Core Ops, SparseCore 0:
  9.9 113.0 all-gather.3
  198.1 117.5 all-reduce.2
where the time goes:
time: 326 us; the launch traced here: 324 us
  waiting for transfers between devices  221 us (68%)
  matrix products  34.5 us (11%)
  blocking collectives  20.7 us (6%)
  between operations  14.2 us (4%)
  local copies, waits for them, and re-layouts  13.6 us (4%)
  other arithmetic  12.7 us (4%)
  starting transfers between devices  7.72 us (2%)
    psum x1, waiting for transfers between devices, per_device(): grad_flip = lax.psum(grad_term, ('dp', 'seq', 'mp'))  117 us
    all_gather x1, waiting for transfers between devices, per_device(): lax.all_gather(conv_weight, ('seq', 'mp'), axis=1, tiled=True)  99.2 us
    dot_general x5, matrix products, tap_sum(): jnp.dot(source[lag_index:lag_index + out_rows], filter_rows[lag_index], p...  19.5 us
    all_gather x1, blocking collectives, per_device(): lax.all_gather(keyvals[None], ('seq', 'mp'), axis=1, tiled=True)  11.9 us
    all_gather x1, blocking collectives, per_device(): lax.all_gather(pair_k[None], ('seq', 'mp'), axis=1, tiled=True)  8.85 us
  transfers between devices with their start and end apart: 5, of which 3 were waited for; matrix products, arithmetic and copies ran while one was open for 9% of the time, Pallas kernels for 0%

commit v1 on v0

v1 whole, which is shorter than its diff:
```python
import functools
import math

import jax
import jax.numpy as jnp
from jax import lax
from jax.experimental import pallas as pl
from jax.experimental.pallas import tpu as pltpu
from jax.sharding import PartitionSpec as P

PAIR_POOL = 16
norm_eps = 1e-06
logit_cap = 50.0
MIB = 1 << 20
GROUP = ("seq", "mp")
f32, bf16 = jnp.float32, jnp.bfloat16


def whole_vmem():
    return pl.BlockSpec(memory_space=pltpu.VMEM)


def smem():
    return pl.BlockSpec(memory_space=pltpu.SMEM)


def tree_sum(terms):
    while len(terms) > 1:
        terms = [terms[i] + terms[i + 1] for i in range(0, len(terms), 2)]
    return terms[0]


def flipped_bits(mask, bits):
    return sum(((mask >> b) & 1) << (bits - 1 - b) for b in range(bits))


def hop_pairs(chips, core_masks, core_flip):
    pairs = []
    for chip in range(chips):
        for core in range(2):
            target = (chip ^ core_masks[core]) * 2 + (core ^ core_flip)
            pairs.append((chip * 2 + core, target))
    return pairs


def prep_kernel(chips, width, order_ref, order2_ref, feat_ref, raw_ref, *rest):
    block_refs = rest[:chips]
    edge_refs = rest[chips : 2 * chips]
    wide, split = rest[2 * chips :]
    rows = feat_ref.shape[0]
    half = rows // 2
    target = lax.broadcasted_iota(jnp.int32, (rows, rows), 0)
    source = lax.broadcasted_iota(jnp.int32, (rows, rows), 1)
    wanted = jnp.where(target < half, 2 * target, 2 * (target - half) + 1)
    pick = jnp.where(source == wanted, 1.0, 0.0).astype(bf16)
    wide[...] = jnp.dot(pick, feat_ref[...], preferred_element_type=f32)
    step = 16

    def body(i, carry):
        at = pl.ds(pl.multiple_of(i * step, step), step)
        x = wide[at, :]
        raw_ref[at, :] = x.astype(bf16)
        v = x * lax.rsqrt(jnp.mean(x * x, axis=-1, keepdims=True) + norm_eps)
        g = (0.5 * v) * (1.0 + lax.erf(v * math.sqrt(0.5)))
        g = g.astype(bf16)
        for q in range(chips):
            split[q, at, :] = g[:, q * width : (q + 1) * width]
        return carry

    lax.fori_loop(0, rows // step, body, 0)
    for k in range(chips):
        block_refs[k][...] = split[order_ref[k]]
        strip = split[order2_ref[k]]
        head = strip[0:16].astype(f32)
        head2 = strip[half : half + 16].astype(f32)
        tail = strip[half - 16 : half].astype(f32)
        tail2 = strip[rows - 16 : rows].astype(f32)
        edge_refs[k][...] = jnp.concatenate(
            [head[0:1], head2[0:1], tail[15:16], tail2[15:16], jnp.zeros((4, width), f32)], axis=0
        )


def prep(features, order, order2, chips):
    rows, channels = features.shape
    width = channels // chips
    outs = [jax.ShapeDtypeStruct((rows, channels), bf16)]
    outs += [jax.ShapeDtypeStruct((rows, width), bf16)] * chips
    outs += [jax.ShapeDtypeStruct((8, width), f32)] * chips
    got = pl.pallas_call(
        functools.partial(prep_kernel, chips, width),
        name="prep",
        out_shape=outs,
        in_specs=[smem(), smem(), whole_vmem()],
        out_specs=[whole_vmem()] * len(outs),
        scratch_shapes=[
            pltpu.VMEM((rows, channels), f32),
            pltpu.VMEM((chips, rows, width), bf16),
        ],
        compiler_params=pltpu.CompilerParams(vmem_limit_bytes=16 * MIB),
        cost_estimate=pl.CostEstimate(
            flops=40 * rows * channels, bytes_accessed=6 * rows * channels, transcendentals=0
        ),
    )(order, order2, features)
    return got[0], got[1 : 1 + chips], got[1 + chips :]


def conv_kernel(chips, taps, where_ref, block_ref, *rest):
    edge_refs = rest[:chips]
    weight_ref, out_ref, cols = rest[chips:]
    rows, width = block_ref.shape
    half = rows // 2

    @pl.when(pl.program_id(0) == 0)
    def _():
        before = jnp.zeros((8, width), f32)
        after = jnp.zeros((8, width), f32)
        for k in range(chips):
            strip = edge_refs[k][...]
            before = jnp.where(where_ref[0] == k, strip, before)
            after = jnp.where(where_ref[1] == k, strip, after)
        even = block_ref[0:half, :].astype(f32)
        odd = block_ref[half:rows, :].astype(f32)
        row = lax.broadcasted_iota(jnp.int32, (half, width), 0)

        def back(v, strip_row):
            return jnp.where(row == 0, before[strip_row : strip_row + 1], pltpu.roll(v, 1, 0))

        def ahead(v, strip_row):
            return jnp.where(
                row == half - 1, after[strip_row : strip_row + 1], pltpu.roll(v, half - 1, 0)
            )

        lagged = [back(even, 2), back(odd, 3), even, odd, ahead(even, 0), ahead(odd, 1)]
        lagged = [v.astype(bf16) for v in lagged]
        for k in range(taps):
            cols[0:half, k * width : (k + 1) * width] = lagged[k]
            cols[half:rows, k * width : (k + 1) * width] = lagged[k + 1]

    out_ref[...] = jnp.dot(cols[...], weight_ref[...], preferred_element_type=f32).astype(
        out_ref.dtype
    )


def conv(block, edges, weight, where, taps, out_dtype):
    rows, width = block.shape
    depth, model_dim = weight.shape
    chips = len(edges)
    tile = 512
    return pl.pallas_call(
        functools.partial(conv_kernel, chips, taps),
        name="conv",
        grid=(model_dim // tile,),
        out_shape=jax.ShapeDtypeStruct((rows, model_dim), out_dtype),
        in_specs=[smem()]
        + [whole_vmem()] * (1 + chips)
        + [pl.BlockSpec((depth, tile), lambda n: (0, n))],
        out_specs=pl.BlockSpec((rows, tile), lambda n: (0, n)),
        scratch_shapes=[pltpu.VMEM((rows, depth), bf16)],
        compiler_params=pltpu.CompilerParams(vmem_limit_bytes=20 * MIB),
        cost_estimate=pl.CostEstimate(
            flops=2 * rows * depth * model_dim,
            bytes_accessed=2 * depth * model_dim,
            transcendentals=0,
        ),
    )(where, block, *edges, weight)


def encode_kernel(
    arrivals, raw_ref, gain_ref, keyval_weight_ref, pair_weight_ref, own_ref, *rest
):
    come_refs = rest[:arrivals]
    encoded_ref, normed_ref, keyval_ref, feats_ref = rest[arrivals:]
    rows, model_dim = own_ref.shape
    half = rows // 2
    channels = raw_ref.shape[1]
    total = own_ref[...]
    for ref in come_refs:
        total = total + ref[...].astype(f32)
    skip = raw_ref[...].astype(f32)
    if channels < model_dim:
        skip = jnp.concatenate([skip, jnp.zeros((rows, model_dim - channels), f32)], axis=1)
    total = total + skip
    encoded = jnp.maximum(total[:half], total[half:]).astype(bf16)
    encoded_ref[...] = encoded
    wide = encoded.astype(f32)
    scale = lax.rsqrt(jnp.mean(wide * wide, axis=-1, keepdims=True) + norm_eps)
    normed = (wide * scale * gain_ref[...]).astype(bf16)
    normed_ref[...] = normed
    pairs = half // PAIR_POOL
    at = lax.broadcasted_iota(jnp.int32, (pairs, half), 0)
    of = lax.broadcasted_iota(jnp.int32, (pairs, half), 1) // PAIR_POOL
    spread = jnp.where(at == of, 1.0 / PAIR_POOL, 0.0).astype(bf16)
    pooled = jnp.dot(spread, encoded, preferred_element_type=f32).astype(bf16)
    feats_ref[...] = (
        jnp.dot(pooled, pair_weight_ref[...], preferred_element_type=f32).astype(bf16).astype(f32)
    )
    keyval_ref[...] = jnp.dot(
        normed, keyval_weight_ref[...], preferred_element_type=f32
    ).astype(bf16)


def encode(own, come, raw, gain, keyval_weight, pair_weight):
    rows, model_dim = own.shape
    half = rows // 2
    return pl.pallas_call(
        functools.partial(encode_kernel, len(come)),
        name="encode",
        out_shape=[
            jax.ShapeDtypeStruct((half, model_dim), bf16),
            jax.ShapeDtypeStruct((half, model_dim), bf16),
            jax.ShapeDtypeStruct((half, keyval_weight.shape[1]), bf16),
            jax.ShapeDtypeStruct((half // PAIR_POOL, pair_weight.shape[1]), f32),
        ],
        in_specs=[whole_vmem()] * (5 + len(come)),
        out_specs=[whole_vmem()] * 4,
        compiler_params=pltpu.CompilerParams(vmem_limit_bytes=24 * MIB),
        cost_estimate=pl.CostEstimate(
            flops=2 * half * model_dim * keyval_weight.shape[1],
            bytes_accessed=6 * rows * model_dim,
            transcendentals=0,
        ),
    )(raw, gain, keyval_weight, pair_weight, own, *come)


def query_kernel(normed_ref, weight_ref, scale_ref, out_ref):
    got = jnp.dot(normed_ref[...], weight_ref[...], preferred_element_type=f32)
    out_ref[...] = (got * scale_ref[...]).astype(bf16)


def project_queries(normed, weight, scale_row):
    rows, model_dim = normed.shape
    columns = weight.shape[1]
    tile = 256
    return pl.pallas_call(
        query_kernel,
        name="queries",
        grid=(columns // tile,),
        out_shape=jax.ShapeDtypeStruct((rows, columns), bf16),
        in_specs=[
            whole_vmem(),
            pl.BlockSpec((model_dim, tile), lambda n: (0, n)),
            pl.BlockSpec((1, tile), lambda n: (0, n)),
        ],
        out_specs=pl.BlockSpec((rows, tile), lambda n: (0, n)),
        compiler_params=pltpu.CompilerParams(vmem_limit_bytes=16 * MIB),
        cost_estimate=pl.CostEstimate(
            flops=2 * rows * columns * model_dim,
            bytes_accessed=2 * columns * model_dim,
            transcendentals=0,
        ),
    )(normed, weight, scale_row)


def attend_kernel(parts, heads_step, key_dim, query_ref, encoded_ref, weight_ref, *rest):
    part_refs = rest[:parts]
    out_ref, keys, values, total = rest[parts:]
    rows = query_ref.shape[0]
    span = part_refs[0].shape[0]
    value_dim = values.shape[1]

    @pl.when(pl.program_id(0) == 0)
    def _():
        for k in range(parts):
            got = part_refs[k][...]
            keys[k * span : (k + 1) * span, :] = got[:, :key_dim]
            values[k * span : (k + 1) * span, :] = got[:, key_dim:]
        total[...] = encoded_ref[...].astype(f32)

    queries = query_ref[...]
    queries = jnp.concatenate(
        [queries[:, h * key_dim : (h + 1) * key_dim] for h in range(heads_step)], axis=0
    )
    scores = lax.dot_general(
        queries, keys[...], (((1,), (1,)), ((), ())), preferred_element_type=f32
    )
    weights = jnp.exp(logit_cap * jnp.tanh(scores * (1.0 / logit_cap)))
    sums = jnp.sum(weights, axis=-1, keepdims=True)
    mixed = jnp.dot(weights.astype(bf16), values[...], preferred_element_type=f32) / sums
    mixed = mixed.astype(bf16)
    update = total[...]
    for h in range(heads_step):
        update = update + jnp.dot(
            mixed[h * rows : (h + 1) * rows],
            weight_ref[h * value_dim : (h + 1) * value_dim, :],
            preferred_element_type=f32,
        )
    total[...] = update

    @pl.when(pl.program_id(0) == pl.num_programs(0) - 1)
    def _():
        out_ref[...] = update.astype(bf16)


def attend(queries, encoded, output_weight, parts, heads):
    rows, model_dim = encoded.shape
    key_dim = queries.shape[1] // heads
    value_dim = output_weight.shape[0] // heads
    span = parts[0].shape[0]
    total_keys = span * len(parts)
    heads_step = 2
    return pl.pallas_call(
        functools.partial(attend_kernel, len(parts), heads_step, key_dim),
        name="attend",
        grid=(heads // heads_step,),
        out_shape=jax.ShapeDtypeStruct((rows, model_dim), bf16),
        in_specs=[
            pl.BlockSpec((rows, heads_step * key_dim), lambda h: (0, h)),
            whole_vmem(),
            pl.BlockSpec((heads_step * value_dim, model_dim), lambda h: (h, 0)),
        ]
        + [whole_vmem()] * len(parts),
        out_specs=pl.BlockSpec((rows, model_dim), lambda h: (0, 0)),
        scratch_shapes=[
            pltpu.VMEM((total_keys, key_dim), bf16),
            pltpu.VMEM((total_keys, value_dim), bf16),
            pltpu.VMEM((rows, model_dim), f32),
        ],
        compiler_params=pltpu.CompilerParams(vmem_limit_bytes=32 * MIB),
        cost_estimate=pl.CostEstimate(
            flops=2 * rows * heads * (total_keys * (key_dim + value_dim) + value_dim * model_dim),
            bytes_accessed=2 * heads * value_dim * model_dim,
            transcendentals=2 * rows * heads * total_keys,
        ),
    )(queries, encoded, output_weight, *parts)


def pair_kernel(parts, slot_ref, input_ref, turned_ref, cotangent_ref, flip_ref, *rest):
    feat_refs = rest[:parts]
    out_ref, grad_ref, stack, summed, flipped = rest[parts:]
    rows, columns, dim = input_ref.shape
    for k in range(parts):
        stack[k] = feat_refs[k][...]
    every = jnp.concatenate([stack[slot_ref[b]] for b in range(parts)], axis=0)
    own = feat_refs[0][...]
    for i in range(rows):
        at = pl.ds(i * columns, columns)
        mine = own[i : i + 1]
        summed[at, :] = (
            input_ref[i].astype(f32) + mine[:, :dim] * every[:, dim:]
        ).astype(bf16)
        flipped[at, :] = (
            turned_ref[i].astype(f32) + every[:, :dim] * mine[:, dim:]
        ).astype(bf16)
    update = jnp.dot(flipped[...], flip_ref[...], preferred_element_type=f32)
    update = update + summed[...].astype(f32)
    out_ref[...] = update.astype(bf16).reshape(rows, columns, dim)
    grad_ref[...] = lax.dot_general(
        flipped[...],
        cotangent_ref[...].reshape(rows * columns, dim),
        (((0,), (0,)), ((), ())),
        preferred_element_type=f32,
    )


def pair_update(pair_input, turned, cotangent, flip_weight, feats, slots):
    rows, columns, dim = pair_input.shape
    parts = len(feats)
    return pl.pallas_call(
        functools.partial(pair_kernel, parts),
        name="pair",
        out_shape=[
            jax.ShapeDtypeStruct((rows, columns, dim), bf16),
            jax.ShapeDtypeStruct((dim, dim), f32),
        ],
        in_specs=[smem()] + [whole_vmem()] * (4 + parts),
        out_specs=[whole_vmem()] * 2,
        scratch_shapes=[
            pltpu.VMEM((parts, rows, 2 * dim), f32),
            pltpu.VMEM((rows * columns, dim), bf16),
            pltpu.VMEM((rows * columns, dim), bf16),
        ],
        compiler_params=pltpu.CompilerParams(vmem_limit_bytes=24 * MIB),
        cost_estimate=pl.CostEstimate(
            flops=4 * rows * columns * dim * dim,
            bytes_accessed=8 * rows * columns * dim,
            transcendentals=0,
        ),
    )(slots, pair_input, turned, cotangent, flip_weight, *feats)


def per_device(
    features,
    conv_weight,
    norm_gain,
    query_weight,
    keyval_weight,
    head_scale,
    output_weight,
    pair_weight,
    pair_input,
    flip_weight,
    pair_cotangent,
):
    chips = lax.axis_size("seq")
    bits = chips.bit_length() - 1
    windows = lax.axis_size("dp")
    taps = conv_weight.shape[0]
    model_dim = output_weight.shape[1]
    heads = head_scale.shape[0]
    key_dim = query_weight.shape[1] // heads
    chip = lax.axis_index("seq")
    core = lax.axis_index("mp")

    masks = [(k, flipped_bits(k, bits)) for k in range(chips)]
    plain = jnp.arange(chips, dtype=jnp.int32)
    mirrored = jnp.array([k[1] for k in masks], jnp.int32)
    owner = chip ^ jnp.where(core == 0, plain, mirrored)
    order2 = chip ^ plain

    def send(value, mask, flip=0):
        cores = mask if isinstance(mask, tuple) else (mask, mask)
        return lax.ppermute(value, GROUP, hop_pairs(chips, cores, flip))

    def spots(k):
        place = owner[k]
        left = jnp.where(core == 0, place - 1, place)
        right = jnp.where(core == 0, place, place + 1)
        left = jnp.where(left >= 0, left ^ chip, -1)
        right = jnp.where(right < chips, right ^ chip, -1)
        return jnp.stack([left, right]).astype(jnp.int32)

    weight = lax.all_gather(conv_weight, "mp", axis=1, tiled=True)
    weight = weight.reshape(-1, model_dim)

    raw, blocks, strips = prep(features[0], owner, order2, chips)
    edges = [send(strips[k], k, 1) for k in range(chips)]
    held = {0: blocks[0]}
    for k in range(chips - 1, 0, -1):
        held[k] = send(blocks[k], masks[k])

    order = sorted(range(1, chips), key=lambda k: ([(k >> b) & 1 for b in range(bits)], k))[::-1]
    partial = {}
    for k in order:
        first = k & 1
        partial[k] = conv(held[k], edges, weight, spots(k), taps, bf16 if first else f32)
    partial[0] = conv(held[0], edges, weight, spots(0), taps, f32)
    arrived = []
    for b in range(bits):
        bit = 1 << b
        leaving = [k for k in order if k in partial and k & bit]
        got = {k ^ bit: send(partial.pop(k).astype(bf16), masks[bit]) for k in leaving}
        for k, value in got.items():
            if k == 0:
                arrived.append(value)
            else:
                partial[k] = partial[k] + value.astype(f32)

    encoded, normed, keyval, feats = encode(
        partial[0], arrived, raw, norm_gain[None], keyval_weight, pair_weight
    )

    all_feats = [feats] + [
        send(feats, k >> 1, k & 1) for k in range(1, 2 * chips)
    ]
    keyvals = [keyval] + [send(keyval, k >> 1, k & 1) for k in range(1, 2 * chips)]
    scale_row = jnp.repeat(head_scale, key_dim) / math.sqrt(key_dim)
    queries = project_queries(normed, query_weight, scale_row[None])

    turned = lax.all_to_all(pair_input[0], GROUP, split_axis=1, concat_axis=0, tiled=True)
    turned = jnp.swapaxes(turned, 0, 1)
    places = jnp.arange(2 * chips, dtype=jnp.int32)
    slots = ((places >> 1) ^ chip) * 2 + ((places & 1) ^ core)
    pair_out, grad = pair_update(
        pair_input[0], turned, pair_cotangent[0], flip_weight, all_feats, slots.astype(jnp.int32)
    )
    grad = tree_sum([grad] + [send(grad, k >> 1, k & 1) for k in range(1, 2 * chips)])
    grad = tree_sum(
        [grad]
        + [
            lax.ppermute(grad, "dp", [(w, w ^ k) for w in range(windows)])
            for k in range(1, windows)
        ]
    )
    block_out = attend(queries, encoded, output_weight, keyvals, heads)
    return (block_out[None], pair_out[None], grad)


def solution(mesh):
    placed = (
        P("dp", ("seq", "mp"), None),
        P(None, ("seq", "mp"), None),
        P(),
        P(),
        P(),
        P(),
        P(),
        P(),
        P("dp", ("seq", "mp"), None, None),
        P(),
        P("dp", ("seq", "mp"), None, None),
    )
    return jax.shard_map(
        per_device,
        mesh=mesh,
        in_specs=placed,
        out_specs=(P("dp", ("seq", "mp"), None), P("dp", ("seq", "mp"), None, None), P()),
        check_vma=False,
    )
```

time: 326 us -> 140 us (0.43)
  waiting for transfers between devices: 221 us -> 17.8 us
  starting transfers between devices: 7.72 us -> 44.3 us
  matrix products: 34.5 us -> 0 us
  Pallas kernels: 0 us -> 26 us
  blocking collectives: 20.7 us -> 0 us
  between operations: 14.2 us -> 24.5 us
  local copies, waits for them, and re-layouts: 13.6 us -> 23.1 us
  other arithmetic: 12.7 us -> 3.23 us
    psum x1 -> x0, waiting for transfers between devices: 117 us -> none  [per_device(): grad_flip = lax.psum(grad_term, ('dp', 'seq', 'mp'))]
    all_gather x1, waiting for transfers between devices: 99.2 us -> 1.16 us  [per_device(): weight = lax.all_gather(conv_weight, 'mp', axis=1, tiled=True)]
    ppermute x2 -> x34, starting transfers between devices: 3.65 us -> 40.9 us  [the longest x31 33.3 us: send(): return lax.ppermute(value, GROUP, hop_pairs(chips, cores, flip))]
    dot_general x13 -> x0, matrix products: 34.5 us -> none  [the longest x5 19.5 us: tap_sum(): jnp.dot(source[lag_index:lag_index + out_rows], filter_rows[lag_index], p...]
    pallas_call x0 -> x9, Pallas kernels: none -> 26 us  [the longest x4 12.4 us: conv(): pl.pallas_call(functools.partial(conv_kernel, chips, taps), name='conv',...]
    all_gather x2 -> x0, blocking collectives: 20.7 us -> none  [the longest x1 11.9 us: per_device(): lax.all_gather(keyvals[None], ('seq', 'mp'), axis=1, tiled=True)]
    unnamed x24 -> x51, local copies, waits for them, and re-layouts: 2.81 us -> 20.3 us
    ppermute x2 -> x34, waiting for transfers between devices: 3.78 us -> 16 us  [the longest x31 15.9 us: send(): return lax.ppermute(value, GROUP, hop_pairs(chips, cores, flip))]
  transfers between devices with their start and end apart: 5 -> 36, of which waited for: 3 -> 9; matrix products, arithmetic and copies ran while one was open for 9% -> 5% of each run, Pallas kernels for 0% -> 15%
where the time goes in v1:
time: 140 us; the launch traced here: 139 us
  starting transfers between devices  44.3 us (32%)
  Pallas kernels  26 us (19%)
  between operations  24.5 us (18%)
  local copies, waits for them, and re-layouts  23.1 us (16%)
  waiting for transfers between devices  17.8 us (13%)
  other arithmetic  3.23 us (2%)
    ppermute x31, starting transfers between devices, send(): return lax.ppermute(value, GROUP, hop_pairs(chips, cores, flip))  33.3 us
    unnamed x51, local copies, waits for them, and re-layouts  20.3 us
    ppermute x31, waiting for transfers between devices, send(): return lax.ppermute(value, GROUP, hop_pairs(chips, cores, flip))  15.9 us
    pallas_call x4, Pallas kernels, conv(): pl.pallas_call(functools.partial(conv_kernel, chips, taps), name='conv',...  12.4 us
    ppermute x3, starting transfers between devices, per_device(): lax.ppermute(grad, 'dp', [(w, w ^ k) for w in range(windows)])  7.6 us
    pallas_call x1, Pallas kernels, attend(): pl.pallas_call(functools.partial(attend_kernel, len(parts), heads_step, k...  5.42 us
    pallas_call x1, Pallas kernels, prep(): pl.pallas_call(functools.partial(prep_kernel, chips, width), name='prep',...  4.11 us
    all_to_all x1, starting transfers between devices, per_device(): lax.all_to_all(pair_input[0], GROUP, split_axis=1, concat_axis=0, tiled=T...  3.37 us
  transfers between devices with their start and end apart: 36, of which 9 were waited for; matrix products, arithmetic and copies ran while one was open for 5% of the time, Pallas kernels for 15%

profile of v1, /device:TPU:0, one launch (start us, length us, event | category | flops | bytes accessed | tf_op | source)
XLA Modules:
  0.0 138.9 jit_solution(5797702324038102048)
XLA Ops:
  8.3 4.1 %prep.1 = (bf16[256,1408]{1,0:T(8,128)(2,1)S(1)}, bf16[256,352]{1,0:T(8,128)(2,1)S(1)}, bf16[256,352]{1,0:T(8,128)(2,1)S(1)}, bf16[256,352]{1,0:T(8,128)(2,1)S(1...) custom-call(s32[4]{0:T(128)S(1)} %get-tuple-element.37.order_ref, ...), custom_call_target="tpu_custom_call" | custom-call | flops 14417920 | bytes 2162688 | tf_op jit(solution)/shard_map/prep/pallas_call | solution.py:89
  14.5 2.6 %collective-permute-start.1 = (f32[8,352]{1,0:T(8,128)S(1)}, f32[8,352]{1,0:T(8,128)S(1)}, u32[]{:S(2)}, u32[]{:S(2)}) collective-permute-start(f32[8,352]{1,0:T(8,128)S(1)} %get-tuple-element.21), channel_id=1, source_target_pairs={{0,3},{1,2},{2,1},{3,0},{4,7},{5,6},{6,5},{7,4},{8,11},{9,10},{10,... | collective-permute-start | bytes 33800 | tf_op jit(solution)/shard_map/ppermute | solution.py:412
  18.2 3.0 %collective-permute-start.7 = (bf16[256,352]{1,0:T(8,128)(2,1)S(1)}, bf16[256,352]{1,0:T(8,128)(2,1)S(1)}, u32[]{:S(2)}, u32[]{:S(2)}) collective-permute-start(bf16[256,352]{1,0:T(8,128)(2,1)S(1)} %get-tuple-element.26), channel_id=1, source_target_pairs={{0,6},{1,7},{2,4},{3,5},{4,2},{5,3},{6,0},{7,1},{8,14},{9,15},{10,... | collective-permute-start | bytes 540680 | tf_op jit(solution)/shard_map/ppermute | solution.py:412
  24.7 1.9 %collective-permute-done.7.block_ref = bf16[256,352]{1,0:T(8,128)(2,1)S(1)} collective-permute-done((bf16[256,352]{1,0:T(8,128)(2,1)S(1)}, bf16[256,352]{1,0:T(8,128)(2,1)S(1)}, u32[]{:S(2)}, u32[]{:S(2)}) %collective-permute-start.7) | collective-permute-done | bytes 180256 | tf_op jit(solution)/shard_map/ppermute | solution.py:412
  27.8 2.5 %copy-done = bf16[5,352,1536]{2,1,0:T(8,128)(2,1)S(1)} copy-done((bf16[5,352,1536]{2,1,0:T(8,128)(2,1)S(1)}, bf16[5,352,1536]{2,1,0:T(8,128)(2,1)}, u32[]{:S(2)}) %copy-start) | copy-done | bytes 5406744
  30.3 3.1 %conv.7 = bf16[256,1536]{1,0:T(8,128)(2,1)S(1)} custom-call(s32[2]{0:T(128)S(1)} %pad_add_fusion.3.where_ref, bf16[256,352]{1,0:T(8,128)(2,1)S(1)} %collective-permute-done.7.block_ref, f32[8,352]{1,0:T(8,128)S(1)} %collective-permute-done.rest_0_, f32[8,352]{1,0:T(8,128)S(1)} %collective-permute-done.1.rest_1_, ...), custom_call_target="tpu_custom_call" | custom-call | flops 1384120320 | bytes 5406720 | tf_op jit(solution)/shard_map/conv/pallas_call | solution.py:149
  33.4 1.8 %collective-permute-start.8 = (bf16[256,1536]{1,0:T(8,128)(2,1)S(1)}, bf16[256,1536]{1,0:T(8,128)(2,1)}, u32[]{:S(2)}, u32[]{:S(2)}) collective-permute-start(bf16[256,1536]{1,0:T(8,128)(2,1)S(1)} %conv.7), channel_id=1, source_target_pairs={{0,2},{1,5},{2,0},{3,7},{4,6},{5,1},{6,4},{7,3},{8,10},{9,13},{10,... | collective-permute-start | bytes 2359304 | tf_op jit(solution)/shard_map/ppermute | solution.py:412
  42.4 7.3 %collective-permute-done.4.block_ref = bf16[256,352]{1,0:T(8,128)(2,1)S(1)} collective-permute-done((bf16[256,352]{1,0:T(8,128)(2,1)S(1)}, bf16[256,352]{1,0:T(8,128)(2,1)S(1)}, u32[]{:S(2)}, u32[]{:S(2)}) %collective-permute-start.4) | collective-permute-done | bytes 180256 | tf_op jit(solution)/shard_map/ppermute | solution.py:412
  49.6 2.5 %copy-done.1 = bf16[5,352,1536]{2,1,0:T(8,128)(2,1)S(1)} copy-done((bf16[5,352,1536]{2,1,0:T(8,128)(2,1)S(1)}, bf16[5,352,1536]{2,1,0:T(8,128)(2,1)}, u32[]{:S(2)}) %copy-start.1) | copy-done | bytes 5406744
  52.2 3.1 %conv.5 = bf16[256,1536]{1,0:T(8,128)(2,1)S(1)} custom-call(s32[2]{0:T(128)S(1)} %pad_add_fusion.1.where_ref, bf16[256,352]{1,0:T(8,128)(2,1)S(1)} %collective-permute-done.4.block_ref, f32[8,352]{1,0:T(8,128)S(1)} %collective-permute-done.rest_0_, f32[8,352]{1,0:T(8,128)S(1)} %collective-permute-done.1.rest_1_, ...), custom_call_target="tpu_custom_call" | custom-call | flops 1384120320 | bytes 5406720 | tf_op jit(solution)/shard_map/conv/pallas_call | solution.py:149
  55.2 1.8 %collective-permute-start.5 = (bf16[256,1536]{1,0:T(8,128)(2,1)S(1)}, bf16[256,1536]{1,0:T(8,128)(2,1)S(1)}, u32[]{:S(2)}, u32[]{:S(2)}) collective-permute-start(bf16[256,1536]{1,0:T(8,128)(2,1)S(1)} %conv.5), channel_id=1, source_target_pairs={{0,2},{1,5},{2,0},{3,7},{4,6},{5,1},{6,4},{7,3},{8,10},{9,13},{10,... | collective-permute-start | bytes 2359304 | tf_op jit(solution)/shard_map/ppermute | solution.py:412
  57.1 3.2 %conv.6 = f32[256,1536]{1,0:T(8,128)S(1)} custom-call(s32[2]{0:T(128)S(1)} %pad_add_fusion.2.where_ref, bf16[256,352]{1,0:T(8,128)(2,1)S(1)} %collective-permute-done.6.block_ref, f32[8,352]{1,0:T(8,128)S(1)} %collective-permute-done.rest_0_, f32[8,352]{1,0:T(8,128)S(1)} %collective-permute-done.1.rest_1_, f32[8,352]{1,0:T(8,128)S(1)} %collective-permute-done.2.rest_2_, ...), custom_call_target="tpu_custom_call" | custom-call | flops 1384120320 | bytes 5406720 | tf_op jit(solution)/shard_map/conv/pallas_call | solution.py:149
  60.2 2.2 %add_convert_fusion = bf16[256,1536]{1,0:T(8,128)(2,1)} fusion(f32[256,1536]{1,0:T(8,128)S(1)} %conv.6, bf16[256,1536]{1,0:T(8,128)(2,1)} %collective-permute-done.8), kind=kLoop, calls=%fused_computation | loop fusion | flops 1179648 | bytes 3145728 | tf_op jit(solution)/shard_map/convert_element_type | solution.py:441
  69.1 2.5 %copy-done.2 = bf16[5,352,1536]{2,1,0:T(8,128)(2,1)S(1)} copy-done((bf16[5,352,1536]{2,1,0:T(8,128)(2,1)S(1)}, bf16[5,352,1536]{2,1,0:T(8,128)(2,1)}, u32[]{:S(2)}) %copy-start.2) | copy-done | bytes 5406744
  74.7 3.2 %conv.4.own_ref = f32[256,1536]{1,0:T(8,128)S(1)} custom-call(s32[2]{0:T(128)S(1)} %pad_add_fusion.where_ref, bf16[256,352]{1,0:T(8,128)(2,1)S(1)} %copy-done.13, f32[8,352]{1,0:T(8,128)S(1)} %collective-permute-done.rest_0_, f32[8,352]{1,0:T(8,128)S(1)} %copy-done.15, f32[8,352]{1,0:T(8,128)S(1)} %copy-done.17, f32[8,352]{1,0:T(8,128)S(1)} %copy-done.19, ...), custom_call_target="tpu_custom_call" | custom-call | flops 1384120320 | bytes 5406720 | tf_op jit(solution)/shard_map/conv/pallas_call | solution.py:149
  80.8 3.4 %all-to-all-start = ((bf16[8,64,128]{2,0,1:T(8,128)(2,1)}), bf16[8,64,128]{2,0,1:T(8,128)(2,1)S(1)}, u32[]{:S(2)}, u32[]{:S(2)}) async-start(bf16[8,64,128]{2,0,1:T(8,128)(2,1)} %copy.18), calls=%async_computation | async-start | bytes 262144 | tf_op jit(solution)/shard_map/all_to_all | solution.py:459
  101.3 1.8 %collective-permute-start.30 = (f32[128,128]{1,0:T(8,128)S(1)}, f32[128,128]{1,0:T(8,128)S(1)}, u32[]{:S(2)}, u32[]{:S(2)}) collective-permute-start(f32[128,128]{1,0:T(8,128)S(1)} %get-tuple-element.32), channel_id=1, source_target_pairs={{0,7},{1,6},{2,5},{3,4},{4,3},{5,2},{6,1},{7,0},{8,15},{9,14},{10,... | collective-permute-start | bytes 196616 | tf_op jit(solution)/shard_map/ppermute | solution.py:412
  103.2 1.9 %copy-done.4 = bf16[1536,1024]{1,0:T(8,128)(2,1)S(1)} copy-done((bf16[1536,1024]{1,0:T(8,128)(2,1)S(1)}, bf16[1536,1024]{1,0:T(8,128)(2,1)}, u32[]{:S(2)}) %copy-start.4) | copy-done | bytes 3145752
  111.2 1.9 %collective-permute-start.16 = (bf16[128,320]{1,0:T(8,128)(2,1)S(1)}, bf16[128,320]{1,0:T(8,128)(2,1)S(1)}, u32[]{:S(2)}, u32[]{:S(2)}) collective-permute-start(bf16[128,320]{1,0:T(8,128)(2,1)S(1)} %get-tuple-element.29.rest_0_), channel_id=1, source_target_pairs={{0,7},{1,6},{2,5},{3,4},{4,3},{5,2},{6,1},{7,0},{8,15},{9,14},{10,... | collective-permute-start | bytes 245768 | tf_op jit(solution)/shard_map/ppermute | solution.py:412
  114.8 2.4 %collective-permute-start.32 = (f32[128,128]{1,0:T(8,128)S(1)}, f32[128,128]{1,0:T(8,128)S(1)}, u32[]{:S(2)}, u32[]{:S(2)}) collective-permute-start(f32[128,128]{1,0:T(8,128)S(1)} %add_add_fusion.1), channel_id=1, source_target_pairs={{0,16},{8,24},{16,0},{24,8},{1,17},{9,25},{17,1},{25,9},{2,18},{10... | collective-permute-start | bytes 196616 | tf_op jit(solution)/shard_map/ppermute | solution.py:470
  117.2 3.0 %collective-permute-done.14.rest_5_ = bf16[128,320]{1,0:T(8,128)(2,1)S(1)} collective-permute-done((bf16[128,320]{1,0:T(8,128)(2,1)S(1)}, bf16[128,320]{1,0:T(8,128)(2,1)S(1)}, u32[]{:S(2)}, u32[]{:S(2)}) %collective-permute-start.14) | collective-permute-done | bytes 81952 | tf_op jit(solution)/shard_map/ppermute | solution.py:412
  120.2 3.5 %collective-permute-start.33 = (f32[128,128]{1,0:T(8,128)S(1)}, f32[128,128]{1,0:T(8,128)S(1)}, u32[]{:S(2)}, u32[]{:S(2)}) collective-permute-start(f32[128,128]{1,0:T(8,128)S(1)} %add_add_fusion.1), channel_id=1, source_target_pairs={{0,24},{8,16},{16,8},{24,0},{1,25},{9,17},{17,9},{25,1},{2,26},{10... | collective-permute-start | bytes 196616 | tf_op jit(solution)/shard_map/ppermute | solution.py:470
  123.7 2.3 %copy-done.3 = bf16[1536,1536]{1,0:T(8,128)(2,1)S(1)} copy-done((bf16[1536,1536]{1,0:T(8,128)(2,1)S(1)}, bf16[1536,1536]{1,0:T(8,128)(2,1)}, u32[]{:S(2)}) %copy-start.3) | copy-done | bytes 4718616
  126.0 5.4 %attend.1 = bf16[128,1536]{1,0:T(8,128)(2,1)} custom-call(bf16[128,1024]{1,0:T(8,128)(2,1)S(1)} %queries.1.query_ref, bf16[128,1536]{1,0:T(8,128)(2,1)S(1)} %get-tuple-element.28.encoded_ref, bf16[1536,1536]{1,0:T(8,128)(2,1)S(1)} %copy-done.3, bf16[128,320]{1,0:T(8,128)(2,1)S(1)} %get-tuple-element.29.rest_0_, ...), custom_call_target="tpu_custom_call" | custom-call | flops 1275068416 | bytes 4718592 | tf_op jit(solution)/shard_map/attend/pallas_call | solution.py:301
  (124 shorter events, 44.0 us)
Async XLA Ops:
  7.2 20.6 %all-gather.2.cloned.1.call-start = ((), (), s32[]{:S(2)}) async-start(), calls=%async_computation.1 | async-start | bytes 8110080 | tf_op jit(solution)/shard_map/all_gather | solution.py:422
  14.0 10.6 %collective-permute-start = (f32[8,352]{1,0:T(8,128)S(1)}, f32[8,352]{1,0:T(8,128)S(1)}, u32[]{:S(2)}, u32[]{:S(2)}) collective-permute-start(f32[8,352]{1,0:T(8,128)S(1)} %get-tuple-element.20), channel_id=1, source_target_pairs={{0,1},{1,0},{2,3},{3,2},{4,5},{5,4},{6,7},{7,6},{8,9},{9,8},{10,11... | collective-permute-start | bytes 33800 | tf_op jit(solution)/shard_map/ppermute | solution.py:412
  14.5 10.1 %collective-permute-start.1 = (f32[8,352]{1,0:T(8,128)S(1)}, f32[8,352]{1,0:T(8,128)S(1)}, u32[]{:S(2)}, u32[]{:S(2)}) collective-permute-start(f32[8,352]{1,0:T(8,128)S(1)} %get-tuple-element.21), channel_id=1, source_target_pairs={{0,3},{1,2},{2,1},{3,0},{4,7},{5,6},{6,5},{7,4},{8,11},{9,10},{10,... | collective-permute-start | bytes 33800 | tf_op jit(solution)/shard_map/ppermute | solution.py:412
  17.1 7.6 %collective-permute-start.2 = (f32[8,352]{1,0:T(8,128)S(1)}, f32[8,352]{1,0:T(8,128)S(1)}, u32[]{:S(2)}, u32[]{:S(2)}) collective-permute-start(f32[8,352]{1,0:T(8,128)S(1)} %get-tuple-element.22), channel_id=1, source_target_pairs={{0,5},{1,4},{2,7},{3,6},{4,1},{5,0},{6,3},{7,2},{8,13},{9,12},{10,... | collective-permute-start | bytes 33800 | tf_op jit(solution)/shard_map/ppermute | solution.py:412
  18.2 8.4 %collective-permute-start.7 = (bf16[256,352]{1,0:T(8,128)(2,1)S(1)}, bf16[256,352]{1,0:T(8,128)(2,1)S(1)}, u32[]{:S(2)}, u32[]{:S(2)}) collective-permute-start(bf16[256,352]{1,0:T(8,128)(2,1)S(1)} %get-tuple-element.26), channel_id=1, source_target_pairs={{0,6},{1,7},{2,4},{3,5},{4,2},{5,3},{6,0},{7,1},{8,14},{9,15},{10,... | collective-permute-start | bytes 540680 | tf_op jit(solution)/shard_map/ppermute | solution.py:412
  33.4 26.9 %collective-permute-start.8 = (bf16[256,1536]{1,0:T(8,128)(2,1)S(1)}, bf16[256,1536]{1,0:T(8,128)(2,1)}, u32[]{:S(2)}, u32[]{:S(2)}) collective-permute-start(bf16[256,1536]{1,0:T(8,128)(2,1)S(1)} %conv.7), channel_id=1, source_target_pairs={{0,2},{1,5},{2,0},{3,7},{4,6},{5,1},{6,4},{7,3},{8,10},{9,13},{10,... | collective-permute-start | bytes 2359304 | tf_op jit(solution)/shard_map/ppermute | solution.py:412
  35.2 21.9 %collective-permute-start.6 = (bf16[256,352]{1,0:T(8,128)(2,1)S(1)}, bf16[256,352]{1,0:T(8,128)(2,1)S(1)}, u32[]{:S(2)}, u32[]{:S(2)}) collective-permute-start(bf16[256,352]{1,0:T(8,128)(2,1)S(1)} %get-tuple-element.25), channel_id=1, source_target_pairs={{0,4},{1,3},{2,6},{3,1},{4,0},{5,7},{6,2},{7,5},{8,12},{9,11},{10,... | collective-permute-start | bytes 540680 | tf_op jit(solution)/shard_map/ppermute | solution.py:412
  36.6 13.0 %collective-permute-start.4 = (bf16[256,352]{1,0:T(8,128)(2,1)S(1)}, bf16[256,352]{1,0:T(8,128)(2,1)S(1)}, u32[]{:S(2)}, u32[]{:S(2)}) collective-permute-start(bf16[256,352]{1,0:T(8,128)(2,1)S(1)} %get-tuple-element.24), channel_id=1, source_target_pairs={{0,2},{1,5},{2,0},{3,7},{4,6},{5,1},{6,4},{7,3},{8,10},{9,13},{10,... | collective-permute-start | bytes 540680 | tf_op jit(solution)/shard_map/ppermute | solution.py:412
  55.2 22.7 %collective-permute-start.5 = (bf16[256,1536]{1,0:T(8,128)(2,1)S(1)}, bf16[256,1536]{1,0:T(8,128)(2,1)S(1)}, u32[]{:S(2)}, u32[]{:S(2)}) collective-permute-start(bf16[256,1536]{1,0:T(8,128)(2,1)S(1)} %conv.5), channel_id=1, source_target_pairs={{0,2},{1,5},{2,0},{3,7},{4,6},{5,1},{6,4},{7,3},{8,10},{9,13},{10,... | collective-permute-start | bytes 2359304 | tf_op jit(solution)/shard_map/ppermute | solution.py:412
  62.5 15.4 %collective-permute-start.9 = (bf16[256,1536]{1,0:T(8,128)(2,1)}, bf16[256,1536]{1,0:T(8,128)(2,1)S(1)}, u32[]{:S(2)}, u32[]{:S(2)}) collective-permute-start(bf16[256,1536]{1,0:T(8,128)(2,1)} %add_convert_fusion), channel_id=1, source_target_pairs={{0,4},{1,3},{2,6},{3,1},{4,0},{5,7},{6,2},{7,5},{8,12},{9,11},{10,... | collective-permute-start | bytes 2359304 | tf_op jit(solution)/shard_map/ppermute | solution.py:412
  79.7 7.9 %collective-permute-start.17 = (f32[8,256]{1,0:T(8,128)S(1)}, f32[8,256]{1,0:T(8,128)S(1)}, u32[]{:S(2)}, u32[]{:S(2)}) collective-permute-start(f32[8,256]{1,0:T(8,128)S(1)} %get-tuple-element.30.rest_0_), channel_id=1, source_target_pairs={{0,1},{1,0},{2,3},{3,2},{4,5},{5,4},{6,7},{7,6},{8,9},{9,8},{10,11... | collective-permute-start | bytes 24584 | tf_op jit(solution)/shard_map/ppermute | solution.py:412
  79.7 9.4 %collective-permute-start.18 = (f32[8,256]{1,0:T(8,128)S(1)}, f32[8,256]{1,0:T(8,128)S(1)}, u32[]{:S(2)}, u32[]{:S(2)}) collective-permute-start(f32[8,256]{1,0:T(8,128)S(1)} %get-tuple-element.30.rest_0_), channel_id=1, source_target_pairs={{0,2},{1,3},{2,0},{3,1},{4,6},{5,7},{6,4},{7,5},{8,10},{9,11},{10,... | collective-permute-start | bytes 24584 | tf_op jit(solution)/shard_map/ppermute | solution.py:412
  80.8 9.5 %all-to-all-start = ((bf16[8,64,128]{2,0,1:T(8,128)(2,1)}), bf16[8,64,128]{2,0,1:T(8,128)(2,1)S(1)}, u32[]{:S(2)}, u32[]{:S(2)}) async-start(bf16[8,64,128]{2,0,1:T(8,128)(2,1)} %copy.18), calls=%async_computation | async-start | bytes 262144 | tf_op jit(solution)/shard_map/all_to_all | solution.py:459
  97.0 13.7 %collective-permute-start.10 = (bf16[128,320]{1,0:T(8,128)(2,1)S(1)}, bf16[128,320]{1,0:T(8,128)(2,1)S(1)}, u32[]{:S(2)}, u32[]{:S(2)}) collective-permute-start(bf16[128,320]{1,0:T(8,128)(2,1)S(1)} %get-tuple-element.29.rest_0_), channel_id=1, source_target_pairs={{0,1},{1,0},{2,3},{3,2},{4,5},{5,4},{6,7},{7,6},{8,9},{9,8},{10,11... | collective-permute-start | bytes 245768 | tf_op jit(solution)/shard_map/ppermute | solution.py:412
  97.1 14.1 %collective-permute-start.11 = (bf16[128,320]{1,0:T(8,128)(2,1)S(1)}, bf16[128,320]{1,0:T(8,128)(2,1)S(1)}, u32[]{:S(2)}, u32[]{:S(2)}) collective-permute-start(bf16[128,320]{1,0:T(8,128)(2,1)S(1)} %get-tuple-element.29.rest_0_), channel_id=1, source_target_pairs={{0,2},{1,3},{2,0},{3,1},{4,6},{5,7},{6,4},{7,5},{8,10},{9,11},{10,... | collective-permute-start | bytes 245768 | tf_op jit(solution)/shard_map/ppermute | solution.py:412
  99.0 8.7 %collective-permute-start.28 = (f32[128,128]{1,0:T(8,128)S(1)}, f32[128,128]{1,0:T(8,128)S(1)}, u32[]{:S(2)}, u32[]{:S(2)}) collective-permute-start(f32[128,128]{1,0:T(8,128)S(1)} %get-tuple-element.32), channel_id=1, source_target_pairs={{0,5},{1,4},{2,7},{3,6},{4,1},{5,0},{6,3},{7,2},{8,13},{9,12},{10,... | collective-permute-start | bytes 196616 | tf_op jit(solution)/shard_map/ppermute | solution.py:412
  100.3 8.3 %collective-permute-start.29 = (f32[128,128]{1,0:T(8,128)S(1)}, f32[128,128]{1,0:T(8,128)S(1)}, u32[]{:S(2)}, u32[]{:S(2)}) collective-permute-start(f32[128,128]{1,0:T(8,128)S(1)} %get-tuple-element.32), channel_id=1, source_target_pairs={{0,6},{1,7},{2,4},{3,5},{4,2},{5,3},{6,0},{7,1},{8,14},{9,15},{10,... | collective-permute-start | bytes 196616 | tf_op jit(solution)/shard_map/ppermute | solution.py:412
  101.3 7.9 %collective-permute-start.30 = (f32[128,128]{1,0:T(8,128)S(1)}, f32[128,128]{1,0:T(8,128)S(1)}, u32[]{:S(2)}, u32[]{:S(2)}) collective-permute-start(f32[128,128]{1,0:T(8,128)S(1)} %get-tuple-element.32), channel_id=1, source_target_pairs={{0,7},{1,6},{2,5},{3,4},{4,3},{5,2},{6,1},{7,0},{8,15},{9,14},{10,... | collective-permute-start | bytes 196616 | tf_op jit(solution)/shard_map/ppermute | solution.py:412
  109.2 11.0 %collective-permute-start.14 = (bf16[128,320]{1,0:T(8,128)(2,1)S(1)}, bf16[128,320]{1,0:T(8,128)(2,1)S(1)}, u32[]{:S(2)}, u32[]{:S(2)}) collective-permute-start(bf16[128,320]{1,0:T(8,128)(2,1)S(1)} %get-tuple-element.29.rest_0_), channel_id=1, source_target_pairs={{0,5},{1,4},{2,7},{3,6},{4,1},{5,0},{6,3},{7,2},{8,13},{9,12},{10,... | collective-permute-start | bytes 245768 | tf_op jit(solution)/shard_map/ppermute | solution.py:412
  110.7 12.9 %collective-permute-start.15 = (bf16[128,320]{1,0:T(8,128)(2,1)S(1)}, bf16[128,320]{1,0:T(8,128)(2,1)S(1)}, u32[]{:S(2)}, u32[]{:S(2)}) collective-permute-start(bf16[128,320]{1,0:T(8,128)(2,1)S(1)} %get-tuple-element.29.rest_0_), channel_id=1, source_target_pairs={{0,6},{1,7},{2,4},{3,5},{4,2},{5,3},{6,0},{7,1},{8,14},{9,15},{10,... | collective-permute-start | bytes 245768 | tf_op jit(solution)/shard_map/ppermute | solution.py:412
  111.2 12.5 %collective-permute-start.16 = (bf16[128,320]{1,0:T(8,128)(2,1)S(1)}, bf16[128,320]{1,0:T(8,128)(2,1)S(1)}, u32[]{:S(2)}, u32[]{:S(2)}) collective-permute-start(bf16[128,320]{1,0:T(8,128)(2,1)S(1)} %get-tuple-element.29.rest_0_), channel_id=1, source_target_pairs={{0,7},{1,6},{2,5},{3,4},{4,3},{5,2},{6,1},{7,0},{8,15},{9,14},{10,... | collective-permute-start | bytes 245768 | tf_op jit(solution)/shard_map/ppermute | solution.py:412
  113.1 18.3 %collective-permute-start.31 = (f32[128,128]{1,0:T(8,128)S(1)}, f32[128,128]{1,0:T(8,128)S(1)}, u32[]{:S(2)}, u32[]{:S(2)}) collective-permute-start(f32[128,128]{1,0:T(8,128)S(1)} %add_add_fusion.1), channel_id=1, source_target_pairs={{0,8},{8,0},{16,24},{24,16},{1,9},{9,1},{17,25},{25,17},{2,10},{10... | collective-permute-start | bytes 196616 | tf_op jit(solution)/shard_map/ppermute | solution.py:470
  114.8 16.6 %collective-permute-start.32 = (f32[128,128]{1,0:T(8,128)S(1)}, f32[128,128]{1,0:T(8,128)S(1)}, u32[]{:S(2)}, u32[]{:S(2)}) collective-permute-start(f32[128,128]{1,0:T(8,128)S(1)} %add_add_fusion.1), channel_id=1, source_target_pairs={{0,16},{8,24},{16,0},{24,8},{1,17},{9,25},{17,1},{25,9},{2,18},{10... | collective-permute-start | bytes 196616 | tf_op jit(solution)/shard_map/ppermute | solution.py:470
  120.2 11.3 %collective-permute-start.33 = (f32[128,128]{1,0:T(8,128)S(1)}, f32[128,128]{1,0:T(8,128)S(1)}, u32[]{:S(2)}, u32[]{:S(2)}) collective-permute-start(f32[128,128]{1,0:T(8,128)S(1)} %add_add_fusion.1), channel_id=1, source_target_pairs={{0,24},{8,16},{16,8},{24,0},{1,25},{9,17},{17,9},{25,1},{2,26},{10... | collective-permute-start | bytes 196616 | tf_op jit(solution)/shard_map/ppermute | solution.py:470
  (37 other events, 240.5 us)
Sparse Core Ops, SparseCore 0:
  9.6 18.1 all-gather.1

commit v2 on v1

v2 whole, which is shorter than its diff:
```python
import functools
import math

import jax
import jax.numpy as jnp
from jax import lax
from jax.experimental import pallas as pl
from jax.experimental.pallas import tpu as pltpu
from jax.sharding import PartitionSpec as P

PAIR_POOL = 16
norm_eps = 1e-06
logit_cap = 50.0
MIB = 1 << 20
GROUP = ("seq", "mp")
f32, bf16 = jnp.float32, jnp.bfloat16


def whole_vmem():
    return pl.BlockSpec(memory_space=pltpu.VMEM)


def anywhere():
    return pl.BlockSpec(memory_space=pl.ANY)


def smem():
    return pl.BlockSpec(memory_space=pltpu.SMEM)


def in_hbm(value):
    return pltpu.with_memory_space_constraint(value, pltpu.HBM)


def array(shape, dtype):
    return jax.ShapeDtypeStruct(shape, dtype)


def lane_pad(width):
    return (width + 127) // 128 * 128


def tree_sum(terms):
    while len(terms) > 1:
        terms = [terms[i] + terms[i + 1] for i in range(0, len(terms), 2)]
    return terms[0]


def flipped_bits(mask, bits):
    return sum(((mask >> b) & 1) << (bits - 1 - b) for b in range(bits))


def here():
    return lax.axis_index("seq"), lax.axis_index("mp")


def hop_pairs(chips, core_masks, core_flip):
    pairs = []
    for chip in range(chips):
        for core in range(2):
            target = (chip ^ core_masks[core]) * 2 + (core ^ core_flip)
            pairs.append((chip * 2 + core, target))
    return pairs


def strip_kernel(margin, feat_hbm, out_ref, top, bottom, sems):
    rows = feat_hbm.shape[0]
    copies = [
        pltpu.make_async_copy(feat_hbm.at[0:16, :], top, sems.at[0]),
        pltpu.make_async_copy(feat_hbm.at[rows - 16 : rows, :], bottom, sems.at[1]),
    ]
    for c in copies:
        c.start()
    for c in copies:
        c.wait()
    first = top[...].astype(f32)[:margin]
    last = bottom[...].astype(f32)[16 - margin :]
    rest = jnp.zeros((16 - 2 * margin, first.shape[1]), f32)
    out_ref[...] = jnp.concatenate([first, last, rest], axis=0).astype(bf16)


def edge_strip(features, margin):
    channels = features.shape[1]
    return pl.pallas_call(
        functools.partial(strip_kernel, margin),
        name="edge_strip",
        out_shape=array((16, channels), bf16),
        in_specs=[anywhere()],
        out_specs=whole_vmem(),
        scratch_shapes=[
            pltpu.VMEM((16, channels), bf16),
            pltpu.VMEM((16, channels), bf16),
            pltpu.SemaphoreType.DMA((2,)),
        ],
        compiler_params=pltpu.CompilerParams(vmem_limit_bytes=2 * MIB),
    )(in_hbm(features))


def pick_rows(rows):
    half = rows // 2
    target = lax.broadcasted_iota(jnp.int32, (rows, rows), 0)
    source = lax.broadcasted_iota(jnp.int32, (rows, rows), 1)
    wanted = jnp.where(target < half, 2 * target, 2 * (target - half) + 1)
    return jnp.where(source == wanted, 1.0, 0.0).astype(bf16)


def prep_kernel(chips, width, feat_hbm, strip_ref, *rest):
    block_refs = rest[:chips]
    feat, wide, split, sem = rest[chips:]
    rows = feat.shape[0]
    chip, _ = here()
    copy = pltpu.make_async_copy(feat_hbm, feat, sem)
    copy.start()
    split[:, :, width:] = jnp.zeros((chips, split.shape[1], split.shape[2] - width), bf16)
    pick = pick_rows(rows)
    wide[rows:, :] = strip_ref[...].astype(f32)
    copy.wait()
    wide[0:rows, :] = jnp.dot(pick, feat[...], preferred_element_type=f32)

    def gelu_rows(at):
        x = wide[at, :]
        v = x * lax.rsqrt(jnp.mean(x * x, axis=-1, keepdims=True) + norm_eps)
        g = (0.5 * v) * (1.0 + lax.erf(v * math.sqrt(0.5)))
        g = g.astype(bf16)
        for q in range(chips):
            split[q, at, 0:width] = g[:, q * width : (q + 1) * width]

    step = 32

    def body(i, carry):
        gelu_rows(pl.ds(pl.multiple_of(i * step, step), step))
        return carry

    lax.fori_loop(0, rows // step, body, 0)
    gelu_rows(pl.ds(rows, wide.shape[0] - rows))
    for k in range(chips):
        block_refs[k][...] = split[chip ^ k]


def prep(features, strip, chips):
    rows, channels = features.shape
    width = channels // chips
    padded = lane_pad(width)
    tall = rows + strip.shape[0]
    return pl.pallas_call(
        functools.partial(prep_kernel, chips, width),
        name="prep",
        out_shape=[array((tall, padded), bf16)] * chips,
        in_specs=[anywhere(), whole_vmem()],
        out_specs=[whole_vmem()] * chips,
        scratch_shapes=[
            pltpu.VMEM((rows, channels), bf16),
            pltpu.VMEM((tall, channels), f32),
            pltpu.VMEM((chips, tall, padded), bf16),
            pltpu.SemaphoreType.DMA,
        ],
        compiler_params=pltpu.CompilerParams(vmem_limit_bytes=6 * MIB),
        cost_estimate=pl.CostEstimate(
            flops=40 * rows * channels, bytes_accessed=6 * rows * channels, transcendentals=0
        ),
    )(in_hbm(features), strip)


def pack_kernel(taps, padded, own_hbm, peer_hbm, out_ref, sems):
    part = own_hbm.shape[0] // taps
    _, core = here()
    copies = []
    for p, source in enumerate((own_hbm, peer_hbm)):
        place = core if p == 0 else 1 - core
        for k in range(taps):
            to = pl.ds(pl.multiple_of(k * padded + place * part, 16), part)
            copies.append(
                pltpu.make_async_copy(
                    source.at[k * part : (k + 1) * part, :], out_ref.at[to, :], sems.at[p, k]
                )
            )
    for c in copies:
        c.start()
    if padded > 2 * part:
        for k in range(taps):
            out_ref[k * padded + 2 * part : (k + 1) * padded, :] = jnp.zeros(
                (padded - 2 * part, out_ref.shape[1]), bf16
            )
    for c in copies:
        c.wait()


def pack_filter(own, peer, taps, padded):
    model_dim = own.shape[1]
    part = own.shape[0] // taps
    if part % 16:
        own, peer = (w.reshape(taps, part, model_dim) for w in (own, peer))
        first = lax.axis_index("mp") == 0
        low, high = jnp.where(first, own, peer), jnp.where(first, peer, own)
        both = jnp.concatenate([low, high], axis=1)
        both = jnp.pad(both, ((0, 0), (0, padded - 2 * part), (0, 0)))
        return both.reshape(taps * padded, model_dim)
    return pl.pallas_call(
        functools.partial(pack_kernel, taps, padded),
        name="pack_filter",
        out_shape=array((taps * padded, model_dim), bf16),
        in_specs=[anywhere()] * 2,
        out_specs=whole_vmem(),
        scratch_shapes=[pltpu.SemaphoreType.DMA((2, taps))],
        compiler_params=pltpu.CompilerParams(vmem_limit_bytes=2 * MIB),
        cost_estimate=pl.CostEstimate(
            flops=0, bytes_accessed=4 * own.shape[0] * model_dim, transcendentals=0
        ),
    )(in_hbm(own), peer)


def conv_kernel(chips, bits, taps, tile, wanted, *rest):
    count = len(wanted)
    message_refs = rest[:chips]
    weight_ref = rest[chips]
    out_refs = rest[chips + 1 : chips + 1 + count]
    held, cols = rest[chips + 1 + count :]
    tall, padded = held.shape[1:]
    rows, model_dim = out_refs[0].shape
    half = rows // 2
    chip, core = here()
    for k in range(chips):
        held[k] = message_refs[k][...]
    row = lax.broadcasted_iota(jnp.int32, (half, padded), 0)
    for j, k in enumerate(wanted):
        mask = jnp.where(core == 0, k, flipped_bits(k, bits))
        left = (chip ^ mask) - (1 - core)
        right = (chip ^ mask) + core
        block = held[mask]
        before = held[jnp.where(left >= 0, left ^ chip, 0), rows:tall, :].astype(f32)
        before = jnp.where(left >= 0, before, 0.0)
        after = held[jnp.where(right < chips, right ^ chip, 0), rows:tall, :].astype(f32)
        after = jnp.where(right < chips, after, 0.0)
        even = block[0:half].astype(f32)
        odd = block[half:rows].astype(f32)

        def back(v, strip_row):
            return jnp.where(row == 0, before[strip_row : strip_row + 1], pltpu.roll(v, 1, 0))

        def ahead(v, strip_row):
            return jnp.where(
                row == half - 1, after[strip_row : strip_row + 1], pltpu.roll(v, half - 1, 0)
            )

        lagged = [back(even, 2), back(odd, 3), even, odd, ahead(even, 0), ahead(odd, 1)]
        for i, v in enumerate(lagged):
            piece = v.astype(bf16)
            if i < taps:
                cols[j * rows : j * rows + half, i * padded : (i + 1) * padded] = piece
            if i > 0:
                cols[j * rows + half : (j + 1) * rows, (i - 1) * padded : i * padded] = piece
    for j in range(count):
        for n in range(model_dim // tile):
            at = pl.ds(n * tile, tile)
            got = jnp.dot(
                cols[j * rows : (j + 1) * rows], weight_ref[:, at], preferred_element_type=f32
            )
            out_refs[j][:, at] = got.astype(out_refs[j].dtype)


def conv(messages, weight, taps, wanted, dtypes):
    chips = len(messages)
    bits = chips.bit_length() - 1
    tall, padded = messages[0].shape
    depth, model_dim = weight.shape
    rows = tall - 16
    count = len(wanted)
    return pl.pallas_call(
        functools.partial(conv_kernel, chips, bits, taps, 512, wanted),
        name="conv",
        out_shape=[array((rows, model_dim), d) for d in dtypes],
        in_specs=[whole_vmem()] * (chips + 1),
        out_specs=[whole_vmem()] * count,
        scratch_shapes=[
            pltpu.VMEM((chips, tall, padded), bf16),
            pltpu.VMEM((count * rows, depth), bf16),
        ],
        compiler_params=pltpu.CompilerParams(vmem_limit_bytes=(4 + 2 * count) * MIB),
        cost_estimate=pl.CostEstimate(
            flops=2 * count * rows * depth * model_dim,
            bytes_accessed=2 * depth * model_dim,
            transcendentals=0,
        ),
    )(*messages, weight)


def sum_kernel(count, *refs):
    out_ref = refs[-1]
    out_ref[...] = tree_sum([r[...].astype(f32) for r in refs[:count]]).astype(out_ref.dtype)


def add_up(terms, dtype, after=()):
    return pl.pallas_call(
        functools.partial(sum_kernel, len(terms)),
        name="add_up",
        out_shape=array(terms[0].shape, dtype),
        in_specs=[whole_vmem()] * len(terms) + [anywhere()] * len(after),
        out_specs=whole_vmem(),
        compiler_params=pltpu.CompilerParams(vmem_limit_bytes=4 * MIB),
    )(*terms, *after)


def encode_kernel(
    arrivals, gain_ref, feat_hbm, keyval_weight_ref, pair_weight_ref, own_ref, *rest
):
    come_refs = rest[:arrivals]
    encoded_ref, normed_ref, keyval_ref, feats_ref, feat, sem = rest[-6:]
    copy = pltpu.make_async_copy(feat_hbm, feat, sem)
    copy.start()
    rows, model_dim = own_ref.shape
    half = rows // 2
    channels = feat.shape[1]
    pick = pick_rows(rows)
    total = own_ref[...]
    for ref in come_refs:
        total = total + ref[...].astype(f32)
    copy.wait()
    skip = jnp.dot(pick, feat[...], preferred_element_type=f32)
    if channels < model_dim:
        skip = jnp.concatenate([skip, jnp.zeros((rows, model_dim - channels), f32)], axis=1)
    total = total + skip
    encoded = jnp.maximum(total[:half], total[half:]).astype(bf16)
    encoded_ref[...] = encoded
    wide = encoded.astype(f32)
    scale = lax.rsqrt(jnp.mean(wide * wide, axis=-1, keepdims=True) + norm_eps)
    normed = (wide * scale * gain_ref[...][None]).astype(bf16)
    normed_ref[...] = normed
    pairs = half // PAIR_POOL
    at = lax.broadcasted_iota(jnp.int32, (pairs, half), 0)
    of = lax.broadcasted_iota(jnp.int32, (pairs, half), 1) // PAIR_POOL
    spread = jnp.where(at == of, 1.0 / PAIR_POOL, 0.0).astype(bf16)
    pooled = jnp.dot(spread, encoded, preferred_element_type=f32).astype(bf16)
    feats_ref[...] = (
        jnp.dot(pooled, pair_weight_ref[...], preferred_element_type=f32)
        .astype(bf16)
        .astype(f32)
    )
    keyval_ref[...] = lax.dot_general(
        normed, keyval_weight_ref[...], (((1,), (1,)), ((), ())), preferred_element_type=f32
    ).astype(bf16)


def encode(own, come, features, gain, keyval_weight_t, pair_weight, after):
    rows, model_dim = own.shape
    half = rows // 2
    columns = keyval_weight_t.shape[0]
    return pl.pallas_call(
        functools.partial(encode_kernel, len(come)),
        name="encode",
        out_shape=[
            array((half, model_dim), bf16),
            array((half, model_dim), bf16),
            array((half, columns), bf16),
            array((half // PAIR_POOL, pair_weight.shape[1]), f32),
        ],
        in_specs=[whole_vmem(), anywhere()]
        + [whole_vmem()] * (3 + len(come))
        + [anywhere()] * len(after),
        out_specs=[whole_vmem()] * 4,
        scratch_shapes=[pltpu.VMEM(features.shape, bf16), pltpu.SemaphoreType.DMA],
        compiler_params=pltpu.CompilerParams(vmem_limit_bytes=8 * MIB),
        cost_estimate=pl.CostEstimate(
            flops=2 * half * model_dim * columns,
            bytes_accessed=6 * rows * model_dim,
            transcendentals=0,
        ),
    )(gain, in_hbm(features), keyval_weight_t, pair_weight, own, *come, *after)


def query_kernel(heads, normed_ref, scale_ref, weight_ref, out_ref):
    columns = weight_ref.shape[1]
    key_dim = columns // heads
    tile = 2 * key_dim
    for n in range(columns // tile):
        at = pl.ds(n * tile, tile)
        got = jnp.dot(normed_ref[...], weight_ref[:, at], preferred_element_type=f32)
        for h in range(2):
            head = n * 2 + h
            piece = got[:, h * key_dim : (h + 1) * key_dim]
            piece = piece * (scale_ref[head] / math.sqrt(key_dim))
            out_ref[:, head * key_dim : (head + 1) * key_dim] = piece.astype(bf16)


def project_queries(normed, weight, scale):
    rows, model_dim = normed.shape
    columns = weight.shape[1]
    return pl.pallas_call(
        functools.partial(query_kernel, scale.shape[0]),
        name="queries",
        out_shape=array((rows, columns), bf16),
        in_specs=[whole_vmem(), smem(), whole_vmem()],
        out_specs=whole_vmem(),
        compiler_params=pltpu.CompilerParams(vmem_limit_bytes=3 * MIB),
        cost_estimate=pl.CostEstimate(
            flops=2 * rows * columns * model_dim,
            bytes_accessed=2 * columns * model_dim,
            transcendentals=0,
        ),
    )(normed, scale, weight)


def attend_kernel(parts, heads, first, last, group, query_ref, start_ref, weight_ref, *rest):
    part_refs = rest[:parts]
    out_ref, keys, values = rest[-3:]
    rows = query_ref.shape[0]
    key_dim = query_ref.shape[1] // heads
    span = part_refs[0].shape[0]
    value_dim = values.shape[1]
    for k in range(parts):
        got = part_refs[k][...]
        keys[k * span : (k + 1) * span, :] = got[:, :key_dim]
        values[k * span : (k + 1) * span, :] = got[:, key_dim:]
    total = start_ref[...].astype(f32)
    for n in range(first, last, group):
        queries = jnp.concatenate(
            [query_ref[:, (n + h) * key_dim : (n + h + 1) * key_dim] for h in range(group)],
            axis=0,
        )
        scores = lax.dot_general(
            queries, keys[...], (((1,), (1,)), ((), ())), preferred_element_type=f32
        )
        weights = jnp.exp(logit_cap * jnp.tanh(scores * (1.0 / logit_cap)))
        sums = jnp.sum(weights, axis=-1, keepdims=True)
        mixed = jnp.dot(weights.astype(bf16), values[...], preferred_element_type=f32) / sums
        mixed = mixed.astype(bf16)
        for h in range(group):
            at = (n + h) * value_dim
            total = total + jnp.dot(
                mixed[h * rows : (h + 1) * rows],
                weight_ref[at : at + value_dim, :],
                preferred_element_type=f32,
            )
    out_ref[...] = total.astype(out_ref.dtype)


def attend(queries, start, output_weight, parts, heads, first, last, dtype, after=()):
    rows, model_dim = start.shape
    key_dim = queries.shape[1] // heads
    value_dim = output_weight.shape[0] // heads
    total_keys = parts[0].shape[0] * len(parts)
    group = 2
    return pl.pallas_call(
        functools.partial(attend_kernel, len(parts), heads, first, last, group),
        name="attend",
        out_shape=array((rows, model_dim), dtype),
        in_specs=[whole_vmem()] * (3 + len(parts)) + [anywhere()] * len(after),
        out_specs=whole_vmem(),
        scratch_shapes=[
            pltpu.VMEM((total_keys, key_dim), bf16),
            pltpu.VMEM((total_keys, value_dim), bf16),
        ],
        compiler_params=pltpu.CompilerParams(
            vmem_limit_bytes=8 * MIB if total_keys <= 1024 else 32 * MIB
        ),
        cost_estimate=pl.CostEstimate(
            flops=2
            * rows
            * (last - first)
            * (total_keys * (key_dim + value_dim) + value_dim * model_dim),
            bytes_accessed=2 * (last - first) * value_dim * model_dim,
            transcendentals=2 * rows * (last - first) * total_keys,
        ),
    )(queries, start, output_weight, *parts, *after)


def split_kernel(parts, input_ref, *rest):
    out_refs = rest[-1 - parts : -1]
    wide = rest[-1]
    rows = input_ref.shape[0]
    chip, core = here()
    me = chip * 2 + core
    wide[...] = input_ref[...].astype(f32)
    for k in range(parts):
        at = pl.ds(pl.multiple_of((me ^ k) * rows, 8), rows)
        out_refs[k][...] = wide[:, at, :].astype(bf16)


def split_pairs(pair_input, parts, after):
    rows, columns, dim = pair_input.shape
    return pl.pallas_call(
        functools.partial(split_kernel, parts),
        name="split_pairs",
        out_shape=[array((rows, rows, dim), bf16)] * parts,
        in_specs=[whole_vmem()] + [anywhere()] * len(after),
        out_specs=[whole_vmem()] * parts,
        scratch_shapes=[pltpu.VMEM((rows, columns, dim), f32)],
        compiler_params=pltpu.CompilerParams(vmem_limit_bytes=4 * MIB),
    )(pair_input, *after)


def pair_kernel(parts, input_ref, cotangent_ref, flip_ref, *rest):
    turned_refs = rest[:parts]
    feat_refs = rest[parts : 2 * parts]
    out_ref, keep_ref, give_ref, stack, mirror, summed, flipped = rest[2 * parts :]
    rows, columns, dim = input_ref.shape
    chip, core = here()
    me = chip * 2 + core
    own = feat_refs[0][...]
    mine_k = own[:, dim:][None]
    for k in range(parts):
        got = feat_refs[k][...]
        stack[k] = got
        value = turned_refs[k][...].astype(f32) + got[:, None, :dim] * mine_k
        mirror[k] = value.reshape(rows * rows, dim).astype(bf16)
    target = lax.broadcasted_iota(jnp.int32, (rows * rows, rows * rows), 0)
    source = lax.broadcasted_iota(jnp.int32, (rows * rows, rows * rows), 1)
    swap = jnp.where(source == (target % rows) * rows + target // rows, 1.0, 0.0).astype(bf16)
    for b in range(parts):
        turned = jnp.dot(swap, mirror[b ^ me], preferred_element_type=f32)
        flipped[:, b * rows : (b + 1) * rows, :] = turned.reshape(rows, rows, dim)
    every = jnp.concatenate([stack[b ^ me] for b in range(parts)], axis=0)[:, dim:]
    for i in range(rows):
        at = pl.ds(i * columns, columns)
        value = input_ref[i].astype(f32) + own[i : i + 1, :dim] * every
        summed[at, :] = value.astype(bf16)
    facing = flipped[...].reshape(rows * columns, dim).astype(bf16)
    update = jnp.dot(facing, flip_ref[...], preferred_element_type=f32)
    update = update + summed[...].astype(f32)
    out_ref[...] = update.astype(bf16).reshape(rows, columns, dim)
    grad = lax.dot_general(
        facing,
        cotangent_ref[...].reshape(rows * columns, dim),
        (((0,), (0,)), ((), ())),
        preferred_element_type=f32,
    )
    low, high = grad[: dim // 2], grad[dim // 2 :]
    keep_ref[...] = jnp.where(core == 0, low, high)
    give_ref[...] = jnp.where(core == 0, high, low)


def pair_update(pair_input, cotangent, flip_weight, turned, feats):
    rows, columns, dim = pair_input.shape
    parts = len(feats)
    return pl.pallas_call(
        functools.partial(pair_kernel, parts),
        name="pair",
        out_shape=[
            array((rows, columns, dim), bf16),
            array((dim // 2, dim), f32),
            array((dim // 2, dim), f32),
        ],
        in_specs=[whole_vmem()] * (3 + 2 * parts),
        out_specs=[whole_vmem()] * 3,
        scratch_shapes=[
            pltpu.VMEM((parts, rows, 2 * dim), f32),
            pltpu.VMEM((parts, rows * rows, dim), bf16),
            pltpu.VMEM((rows * columns, dim), bf16),
            pltpu.VMEM((rows, columns, dim), f32),
        ],
        compiler_params=pltpu.CompilerParams(
            vmem_limit_bytes=4 * MIB if parts <= 8 else 24 * MIB
        ),
        cost_estimate=pl.CostEstimate(
            flops=4 * rows * columns * dim * dim,
            bytes_accessed=8 * rows * columns * dim,
            transcendentals=0,
        ),
    )(pair_input, cotangent, flip_weight, *turned, *feats)


def join_kernel(mine_ref, other_ref, out_ref):
    _, core = here()
    half = mine_ref.shape[0]
    mine, other = mine_ref[...], other_ref[...]
    out_ref[0:half, :] = jnp.where(core == 0, mine, other)
    out_ref[half:, :] = jnp.where(core == 0, other, mine)


def join_halves(mine, other):
    half, dim = mine.shape
    return pl.pallas_call(
        join_kernel,
        name="join_halves",
        out_shape=array((2 * half, dim), f32),
        in_specs=[whole_vmem()] * 2,
        out_specs=whole_vmem(),
        compiler_params=pltpu.CompilerParams(vmem_limit_bytes=2 * MIB),
    )(mine, other)


def per_device(
    features,
    conv_weight,
    norm_gain,
    query_weight,
    keyval_weight,
    head_scale,
    output_weight,
    pair_weight,
    pair_input,
    flip_weight,
    pair_cotangent,
):
    chips = lax.axis_size("seq")
    bits = chips.bit_length() - 1
    windows = lax.axis_size("dp")
    taps = conv_weight.shape[0]
    model_dim = output_weight.shape[1]
    heads = head_scale.shape[0]
    features = features[0]

    masks = [(k, flipped_bits(k, bits)) for k in range(chips)]

    def send(value, mask, flip=0):
        cores = mask if isinstance(mask, tuple) else (mask, mask)
        return lax.ppermute(value, GROUP, hop_pairs(chips, cores, flip))

    strip = send(edge_strip(features, taps // 2), 0, 1)
    own_weight = conv_weight.reshape(-1, model_dim)
    peer_weight = send(own_weight, 0, 1)

    blocks = prep(features, strip, chips)
    messages = [blocks[0]] + [None] * (chips - 1)
    for k in range(chips - 1, 0, -1):
        messages[k] = send(blocks[k], k)
    weight = pack_filter(own_weight, peer_weight, taps, messages[0].shape[1])

    last = chips - 1
    rest = sorted(range(last), key=lambda k: (1 - (k & 1), -k))

    def partials(ks):
        dtypes = [bf16 if k & 1 else f32 for k in ks]
        return dict(zip(ks, conv(messages, weight, taps, ks, dtypes)))

    partial = partials([last])
    partial.update(partials(rest))
    pieces = split_pairs(pair_input[0], 2 * chips, [partial[1]])
    turned = [pieces[0]] + [send(pieces[k], k >> 1, k & 1) for k in range(1, 2 * chips)]
    arrived = []
    for b in range(bits):
        bit = 1 << b
        leaving = [k for k in [last] + rest if k in partial and k & bit]
        got = {k ^ bit: send(partial.pop(k), masks[bit]) for k in leaving}
        for k, value in got.items():
            if k == 0:
                arrived.append(value)
            else:
                goes = k & (2 * bit)
                partial[k] = add_up([partial[k], value], bf16 if goes else f32)

    encoded, normed, keyval, feats = encode(
        partial[0], arrived, features, norm_gain, keyval_weight.T, pair_weight, turned
    )

    def gather(value):
        mine = [value] + [send(value, k) for k in range(chips - 1, 0, -1)][::-1]
        return sum(([v, send(v, 0, 1)] for v in mine), [])

    all_feats = gather(feats)
    keyvals = gather(keyval)
    queries = project_queries(normed, query_weight, head_scale)
    pair_out, keep, give = pair_update(
        pair_input[0], pair_cotangent[0], flip_weight, turned, all_feats
    )
    grad = add_up([keep, send(give, 0, 1)], f32)
    grad = add_up([grad] + [send(grad, k) for k in range(1, chips)], f32)
    grad = add_up(
        [grad]
        + [
            lax.ppermute(grad, "dp", [(w, w ^ k) for w in range(windows)])
            for k in range(1, windows)
        ],
        f32,
    )
    grad = join_halves(grad, send(grad, 0, 1))
    block_out = attend(queries, encoded, output_weight, keyvals, heads, 0, heads, bf16)
    return (block_out[None], pair_out[None], grad)


def solution(mesh):
    placed = (
        P("dp", ("seq", "mp"), None),
        P(None, ("seq", "mp"), None),
        P(),
        P(),
        P(),
        P(),
        P(),
        P(),
        P("dp", ("seq", "mp"), None, None),
        P(),
        P("dp", ("seq", "mp"), None, None),
    )
    return jax.shard_map(
        per_device,
        mesh=mesh,
        in_specs=placed,
        out_specs=(P("dp", ("seq", "mp"), None), P("dp", ("seq", "mp"), None, None), P()),
        check_vma=False,
    )
```

time: 140 us -> 102 us (0.73)
  waiting for transfers between devices: 17.8 us -> 47.8 us
  between operations: 24.5 us -> 0.9 us
  local copies, waits for them, and re-layouts: 23.1 us -> 0.05 us
  starting transfers between devices: 44.3 us -> 30.3 us
  Pallas kernels: 26 us -> 22.3 us
  other arithmetic: 3.23 us -> 0.01 us
    ppermute x31 -> x34, waiting for transfers between devices: 15.9 us -> 39.7 us  [send(): return lax.ppermute(value, GROUP, hop_pairs(chips, cores, flip))]
    unnamed x51 -> x20, local copies, waits for them, and re-layouts: 20.3 us -> 0.05 us
    ppermute x3, waiting for transfers between devices: 0.01 us -> 8.12 us  [per_device(): lax.ppermute(grad, 'dp', [(w, w ^ k) for w in range(windows)])]
    ppermute x31 -> x34, starting transfers between devices: 33.3 us -> 26.6 us  [send(): return lax.ppermute(value, GROUP, hop_pairs(chips, cores, flip))]
    pallas_call x6 -> x12, Pallas kernels: 19.5 us -> 15.5 us  [the longest x2 6.99 us: conv(): pl.pallas_call(functools.partial(conv_kernel, chips, bits, taps, 512, wan...]
    ppermute x3, starting transfers between devices: 7.6 us -> 3.67 us  [per_device(): lax.ppermute(grad, 'dp', [(w, w ^ k) for w in range(windows)])]
    all_to_all x1 -> x0, starting transfers between devices: 3.37 us -> none  [per_device(): lax.all_to_all(pair_input[0], GROUP, split_axis=1, concat_axis=0, tiled=T...]
    convert_element_type x1 -> x0, other arithmetic: 2.23 us -> none  [per_device(): partial.pop(k).astype(bf16)]
  transfers between devices with their start and end apart: 36 -> 37, of which waited for: 9 -> 18; matrix products, arithmetic and copies ran while one was open for 5% -> 0% of each run, Pallas kernels for 15% -> 13%
where the time goes in v2:
time: 102 us; the launch traced here: 101 us
  waiting for transfers between devices  47.8 us (47%)
  starting transfers between devices  30.3 us (30%)
  Pallas kernels  22.3 us (22%)
    ppermute x34, waiting for transfers between devices, send(): return lax.ppermute(value, GROUP, hop_pairs(chips, cores, flip))  39.7 us
    ppermute x34, starting transfers between devices, send(): return lax.ppermute(value, GROUP, hop_pairs(chips, cores, flip))  26.6 us
    ppermute x3, waiting for transfers between devices, per_device(): lax.ppermute(grad, 'dp', [(w, w ^ k) for w in range(windows)])  8.12 us
    pallas_call x2, Pallas kernels, conv(): pl.pallas_call(functools.partial(conv_kernel, chips, bits, taps, 512, wan...  6.99 us
    pallas_call x1, Pallas kernels, attend(): pl.pallas_call(functools.partial(attend_kernel, len(parts), heads, first,...  3.92 us
    ppermute x3, starting transfers between devices, per_device(): lax.ppermute(grad, 'dp', [(w, w ^ k) for w in range(windows)])  3.67 us
    pallas_call x1, Pallas kernels, prep(): pl.pallas_call(functools.partial(prep_kernel, chips, width), name='prep',...  3.45 us
    pallas_call x1, Pallas kernels, encode(): pl.pallas_call(functools.partial(encode_kernel, len(come)), name='encode'...  2.3 us
  transfers between devices with their start and end apart: 37, of which 18 were waited for; matrix products, arithmetic and copies ran while one was open for 0% of the time, Pallas kernels for 13%

profile of v2, /device:TPU:0, one launch (start us, length us, event | category | flops | bytes accessed | tf_op | source)
XLA Modules:
  0.0 101.4 jit_solution(3887710544735391147)
XLA Ops:
  2.1 3.8 %collective-permute-done.strip_ref = bf16[16,1408]{1,0:T(8,128)(2,1)S(1)} collective-permute-done((bf16[16,1408]{1,0:T(8,128)(2,1)S(1)}, bf16[16,1408]{1,0:T(8,128)(2,1)S(1)}, u32[]{:S(2)}, u32[]{:S(2)}) %collective-permute-start) | collective-permute-done | bytes 45088 | tf_op jit(solution)/shard_map/ppermute | solution.py:606
  5.9 3.4 %prep.1 = (bf16[272,384]{1,0:T(8,128)(2,1)S(1)}, bf16[272,384]{1,0:T(8,128)(2,1)S(1)}, bf16[272,384]{1,0:T(8,128)(2,1)S(1)}, bf16[272,384]{1,0:T(8,128)(2,1)S(1)}) custom-call(bf16[256,1408]{1,0:T(8,128)(2,1)} %bitcast.14, bf16[16,1408]{1,0:T(8,128)(2,1)S(1)} %collective-permute-done.strip_ref), custom_call_target="tpu_custom_call" | custom-call | flops 14417920 | bytes 2162688 | tf_op jit(solution)/shard_map/prep/pallas_call | solution.py:145
  9.3 2.9 %collective-permute-start.1 = (bf16[272,384]{1,0:T(8,128)(2,1)S(1)}, bf16[272,384]{1,0:T(8,128)(2,1)S(1)}, u32[]{:S(2)}, u32[]{:S(2)}) collective-permute-start(bf16[272,384]{1,0:T(8,128)(2,1)S(1)} %get-tuple-element.26), channel_id=1, source_target_pairs={{0,2},{1,3},{2,0},{3,1},{4,6},{5,7},{6,4},{7,5},{8,10},{9,11},{10,... | collective-permute-start | bytes 626696 | tf_op jit(solution)/shard_map/ppermute | solution.py:606
  12.2 1.5 %collective-permute-start.2 = (bf16[272,384]{1,0:T(8,128)(2,1)S(1)}, bf16[272,384]{1,0:T(8,128)(2,1)S(1)}, u32[]{:S(2)}, u32[]{:S(2)}) collective-permute-start(bf16[272,384]{1,0:T(8,128)(2,1)S(1)} %get-tuple-element.27), channel_id=1, source_target_pairs={{0,4},{1,5},{2,6},{3,7},{4,0},{5,1},{6,2},{7,3},{8,12},{9,13},{10,... | collective-permute-start | bytes 626696 | tf_op jit(solution)/shard_map/ppermute | solution.py:606
  13.8 1.8 %pack_filter.1.rest_4_ = bf16[1920,1536]{1,0:T(8,128)(2,1)S(1)} custom-call(bf16[880,1536]{1,0:T(8,128)(2,1)} %bitcast.17, bf16[880,1536]{1,0:T(8,128)(2,1)S(1)} %collective-permute-done.4.peer_hbm), custom_call_target="tpu_custom_call" | custom-call | bytes 5406720 | tf_op jit(solution)/shard_map/pack_filter/pallas_call | solution.py:198
  15.6 2.6 %collective-permute-done.1.rest_1_ = bf16[272,384]{1,0:T(8,128)(2,1)S(1)} collective-permute-done((bf16[272,384]{1,0:T(8,128)(2,1)S(1)}, bf16[272,384]{1,0:T(8,128)(2,1)S(1)}, u32[]{:S(2)}, u32[]{:S(2)}) %collective-permute-start.1) | collective-permute-done | bytes 208928 | tf_op jit(solution)/shard_map/ppermute | solution.py:606
  18.2 5.5 %collective-permute-done.2.rest_2_ = bf16[272,384]{1,0:T(8,128)(2,1)S(1)} collective-permute-done((bf16[272,384]{1,0:T(8,128)(2,1)S(1)}, bf16[272,384]{1,0:T(8,128)(2,1)S(1)}, u32[]{:S(2)}, u32[]{:S(2)}) %collective-permute-start.2) | collective-permute-done | bytes 208928 | tf_op jit(solution)/shard_map/ppermute | solution.py:606
  23.7 1.9 %conv.3 = bf16[256,1536]{1,0:T(8,128)(2,1)S(1)} custom-call(bf16[272,384]{1,0:T(8,128)(2,1)S(1)} %get-tuple-element.25.rest_0_, bf16[272,384]{1,0:T(8,128)(2,1)S(1)} %collective-permute-done.1.rest_1_, bf16[272,384]{1,0:T(8,128)(2,1)S(1)} %collective-permute-done.2.rest_2_, bf16[272,384]{1,0:T(8,128)(2,1)S(1)} %collective-permute-done.3.rest_3_, ...), custom_call_target="tpu_custom_call" | custom-call | flops 1509949440 | bytes 5898240 | tf_op jit(solution)/shard_map/conv/pallas_call | solution.py:268
  25.5 1.3 %collective-permute-start.6 = (bf16[256,1536]{1,0:T(8,128)(2,1)S(1)}, bf16[256,1536]{1,0:T(8,128)(2,1)S(1)}, u32[]{:S(2)}, u32[]{:S(2)}) collective-permute-start(bf16[256,1536]{1,0:T(8,128)(2,1)S(1)} %conv.3), channel_id=1, source_target_pairs={{0,2},{1,5},{2,0},{3,7},{4,6},{5,1},{6,4},{7,3},{8,10},{9,13},{10,... | collective-permute-start | bytes 2359304 | tf_op jit(solution)/shard_map/ppermute | solution.py:606
  26.8 5.1 %conv.2 = (bf16[256,1536]{1,0:T(8,128)(2,1)S(1)}, f32[256,1536]{1,0:T(8,128)S(1)}, f32[256,1536]{1,0:T(8,128)S(1)}) custom-call(bf16[272,384]{1,0:T(8,128)(2,1)S(1)} %get-tuple-element.25.rest_0_, bf16[272,384]{1,0:T(8,128)(2,1)S(1)} %collective-permute-done.1.rest_1_, bf16[272,384]{1,0:T(8,128)(2,1)S(1)} %collective-permute-done.2.rest_2_, ...), custom_call_target="tpu_custom_call" | custom-call | flops 4529848320 | bytes 5898240 | tf_op jit(solution)/shard_map/conv/pallas_call | solution.py:268
  32.9 4.7 %collective-permute-done.6.refs_1_ = bf16[256,1536]{1,0:T(8,128)(2,1)S(1)} collective-permute-done((bf16[256,1536]{1,0:T(8,128)(2,1)S(1)}, bf16[256,1536]{1,0:T(8,128)(2,1)S(1)}, u32[]{:S(2)}, u32[]{:S(2)}) %collective-permute-start.6) | collective-permute-done | bytes 786464 | tf_op jit(solution)/shard_map/ppermute | solution.py:606
  37.7 1.6 %collective-permute-start.7 = (bf16[256,1536]{1,0:T(8,128)(2,1)S(1)}, bf16[256,1536]{1,0:T(8,128)(2,1)S(1)}, u32[]{:S(2)}, u32[]{:S(2)}) collective-permute-start(bf16[256,1536]{1,0:T(8,128)(2,1)S(1)} %add_up.4), channel_id=1, source_target_pairs={{0,4},{1,3},{2,6},{3,1},{4,0},{5,7},{6,2},{7,5},{8,12},{9,11},{10,... | collective-permute-start | bytes 2359304 | tf_op jit(solution)/shard_map/ppermute | solution.py:606
  41.8 11.9 %collective-permute-done.9.rest_4_.rest_2_ = bf16[8,8,128]{2,1,0:T(8,128)(2,1)S(1)} collective-permute-done((bf16[8,8,128]{2,1,0:T(8,128)(2,1)S(1)}, bf16[8,8,128]{2,1,0:T(8,128)(2,1)S(1)}, u32[]{:S(2)}, u32[]{:S(2)}) %collective-permute-start.9) | collective-permute-done | bytes 16416 | tf_op jit(solution)/shard_map/ppermute | solution.py:606
  53.7 2.2 %collective-permute-start.12 = (bf16[8,8,128]{2,1,0:T(8,128)(2,1)S(1)}, bf16[8,8,128]{2,1,0:T(8,128)(2,1)S(1)}, u32[]{:S(2)}, u32[]{:S(2)}) collective-permute-start(bf16[8,8,128]{2,1,0:T(8,128)(2,1)S(1)} %get-tuple-element.37), channel_id=1, source_target_pairs={{0,5},{1,4},{2,7},{3,6},{4,1},{5,0},{6,3},{7,2},{8,13},{9,12},{10,... | collective-permute-start | bytes 49160 | tf_op jit(solution)/shard_map/ppermute | solution.py:606
  57.7 2.9 %collective-permute-done.13.rest_8_.rest_6_ = bf16[8,8,128]{2,1,0:T(8,128)(2,1)S(1)} collective-permute-done((bf16[8,8,128]{2,1,0:T(8,128)(2,1)S(1)}, bf16[8,8,128]{2,1,0:T(8,128)(2,1)S(1)}, u32[]{:S(2)}, u32[]{:S(2)}) %collective-permute-start.13) | collective-permute-done | bytes 16416 | tf_op jit(solution)/shard_map/ppermute | solution.py:606
  61.2 2.3 %encode.1 = (bf16[128,1536]{1,0:T(8,128)(2,1)S(1)}, bf16[128,1536]{1,0:T(8,128)(2,1)S(1)}, bf16[128,320]{1,0:T(8,128)(2,1)S(1)}, f32[8,256]{1,0:T(8,128)S(1)}) custom-call(f32[1536]{0:T(1024)S(1)} %copy-done.6, bf16[256,1408]{1,0:T(8,128)(2,1)} %bitcast.15, bf16[320,1536]{1,0:T(8,128)(2,1)S(1)} %bitcast.9, bf16[1536,256]{1,0:T(8,128)(2,1)S(1)} %copy-done.2, ...), custom_call_target="tpu_custom_call" | custom-call | flops 125829120 | bytes 2359296 | tf_op jit(solution)/shard_map/encode/pallas_call | solution.py:347
  63.5 1.8 %collective-permute-start.27 = (f32[8,256]{1,0:T(8,128)S(1)}, f32[8,256]{1,0:T(8,128)S(1)}, u32[]{:S(2)}, u32[]{:S(2)}) collective-permute-start(f32[8,256]{1,0:T(8,128)S(1)} %get-tuple-element.43.rest_8_), channel_id=1, source_target_pairs={{0,6},{1,7},{2,4},{3,5},{4,2},{5,3},{6,0},{7,1},{8,14},{9,15},{10,... | collective-permute-start | bytes 24584 | tf_op jit(solution)/shard_map/ppermute | solution.py:606
  74.4 1.7 %collective-permute-start.20 = (bf16[128,320]{1,0:T(8,128)(2,1)S(1)}, bf16[128,320]{1,0:T(8,128)(2,1)S(1)}, u32[]{:S(2)}, u32[]{:S(2)}) collective-permute-start(bf16[128,320]{1,0:T(8,128)(2,1)S(1)} %get-tuple-element.42.rest_0_), channel_id=1, source_target_pairs={{0,6},{1,7},{2,4},{3,5},{4,2},{5,3},{6,0},{7,1},{8,14},{9,15},{10,... | collective-permute-start | bytes 245768 | tf_op jit(solution)/shard_map/ppermute | solution.py:606
  80.2 2.7 %collective-permute-done.31.refs_2_ = f32[64,128]{1,0:T(8,128)S(1)} collective-permute-done((f32[64,128]{1,0:T(8,128)S(1)}, f32[64,128]{1,0:T(8,128)S(1)}, u32[]{:S(2)}, u32[]{:S(2)}) %collective-permute-start.31) | collective-permute-done | bytes 32800 | tf_op jit(solution)/shard_map/ppermute | solution.py:606
  83.1 3.7 %collective-permute-start.35 = (f32[64,128]{1,0:T(8,128)S(1)}, f32[64,128]{1,0:T(8,128)S(1)}, u32[]{:S(2)}, u32[]{:S(2)}) collective-permute-start(f32[64,128]{1,0:T(8,128)S(1)} %add_up.6.refs_0_), channel_id=1, source_target_pairs={{0,24},{8,16},{16,8},{24,0},{1,25},{9,17},{17,9},{25,1},{2,26},{10... | collective-permute-start | bytes 98312 | tf_op jit(solution)/shard_map/ppermute | solution.py:660
  87.4 1.6 %collective-permute-done.35.refs_3_ = f32[64,128]{1,0:T(8,128)S(1)} collective-permute-done((f32[64,128]{1,0:T(8,128)S(1)}, f32[64,128]{1,0:T(8,128)S(1)}, u32[]{:S(2)}, u32[]{:S(2)}) %collective-permute-start.35) | collective-permute-done | bytes 32800 | tf_op jit(solution)/shard_map/ppermute | solution.py:660
  88.9 2.6 %collective-permute-done.34.refs_2_ = f32[64,128]{1,0:T(8,128)S(1)} collective-permute-done((f32[64,128]{1,0:T(8,128)S(1)}, f32[64,128]{1,0:T(8,128)S(1)}, u32[]{:S(2)}, u32[]{:S(2)}) %collective-permute-start.34) | collective-permute-done | bytes 32800 | tf_op jit(solution)/shard_map/ppermute | solution.py:660
  91.6 3.9 %collective-permute-done.33.refs_1_ = f32[64,128]{1,0:T(8,128)S(1)} collective-permute-done((f32[64,128]{1,0:T(8,128)S(1)}, f32[64,128]{1,0:T(8,128)S(1)}, u32[]{:S(2)}, u32[]{:S(2)}) %collective-permute-start.33) | collective-permute-done | bytes 32800 | tf_op jit(solution)/shard_map/ppermute | solution.py:660
  97.5 3.9 %attend.1 = bf16[128,1536]{1,0:T(8,128)(2,1)} custom-call(bf16[128,1024]{1,0:T(8,128)(2,1)S(1)} %queries.1.query_ref, bf16[128,1536]{1,0:T(8,128)(2,1)S(1)} %get-tuple-element.41.start_ref, bf16[1536,1536]{1,0:T(8,128)(2,1)S(1)} %bitcast.8, bf16[128,320]{1,0:T(8,128)(2,1)S(1)} %get-tuple-element.42.rest_0_, ...), custom_call_target="tpu_custom_call" | custom-call | flops 1275068416 | bytes 4718592 | tf_op jit(solution)/shard_map/attend/pallas_call | solution.py:442
  (86 shorter events, 23.2 us)
Async XLA Ops:
  0.6 13.2 %collective-permute-start.4 = (bf16[880,1536]{1,0:T(8,128)(2,1)}, bf16[880,1536]{1,0:T(8,128)(2,1)S(1)}, u32[]{:S(2)}, u32[]{:S(2)}) collective-permute-start(bf16[880,1536]{1,0:T(8,128)(2,1)} %bitcast.16), channel_id=1, source_target_pairs={{0,1},{1,0},{2,3},{3,2},{4,5},{5,4},{6,7},{7,6},{8,9},{9,8},{10,11... | collective-permute-start | bytes 8110088 | tf_op jit(solution)/shard_map/ppermute | solution.py:606
  9.3 8.9 %collective-permute-start.1 = (bf16[272,384]{1,0:T(8,128)(2,1)S(1)}, bf16[272,384]{1,0:T(8,128)(2,1)S(1)}, u32[]{:S(2)}, u32[]{:S(2)}) collective-permute-start(bf16[272,384]{1,0:T(8,128)(2,1)S(1)} %get-tuple-element.26), channel_id=1, source_target_pairs={{0,2},{1,3},{2,0},{3,1},{4,6},{5,7},{6,4},{7,5},{8,10},{9,11},{10,... | collective-permute-start | bytes 626696 | tf_op jit(solution)/shard_map/ppermute | solution.py:606
  12.2 11.4 %collective-permute-start.2 = (bf16[272,384]{1,0:T(8,128)(2,1)S(1)}, bf16[272,384]{1,0:T(8,128)(2,1)S(1)}, u32[]{:S(2)}, u32[]{:S(2)}) collective-permute-start(bf16[272,384]{1,0:T(8,128)(2,1)S(1)} %get-tuple-element.27), channel_id=1, source_target_pairs={{0,4},{1,5},{2,6},{3,7},{4,0},{5,1},{6,2},{7,3},{8,12},{9,13},{10,... | collective-permute-start | bytes 626696 | tf_op jit(solution)/shard_map/ppermute | solution.py:606
  13.8 9.9 %collective-permute-start.3 = (bf16[272,384]{1,0:T(8,128)(2,1)S(1)}, bf16[272,384]{1,0:T(8,128)(2,1)S(1)}, u32[]{:S(2)}, u32[]{:S(2)}) collective-permute-start(bf16[272,384]{1,0:T(8,128)(2,1)S(1)} %get-tuple-element.28), channel_id=1, source_target_pairs={{0,6},{1,7},{2,4},{3,5},{4,2},{5,3},{6,0},{7,1},{8,14},{9,15},{10,... | collective-permute-start | bytes 626696 | tf_op jit(solution)/shard_map/ppermute | solution.py:606
  25.5 12.1 %collective-permute-start.6 = (bf16[256,1536]{1,0:T(8,128)(2,1)S(1)}, bf16[256,1536]{1,0:T(8,128)(2,1)S(1)}, u32[]{:S(2)}, u32[]{:S(2)}) collective-permute-start(bf16[256,1536]{1,0:T(8,128)(2,1)S(1)} %conv.3), channel_id=1, source_target_pairs={{0,2},{1,5},{2,0},{3,7},{4,6},{5,1},{6,4},{7,3},{8,10},{9,13},{10,... | collective-permute-start | bytes 2359304 | tf_op jit(solution)/shard_map/ppermute | solution.py:606
  32.0 29.2 %collective-permute-start.5 = (bf16[256,1536]{1,0:T(8,128)(2,1)S(1)}, bf16[256,1536]{1,0:T(8,128)(2,1)S(1)}, u32[]{:S(2)}, u32[]{:S(2)}) collective-permute-start(bf16[256,1536]{1,0:T(8,128)(2,1)S(1)} %get-tuple-element.30.rest_0_), channel_id=1, source_target_pairs={{0,2},{1,5},{2,0},{3,7},{4,6},{5,1},{6,4},{7,3},{8,10},{9,13},{10,... | collective-permute-start | bytes 2359304 | tf_op jit(solution)/shard_map/ppermute | solution.py:606
  37.7 23.4 %collective-permute-start.7 = (bf16[256,1536]{1,0:T(8,128)(2,1)S(1)}, bf16[256,1536]{1,0:T(8,128)(2,1)S(1)}, u32[]{:S(2)}, u32[]{:S(2)}) collective-permute-start(bf16[256,1536]{1,0:T(8,128)(2,1)S(1)} %add_up.4), channel_id=1, source_target_pairs={{0,4},{1,3},{2,6},{3,1},{4,0},{5,7},{6,2},{7,5},{8,12},{9,11},{10,... | collective-permute-start | bytes 2359304 | tf_op jit(solution)/shard_map/ppermute | solution.py:606
  39.5 14.2 %collective-permute-start.9 = (bf16[8,8,128]{2,1,0:T(8,128)(2,1)S(1)}, bf16[8,8,128]{2,1,0:T(8,128)(2,1)S(1)}, u32[]{:S(2)}, u32[]{:S(2)}) collective-permute-start(bf16[8,8,128]{2,1,0:T(8,128)(2,1)S(1)} %get-tuple-element.34), channel_id=1, source_target_pairs={{0,2},{1,3},{2,0},{3,1},{4,6},{5,7},{6,4},{7,5},{8,10},{9,11},{10,... | collective-permute-start | bytes 49160 | tf_op jit(solution)/shard_map/ppermute | solution.py:606
  40.1 15.9 %collective-permute-start.10 = (bf16[8,8,128]{2,1,0:T(8,128)(2,1)S(1)}, bf16[8,8,128]{2,1,0:T(8,128)(2,1)S(1)}, u32[]{:S(2)}, u32[]{:S(2)}) collective-permute-start(bf16[8,8,128]{2,1,0:T(8,128)(2,1)S(1)} %get-tuple-element.35), channel_id=1, source_target_pairs={{0,3},{1,2},{2,1},{3,0},{4,7},{5,6},{6,5},{7,4},{8,11},{9,10},{10,... | collective-permute-start | bytes 49160 | tf_op jit(solution)/shard_map/ppermute | solution.py:606
  41.3 15.8 %collective-permute-start.11 = (bf16[8,8,128]{2,1,0:T(8,128)(2,1)S(1)}, bf16[8,8,128]{2,1,0:T(8,128)(2,1)S(1)}, u32[]{:S(2)}, u32[]{:S(2)}) collective-permute-start(bf16[8,8,128]{2,1,0:T(8,128)(2,1)S(1)} %get-tuple-element.36), channel_id=1, source_target_pairs={{0,4},{1,5},{2,6},{3,7},{4,0},{5,1},{6,2},{7,3},{8,12},{9,13},{10,... | collective-permute-start | bytes 49160 | tf_op jit(solution)/shard_map/ppermute | solution.py:606
  55.9 4.6 %collective-permute-start.13 = (bf16[8,8,128]{2,1,0:T(8,128)(2,1)S(1)}, bf16[8,8,128]{2,1,0:T(8,128)(2,1)S(1)}, u32[]{:S(2)}, u32[]{:S(2)}) collective-permute-start(bf16[8,8,128]{2,1,0:T(8,128)(2,1)S(1)} %get-tuple-element.38), channel_id=1, source_target_pairs={{0,6},{1,7},{2,4},{3,5},{4,2},{5,3},{6,0},{7,1},{8,14},{9,15},{10,... | collective-permute-start | bytes 49160 | tf_op jit(solution)/shard_map/ppermute | solution.py:606
  57.1 4.1 %collective-permute-start.14 = (bf16[8,8,128]{2,1,0:T(8,128)(2,1)S(1)}, bf16[8,8,128]{2,1,0:T(8,128)(2,1)S(1)}, u32[]{:S(2)}, u32[]{:S(2)}) collective-permute-start(bf16[8,8,128]{2,1,0:T(8,128)(2,1)S(1)} %get-tuple-element.39), channel_id=1, source_target_pairs={{0,7},{1,6},{2,5},{3,4},{4,3},{5,2},{6,1},{7,0},{8,15},{9,14},{10,... | collective-permute-start | bytes 49160 | tf_op jit(solution)/shard_map/ppermute | solution.py:606
  63.5 4.7 %collective-permute-start.27 = (f32[8,256]{1,0:T(8,128)S(1)}, f32[8,256]{1,0:T(8,128)S(1)}, u32[]{:S(2)}, u32[]{:S(2)}) collective-permute-start(f32[8,256]{1,0:T(8,128)S(1)} %get-tuple-element.43.rest_8_), channel_id=1, source_target_pairs={{0,6},{1,7},{2,4},{3,5},{4,2},{5,3},{6,0},{7,1},{8,14},{9,15},{10,... | collective-permute-start | bytes 24584 | tf_op jit(solution)/shard_map/ppermute | solution.py:606
  73.2 6.0 %collective-permute-start.32 = (f32[64,128]{1,0:T(8,128)S(1)}, f32[64,128]{1,0:T(8,128)S(1)}, u32[]{:S(2)}, u32[]{:S(2)}) collective-permute-start(f32[64,128]{1,0:T(8,128)S(1)} %add_up.5.refs_0_), channel_id=1, source_target_pairs={{0,6},{1,7},{2,4},{3,5},{4,2},{5,3},{6,0},{7,1},{8,14},{9,15},{10,... | collective-permute-start | bytes 98312 | tf_op jit(solution)/shard_map/ppermute | solution.py:606
  74.4 12.3 %collective-permute-start.20 = (bf16[128,320]{1,0:T(8,128)(2,1)S(1)}, bf16[128,320]{1,0:T(8,128)(2,1)S(1)}, u32[]{:S(2)}, u32[]{:S(2)}) collective-permute-start(bf16[128,320]{1,0:T(8,128)(2,1)S(1)} %get-tuple-element.42.rest_0_), channel_id=1, source_target_pairs={{0,6},{1,7},{2,4},{3,5},{4,2},{5,3},{6,0},{7,1},{8,14},{9,15},{10,... | collective-permute-start | bytes 245768 | tf_op jit(solution)/shard_map/ppermute | solution.py:606
  76.1 10.6 %collective-permute-start.18 = (bf16[128,320]{1,0:T(8,128)(2,1)S(1)}, bf16[128,320]{1,0:T(8,128)(2,1)S(1)}, u32[]{:S(2)}, u32[]{:S(2)}) collective-permute-start(bf16[128,320]{1,0:T(8,128)(2,1)S(1)} %get-tuple-element.42.rest_0_), channel_id=1, source_target_pairs={{0,4},{1,5},{2,6},{3,7},{4,0},{5,1},{6,2},{7,3},{8,12},{9,13},{10,... | collective-permute-start | bytes 245768 | tf_op jit(solution)/shard_map/ppermute | solution.py:606
  77.4 9.9 %collective-permute-start.16 = (bf16[128,320]{1,0:T(8,128)(2,1)S(1)}, bf16[128,320]{1,0:T(8,128)(2,1)S(1)}, u32[]{:S(2)}, u32[]{:S(2)}) collective-permute-start(bf16[128,320]{1,0:T(8,128)(2,1)S(1)} %get-tuple-element.42.rest_0_), channel_id=1, source_target_pairs={{0,2},{1,3},{2,0},{3,1},{4,6},{5,7},{6,4},{7,5},{8,10},{9,11},{10,... | collective-permute-start | bytes 245768 | tf_op jit(solution)/shard_map/ppermute | solution.py:606
  77.9 5.0 %collective-permute-start.31 = (f32[64,128]{1,0:T(8,128)S(1)}, f32[64,128]{1,0:T(8,128)S(1)}, u32[]{:S(2)}, u32[]{:S(2)}) collective-permute-start(f32[64,128]{1,0:T(8,128)S(1)} %add_up.5.refs_0_), channel_id=1, source_target_pairs={{0,4},{1,5},{2,6},{3,7},{4,0},{5,1},{6,2},{7,3},{8,12},{9,13},{10,... | collective-permute-start | bytes 98312 | tf_op jit(solution)/shard_map/ppermute | solution.py:606
  83.1 5.8 %collective-permute-start.35 = (f32[64,128]{1,0:T(8,128)S(1)}, f32[64,128]{1,0:T(8,128)S(1)}, u32[]{:S(2)}, u32[]{:S(2)}) collective-permute-start(f32[64,128]{1,0:T(8,128)S(1)} %add_up.6.refs_0_), channel_id=1, source_target_pairs={{0,24},{8,16},{16,8},{24,0},{1,25},{9,17},{17,9},{25,1},{2,26},{10... | collective-permute-start | bytes 98312 | tf_op jit(solution)/shard_map/ppermute | solution.py:660
  86.7 4.8 %collective-permute-start.34 = (f32[64,128]{1,0:T(8,128)S(1)}, f32[64,128]{1,0:T(8,128)S(1)}, u32[]{:S(2)}, u32[]{:S(2)}) collective-permute-start(f32[64,128]{1,0:T(8,128)S(1)} %add_up.6.refs_0_), channel_id=1, source_target_pairs={{0,16},{8,24},{16,0},{24,8},{1,17},{9,25},{17,1},{25,9},{2,18},{10... | collective-permute-start | bytes 98312 | tf_op jit(solution)/shard_map/ppermute | solution.py:660
  86.8 10.7 %collective-permute-start.15 = (bf16[128,320]{1,0:T(8,128)(2,1)S(1)}, bf16[128,320]{1,0:T(8,128)(2,1)S(1)}, u32[]{:S(2)}, u32[]{:S(2)}) collective-permute-start(bf16[128,320]{1,0:T(8,128)(2,1)S(1)} %get-tuple-element.42.rest_0_), channel_id=1, source_target_pairs={{0,1},{1,0},{2,3},{3,2},{4,5},{5,4},{6,7},{7,6},{8,9},{9,8},{10,11... | collective-permute-start | bytes 245768 | tf_op jit(solution)/shard_map/ppermute | solution.py:606
  86.8 10.6 %collective-permute-start.21 = (bf16[128,320]{1,0:T(8,128)(2,1)S(1)}, bf16[128,320]{1,0:T(8,128)(2,1)S(1)}, u32[]{:S(2)}, u32[]{:S(2)}) collective-permute-start(bf16[128,320]{1,0:T(8,128)(2,1)S(1)} %collective-permute-done.20.rest_6_), channel_id=1, source_target_pairs={{0,1},{1,0},{2,3},{3,2},{4,5},{5,4},{6,7},{7,6},{8,9},{9,8},{10,11... | collective-permute-start | bytes 245768 | tf_op jit(solution)/shard_map/ppermute | solution.py:606
  87.3 10.1 %collective-permute-start.19 = (bf16[128,320]{1,0:T(8,128)(2,1)S(1)}, bf16[128,320]{1,0:T(8,128)(2,1)S(1)}, u32[]{:S(2)}, u32[]{:S(2)}) collective-permute-start(bf16[128,320]{1,0:T(8,128)(2,1)S(1)} %collective-permute-done.18.rest_4_), channel_id=1, source_target_pairs={{0,1},{1,0},{2,3},{3,2},{4,5},{5,4},{6,7},{7,6},{8,9},{9,8},{10,11... | collective-permute-start | bytes 245768 | tf_op jit(solution)/shard_map/ppermute | solution.py:606
  88.9 8.5 %collective-permute-start.17 = (bf16[128,320]{1,0:T(8,128)(2,1)S(1)}, bf16[128,320]{1,0:T(8,128)(2,1)S(1)}, u32[]{:S(2)}, u32[]{:S(2)}) collective-permute-start(bf16[128,320]{1,0:T(8,128)(2,1)S(1)} %collective-permute-done.16.rest_2_), channel_id=1, source_target_pairs={{0,1},{1,0},{2,3},{3,2},{4,5},{5,4},{6,7},{7,6},{8,9},{9,8},{10,11... | collective-permute-start | bytes 245768 | tf_op jit(solution)/shard_map/ppermute | solution.py:606
  (23 other events, 355.3 us)

commit v3 on v2

--- a/solution.py
+++ b/solution.py
@@ -104,13 +104,15 @@
     return jnp.where(source == wanted, 1.0, 0.0).astype(bf16)
 
 
-def prep_kernel(chips, width, feat_hbm, strip_ref, *rest):
+def prep_kernel(chips, width, feat_hbm, pair_hbm, strip_ref, *rest):
     block_refs = rest[:chips]
-    feat, wide, split, sem = rest[chips:]
+    feat, pair, wide, split, sems = rest[chips:]
     rows = feat.shape[0]
     chip, _ = here()
-    copy = pltpu.make_async_copy(feat_hbm, feat, sem)
+    copy = pltpu.make_async_copy(feat_hbm, feat, sems.at[0])
+    pair_copy = pltpu.make_async_copy(pair_hbm, pair, sems.at[1])
     copy.start()
+    pair_copy.start()
     split[:, :, width:] = jnp.zeros((chips, split.shape[1], split.shape[2] - width), bf16)
     pick = pick_rows(rows)
     wide[rows:, :] = strip_ref[...].astype(f32)
@@ -133,32 +135,43 @@
 
     lax.fori_loop(0, rows // step, body, 0)
     gelu_rows(pl.ds(rows, wide.shape[0] - rows))
+    pair_copy.wait()
+    pairs, columns, dim = pair.shape
+    lanes = split.shape[2] // dim
+    extra = block_refs[0].shape[0] - wide.shape[0]
     for k in range(chips):
-        block_refs[k][...] = split[chip ^ k]
-
-
-def prep(features, strip, chips):
+        block_refs[k][0 : wide.shape[0], :] = split[chip ^ k]
+        at = pl.ds(pl.multiple_of((chip ^ k) * 2 * pairs, 16), 2 * pairs)
+        piece = pair[:, at, :].reshape(2 * pairs * pairs, dim)
+        for g in range(lanes):
+            part = piece[g * extra : (g + 1) * extra]
+            to = wide.shape[0]
+            block_refs[k][to : to + part.shape[0], g * dim : (g + 1) * dim] = part
+
+
+def prep(features, strip, pair_input, chips):
     rows, channels = features.shape
     width = channels // chips
     padded = lane_pad(width)
     tall = rows + strip.shape[0]
+    pairs, columns, dim = pair_input.shape
+    lanes = padded // dim
+    extra = -(-2 * pairs * pairs // (16 * lanes)) * 16
     return pl.pallas_call(
         functools.partial(prep_kernel, chips, width),
         name="prep",
-        out_shape=[array((tall, padded), bf16)] * chips,
-        in_specs=[anywhere(), whole_vmem()],
+        out_shape=[array((tall + extra, padded), bf16)] * chips,
+        in_specs=[anywhere(), anywhere(), whole_vmem()],
         out_specs=[whole_vmem()] * chips,
         scratch_shapes=[
             pltpu.VMEM((rows, channels), bf16),
+            pltpu.VMEM(pair_input.shape, bf16),
             pltpu.VMEM((tall, channels), f32),
             pltpu.VMEM((chips, tall, padded), bf16),
-            pltpu.SemaphoreType.DMA,
+            pltpu.SemaphoreType.DMA((2,)),
         ],
         compiler_params=pltpu.CompilerParams(vmem_limit_bytes=6 * MIB),
-        cost_estimate=pl.CostEstimate(
-            flops=40 * rows * channels, bytes_accessed=6 * rows * channels, transcendentals=0
-        ),
-    )(in_hbm(features), strip)
+    )(in_hbm(features), in_hbm(pair_input), strip)
 
 
 def pack_kernel(taps, padded, own_hbm, peer_hbm, out_ref, sems):
@@ -203,9 +216,6 @@
         out_specs=whole_vmem(),
         scratch_shapes=[pltpu.SemaphoreType.DMA((2, taps))],
         compiler_params=pltpu.CompilerParams(vmem_limit_bytes=2 * MIB),
-        cost_estimate=pl.CostEstimate(
-            flops=0, bytes_accessed=4 * own.shape[0] * model_dim, transcendentals=0
-        ),
     )(in_hbm(own), peer)
 
 
@@ -220,7 +230,7 @@
     half = rows // 2
     chip, core = here()
     for k in range(chips):
-        held[k] = message_refs[k][...]
+        held[k] = message_refs[k][0:tall, :]
     row = lax.broadcasted_iota(jnp.int32, (half, padded), 0)
     for j, k in enumerate(wanted):
         mask = jnp.where(core == 0, k, flipped_bits(k, bits))
@@ -258,12 +268,12 @@
             out_refs[j][:, at] = got.astype(out_refs[j].dtype)
 
 
-def conv(messages, weight, taps, wanted, dtypes):
+def conv(messages, rows, weight, taps, wanted, dtypes):
     chips = len(messages)
     bits = chips.bit_length() - 1
-    tall, padded = messages[0].shape
+    padded = messages[0].shape[1]
+    tall = rows + 16
     depth, model_dim = weight.shape
-    rows = tall - 16
     count = len(wanted)
     return pl.pallas_call(
         functools.partial(conv_kernel, chips, bits, taps, 512, wanted),
@@ -276,11 +286,6 @@
             pltpu.VMEM((count * rows, depth), bf16),
         ],
         compiler_params=pltpu.CompilerParams(vmem_limit_bytes=(4 + 2 * count) * MIB),
-        cost_estimate=pl.CostEstimate(
-            flops=2 * count * rows * depth * model_dim,
-            bytes_accessed=2 * depth * model_dim,
-            transcendentals=0,
-        ),
     )(*messages, weight)
 
 
@@ -300,11 +305,9 @@
     )(*terms, *after)
 
 
-def encode_kernel(
-    arrivals, gain_ref, feat_hbm, keyval_weight_ref, pair_weight_ref, own_ref, *rest
-):
+def encode_kernel(arrivals, gain_ref, feat_hbm, pair_weight_ref, own_ref, *rest):
     come_refs = rest[:arrivals]
-    encoded_ref, normed_ref, keyval_ref, feats_ref, feat, sem = rest[-6:]
+    encoded_ref, normed_ref, feats_ref, feat, sem = rest[-5:]
     copy = pltpu.make_async_copy(feat_hbm, feat, sem)
     copy.start()
     rows, model_dim = own_ref.shape
@@ -335,36 +338,55 @@
         .astype(bf16)
         .astype(f32)
     )
-    keyval_ref[...] = lax.dot_general(
-        normed, keyval_weight_ref[...], (((1,), (1,)), ((), ())), preferred_element_type=f32
-    ).astype(bf16)
-
-
-def encode(own, come, features, gain, keyval_weight_t, pair_weight, after):
+
+
+def encode(own, come, features, gain, pair_weight, after):
     rows, model_dim = own.shape
     half = rows // 2
-    columns = keyval_weight_t.shape[0]
     return pl.pallas_call(
         functools.partial(encode_kernel, len(come)),
         name="encode",
         out_shape=[
             array((half, model_dim), bf16),
             array((half, model_dim), bf16),
-            array((half, columns), bf16),
             array((half // PAIR_POOL, pair_weight.shape[1]), f32),
         ],
         in_specs=[whole_vmem(), anywhere()]
-        + [whole_vmem()] * (3 + len(come))
+        + [whole_vmem()] * (2 + len(come))
         + [anywhere()] * len(after),
-        out_specs=[whole_vmem()] * 4,
+        out_specs=[whole_vmem()] * 3,
         scratch_shapes=[pltpu.VMEM(features.shape, bf16), pltpu.SemaphoreType.DMA],
         compiler_params=pltpu.CompilerParams(vmem_limit_bytes=8 * MIB),
-        cost_estimate=pl.CostEstimate(
-            flops=2 * half * model_dim * columns,
-            bytes_accessed=6 * rows * model_dim,
-            transcendentals=0,
-        ),
-    )(gain, in_hbm(features), keyval_weight_t, pair_weight, own, *come, *after)
+    )(gain, in_hbm(features), pair_weight, own, *come, *after)
+
+
+def bundle_kernel(normed_ref, weight_ref, mine_ref, other_ref, out_ref):
+    keyval = lax.dot_general(
+        normed_ref[...], weight_ref[...], (((1,), (1,)), ((), ())), preferred_element_type=f32
+    )
+    rows, columns = keyval.shape
+    spare = out_ref.shape[1] - columns
+    pieces = []
+    for ref in (mine_ref, other_ref):
+        feats = ref[...]
+        pieces += [feats[:, g : g + spare] for g in range(0, feats.shape[1], spare)]
+    used = sum(p.shape[0] for p in pieces)
+    pieces.append(jnp.zeros((rows - used, spare), f32))
+    out_ref[...] = jnp.concatenate(
+        [keyval, jnp.concatenate(pieces, axis=0)], axis=1
+    ).astype(bf16)
+
+
+def bundle(normed, keyval_weight_t, mine, other):
+    rows = normed.shape[0]
+    return pl.pallas_call(
+        bundle_kernel,
+        name="bundle",
+        out_shape=array((rows, lane_pad(keyval_weight_t.shape[0])), bf16),
+        in_specs=[whole_vmem()] * 4,
+        out_specs=whole_vmem(),
+        compiler_params=pltpu.CompilerParams(vmem_limit_bytes=3 * MIB),
+    )(normed, keyval_weight_t, mine, other)
 
 
 def query_kernel(heads, normed_ref, scale_ref, weight_ref, out_ref):
@@ -391,17 +413,12 @@
         in_specs=[whole_vmem(), smem(), whole_vmem()],
         out_specs=whole_vmem(),
         compiler_params=pltpu.CompilerParams(vmem_limit_bytes=3 * MIB),
-        cost_estimate=pl.CostEstimate(
-            flops=2 * rows * columns * model_dim,
-            bytes_accessed=2 * columns * model_dim,
-            transcendentals=0,
-        ),
     )(normed, scale, weight)
 
 
 def attend_kernel(parts, heads, first, last, group, query_ref, start_ref, weight_ref, *rest):
     part_refs = rest[:parts]
-    out_ref, keys, values = rest[-3:]
+    out_ref, done_ref, keys, values = rest[-4:]
     rows = query_ref.shape[0]
     key_dim = query_ref.shape[1] // heads
     span = part_refs[0].shape[0]
@@ -409,7 +426,7 @@
     for k in range(parts):
         got = part_refs[k][...]
         keys[k * span : (k + 1) * span, :] = got[:, :key_dim]
-        values[k * span : (k + 1) * span, :] = got[:, key_dim:]
+        values[k * span : (k + 1) * span, :] = got[:, key_dim : key_dim + value_dim]
     total = start_ref[...].astype(f32)
     for n in range(first, last, group):
         queries = jnp.concatenate(
@@ -431,6 +448,7 @@
                 preferred_element_type=f32,
             )
     out_ref[...] = total.astype(out_ref.dtype)
+    done_ref[...] = total[0:8, 0:128]
 
 
 def attend(queries, start, output_weight, parts, heads, first, last, dtype, after=()):
@@ -442,9 +460,9 @@
     return pl.pallas_call(
         functools.partial(attend_kernel, len(parts), heads, first, last, group),
         name="attend",
-        out_shape=array((rows, model_dim), dtype),
+        out_shape=[array((rows, model_dim), dtype), array((8, 128), f32)],
         in_specs=[whole_vmem()] * (3 + len(parts)) + [anywhere()] * len(after),
-        out_specs=whole_vmem(),
+        out_specs=[whole_vmem()] * 2,
         scratch_shapes=[
             pltpu.VMEM((total_keys, key_dim), bf16),
             pltpu.VMEM((total_keys, value_dim), bf16),
@@ -452,55 +470,59 @@
         compiler_params=pltpu.CompilerParams(
             vmem_limit_bytes=8 * MIB if total_keys <= 1024 else 32 * MIB
         ),
-        cost_estimate=pl.CostEstimate(
-            flops=2
-            * rows
-            * (last - first)
-            * (total_keys * (key_dim + value_dim) + value_dim * model_dim),
-            bytes_accessed=2 * (last - first) * value_dim * model_dim,
-            transcendentals=2 * rows * (last - first) * total_keys,
-        ),
     )(queries, start, output_weight, *parts, *after)
 
 
-def split_kernel(parts, input_ref, *rest):
-    out_refs = rest[-1 - parts : -1]
-    wide = rest[-1]
-    rows = input_ref.shape[0]
-    chip, core = here()
-    me = chip * 2 + core
-    wide[...] = input_ref[...].astype(f32)
-    for k in range(parts):
-        at = pl.ds(pl.multiple_of((me ^ k) * rows, 8), rows)
-        out_refs[k][...] = wide[:, at, :].astype(bf16)
-
-
-def split_pairs(pair_input, parts, after):
-    rows, columns, dim = pair_input.shape
-    return pl.pallas_call(
-        functools.partial(split_kernel, parts),
-        name="split_pairs",
-        out_shape=[array((rows, rows, dim), bf16)] * parts,
-        in_specs=[whole_vmem()] + [anywhere()] * len(after),
-        out_specs=[whole_vmem()] * parts,
-        scratch_shapes=[pltpu.VMEM((rows, columns, dim), f32)],
+def unpack_kernel(chips, pairs, tall, *refs):
+    message_refs = refs[:chips]
+    keep_ref, give_ref, wide = refs[-3:]
+    _, core = here()
+    dim = keep_ref.shape[3]
+    padded = message_refs[0].shape[1]
+    for k in range(chips):
+        piece = message_refs[k][tall:, :]
+        piece = jnp.concatenate([piece[:, g : g + dim] for g in range(0, padded, dim)], axis=0)
+        piece = piece[: 2 * pairs * pairs].astype(f32)
+        wide[...] = piece.reshape(pairs, 2 * pairs, dim)
+        mine = pl.ds(pl.multiple_of(core * pairs, 8), pairs)
+        other = pl.ds(pl.multiple_of((1 - core) * pairs, 8), pairs)
+        keep_ref[k] = wide[:, mine, :].astype(bf16)
+        give_ref[k] = wide[:, other, :].astype(bf16)
+
+
+def unpack_pairs(messages, pairs, dim, tall, after):
+    chips = len(messages)
+    return pl.pallas_call(
+        functools.partial(unpack_kernel, chips, pairs, tall),
+        name="unpack_pairs",
+        out_shape=[array((chips, pairs, pairs, dim), bf16)] * 2,
+        in_specs=[whole_vmem()] * chips + [anywhere()] * len(after),
+        out_specs=[whole_vmem()] * 2,
+        scratch_shapes=[pltpu.VMEM((pairs, 2 * pairs, dim), f32)],
         compiler_params=pltpu.CompilerParams(vmem_limit_bytes=4 * MIB),
-    )(pair_input, *after)
-
-
-def pair_kernel(parts, input_ref, cotangent_ref, flip_ref, *rest):
-    turned_refs = rest[:parts]
-    feat_refs = rest[parts : 2 * parts]
-    out_ref, keep_ref, give_ref, stack, mirror, summed, flipped = rest[2 * parts :]
+    )(*messages, *after)
+
+
+def pair_kernel(parts, columns_used, input_ref, cotangent_ref, flip_ref, *rest):
+    turned_refs = rest[:2]
+    bundle_refs = rest[2 : 2 + parts // 2]
+    out_ref, keep_ref, give_ref, stack, mirror, summed, flipped = rest[-7:]
     rows, columns, dim = input_ref.shape
     chip, core = here()
     me = chip * 2 + core
-    own = feat_refs[0][...]
+    for k in range(parts // 2):
+        got = bundle_refs[k][:, columns_used:].astype(f32)
+        spare = got.shape[1]
+        count = 2 * dim // spare
+        for f in range(2):
+            at = f * count * rows
+            pieces = [got[at + g * rows : at + (g + 1) * rows] for g in range(count)]
+            stack[2 * k + f] = jnp.concatenate(pieces, axis=1)
+    own = stack[0]
     mine_k = own[:, dim:][None]
     for k in range(parts):
-        got = feat_refs[k][...]
-        stack[k] = got
-        value = turned_refs[k][...].astype(f32) + got[:, None, :dim] * mine_k
+        got = stack[k]
+        value = turned_refs[k % 2][k // 2].astype(f32) + got[:, None, :dim] * mine_k
         mirror[k] = value.reshape(rows * rows, dim).astype(bf16)
     target = lax.broadcasted_iota(jnp.int32, (rows * rows, rows * rows), 0)
     source = lax.broadcasted_iota(jnp.int32, (rows * rows, rows * rows), 1)
@@ -528,18 +550,18 @@
     give_ref[...] = jnp.where(core == 0, high, low)
 
 
-def pair_update(pair_input, cotangent, flip_weight, turned, feats):
+def pair_update(pair_input, cotangent, flip_weight, turned, bundles, columns_used, after):
     rows, columns, dim = pair_input.shape
-    parts = len(feats)
-    return pl.pallas_call(
-        functools.partial(pair_kernel, parts),
+    parts = 2 * len(bundles)
+    return pl.pallas_call(
+        functools.partial(pair_kernel, parts, columns_used),
         name="pair",
         out_shape=[
             array((rows, columns, dim), bf16),
             array((dim // 2, dim), f32),
             array((dim // 2, dim), f32),
         ],
-        in_specs=[whole_vmem()] * (3 + 2 * parts),
+        in_specs=[whole_vmem()] * (5 + len(bundles)) + [anywhere()] * len(after),
         out_specs=[whole_vmem()] * 3,
         scratch_shapes=[
             pltpu.VMEM((parts, rows, 2 * dim), f32),
@@ -550,12 +572,7 @@
         compiler_params=pltpu.CompilerParams(
             vmem_limit_bytes=4 * MIB if parts <= 8 else 24 * MIB
         ),
-        cost_estimate=pl.CostEstimate(
-            flops=4 * rows * columns * dim * dim,
-            bytes_accessed=8 * rows * columns * dim,
-            transcendentals=0,
-        ),
-    )(pair_input, cotangent, flip_weight, *turned, *feats)
+    )(pair_input, cotangent, flip_weight, *turned, *bundles, *after)
 
 
 def join_kernel(mine_ref, other_ref, out_ref):
@@ -607,9 +624,10 @@
 
     strip = send(edge_strip(features, taps // 2), 0, 1)
     own_weight = conv_weight.reshape(-1, model_dim)
+    own_weight, strip = lax.optimization_barrier((own_weight, strip))
     peer_weight = send(own_weight, 0, 1)
 
-    blocks = prep(features, strip, chips)
+    blocks = prep(features, strip, pair_input[0], chips)
     messages = [blocks[0]] + [None] * (chips - 1)
     for k in range(chips - 1, 0, -1):
         messages[k] = send(blocks[k], k)
@@ -620,12 +638,15 @@
 
     def partials(ks):
         dtypes = [bf16 if k & 1 else f32 for k in ks]
-        return dict(zip(ks, conv(messages, weight, taps, ks, dtypes)))
+        return dict(zip(ks, conv(messages, features.shape[0], weight, taps, ks, dtypes)))
 
     partial = partials([last])
     partial.update(partials(rest))
-    pieces = split_pairs(pair_input[0], 2 * chips, [partial[1]])
-    turned = [pieces[0]] + [send(pieces[k], k >> 1, k & 1) for k in range(1, 2 * chips)]
+    pairs, _, pair_dim = pair_input.shape[1:]
+    kept, given = unpack_pairs(
+        messages, pairs, pair_dim, features.shape[0] + strip.shape[0], [partial[1]]
+    )
+    turned = [kept, send(given, 0, 1)]
     arrived = []
     for b in range(bits):
         bit = 1 << b
@@ -638,22 +659,29 @@
                 goes = k & (2 * bit)
                 partial[k] = add_up([partial[k], value], bf16 if goes else f32)
 
-    encoded, normed, keyval, feats = encode(
-        partial[0], arrived, features, norm_gain, keyval_weight.T, pair_weight, turned
-    )
-
-    def gather(value):
-        mine = [value] + [send(value, k) for k in range(chips - 1, 0, -1)][::-1]
-        return sum(([v, send(v, 0, 1)] for v in mine), [])
-
-    all_feats = gather(feats)
-    keyvals = gather(keyval)
+    encoded, normed, feats = encode(
+        partial[0], arrived, features, norm_gain, pair_weight, turned
+    )
+    own_bundle = bundle(normed, keyval_weight.T, feats, send(feats, 0, 1))
+    bundles = [own_bundle] + [send(own_bundle, k) for k in range(chips - 1, 0, -1)][::-1]
     queries = project_queries(normed, query_weight, head_scale)
     pair_out, keep, give = pair_update(
-        pair_input[0], pair_cotangent[0], flip_weight, turned, all_feats
-    )
+        pair_input[0],
+        pair_cotangent[0],
+        flip_weight,
+        turned,
+        bundles,
+        keyval_weight.shape[1],
+        [queries],
+    )
+    keyvals = bundles + [send(v, 0, 1) for v in bundles]
     grad = add_up([keep, send(give, 0, 1)], f32)
-    grad = add_up([grad] + [send(grad, k) for k in range(1, chips)], f32)
+    halfway = heads // 2
+    first_half, done = attend(queries, encoded, output_weight, keyvals, heads, 0, halfway, f32)
+    grad = add_up([grad] + [send(grad, k) for k in range(1, chips)], f32, [done])
+    block_out, done = attend(
+        queries, first_half, output_weight, keyvals, heads, halfway, heads, bf16, [grad]
+    )
     grad = add_up(
         [grad]
         + [
@@ -661,9 +689,9 @@
             for k in range(1, windows)
         ],
         f32,
+        [done],
     )
     grad = join_halves(grad, send(grad, 0, 1))
-    block_out = attend(queries, encoded, output_weight, keyvals, heads, 0, heads, bf16)
     return (block_out[None], pair_out[None], grad)
 
 

time: 102 us -> 86.2 us (0.85)
  waiting for transfers between devices: 47.8 us -> 39.5 us
  starting transfers between devices: 30.3 us -> 22.3 us
    ppermute x34 -> x22, starting transfers between devices: 26.6 us -> 17.8 us  [send(): return lax.ppermute(value, GROUP, hop_pairs(chips, cores, flip))]
    ppermute x3, waiting for transfers between devices: 8.12 us -> 1.41 us  [per_device(): lax.ppermute(grad, 'dp', [(w, w ^ k) for w in range(windows)])]
    ppermute x34 -> x22, waiting for transfers between devices: 39.7 us -> 38 us  [send(): return lax.ppermute(value, GROUP, hop_pairs(chips, cores, flip))]
    pallas_call x1 -> x2, Pallas kernels: 3.92 us -> 4.49 us  [attend(): pl.pallas_call(functools.partial(attend_kernel, len(parts), heads, first,...]
  transfers between devices with their start and end apart: 37 -> 25, of which waited for: 18 -> 14; matrix products, arithmetic and copies ran while one was open for 0% -> 0% of each run, Pallas kernels for 13% -> 20%
where the time goes in v3:
time: 86.2 us; the launch traced here: 85.9 us
  waiting for transfers between devices  39.5 us (46%)
  Pallas kernels  23.3 us (27%)
  starting transfers between devices  22.3 us (26%)
  between operations  0.88 us (1%)
    ppermute x22, waiting for transfers between devices, send(): return lax.ppermute(value, GROUP, hop_pairs(chips, cores, flip))  38 us
    ppermute x22, starting transfers between devices, send(): return lax.ppermute(value, GROUP, hop_pairs(chips, cores, flip))  17.8 us
    pallas_call x2, Pallas kernels, conv(): pl.pallas_call(functools.partial(conv_kernel, chips, bits, taps, 512, wan...  6.98 us
    pallas_call x2, Pallas kernels, attend(): pl.pallas_call(functools.partial(attend_kernel, len(parts), heads, first,...  4.49 us
    ppermute x3, starting transfers between devices, per_device(): lax.ppermute(grad, 'dp', [(w, w ^ k) for w in range(windows)])  4.45 us
    pallas_call x1, Pallas kernels, prep(): pl.pallas_call(functools.partial(prep_kernel, chips, width), name='prep',...  3.5 us
    pallas_call x1, Pallas kernels, encode(): pl.pallas_call(functools.partial(encode_kernel, len(come)), name='encode'...  2.02 us
    pallas_call x1, Pallas kernels, pack_filter(): pl.pallas_call(functools.partial(pack_kernel, taps, padded), name='pack_f...  1.79 us
  transfers between devices with their start and end apart: 25, of which 14 were waited for; matrix products, arithmetic and copies ran while one was open for 0% of the time, Pallas kernels for 20%

profile of v3, /device:TPU:0, one launch (start us, length us, event | category | flops | bytes accessed | tf_op | source)
XLA Modules:
  0.0 85.9 jit_solution(1046852312712477881)
XLA Ops:
  3.2 3.5 %prep.1 = (bf16[320,384]{1,0:T(8,128)(2,1)S(1)}, bf16[320,384]{1,0:T(8,128)(2,1)S(1)}, bf16[320,384]{1,0:T(8,128)(2,1)S(1)}, bf16[320,384]{1,0:T(8,128)(2,1)S(1)}) custom-call(bf16[256,1408]{1,0:T(8,128)(2,1)} %bitcast.14, bf16[8,64,128]{2,1,0:T(8,128)(2,1)} %bitcast.10, bf16[16,1408]{1,0:T(8,128)(2,1)S(1)} %collective-permute-done.strip_ref), custom_call_target="tpu_custom_call" | custom-call | tf_op jit(solution)/shard_map/prep/pallas_call | solution.py:160
  6.7 2.7 %collective-permute-start.1 = (bf16[320,384]{1,0:T(8,128)(2,1)S(1)}, bf16[320,384]{1,0:T(8,128)(2,1)S(1)}, u32[]{:S(2)}, u32[]{:S(2)}) collective-permute-start(bf16[320,384]{1,0:T(8,128)(2,1)S(1)} %get-tuple-element.26), channel_id=1, source_target_pairs={{0,2},{1,3},{2,0},{3,1},{4,6},{5,7},{6,4},{7,5},{8,10},{9,11},{10,... | collective-permute-start | bytes 737288 | tf_op jit(solution)/shard_map/ppermute | solution.py:623
  9.4 1.5 %collective-permute-start.2 = (bf16[320,384]{1,0:T(8,128)(2,1)S(1)}, bf16[320,384]{1,0:T(8,128)(2,1)S(1)}, u32[]{:S(2)}, u32[]{:S(2)}) collective-permute-start(bf16[320,384]{1,0:T(8,128)(2,1)S(1)} %get-tuple-element.27), channel_id=1, source_target_pairs={{0,4},{1,5},{2,6},{3,7},{4,0},{5,1},{6,2},{7,3},{8,12},{9,13},{10,... | collective-permute-start | bytes 737288 | tf_op jit(solution)/shard_map/ppermute | solution.py:623
  11.0 1.8 %pack_filter.1.rest_4_ = bf16[1920,1536]{1,0:T(8,128)(2,1)S(1)} custom-call(bf16[880,1536]{1,0:T(8,128)(2,1)} %bitcast.17, bf16[880,1536]{1,0:T(8,128)(2,1)S(1)} %collective-permute-done.4.peer_hbm), custom_call_target="tpu_custom_call" | custom-call | tf_op jit(solution)/shard_map/pack_filter/pallas_call | solution.py:211
  12.8 3.5 %collective-permute-done.1.rest_1_.refs_1_ = bf16[320,384]{1,0:T(8,128)(2,1)S(1)} collective-permute-done((bf16[320,384]{1,0:T(8,128)(2,1)S(1)}, bf16[320,384]{1,0:T(8,128)(2,1)S(1)}, u32[]{:S(2)}, u32[]{:S(2)}) %collective-permute-start.1) | collective-permute-done | bytes 245792 | tf_op jit(solution)/shard_map/ppermute | solution.py:623
  16.2 6.4 %collective-permute-done.2.rest_2_.refs_2_ = bf16[320,384]{1,0:T(8,128)(2,1)S(1)} collective-permute-done((bf16[320,384]{1,0:T(8,128)(2,1)S(1)}, bf16[320,384]{1,0:T(8,128)(2,1)S(1)}, u32[]{:S(2)}, u32[]{:S(2)}) %collective-permute-start.2) | collective-permute-done | bytes 245792 | tf_op jit(solution)/shard_map/ppermute | solution.py:623
  22.6 1.9 %conv.3 = bf16[256,1536]{1,0:T(8,128)(2,1)S(1)} custom-call(bf16[320,384]{1,0:T(8,128)(2,1)S(1)} %get-tuple-element.25.rest_0_.refs_0_, bf16[320,384]{1,0:T(8,128)(2,1)S(1)} %collective-permute-done.1.rest_1_.refs_1_, bf16[320,384]{1,0:T(8,128)(2,1)S(1)} %collective-permute-done.2.rest_2_.refs_2_, ...), custom_call_target="tpu_custom_call" | custom-call | tf_op jit(solution)/shard_map/conv/pallas_call | solution.py:278
  24.5 1.3 %collective-permute-start.6 = (bf16[256,1536]{1,0:T(8,128)(2,1)S(1)}, bf16[256,1536]{1,0:T(8,128)(2,1)S(1)}, u32[]{:S(2)}, u32[]{:S(2)}) collective-permute-start(bf16[256,1536]{1,0:T(8,128)(2,1)S(1)} %conv.3), channel_id=1, source_target_pairs={{0,2},{1,5},{2,0},{3,7},{4,6},{5,1},{6,4},{7,3},{8,10},{9,13},{10,... | collective-permute-start | bytes 2359304 | tf_op jit(solution)/shard_map/ppermute | solution.py:623
  25.8 5.1 %conv.2 = (bf16[256,1536]{1,0:T(8,128)(2,1)S(1)}, f32[256,1536]{1,0:T(8,128)S(1)}, f32[256,1536]{1,0:T(8,128)S(1)}) custom-call(bf16[320,384]{1,0:T(8,128)(2,1)S(1)} %get-tuple-element.25.rest_0_.refs_0_, bf16[320,384]{1,0:T(8,128)(2,1)S(1)} %collective-permute-done.1.rest_1_.refs_1_, bf16[320,384]{1,0:T(8,128)(2,1)S(1)} %collective-permute-done.2.rest_2_.refs_2_, ...), custom_call_target="tpu_custom_call" | custom-call | tf_op jit(solution)/shard_map/conv/pallas_call | solution.py:278
  31.8 4.8 %collective-permute-done.6.refs_1_ = bf16[256,1536]{1,0:T(8,128)(2,1)S(1)} collective-permute-done((bf16[256,1536]{1,0:T(8,128)(2,1)S(1)}, bf16[256,1536]{1,0:T(8,128)(2,1)S(1)}, u32[]{:S(2)}, u32[]{:S(2)}) %collective-permute-start.6) | collective-permute-done | bytes 786464 | tf_op jit(solution)/shard_map/ppermute | solution.py:623
  36.7 1.6 %collective-permute-start.7 = (bf16[256,1536]{1,0:T(8,128)(2,1)S(1)}, bf16[256,1536]{1,0:T(8,128)(2,1)S(1)}, u32[]{:S(2)}, u32[]{:S(2)}) collective-permute-start(bf16[256,1536]{1,0:T(8,128)(2,1)S(1)} %add_up.4), channel_id=1, source_target_pairs={{0,4},{1,3},{2,6},{3,1},{4,0},{5,7},{6,2},{7,5},{8,12},{9,11},{10,... | collective-permute-start | bytes 2359304 | tf_op jit(solution)/shard_map/ppermute | solution.py:623
  38.5 1.2 %collective-permute-done.8.rest_3_.rest_1_ = bf16[4,8,8,128]{3,2,1,0:T(8,128)(2,1)S(1)} collective-permute-done((bf16[4,8,8,128]{3,2,1,0:T(8,128)(2,1)S(1)}, bf16[4,8,8,128]{3,2,1,0:T(8,128)(2,1)S(1)}, u32[]{:S(2)}, u32[]{:S(2)}) %collective-permute-start.8) | collective-permute-done | bytes 65568 | tf_op jit(solution)/shard_map/ppermute | solution.py:623
  39.7 12.3 %collective-permute-done.5.rest_0_ = bf16[256,1536]{1,0:T(8,128)(2,1)S(1)} collective-permute-done((bf16[256,1536]{1,0:T(8,128)(2,1)S(1)}, bf16[256,1536]{1,0:T(8,128)(2,1)S(1)}, u32[]{:S(2)}, u32[]{:S(2)}) %collective-permute-start.5) | collective-permute-done | bytes 786464 | tf_op jit(solution)/shard_map/ppermute | solution.py:623
  52.1 2.0 %encode.1 = (bf16[128,1536]{1,0:T(8,128)(2,1)S(1)}, bf16[128,1536]{1,0:T(8,128)(2,1)S(1)}, f32[8,256]{1,0:T(8,128)S(1)}) custom-call(f32[1536]{0:T(1024)S(1)} %copy-done.6, bf16[256,1408]{1,0:T(8,128)(2,1)} %bitcast.15, bf16[1536,256]{1,0:T(8,128)(2,1)S(1)} %copy-done.2, f32[256,1536]{1,0:T(8,128)S(1)} %get-tuple-element.30.own_ref, ...), custom_call_target="tpu_custom_call" | custom-call | tf_op jit(solution)/shard_map/encode/pallas_call | solution.py:346
  54.2 1.2 %collective-permute-start.9 = (f32[8,256]{1,0:T(8,128)S(1)}, f32[8,256]{1,0:T(8,128)S(1)}, u32[]{:S(2)}, u32[]{:S(2)}) collective-permute-start(f32[8,256]{1,0:T(8,128)S(1)} %get-tuple-element.37.mine_ref), channel_id=1, source_target_pairs={{0,1},{1,0},{2,3},{3,2},{4,5},{5,4},{6,7},{7,6},{8,9},{9,8},{10,11... | collective-permute-start | bytes 24584 | tf_op jit(solution)/shard_map/ppermute | solution.py:623
  56.7 1.6 %collective-permute-start.12 = (bf16[128,384]{1,0:T(8,128)(2,1)S(1)}, bf16[128,384]{1,0:T(8,128)(2,1)S(1)}, u32[]{:S(2)}, u32[]{:S(2)}) collective-permute-start(bf16[128,384]{1,0:T(8,128)(2,1)S(1)} %bundle.1.rest_0_.rest_2_), channel_id=1, source_target_pairs={{0,6},{1,7},{2,4},{3,5},{4,2},{5,3},{6,0},{7,1},{8,14},{9,15},{10,... | collective-permute-start | bytes 294920 | tf_op jit(solution)/shard_map/ppermute | solution.py:623
  58.3 1.2 %collective-permute-start.11 = (bf16[128,384]{1,0:T(8,128)(2,1)S(1)}, bf16[128,384]{1,0:T(8,128)(2,1)S(1)}, u32[]{:S(2)}, u32[]{:S(2)}) collective-permute-start(bf16[128,384]{1,0:T(8,128)(2,1)S(1)} %bundle.1.rest_0_.rest_2_), channel_id=1, source_target_pairs={{0,4},{1,5},{2,6},{3,7},{4,0},{5,1},{6,2},{7,3},{8,12},{9,13},{10,... | collective-permute-start | bytes 294920 | tf_op jit(solution)/shard_map/ppermute | solution.py:623
  60.3 3.0 %collective-permute-done.12.rest_3_.rest_5_ = bf16[128,384]{1,0:T(8,128)(2,1)S(1)} collective-permute-done((bf16[128,384]{1,0:T(8,128)(2,1)S(1)}, bf16[128,384]{1,0:T(8,128)(2,1)S(1)}, u32[]{:S(2)}, u32[]{:S(2)}) %collective-permute-start.12) | collective-permute-done | bytes 98336 | tf_op jit(solution)/shard_map/ppermute | solution.py:623
  63.3 1.5 %collective-permute-done.11.rest_2_.rest_4_ = bf16[128,384]{1,0:T(8,128)(2,1)S(1)} collective-permute-done((bf16[128,384]{1,0:T(8,128)(2,1)S(1)}, bf16[128,384]{1,0:T(8,128)(2,1)S(1)}, u32[]{:S(2)}, u32[]{:S(2)}) %collective-permute-start.11) | collective-permute-done | bytes 98336 | tf_op jit(solution)/shard_map/ppermute | solution.py:623
  68.9 1.5 %collective-permute-start.20 = (f32[64,128]{1,0:T(8,128)S(1)}, f32[64,128]{1,0:T(8,128)S(1)}, u32[]{:S(2)}, u32[]{:S(2)}) collective-permute-start(f32[64,128]{1,0:T(8,128)S(1)} %add_up.5.refs_0_), channel_id=1, source_target_pairs={{0,6},{1,7},{2,4},{3,5},{4,2},{5,3},{6,0},{7,1},{8,14},{9,15},{10,... | collective-permute-start | bytes 98312 | tf_op jit(solution)/shard_map/ppermute | solution.py:623
  72.4 1.9 %attend.2 = (f32[128,1536]{1,0:T(8,128)S(1)}, f32[8,128]{1,0:T(8,128)S(1)}) custom-call(bf16[128,1024]{1,0:T(8,128)(2,1)S(1)} %queries.1.query_ref.rest_6_, bf16[128,1536]{1,0:T(8,128)(2,1)S(1)} %get-tuple-element.36.start_ref, bf16[1536,1536]{1,0:T(8,128)(2,1)S(1)} %bitcast.8, bf16[128,384]{1,0:T(8,128)(2,1)S(1)} %bundle.1.rest_0_.rest_2_, ...), custom_call_target="tpu_custom_call" | custom-call | tf_op jit(solution)/shard_map/attend/pallas_call | solution.py:460
  75.5 3.7 %collective-permute-start.23 = (f32[64,128]{1,0:T(8,128)S(1)}, f32[64,128]{1,0:T(8,128)S(1)}, u32[]{:S(2)}, u32[]{:S(2)}) collective-permute-start(f32[64,128]{1,0:T(8,128)S(1)} %add_up.6.rest_8_.refs_0_), channel_id=1, source_target_pairs={{0,24},{8,16},{16,8},{24,0},{1,25},{9,17},{17,9},{25,1},{2,26},{10... | collective-permute-start | bytes 98312 | tf_op jit(solution)/shard_map/ppermute | solution.py:688
  80.0 2.6 %attend.3 = (bf16[128,1536]{1,0:T(8,128)(2,1)}, f32[8,128]{1,0:T(8,128)S(1)}) custom-call(bf16[128,1024]{1,0:T(8,128)(2,1)S(1)} %queries.1.query_ref.rest_6_, f32[128,1536]{1,0:T(8,128)S(1)} %get-tuple-element.38.start_ref, bf16[1536,1536]{1,0:T(8,128)(2,1)S(1)} %bitcast.8, bf16[128,384]{1,0:T(8,128)(2,1)S(1)} %bundle.1.rest_0_.rest_2_, ...), custom_call_target="tpu_custom_call" | custom-call | tf_op jit(solution)/shard_map/attend/pallas_call | solution.py:460
  82.6 1.4 %collective-permute-done.22.refs_2_ = f32[64,128]{1,0:T(8,128)S(1)} collective-permute-done((f32[64,128]{1,0:T(8,128)S(1)}, f32[64,128]{1,0:T(8,128)S(1)}, u32[]{:S(2)}, u32[]{:S(2)}) %collective-permute-start.22) | collective-permute-done | bytes 32800 | tf_op jit(solution)/shard_map/ppermute | solution.py:688
  (64 shorter events, 15.9 us)
Async XLA Ops:
  1.5 1.4 %collective-permute-start = (bf16[16,1408]{1,0:T(8,128)(2,1)S(1)}, bf16[16,1408]{1,0:T(8,128)(2,1)S(1)}, u32[]{:S(2)}, u32[]{:S(2)}) collective-permute-start(bf16[16,1408]{1,0:T(8,128)(2,1)S(1)} %edge_strip.1), channel_id=1, source_target_pairs={{0,1},{1,0},{2,3},{3,2},{4,5},{5,4},{6,7},{7,6},{8,9},{9,8},{10,11... | collective-permute-start | bytes 135176 | tf_op jit(solution)/shard_map/ppermute | solution.py:623
  2.9 8.1 %collective-permute-start.4 = (bf16[880,1536]{1,0:T(8,128)(2,1)}, bf16[880,1536]{1,0:T(8,128)(2,1)S(1)}, u32[]{:S(2)}, u32[]{:S(2)}) collective-permute-start(bf16[880,1536]{1,0:T(8,128)(2,1)} %bitcast.16), channel_id=1, source_target_pairs={{0,1},{1,0},{2,3},{3,2},{4,5},{5,4},{6,7},{7,6},{8,9},{9,8},{10,11... | collective-permute-start | bytes 8110088 | tf_op jit(solution)/shard_map/ppermute | solution.py:623
  6.7 9.5 %collective-permute-start.1 = (bf16[320,384]{1,0:T(8,128)(2,1)S(1)}, bf16[320,384]{1,0:T(8,128)(2,1)S(1)}, u32[]{:S(2)}, u32[]{:S(2)}) collective-permute-start(bf16[320,384]{1,0:T(8,128)(2,1)S(1)} %get-tuple-element.26), channel_id=1, source_target_pairs={{0,2},{1,3},{2,0},{3,1},{4,6},{5,7},{6,4},{7,5},{8,10},{9,11},{10,... | collective-permute-start | bytes 737288 | tf_op jit(solution)/shard_map/ppermute | solution.py:623
  9.4 13.2 %collective-permute-start.2 = (bf16[320,384]{1,0:T(8,128)(2,1)S(1)}, bf16[320,384]{1,0:T(8,128)(2,1)S(1)}, u32[]{:S(2)}, u32[]{:S(2)}) collective-permute-start(bf16[320,384]{1,0:T(8,128)(2,1)S(1)} %get-tuple-element.27), channel_id=1, source_target_pairs={{0,4},{1,5},{2,6},{3,7},{4,0},{5,1},{6,2},{7,3},{8,12},{9,13},{10,... | collective-permute-start | bytes 737288 | tf_op jit(solution)/shard_map/ppermute | solution.py:623
  11.0 11.7 %collective-permute-start.3 = (bf16[320,384]{1,0:T(8,128)(2,1)S(1)}, bf16[320,384]{1,0:T(8,128)(2,1)S(1)}, u32[]{:S(2)}, u32[]{:S(2)}) collective-permute-start(bf16[320,384]{1,0:T(8,128)(2,1)S(1)} %get-tuple-element.28), channel_id=1, source_target_pairs={{0,6},{1,7},{2,4},{3,5},{4,2},{5,3},{6,0},{7,1},{8,14},{9,15},{10,... | collective-permute-start | bytes 737288 | tf_op jit(solution)/shard_map/ppermute | solution.py:623
  24.5 12.1 %collective-permute-start.6 = (bf16[256,1536]{1,0:T(8,128)(2,1)S(1)}, bf16[256,1536]{1,0:T(8,128)(2,1)S(1)}, u32[]{:S(2)}, u32[]{:S(2)}) collective-permute-start(bf16[256,1536]{1,0:T(8,128)(2,1)S(1)} %conv.3), channel_id=1, source_target_pairs={{0,2},{1,5},{2,0},{3,7},{4,6},{5,1},{6,4},{7,3},{8,10},{9,13},{10,... | collective-permute-start | bytes 2359304 | tf_op jit(solution)/shard_map/ppermute | solution.py:623
  31.0 21.1 %collective-permute-start.5 = (bf16[256,1536]{1,0:T(8,128)(2,1)S(1)}, bf16[256,1536]{1,0:T(8,128)(2,1)S(1)}, u32[]{:S(2)}, u32[]{:S(2)}) collective-permute-start(bf16[256,1536]{1,0:T(8,128)(2,1)S(1)} %get-tuple-element.31.refs_4_), channel_id=1, source_target_pairs={{0,2},{1,5},{2,0},{3,7},{4,6},{5,1},{6,4},{7,3},{8,10},{9,13},{10,... | collective-permute-start | bytes 2359304 | tf_op jit(solution)/shard_map/ppermute | solution.py:623
  36.7 15.3 %collective-permute-start.7 = (bf16[256,1536]{1,0:T(8,128)(2,1)S(1)}, bf16[256,1536]{1,0:T(8,128)(2,1)S(1)}, u32[]{:S(2)}, u32[]{:S(2)}) collective-permute-start(bf16[256,1536]{1,0:T(8,128)(2,1)S(1)} %add_up.4), channel_id=1, source_target_pairs={{0,4},{1,3},{2,6},{3,1},{4,0},{5,7},{6,2},{7,5},{8,12},{9,11},{10,... | collective-permute-start | bytes 2359304 | tf_op jit(solution)/shard_map/ppermute | solution.py:623
  38.4 1.3 %collective-permute-start.8 = (bf16[4,8,8,128]{3,2,1,0:T(8,128)(2,1)S(1)}, bf16[4,8,8,128]{3,2,1,0:T(8,128)(2,1)S(1)}, u32[]{:S(2)}, u32[]{:S(2)}) collective-permute-start(bf16[4,8,8,128]{3,2,1,0:T(8,128)(2,1)S(1)} %get-tuple-element.34), channel_id=1, source_target_pairs={{0,1},{1,0},{2,3},{3,2},{4,5},{5,4},{6,7},{7,6},{8,9},{9,8},{10,11... | collective-permute-start | bytes 196616 | tf_op jit(solution)/shard_map/ppermute | solution.py:623
  54.2 2.1 %collective-permute-start.9 = (f32[8,256]{1,0:T(8,128)S(1)}, f32[8,256]{1,0:T(8,128)S(1)}, u32[]{:S(2)}, u32[]{:S(2)}) collective-permute-start(f32[8,256]{1,0:T(8,128)S(1)} %get-tuple-element.37.mine_ref), channel_id=1, source_target_pairs={{0,1},{1,0},{2,3},{3,2},{4,5},{5,4},{6,7},{7,6},{8,9},{9,8},{10,11... | collective-permute-start | bytes 24584 | tf_op jit(solution)/shard_map/ppermute | solution.py:623
  56.7 6.6 %collective-permute-start.12 = (bf16[128,384]{1,0:T(8,128)(2,1)S(1)}, bf16[128,384]{1,0:T(8,128)(2,1)S(1)}, u32[]{:S(2)}, u32[]{:S(2)}) collective-permute-start(bf16[128,384]{1,0:T(8,128)(2,1)S(1)} %bundle.1.rest_0_.rest_2_), channel_id=1, source_target_pairs={{0,6},{1,7},{2,4},{3,5},{4,2},{5,3},{6,0},{7,1},{8,14},{9,15},{10,... | collective-permute-start | bytes 294920 | tf_op jit(solution)/shard_map/ppermute | solution.py:623
  58.3 6.6 %collective-permute-start.11 = (bf16[128,384]{1,0:T(8,128)(2,1)S(1)}, bf16[128,384]{1,0:T(8,128)(2,1)S(1)}, u32[]{:S(2)}, u32[]{:S(2)}) collective-permute-start(bf16[128,384]{1,0:T(8,128)(2,1)S(1)} %bundle.1.rest_0_.rest_2_), channel_id=1, source_target_pairs={{0,4},{1,5},{2,6},{3,7},{4,0},{5,1},{6,2},{7,3},{8,12},{9,13},{10,... | collective-permute-start | bytes 294920 | tf_op jit(solution)/shard_map/ppermute | solution.py:623
  59.5 5.5 %collective-permute-start.10 = (bf16[128,384]{1,0:T(8,128)(2,1)S(1)}, bf16[128,384]{1,0:T(8,128)(2,1)S(1)}, u32[]{:S(2)}, u32[]{:S(2)}) collective-permute-start(bf16[128,384]{1,0:T(8,128)(2,1)S(1)} %bundle.1.rest_0_.rest_2_), channel_id=1, source_target_pairs={{0,2},{1,3},{2,0},{3,1},{4,6},{5,7},{6,4},{7,5},{8,10},{9,11},{10,... | collective-permute-start | bytes 294920 | tf_op jit(solution)/shard_map/ppermute | solution.py:623
  60.3 10.1 %collective-permute-start.13 = (bf16[128,384]{1,0:T(8,128)(2,1)S(1)}, bf16[128,384]{1,0:T(8,128)(2,1)S(1)}, u32[]{:S(2)}, u32[]{:S(2)}) collective-permute-start(bf16[128,384]{1,0:T(8,128)(2,1)S(1)} %bundle.1.rest_0_.rest_2_), channel_id=1, source_target_pairs={{0,1},{1,0},{2,3},{3,2},{4,5},{5,4},{6,7},{7,6},{8,9},{9,8},{10,11... | collective-permute-start | bytes 294920 | tf_op jit(solution)/shard_map/ppermute | solution.py:623
  63.3 8.3 %collective-permute-start.16 = (bf16[128,384]{1,0:T(8,128)(2,1)S(1)}, bf16[128,384]{1,0:T(8,128)(2,1)S(1)}, u32[]{:S(2)}, u32[]{:S(2)}) collective-permute-start(bf16[128,384]{1,0:T(8,128)(2,1)S(1)} %collective-permute-done.12.rest_3_.rest_5_), channel_id=1, source_target_pairs={{0,1},{1,0},{2,3},{3,2},{4,5},{5,4},{6,7},{7,6},{8,9},{9,8},{10,11... | collective-permute-start | bytes 294920 | tf_op jit(solution)/shard_map/ppermute | solution.py:623
  64.8 7.6 %collective-permute-start.15 = (bf16[128,384]{1,0:T(8,128)(2,1)S(1)}, bf16[128,384]{1,0:T(8,128)(2,1)S(1)}, u32[]{:S(2)}, u32[]{:S(2)}) collective-permute-start(bf16[128,384]{1,0:T(8,128)(2,1)S(1)} %collective-permute-done.11.rest_2_.rest_4_), channel_id=1, source_target_pairs={{0,1},{1,0},{2,3},{3,2},{4,5},{5,4},{6,7},{7,6},{8,9},{9,8},{10,11... | collective-permute-start | bytes 294920 | tf_op jit(solution)/shard_map/ppermute | solution.py:623
  65.0 7.5 %collective-permute-start.14 = (bf16[128,384]{1,0:T(8,128)(2,1)S(1)}, bf16[128,384]{1,0:T(8,128)(2,1)S(1)}, u32[]{:S(2)}, u32[]{:S(2)}) collective-permute-start(bf16[128,384]{1,0:T(8,128)(2,1)S(1)} %collective-permute-done.10.rest_1_.rest_3_), channel_id=1, source_target_pairs={{0,1},{1,0},{2,3},{3,2},{4,5},{5,4},{6,7},{7,6},{8,9},{9,8},{10,11... | collective-permute-start | bytes 294920 | tf_op jit(solution)/shard_map/ppermute | solution.py:623
  68.9 5.4 %collective-permute-start.20 = (f32[64,128]{1,0:T(8,128)S(1)}, f32[64,128]{1,0:T(8,128)S(1)}, u32[]{:S(2)}, u32[]{:S(2)}) collective-permute-start(f32[64,128]{1,0:T(8,128)S(1)} %add_up.5.refs_0_), channel_id=1, source_target_pairs={{0,6},{1,7},{2,4},{3,5},{4,2},{5,3},{6,0},{7,1},{8,14},{9,15},{10,... | collective-permute-start | bytes 98312 | tf_op jit(solution)/shard_map/ppermute | solution.py:623
  70.4 3.9 %collective-permute-start.19 = (f32[64,128]{1,0:T(8,128)S(1)}, f32[64,128]{1,0:T(8,128)S(1)}, u32[]{:S(2)}, u32[]{:S(2)}) collective-permute-start(f32[64,128]{1,0:T(8,128)S(1)} %add_up.5.refs_0_), channel_id=1, source_target_pairs={{0,4},{1,5},{2,6},{3,7},{4,0},{5,1},{6,2},{7,3},{8,12},{9,13},{10,... | collective-permute-start | bytes 98312 | tf_op jit(solution)/shard_map/ppermute | solution.py:623
  71.6 3.9 %collective-permute-start.18 = (f32[64,128]{1,0:T(8,128)S(1)}, f32[64,128]{1,0:T(8,128)S(1)}, u32[]{:S(2)}, u32[]{:S(2)}) collective-permute-start(f32[64,128]{1,0:T(8,128)S(1)} %add_up.5.refs_0_), channel_id=1, source_target_pairs={{0,2},{1,3},{2,0},{3,1},{4,6},{5,7},{6,4},{7,5},{8,10},{9,11},{10,... | collective-permute-start | bytes 98312 | tf_op jit(solution)/shard_map/ppermute | solution.py:623
  75.5 7.1 %collective-permute-start.23 = (f32[64,128]{1,0:T(8,128)S(1)}, f32[64,128]{1,0:T(8,128)S(1)}, u32[]{:S(2)}, u32[]{:S(2)}) collective-permute-start(f32[64,128]{1,0:T(8,128)S(1)} %add_up.6.rest_8_.refs_0_), channel_id=1, source_target_pairs={{0,24},{8,16},{16,8},{24,0},{1,25},{9,17},{17,9},{25,1},{2,26},{10... | collective-permute-start | bytes 98312 | tf_op jit(solution)/shard_map/ppermute | solution.py:688
  79.2 4.8 %collective-permute-start.22 = (f32[64,128]{1,0:T(8,128)S(1)}, f32[64,128]{1,0:T(8,128)S(1)}, u32[]{:S(2)}, u32[]{:S(2)}) collective-permute-start(f32[64,128]{1,0:T(8,128)S(1)} %add_up.6.rest_8_.refs_0_), channel_id=1, source_target_pairs={{0,16},{8,24},{16,0},{24,8},{1,17},{9,25},{17,1},{25,9},{2,18},{10... | collective-permute-start | bytes 98312 | tf_op jit(solution)/shard_map/ppermute | solution.py:688
  79.2 4.8 %collective-permute-start.21 = (f32[64,128]{1,0:T(8,128)S(1)}, f32[64,128]{1,0:T(8,128)S(1)}, u32[]{:S(2)}, u32[]{:S(2)}) collective-permute-start(f32[64,128]{1,0:T(8,128)S(1)} %add_up.6.rest_8_.refs_0_), channel_id=1, source_target_pairs={{0,8},{8,0},{16,24},{24,16},{1,9},{9,1},{17,25},{25,17},{2,10},{10... | collective-permute-start | bytes 98312 | tf_op jit(solution)/shard_map/ppermute | solution.py:688
  84.0 1.3 %collective-permute-start.24 = (f32[64,128]{1,0:T(8,128)S(1)}, f32[64,128]{1,0:T(8,128)S(1)}, u32[]{:S(2)}, u32[]{:S(2)}) collective-permute-start(f32[64,128]{1,0:T(8,128)S(1)} %add_up.7.mine_ref), channel_id=1, source_target_pairs={{0,1},{1,0},{2,3},{3,2},{4,5},{5,4},{6,7},{7,6},{8,9},{9,8},{10,11... | collective-permute-start | bytes 98312 | tf_op jit(solution)/shard_map/ppermute | solution.py:623
  (11 other events, 181.3 us)

commit v4 on v3

v4 whole, which is shorter than its diff:
```python
import functools
import math

import jax
import jax.numpy as jnp
from jax import lax
from jax.experimental import pallas as pl
from jax.experimental.pallas import tpu as pltpu
from jax.sharding import PartitionSpec as P

PAIR_POOL = 16
norm_eps = 1e-06
logit_cap = 50.0
MIB = 1 << 20
GROUP = ("seq", "mp")
f32, bf16 = jnp.float32, jnp.bfloat16


def whole_vmem():
    return pl.BlockSpec(memory_space=pltpu.VMEM)


def anywhere():
    return pl.BlockSpec(memory_space=pl.ANY)


def smem():
    return pl.BlockSpec(memory_space=pltpu.SMEM)


def in_hbm(value):
    return pltpu.with_memory_space_constraint(value, pltpu.HBM)


def array(shape, dtype):
    return jax.ShapeDtypeStruct(shape, dtype)


def lane_pad(width):
    return (width + 127) // 128 * 128


def tree_sum(terms):
    while len(terms) > 1:
        terms = [terms[i] + terms[i + 1] for i in range(0, len(terms), 2)]
    return terms[0]


def flipped_bits(mask, bits):
    return sum(((mask >> b) & 1) << (bits - 1 - b) for b in range(bits))


def here():
    return lax.axis_index("seq"), lax.axis_index("mp")


def hop_pairs(chips, core_masks, core_flip):
    pairs = []
    for chip in range(chips):
        for core in range(2):
            target = (chip ^ core_masks[core]) * 2 + (core ^ core_flip)
            pairs.append((chip * 2 + core, target))
    return pairs


def strip_kernel(margin, feat_hbm, out_ref, top, bottom, sems):
    rows = feat_hbm.shape[0]
    copies = [
        pltpu.make_async_copy(feat_hbm.at[0:16, :], top, sems.at[0]),
        pltpu.make_async_copy(feat_hbm.at[rows - 16 : rows, :], bottom, sems.at[1]),
    ]
    for c in copies:
        c.start()
    for c in copies:
        c.wait()
    first = top[...].astype(f32)[:margin]
    last = bottom[...].astype(f32)[16 - margin :]
    rest = jnp.zeros((16 - 2 * margin, first.shape[1]), f32)
    out_ref[...] = jnp.concatenate([first, last, rest], axis=0).astype(bf16)


def edge_strip(features, margin):
    channels = features.shape[1]
    return pl.pallas_call(
        functools.partial(strip_kernel, margin),
        name="edge_strip",
        out_shape=array((16, channels), bf16),
        in_specs=[anywhere()],
        out_specs=whole_vmem(),
        scratch_shapes=[
            pltpu.VMEM((16, channels), bf16),
            pltpu.VMEM((16, channels), bf16),
            pltpu.SemaphoreType.DMA((2,)),
        ],
        compiler_params=pltpu.CompilerParams(vmem_limit_bytes=2 * MIB),
    )(in_hbm(features))


def pick_rows(rows):
    half = rows // 2
    target = lax.broadcasted_iota(jnp.int32, (rows, rows), 0)
    source = lax.broadcasted_iota(jnp.int32, (rows, rows), 1)
    wanted = jnp.where(target < half, 2 * target, 2 * (target - half) + 1)
    return jnp.where(source == wanted, 1.0, 0.0).astype(bf16)


def gelu_rows(x, out_ref, at, chips, width):
    v = x * lax.rsqrt(jnp.mean(x * x, axis=-1, keepdims=True) + norm_eps)
    g = (0.5 * v) * (1.0 + lax.erf(v * math.sqrt(0.5)))
    g = g.astype(bf16)
    for q in range(chips):
        out_ref[q, at, 0:width] = g[:, q * width : (q + 1) * width]


def prep_kernel(chips, width, feat_hbm, pair_hbm, *rest):
    block_refs = rest[:chips]
    feat, pair, wide, split, sems = rest[chips:]
    rows = feat.shape[0]
    chip, _ = here()
    copy = pltpu.make_async_copy(feat_hbm, feat, sems.at[0])
    pair_copy = pltpu.make_async_copy(pair_hbm, pair, sems.at[1])
    copy.start()
    pair_copy.start()
    split[:, :, width:] = jnp.zeros((chips, rows, split.shape[2] - width), bf16)
    pick = pick_rows(rows)
    copy.wait()
    wide[...] = jnp.dot(pick, feat[...], preferred_element_type=f32)
    step = 32

    def body(i, carry):
        at = pl.ds(pl.multiple_of(i * step, step), step)
        gelu_rows(wide[at, :], split, at, chips, width)
        return carry

    lax.fori_loop(0, rows // step, body, 0)
    pair_copy.wait()
    pairs, _, dim = pair.shape
    lanes = split.shape[2] // dim
    extra = block_refs[0].shape[0] - rows - 16
    for k in range(chips):
        block_refs[k][0:rows, :] = split[chip ^ k]
        at = pl.ds(pl.multiple_of((chip ^ k) * 2 * pairs, 16), 2 * pairs)
        piece = pair[:, at, :].reshape(2 * pairs * pairs, dim)
        for g in range(lanes):
            part = piece[g * extra : (g + 1) * extra]
            to = rows + 16
            block_refs[k][to : to + part.shape[0], g * dim : (g + 1) * dim] = part


def prep(features, pair_input, chips):
    rows, channels = features.shape
    width = channels // chips
    padded = lane_pad(width)
    pairs, _, dim = pair_input.shape
    extra = -(-2 * pairs * pairs // (16 * (padded // dim))) * 16
    return pl.pallas_call(
        functools.partial(prep_kernel, chips, width),
        name="prep",
        out_shape=[array((rows + 16 + extra, padded), bf16)] * chips,
        in_specs=[anywhere()] * 2,
        out_specs=[whole_vmem()] * chips,
        scratch_shapes=[
            pltpu.VMEM((rows, channels), bf16),
            pltpu.VMEM(pair_input.shape, bf16),
            pltpu.VMEM((rows, channels), f32),
            pltpu.VMEM((chips, rows, padded), bf16),
            pltpu.SemaphoreType.DMA((2,)),
        ],
        compiler_params=pltpu.CompilerParams(vmem_limit_bytes=6 * MIB),
    )(in_hbm(features), in_hbm(pair_input))


def edges_kernel(chips, width, rows, strip_ref, *rest):
    block_refs = rest[chips : 2 * chips]
    split = rest[2 * chips]
    chip, _ = here()
    split[:, :, width:] = jnp.zeros((chips, 16, split.shape[2] - width), bf16)
    gelu_rows(strip_ref[...].astype(f32), split, pl.ds(0, 16), chips, width)
    for k in range(chips):
        block_refs[k][rows : rows + 16, :] = split[chip ^ k]


def add_edges(blocks, strip, rows):
    chips = len(blocks)
    width = strip.shape[1] // chips
    padded = blocks[0].shape[1]
    return pl.pallas_call(
        functools.partial(edges_kernel, chips, width, rows),
        name="add_edges",
        out_shape=[array(b.shape, bf16) for b in blocks],
        in_specs=[whole_vmem()] * (1 + chips),
        out_specs=[whole_vmem()] * chips,
        scratch_shapes=[pltpu.VMEM((chips, 16, padded), bf16)],
        input_output_aliases={1 + k: k for k in range(chips)},
        compiler_params=pltpu.CompilerParams(vmem_limit_bytes=2 * MIB),
    )(strip, *blocks)


def pack_kernel(taps, padded, own_hbm, peer_hbm, out_ref, sems):
    part = own_hbm.shape[0] // taps
    _, core = here()
    copies = []
    for p, source in enumerate((own_hbm, peer_hbm)):
        place = core if p == 0 else 1 - core
        for k in range(taps):
            to = pl.ds(pl.multiple_of(k * padded + place * part, 16), part)
            copies.append(
                pltpu.make_async_copy(
                    source.at[k * part : (k + 1) * part, :], out_ref.at[to, :], sems.at[p, k]
                )
            )
    for c in copies:
        c.start()
    if padded > 2 * part:
        for k in range(taps):
            out_ref[k * padded + 2 * part : (k + 1) * padded, :] = jnp.zeros(
                (padded - 2 * part, out_ref.shape[1]), bf16
            )
    for c in copies:
        c.wait()


def pack_filter(own, peer, taps, padded):
    model_dim = own.shape[1]
    part = own.shape[0] // taps
    if part % 16:
        own, peer = (w.reshape(taps, part, model_dim) for w in (own, peer))
        first = lax.axis_index("mp") == 0
        low, high = jnp.where(first, own, peer), jnp.where(first, peer, own)
        both = jnp.concatenate([low, high], axis=1)
        both = jnp.pad(both, ((0, 0), (0, padded - 2 * part), (0, 0)))
        return both.reshape(taps * padded, model_dim)
    return pl.pallas_call(
        functools.partial(pack_kernel, taps, padded),
        name="pack_filter",
        out_shape=array((taps * padded, model_dim), bf16),
        in_specs=[anywhere()] * 2,
        out_specs=whole_vmem(),
        scratch_shapes=[pltpu.SemaphoreType.DMA((2, taps))],
        compiler_params=pltpu.CompilerParams(vmem_limit_bytes=2 * MIB),
    )(in_hbm(own), peer)


def conv_kernel(chips, bits, taps, tile, wanted, first, outs, feat_hbm, *rest):
    count = len(wanted)
    message_refs = rest[:chips][::-1]
    weight_ref = rest[chips]
    held, cols, feat, sem = rest[-4:]
    out_refs = rest[-4 - outs : -4]
    tall, padded = held.shape[1:]
    rows = tall - 16
    half = rows // 2
    chip, core = here()
    if 0 in wanted:
        copy = pltpu.make_async_copy(feat_hbm, feat, sem)
        copy.start()
    for k in range(chips):
        held[k] = message_refs[k][0:tall, :]
    row = lax.broadcasted_iota(jnp.int32, (half, padded), 0)
    for j, k in enumerate(wanted):
        mask = jnp.where(core == 0, k, flipped_bits(k, bits))
        left = (chip ^ mask) - (1 - core)
        right = (chip ^ mask) + core
        block = held[mask]
        before = held[jnp.where(left >= 0, left ^ chip, 0), rows:tall, :].astype(f32)
        before = jnp.where(left >= 0, before, 0.0)
        after = held[jnp.where(right < chips, right ^ chip, 0), rows:tall, :].astype(f32)
        after = jnp.where(right < chips, after, 0.0)
        even = block[0:half].astype(f32)
        odd = block[half:rows].astype(f32)

        def back(v, strip_row):
            return jnp.where(row == 0, before[strip_row : strip_row + 1], pltpu.roll(v, 1, 0))

        def ahead(v, strip_row):
            return jnp.where(
                row == half - 1, after[strip_row : strip_row + 1], pltpu.roll(v, half - 1, 0)
            )

        lagged = [back(even, 2), back(odd, 3), even, odd, ahead(even, 0), ahead(odd, 1)]
        for i, v in enumerate(lagged):
            piece = v.astype(bf16)
            if i < taps:
                cols[j * rows : j * rows + half, i * padded : (i + 1) * padded] = piece
            if i > 0:
                cols[j * rows + half : (j + 1) * rows, (i - 1) * padded : i * padded] = piece
    pick = pick_rows(rows)
    if 0 in wanted:
        copy.wait()
    halves = len(out_refs) // count
    span = out_refs[0].shape[1]
    for j, k in enumerate(wanted):
        for h in range(halves):
            for n in range(0, span, tile):
                at = first + h * span + n
                got = jnp.dot(
                    cols[j * rows : (j + 1) * rows],
                    weight_ref[:, at : at + tile],
                    preferred_element_type=f32,
                )
                if k == 0 and at < feat.shape[1]:
                    width = min(tile, feat.shape[1] - at)
                    skip = jnp.dot(
                        pick, feat[:, at : at + width], preferred_element_type=f32
                    )
                    if width < tile:
                        skip = jnp.concatenate(
                            [skip, jnp.zeros((rows, tile - width), f32)], axis=1
                        )
                    got = got + skip
                out_refs[j * halves + h][:, n : n + tile] = got.astype(out_refs[j * halves].dtype)


def conv(messages, features, weight, taps, wanted, dtypes, columns, after):
    chips = len(messages)
    bits = chips.bit_length() - 1
    padded = messages[0].shape[1]
    depth, model_dim = weight.shape
    rows = features.shape[0]
    tall = rows + 16
    count = len(wanted)
    first, last = columns
    span = model_dim // 2
    halves = (last - first) // span
    got = pl.pallas_call(
        functools.partial(
            conv_kernel, chips, bits, taps, 256, wanted, first, count * halves
        ),
        name="conv",
        out_shape=[array((rows, span), d) for d in dtypes for _ in range(halves)],
        in_specs=[anywhere()] + [whole_vmem()] * (chips + 1) + [anywhere()] * len(after),
        out_specs=[whole_vmem()] * (count * halves),
        scratch_shapes=[
            pltpu.VMEM((chips, tall, padded), bf16),
            pltpu.VMEM((count * rows, depth), bf16),
            pltpu.VMEM(features.shape, bf16),
            pltpu.SemaphoreType.DMA,
        ],
        compiler_params=pltpu.CompilerParams(vmem_limit_bytes=(5 + 2 * count) * MIB),
    )(in_hbm(features), *messages[::-1], weight, *after)
    return [got[j * halves : (j + 1) * halves] for j in range(count)]


def sum_kernel(count, *refs):
    out_ref = refs[-1]
    out_ref[...] = tree_sum([r[...].astype(f32) for r in refs[:count][::-1]]).astype(out_ref.dtype)


def add_up(terms, dtype, after=()):
    return pl.pallas_call(
        functools.partial(sum_kernel, len(terms)),
        name="add_up",
        out_shape=array(terms[0].shape, dtype),
        in_specs=[whole_vmem()] * len(terms) + [anywhere()] * len(after),
        out_specs=whole_vmem(),
        compiler_params=pltpu.CompilerParams(vmem_limit_bytes=4 * MIB),
    )(*terms[::-1], *after)


def encode_kernel(pieces, arrivals, pair_weight_ref, *rest):
    own_refs = rest[:pieces]
    come_refs = rest[pieces : pieces + arrivals * pieces]
    encoded_ref, feats_ref = rest[-2:]
    rows, span = own_refs[0].shape
    half = rows // 2
    pairs = half // PAIR_POOL
    at = lax.broadcasted_iota(jnp.int32, (pairs, half), 0)
    of = lax.broadcasted_iota(jnp.int32, (pairs, half), 1) // PAIR_POOL
    spread = jnp.where(at == of, 1.0 / PAIR_POOL, 0.0).astype(bf16)
    feats = jnp.zeros(feats_ref.shape, f32)
    for h in range(pieces):
        total = own_refs[h][...]
        for a in range(arrivals):
            total = total + come_refs[a * pieces + h][...].astype(f32)
        encoded = jnp.maximum(total[:half], total[half:]).astype(bf16)
        encoded_ref[:, h * span : (h + 1) * span] = encoded
        pooled = jnp.dot(spread, encoded, preferred_element_type=f32).astype(bf16)
        feats = feats + jnp.dot(
            pooled, pair_weight_ref[h * span : (h + 1) * span, :], preferred_element_type=f32
        )
    feats_ref[...] = feats.astype(bf16).astype(f32)


def encode(own, come, pair_weight, after):
    rows, span = own[0].shape
    pieces = len(own)
    half = rows // 2
    return pl.pallas_call(
        functools.partial(encode_kernel, pieces, len(come)),
        name="encode",
        out_shape=[
            array((half, span * pieces), bf16),
            array((half // PAIR_POOL, pair_weight.shape[1]), f32),
        ],
        in_specs=[whole_vmem()] * (1 + pieces * (1 + len(come))) + [anywhere()] * len(after),
        out_specs=[whole_vmem()] * 2,
        compiler_params=pltpu.CompilerParams(vmem_limit_bytes=8 * MIB),
    )(pair_weight, *own, *sum(come, []), *after)


def normalised(encoded_ref, gain_ref):
    wide = encoded_ref[...].astype(f32)
    scale = lax.rsqrt(jnp.mean(wide * wide, axis=-1, keepdims=True) + norm_eps)
    return (wide * scale * gain_ref[...][None]).astype(bf16)


def bundle_kernel(encoded_ref, gain_ref, weight_ref, mine_ref, other_ref, out_ref):
    keyval = lax.dot_general(
        normalised(encoded_ref, gain_ref),
        weight_ref[...],
        (((1,), (1,)), ((), ())),
        preferred_element_type=f32,
    )
    rows, columns = keyval.shape
    spare = out_ref.shape[1] - columns
    pieces = []
    for ref in (mine_ref, other_ref):
        feats = ref[...]
        pieces += [feats[:, g : g + spare] for g in range(0, feats.shape[1], spare)]
    used = sum(p.shape[0] for p in pieces)
    pieces.append(jnp.zeros((rows - used, spare), f32))
    out_ref[...] = jnp.concatenate(
        [keyval, jnp.concatenate(pieces, axis=0)], axis=1
    ).astype(bf16)


def bundle(encoded, gain, weight_t, mine, other):
    return pl.pallas_call(
        bundle_kernel,
        name="bundle",
        out_shape=array((encoded.shape[0], lane_pad(weight_t.shape[0])), bf16),
        in_specs=[whole_vmem()] * 5,
        out_specs=whole_vmem(),
        compiler_params=pltpu.CompilerParams(vmem_limit_bytes=4 * MIB),
    )(encoded, gain, weight_t, mine, other)


def attend_kernel(
    parts,
    heads,
    first,
    last,
    group,
    scale_ref,
    encoded_ref,
    gain_ref,
    query_weight_ref,
    start_ref,
    weight_ref,
    *rest,
):
    part_refs = rest[:parts]
    out_ref, done_ref, keys, values = rest[-4:]
    rows = encoded_ref.shape[0]
    key_dim = query_weight_ref.shape[1] // heads
    normed = normalised(encoded_ref, gain_ref)
    span = part_refs[0].shape[0]
    value_dim = values.shape[1]
    for k in range(parts):
        got = part_refs[k][...]
        keys[k * span : (k + 1) * span, :] = got[:, :key_dim]
        values[k * span : (k + 1) * span, :] = got[:, key_dim : key_dim + value_dim]
    total = start_ref[...].astype(f32)
    for n in range(first, last, group):
        got = jnp.dot(
            normed,
            query_weight_ref[:, n * key_dim : (n + group) * key_dim],
            preferred_element_type=f32,
        )
        queries = jnp.concatenate(
            [
                got[:, h * key_dim : (h + 1) * key_dim]
                * (scale_ref[n + h] / math.sqrt(key_dim))
                for h in range(group)
            ],
            axis=0,
        ).astype(bf16)
        scores = lax.dot_general(
            queries, keys[...], (((1,), (1,)), ((), ())), preferred_element_type=f32
        )
        weights = jnp.exp(logit_cap * jnp.tanh(scores * (1.0 / logit_cap)))
        sums = jnp.sum(weights, axis=-1, keepdims=True)
        mixed = jnp.dot(weights.astype(bf16), values[...], preferred_element_type=f32) / sums
        mixed = mixed.astype(bf16)
        for h in range(group):
            at = (n + h) * value_dim
            total = total + jnp.dot(
                mixed[h * rows : (h + 1) * rows],
                weight_ref[at : at + value_dim, :],
                preferred_element_type=f32,
            )
    out_ref[...] = total.astype(out_ref.dtype)
    done_ref[...] = total[0:8, 0:128]


def attend(
    encoded, gain, query_weight, scale, start, output_weight, parts, first, last, dtype, after
):
    rows, model_dim = start.shape
    heads = scale.shape[0]
    key_dim = query_weight.shape[1] // heads
    value_dim = output_weight.shape[0] // heads
    total_keys = parts[0].shape[0] * len(parts)
    group = 2
    return pl.pallas_call(
        functools.partial(attend_kernel, len(parts), heads, first, last, group),
        name="attend",
        out_shape=[array((rows, model_dim), dtype), array((8, 128), f32)],
        in_specs=[smem()] + [whole_vmem()] * (5 + len(parts)) + [anywhere()] * len(after),
        out_specs=[whole_vmem()] * 2,
        scratch_shapes=[
            pltpu.VMEM((total_keys, key_dim), bf16),
            pltpu.VMEM((total_keys, value_dim), bf16),
        ],
        compiler_params=pltpu.CompilerParams(
            vmem_limit_bytes=8 * MIB if total_keys <= 1024 else 32 * MIB
        ),
    )(scale, encoded, gain, query_weight, start, output_weight, *parts, *after)


def unpack_kernel(chips, pairs, tall, *refs):
    message_refs = refs[:chips][::-1]
    out_ref = refs[-1]
    dim = out_ref.shape[2]
    padded = message_refs[0].shape[1]
    for k in range(chips):
        piece = message_refs[k][tall:, :]
        piece = jnp.concatenate([piece[:, g : g + dim] for g in range(0, padded, dim)], axis=0)
        piece = piece[: 2 * pairs * pairs].reshape(pairs, 2 * pairs, dim)
        out_ref[k * pairs : (k + 1) * pairs] = piece


def unpack_pairs(messages, pairs, dim, tall, after):
    chips = len(messages)
    return pl.pallas_call(
        functools.partial(unpack_kernel, chips, pairs, tall),
        name="unpack_pairs",
        out_shape=array((chips * pairs, 2 * pairs, dim), bf16),
        in_specs=[whole_vmem()] * chips + [anywhere()] * len(after),
        out_specs=whole_vmem(),
        compiler_params=pltpu.CompilerParams(vmem_limit_bytes=4 * MIB),
    )(*messages[::-1], *after)


def pair_kernel(
    chips, columns_used, input_ref, cotangent_ref, other_cotangent_ref, flip_ref, turned_ref, other_ref, *rest
):
    bundle_refs = rest[:chips][::-1]
    out_ref, grad_ref, stacked, mirror, summed, flipped, cotangent = rest[-7:]
    rows, columns, dim = input_ref.shape
    parts = 2 * chips
    wide = 2 * rows
    chip, core = here()
    me = chip * 2 + core
    for k in range(chips):
        got = bundle_refs[k][:, columns_used:].astype(f32)
        count = 2 * dim // got.shape[1]
        for f in range(2):
            at = f * count * rows
            stacked[2 * k + f] = jnp.concatenate(
                [got[at + g * rows : at + (g + 1) * rows] for g in range(count)], axis=1
            )
    own, other = stacked[0], stacked[1]
    both_k = jnp.concatenate(
        [jnp.where(core == 0, own, other), jnp.where(core == 0, other, own)], axis=0
    )[:, dim:][None]
    for k in range(parts):
        source = turned_ref if k % 2 == 0 else other_ref
        value = source[k // 2 * rows : (k // 2 + 1) * rows].astype(f32)
        value = value + stacked[k][:, None, :dim] * both_k
        mirror[k] = value.reshape(rows * wide, dim).astype(bf16)
    target = lax.broadcasted_iota(jnp.int32, (rows * wide, rows * wide), 0)
    origin = lax.broadcasted_iota(jnp.int32, (rows * wide, rows * wide), 1)
    swap = jnp.where(origin == (target % rows) * wide + target // rows, 1.0, 0.0).astype(bf16)
    for b in range(parts):
        turned = jnp.dot(swap, mirror[b ^ me], preferred_element_type=f32)
        flipped[:, b * rows : (b + 1) * rows, :] = turned.reshape(wide, rows, dim)
    every = jnp.concatenate([stacked[b ^ me] for b in range(parts)], axis=0)[:, dim:]
    for i in range(rows):
        at = pl.ds(i * columns, columns)
        value = input_ref[i].astype(f32) + own[i : i + 1, :dim] * every
        summed[at, :] = value.astype(bf16)
    facing = flipped[pl.ds(core * rows, rows)].reshape(rows * columns, dim).astype(bf16)
    update = jnp.dot(facing, flip_ref[...], preferred_element_type=f32)
    update = update + summed[...].astype(f32)
    out_ref[...] = update.astype(bf16).reshape(rows, columns, dim)
    cotangent[pl.ds(core * rows, rows)] = cotangent_ref[...]
    cotangent[pl.ds((1 - core) * rows, rows)] = other_cotangent_ref[...]
    grad = lax.dot_general(
        flipped[...].reshape(wide * columns, dim).astype(bf16),
        cotangent[...].reshape(wide * columns, dim),
        (((0,), (0,)), ((), ())),
        preferred_element_type=f32,
    )
    grad_ref[...] = grad.astype(bf16)


def pair_update(pair_input, cotangents, flip_weight, turned, bundles, columns_used):
    rows, columns, dim = pair_input.shape
    chips = len(bundles)
    return pl.pallas_call(
        functools.partial(pair_kernel, chips, columns_used),
        name="pair",
        out_shape=[array((rows, columns, dim), bf16), array((dim, dim), bf16)],
        in_specs=[whole_vmem()] * (6 + chips),
        out_specs=[whole_vmem()] * 2,
        scratch_shapes=[
            pltpu.VMEM((2 * chips, rows, 2 * dim), f32),
            pltpu.VMEM((2 * chips, 2 * rows * rows, dim), bf16),
            pltpu.VMEM((rows * columns, dim), bf16),
            pltpu.VMEM((2 * rows, columns, dim), f32),
            pltpu.VMEM((2 * rows, columns, dim), bf16),
        ],
        compiler_params=pltpu.CompilerParams(
            vmem_limit_bytes=6 * MIB if chips <= 4 else 32 * MIB
        ),
    )(pair_input, *cotangents, flip_weight, *turned, *bundles[::-1])


def per_device(
    features,
    conv_weight,
    norm_gain,
    query_weight,
    keyval_weight,
    head_scale,
    output_weight,
    pair_weight,
    pair_input,
    flip_weight,
    pair_cotangent,
):
    chips = lax.axis_size("seq")
    bits = chips.bit_length() - 1
    windows = lax.axis_size("dp")
    taps = conv_weight.shape[0]
    model_dim = output_weight.shape[1]
    heads = head_scale.shape[0]
    features = features[0]

    masks = [(k, flipped_bits(k, bits)) for k in range(chips)]

    def send(value, mask, flip=0):
        cores = mask if isinstance(mask, tuple) else (mask, mask)
        return lax.ppermute(value, GROUP, hop_pairs(chips, cores, flip))

    strip = send(edge_strip(features, taps // 2), 0, 1)
    own_weight = conv_weight.reshape(-1, model_dim)
    own_weight, strip = lax.optimization_barrier((own_weight, strip))
    peer_weight = send(own_weight, 0, 1)

    blocks = add_edges(prep(features, pair_input[0], chips), strip, features.shape[0])
    messages = [blocks[0]] + [None] * (chips - 1)
    for k in range(chips - 1, 0, -1):
        messages[k] = send(blocks[k], k)
    weight = pack_filter(own_weight, peer_weight, taps, blocks[0].shape[1])
    cotangent, weight = lax.optimization_barrier((pair_cotangent[0], weight))
    cotangents = (pair_cotangent[0], send(cotangent, 0, 1))

    last = chips - 1
    rest = sorted(range(last), key=lambda k: (1 - (k & 1), -k))

    def partials(ks, columns, after):
        dtypes = [bf16 if k & 1 else f32 for k in ks]
        return dict(zip(ks, conv(messages, features, weight, taps, ks, dtypes, columns, after)))

    partial = partials([last], (0, model_dim // 2), [])
    partial[last] += partials([last], (model_dim // 2, model_dim), [cotangents[1]])[last]
    pairs, _, pair_dim = pair_input.shape[1:]
    turned = unpack_pairs(
        messages, pairs, pair_dim, features.shape[0] + strip.shape[0], partial[last]
    )
    turned = (turned, send(turned, 0, 1))
    for ks in ([k for k in rest if k & 1], [k for k in rest if k and not k & 1], [0]):
        partial.update(partials(ks, (0, model_dim), []))
    arrived = []
    for b in range(bits):
        bit = 1 << b
        leaving = [k for k in [last] + rest if k in partial and k & bit]
        got = {k ^ bit: [send(v, masks[bit]) for v in partial.pop(k)] for k in leaving}
        for k, values in got.items():
            if k == 0:
                arrived.append(values)
            else:
                dtype = bf16 if k & (2 * bit) else f32
                partial[k] = [
                    add_up([p, v], dtype, [turned[1]]) for p, v in zip(partial[k], values)
                ]

    encoded, feats = encode(partial[0], arrived, pair_weight, [])
    own_bundle = bundle(encoded, norm_gain, keyval_weight.T, feats, send(feats, 0, 1))
    bundles = [own_bundle] + [send(own_bundle, k) for k in range(chips - 1, 0, -1)][::-1]
    pair_out, grad = pair_update(
        pair_input[0], cotangents, flip_weight, turned, bundles, keyval_weight.shape[1]
    )
    keyvals = bundles + [send(v, 0, 1) for v in bundles]

    def attend_heads(start, first, end, dtype, after):
        return attend(
            encoded,
            norm_gain,
            query_weight,
            head_scale,
            start,
            output_weight,
            keyvals,
            first,
            end,
            dtype,
            after,
        )

    halfway = heads // 2
    first_half, done = attend_heads(encoded, 0, halfway, f32, [])
    grad = add_up([grad] + [send(grad, k) for k in range(1, chips)], bf16, [done])
    block_out, done = attend_heads(first_half, halfway, heads, bf16, [grad])
    grad = add_up(
        [grad]
        + [
            lax.ppermute(grad, "dp", [(w, w ^ k) for w in range(windows)])
            for k in range(1, windows)
        ],
        f32,
        [done],
    )
    return (block_out[None], pair_out[None], grad)


def solution(mesh):
    placed = (
        P("dp", ("seq", "mp"), None),
        P(None, ("seq", "mp"), None),
        P(),
        P(),
        P(),
        P(),
        P(),
        P(),
        P("dp", ("seq", "mp"), None, None),
        P(),
        P("dp", ("seq", "mp"), None, None),
    )
    return jax.shard_map(
        per_device,
        mesh=mesh,
        in_specs=placed,
        out_specs=(P("dp", ("seq", "mp"), None), P("dp", ("seq", "mp"), None, None), P()),
        check_vma=False,
    )
```

time: 86.2 us -> 80.5 us (0.934)
  waiting for transfers between devices: 39.5 us -> 29.9 us
  starting transfers between devices: 22.3 us -> 24.7 us
  Pallas kernels: 23.3 us -> 24.7 us
    ppermute x22 -> x24, waiting for transfers between devices: 38 us -> 29.5 us  [send(): return lax.ppermute(value, GROUP, hop_pairs(chips, cores, flip))]
    ppermute x22 -> x24, starting transfers between devices: 17.8 us -> 20.2 us  [send(): return lax.ppermute(value, GROUP, hop_pairs(chips, cores, flip))]
    pallas_call x2, Pallas kernels: 4.49 us -> 6.38 us  [attend(): pl.pallas_call(functools.partial(attend_kernel, len(parts), heads, first,...]
    ppermute x3, waiting for transfers between devices: 1.41 us -> 0.46 us  [per_device(): lax.ppermute(grad, 'dp', [(w, w ^ k) for w in range(windows)])]
    pallas_call x7 -> x9, Pallas kernels: 12.4 us -> 11.5 us  [the longest x5 9.14 us: conv(): pl.pallas_call(functools.partial(conv_kernel, chips, bits, taps, 256, wan...]
  transfers between devices with their start and end apart: 25 -> 27, of which waited for: 14 -> 11; matrix products, arithmetic and copies ran while one was open for 0% -> 0% of each run, Pallas kernels for 20% -> 28%
where the time goes in v4:
time: 80.5 us; the launch traced here: 80.3 us
  waiting for transfers between devices  29.9 us (37%)
  Pallas kernels  24.7 us (31%)
  starting transfers between devices  24.7 us (31%)
  between operations  0.92 us (1%)
    ppermute x24, waiting for transfers between devices, send(): return lax.ppermute(value, GROUP, hop_pairs(chips, cores, flip))  29.5 us
    ppermute x24, starting transfers between devices, send(): return lax.ppermute(value, GROUP, hop_pairs(chips, cores, flip))  20.2 us
    pallas_call x5, Pallas kernels, conv(): pl.pallas_call(functools.partial(conv_kernel, chips, bits, taps, 256, wan...  9.14 us
    pallas_call x2, Pallas kernels, attend(): pl.pallas_call(functools.partial(attend_kernel, len(parts), heads, first,...  6.38 us
    ppermute x3, starting transfers between devices, per_device(): lax.ppermute(grad, 'dp', [(w, w ^ k) for w in range(windows)])  4.45 us
    pallas_call x1, Pallas kernels, prep(): pl.pallas_call(functools.partial(prep_kernel, chips, width), name='prep',...  3.31 us
    pallas_call x1, Pallas kernels, pack_filter(): pl.pallas_call(functools.partial(pack_kernel, taps, padded), name='pack_f...  1.79 us
  transfers between devices with their start and end apart: 27, of which 11 were waited for; matrix products, arithmetic and copies ran while one was open for 0% of the time, Pallas kernels for 28%

profile of v4, /device:TPU:0, one launch (start us, length us, event | category | flops | bytes accessed | tf_op | source)
XLA Modules:
  0.0 80.3 jit_solution(859559363344004645)
XLA Ops:
  3.2 3.3 %prep.1 = (bf16[320,384]{1,0:T(8,128)(2,1)S(1)}, bf16[320,384]{1,0:T(8,128)(2,1)S(1)}, bf16[320,384]{1,0:T(8,128)(2,1)S(1)}, bf16[320,384]{1,0:T(8,128)(2,1)S(1)}) custom-call(bf16[256,1408]{1,0:T(8,128)(2,1)} %bitcast.15, bf16[8,64,128]{2,1,0:T(8,128)(2,1)} %bitcast.10), custom_call_target="tpu_custom_call" | custom-call | tf_op jit(solution)/shard_map/prep/pallas_call | solution.py:156
  6.7 3.7 %collective-permute-start.1 = (bf16[320,384]{1,0:T(8,128)(2,1)S(1)}, bf16[320,384]{1,0:T(8,128)(2,1)S(1)}, u32[]{:S(2)}, u32[]{:S(2)}) collective-permute-start(bf16[320,384]{1,0:T(8,128)(2,1)S(1)} %get-tuple-element.34), channel_id=1, source_target_pairs={{0,6},{1,7},{2,4},{3,5},{4,2},{5,3},{6,0},{7,1},{8,14},{9,15},{10,... | collective-permute-start | bytes 737288 | tf_op jit(solution)/shard_map/ppermute | solution.py:645
  11.1 1.8 %pack_filter.1.rest_4_ = bf16[1920,1536]{1,0:T(8,128)(2,1)S(1)} custom-call(bf16[880,1536]{1,0:T(8,128)(2,1)} %bitcast.22, bf16[880,1536]{1,0:T(8,128)(2,1)S(1)} %collective-permute-done.4.peer_hbm), custom_call_target="tpu_custom_call" | custom-call | tf_op jit(solution)/shard_map/pack_filter/pallas_call | solution.py:233
  13.0 4.3 %collective-permute-done.1.rest_0_.refs_0_ = bf16[320,384]{1,0:T(8,128)(2,1)S(1)} collective-permute-done((bf16[320,384]{1,0:T(8,128)(2,1)S(1)}, bf16[320,384]{1,0:T(8,128)(2,1)S(1)}, u32[]{:S(2)}, u32[]{:S(2)}) %collective-permute-start.1) | collective-permute-done | bytes 245792 | tf_op jit(solution)/shard_map/ppermute | solution.py:645
  17.3 4.9 %collective-permute-done.2.rest_1_.refs_1_ = bf16[320,384]{1,0:T(8,128)(2,1)S(1)} collective-permute-done((bf16[320,384]{1,0:T(8,128)(2,1)S(1)}, bf16[320,384]{1,0:T(8,128)(2,1)S(1)}, u32[]{:S(2)}, u32[]{:S(2)}) %collective-permute-start.2) | collective-permute-done | bytes 245792 | tf_op jit(solution)/shard_map/ppermute | solution.py:645
  23.5 1.6 %collective-permute-start.7 = (bf16[256,768]{1,0:T(8,128)(2,1)S(1)}, bf16[256,768]{1,0:T(8,128)(2,1)S(1)}, u32[]{:S(2)}, u32[]{:S(2)}) collective-permute-start(bf16[256,768]{1,0:T(8,128)(2,1)S(1)} %conv.7.refs_4_), channel_id=1, source_target_pairs={{0,2},{1,5},{2,0},{3,7},{4,6},{5,1},{6,4},{7,3},{8,10},{9,13},{10,... | collective-permute-start | bytes 1179656 | tf_op jit(solution)/shard_map/ppermute | solution.py:645
  26.9 1.9 %conv.6 = (bf16[256,768]{1,0:T(8,128)(2,1)S(1)}, bf16[256,768]{1,0:T(8,128)(2,1)S(1)}) custom-call(bf16[256,1408]{1,0:T(8,128)(2,1)} %bitcast.18, bf16[320,384]{1,0:T(8,128)(2,1)S(1)} %collective-permute-done.1.rest_0_.refs_0_, bf16[320,384]{1,0:T(8,128)(2,1)S(1)} %collective-permute-done.2.rest_1_.refs_1_, ...), custom_call_target="tpu_custom_call" | custom-call | tf_op jit(solution)/shard_map/conv/pallas_call | solution.py:325
  28.8 1.6 %collective-permute-start.5 = (bf16[256,768]{1,0:T(8,128)(2,1)S(1)}, bf16[256,768]{1,0:T(8,128)(2,1)S(1)}, u32[]{:S(2)}, u32[]{:S(2)}) collective-permute-start(bf16[256,768]{1,0:T(8,128)(2,1)S(1)} %get-tuple-element.42), channel_id=1, source_target_pairs={{0,2},{1,5},{2,0},{3,7},{4,6},{5,1},{6,4},{7,3},{8,10},{9,13},{10,... | collective-permute-start | bytes 1179656 | tf_op jit(solution)/shard_map/ppermute | solution.py:645
  30.9 1.9 %conv.8 = (f32[256,768]{1,0:T(8,128)S(1)}, f32[256,768]{1,0:T(8,128)S(1)}) custom-call(bf16[256,1408]{1,0:T(8,128)(2,1)} %bitcast.19, bf16[320,384]{1,0:T(8,128)(2,1)S(1)} %collective-permute-done.1.rest_0_.refs_0_, bf16[320,384]{1,0:T(8,128)(2,1)S(1)} %collective-permute-done.2.rest_1_.refs_1_, bf16[320,384]{1,0:T(8,128)(2,1)S(1)} %collective-permute-done.3.rest_2_.refs_2_, ...), custom_call_target="tpu_custom_call" | custom-call | tf_op jit(solution)/shard_map/conv/pallas_call | solution.py:325
  32.9 1.5 %collective-permute-start.10 = (bf16[256,768]{1,0:T(8,128)(2,1)S(1)}, bf16[256,768]{1,0:T(8,128)(2,1)S(1)}, u32[]{:S(2)}, u32[]{:S(2)}) collective-permute-start(bf16[256,768]{1,0:T(8,128)(2,1)S(1)} %add_up.4), channel_id=1, source_target_pairs={{0,4},{1,3},{2,6},{3,1},{4,0},{5,7},{6,2},{7,5},{8,12},{9,11},{10,... | collective-permute-start | bytes 1179656 | tf_op jit(solution)/shard_map/ppermute | solution.py:645
  35.7 1.5 %collective-permute-start.12 = (bf16[256,768]{1,0:T(8,128)(2,1)S(1)}, bf16[256,768]{1,0:T(8,128)(2,1)S(1)}, u32[]{:S(2)}, u32[]{:S(2)}) collective-permute-start(bf16[256,768]{1,0:T(8,128)(2,1)S(1)} %add_up.5), channel_id=1, source_target_pairs={{0,4},{1,3},{2,6},{3,1},{4,0},{5,7},{6,2},{7,5},{8,12},{9,11},{10,... | collective-permute-start | bytes 1179656 | tf_op jit(solution)/shard_map/ppermute | solution.py:645
  37.2 3.2 %conv.5 = (f32[256,768]{1,0:T(8,128)S(1)}, f32[256,768]{1,0:T(8,128)S(1)}) custom-call(bf16[256,1408]{1,0:T(8,128)(2,1)} %bitcast.20, bf16[320,384]{1,0:T(8,128)(2,1)S(1)} %collective-permute-done.1.rest_0_.refs_0_, bf16[320,384]{1,0:T(8,128)(2,1)S(1)} %collective-permute-done.2.rest_1_.refs_1_, bf16[320,384]{1,0:T(8,128)(2,1)S(1)} %collective-permute-done.3.rest_2_.refs_2_, ...), custom_call_target="tpu_custom_call" | custom-call | tf_op jit(solution)/shard_map/conv/pallas_call | solution.py:325
  40.5 3.6 %collective-permute-done.5.rest_2_ = bf16[256,768]{1,0:T(8,128)(2,1)S(1)} collective-permute-done((bf16[256,768]{1,0:T(8,128)(2,1)S(1)}, bf16[256,768]{1,0:T(8,128)(2,1)S(1)}, u32[]{:S(2)}, u32[]{:S(2)}) %collective-permute-start.5) | collective-permute-done | bytes 393248 | tf_op jit(solution)/shard_map/ppermute | solution.py:645
  44.1 8.4 %collective-permute-done.6.rest_3_ = bf16[256,768]{1,0:T(8,128)(2,1)S(1)} collective-permute-done((bf16[256,768]{1,0:T(8,128)(2,1)S(1)}, bf16[256,768]{1,0:T(8,128)(2,1)S(1)}, u32[]{:S(2)}, u32[]{:S(2)}) %collective-permute-start.6) | collective-permute-done | bytes 393248 | tf_op jit(solution)/shard_map/ppermute | solution.py:645
  54.7 1.6 %collective-permute-start.14 = (bf16[128,384]{1,0:T(8,128)(2,1)S(1)}, bf16[128,384]{1,0:T(8,128)(2,1)S(1)}, u32[]{:S(2)}, u32[]{:S(2)}) collective-permute-start(bf16[128,384]{1,0:T(8,128)(2,1)S(1)} %bundle.1.rest_0_.rest_3_), channel_id=1, source_target_pairs={{0,2},{1,3},{2,0},{3,1},{4,6},{5,7},{6,4},{7,5},{8,10},{9,11},{10,... | collective-permute-start | bytes 294920 | tf_op jit(solution)/shard_map/ppermute | solution.py:645
  56.8 1.4 %collective-permute-start.16 = (bf16[128,384]{1,0:T(8,128)(2,1)S(1)}, bf16[128,384]{1,0:T(8,128)(2,1)S(1)}, u32[]{:S(2)}, u32[]{:S(2)}) collective-permute-start(bf16[128,384]{1,0:T(8,128)(2,1)S(1)} %bundle.1.rest_0_.rest_3_), channel_id=1, source_target_pairs={{0,6},{1,7},{2,4},{3,5},{4,2},{5,3},{6,0},{7,1},{8,14},{9,15},{10,... | collective-permute-start | bytes 294920 | tf_op jit(solution)/shard_map/ppermute | solution.py:645
  58.2 1.4 %collective-permute-done.14.rest_1_.rest_2_ = bf16[128,384]{1,0:T(8,128)(2,1)S(1)} collective-permute-done((bf16[128,384]{1,0:T(8,128)(2,1)S(1)}, bf16[128,384]{1,0:T(8,128)(2,1)S(1)}, u32[]{:S(2)}, u32[]{:S(2)}) %collective-permute-start.14) | collective-permute-done | bytes 98336 | tf_op jit(solution)/shard_map/ppermute | solution.py:645
  59.6 3.3 %collective-permute-done.15.rest_2_.rest_1_ = bf16[128,384]{1,0:T(8,128)(2,1)S(1)} collective-permute-done((bf16[128,384]{1,0:T(8,128)(2,1)S(1)}, bf16[128,384]{1,0:T(8,128)(2,1)S(1)}, u32[]{:S(2)}, u32[]{:S(2)}) %collective-permute-start.15) | collective-permute-done | bytes 98336 | tf_op jit(solution)/shard_map/ppermute | solution.py:645
  63.5 1.3 %pair.1 = (bf16[8,64,128]{2,1,0:T(8,128)(2,1)}, bf16[128,128]{1,0:T(8,128)(2,1)S(1)}) custom-call(bf16[8,64,128]{2,1,0:T(8,128)(2,1)S(1)} %bitcast.11, bf16[8,64,128]{2,1,0:T(8,128)(2,1)S(1)} %bitcast.13, bf16[8,64,128]{2,1,0:T(8,128)(2,1)S(1)} %collective-permute-done.8.rest_5_.other_cotangent_ref, bf16[128,128]{1,0:T(8,128)(2,1)S(1)} %copy-done.6, ...), custom_call_target="tpu_custom_call" | custom-call | tf_op jit(solution)/shard_map/pair/pallas_call | solution.py:601
  64.7 1.4 %collective-permute-start.21 = (bf16[128,128]{1,0:T(8,128)(2,1)S(1)}, bf16[128,128]{1,0:T(8,128)(2,1)S(1)}, u32[]{:S(2)}, u32[]{:S(2)}) collective-permute-start(bf16[128,128]{1,0:T(8,128)(2,1)S(1)} %get-tuple-element.50.refs_3_), channel_id=1, source_target_pairs={{0,6},{1,7},{2,4},{3,5},{4,2},{5,3},{6,0},{7,1},{8,14},{9,15},{10,... | collective-permute-start | bytes 98312 | tf_op jit(solution)/shard_map/ppermute | solution.py:645
  66.5 1.8 %collective-permute-start.23 = (bf16[128,128]{1,0:T(8,128)(2,1)S(1)}, bf16[128,128]{1,0:T(8,128)(2,1)S(1)}, u32[]{:S(2)}, u32[]{:S(2)}) collective-permute-start(bf16[128,128]{1,0:T(8,128)(2,1)S(1)} %get-tuple-element.50.refs_3_), channel_id=1, source_target_pairs={{0,2},{1,3},{2,0},{3,1},{4,6},{5,7},{6,4},{7,5},{8,10},{9,11},{10,... | collective-permute-start | bytes 98312 | tf_op jit(solution)/shard_map/ppermute | solution.py:645
  68.3 2.8 %attend.2 = (f32[128,1536]{1,0:T(8,128)S(1)}, f32[8,128]{1,0:T(8,128)S(1)}) custom-call(f32[8]{0:T(128)S(1)} %copy-done.7, bf16[128,1536]{1,0:T(8,128)(2,1)S(1)} %get-tuple-element.47.encoded_ref.start_ref, f32[1536]{0:T(1024)S(1)} %copy-done.5, bf16[1536,1024]{1,0:T(8,128)(2,1)S(1)} %copy-done, ...), custom_call_target="tpu_custom_call" | custom-call | tf_op jit(solution)/shard_map/attend/pallas_call | solution.py:505
  71.2 3.7 %collective-permute-start.24 = (bf16[128,128]{1,0:T(8,128)(2,1)S(1)}, bf16[128,128]{1,0:T(8,128)(2,1)S(1)}, u32[]{:S(2)}, u32[]{:S(2)}) collective-permute-start(bf16[128,128]{1,0:T(8,128)(2,1)S(1)} %add_up.6.rest_8_.refs_3_), channel_id=1, source_target_pairs={{0,24},{8,16},{16,8},{24,0},{1,25},{9,17},{17,9},{25,1},{2,26},{10... | collective-permute-start | bytes 98312 | tf_op jit(solution)/shard_map/ppermute | solution.py:720
  75.6 3.6 %attend.3 = (bf16[128,1536]{1,0:T(8,128)(2,1)}, f32[8,128]{1,0:T(8,128)S(1)}) custom-call(f32[8]{0:T(128)S(1)} %copy-done.7, bf16[128,1536]{1,0:T(8,128)(2,1)S(1)} %get-tuple-element.47.encoded_ref.start_ref, f32[1536]{0:T(1024)S(1)} %copy-done.5, bf16[1536,1024]{1,0:T(8,128)(2,1)S(1)} %copy-done, f32[128,1536]{1,0:T(8,128)S(1)} %get-tuple-element.49.start_ref, ...), custom_call_target="tpu_custom_call" | custom-call | tf_op jit(solution)/shard_map/attend/pallas_call | solution.py:505
  (70 shorter events, 14.2 us)
Async XLA Ops:
  2.9 8.2 %collective-permute-start.4 = (bf16[880,1536]{1,0:T(8,128)(2,1)}, bf16[880,1536]{1,0:T(8,128)(2,1)S(1)}, u32[]{:S(2)}, u32[]{:S(2)}) collective-permute-start(bf16[880,1536]{1,0:T(8,128)(2,1)} %bitcast.21), channel_id=1, source_target_pairs={{0,1},{1,0},{2,3},{3,2},{4,5},{5,4},{6,7},{7,6},{8,9},{9,8},{10,11... | collective-permute-start | bytes 8110088 | tf_op jit(solution)/shard_map/ppermute | solution.py:645
  6.7 10.5 %collective-permute-start.1 = (bf16[320,384]{1,0:T(8,128)(2,1)S(1)}, bf16[320,384]{1,0:T(8,128)(2,1)S(1)}, u32[]{:S(2)}, u32[]{:S(2)}) collective-permute-start(bf16[320,384]{1,0:T(8,128)(2,1)S(1)} %get-tuple-element.34), channel_id=1, source_target_pairs={{0,6},{1,7},{2,4},{3,5},{4,2},{5,3},{6,0},{7,1},{8,14},{9,15},{10,... | collective-permute-start | bytes 737288 | tf_op jit(solution)/shard_map/ppermute | solution.py:645
  10.4 11.7 %collective-permute-start.2 = (bf16[320,384]{1,0:T(8,128)(2,1)S(1)}, bf16[320,384]{1,0:T(8,128)(2,1)S(1)}, u32[]{:S(2)}, u32[]{:S(2)}) collective-permute-start(bf16[320,384]{1,0:T(8,128)(2,1)S(1)} %get-tuple-element.35), channel_id=1, source_target_pairs={{0,4},{1,5},{2,6},{3,7},{4,0},{5,1},{6,2},{7,3},{8,12},{9,13},{10,... | collective-permute-start | bytes 737288 | tf_op jit(solution)/shard_map/ppermute | solution.py:645
  10.9 11.5 %collective-permute-start.3 = (bf16[320,384]{1,0:T(8,128)(2,1)S(1)}, bf16[320,384]{1,0:T(8,128)(2,1)S(1)}, u32[]{:S(2)}, u32[]{:S(2)}) collective-permute-start(bf16[320,384]{1,0:T(8,128)(2,1)S(1)} %get-tuple-element.36), channel_id=1, source_target_pairs={{0,2},{1,3},{2,0},{3,1},{4,6},{5,7},{6,4},{7,5},{8,10},{9,11},{10,... | collective-permute-start | bytes 737288 | tf_op jit(solution)/shard_map/ppermute | solution.py:645
  12.9 12.2 %collective-permute-start.8 = (bf16[8,64,128]{2,1,0:T(8,128)(2,1)S(1)}, bf16[8,64,128]{2,1,0:T(8,128)(2,1)S(1)}, u32[]{:S(2)}, u32[]{:S(2)}) collective-permute-start(bf16[8,64,128]{2,1,0:T(8,128)(2,1)S(1)} %bitcast.12), channel_id=1, source_target_pairs={{0,1},{1,0},{2,3},{3,2},{4,5},{5,4},{6,7},{7,6},{8,9},{9,8},{10,11... | collective-permute-start | bytes 393224 | tf_op jit(solution)/shard_map/ppermute | solution.py:645
  23.5 9.3 %collective-permute-start.7 = (bf16[256,768]{1,0:T(8,128)(2,1)S(1)}, bf16[256,768]{1,0:T(8,128)(2,1)S(1)}, u32[]{:S(2)}, u32[]{:S(2)}) collective-permute-start(bf16[256,768]{1,0:T(8,128)(2,1)S(1)} %conv.7.refs_4_), channel_id=1, source_target_pairs={{0,2},{1,5},{2,0},{3,7},{4,6},{5,1},{6,4},{7,3},{8,10},{9,13},{10,... | collective-permute-start | bytes 1179656 | tf_op jit(solution)/shard_map/ppermute | solution.py:645
  26.2 9.4 %collective-permute-start.11 = (bf16[256,768]{1,0:T(8,128)(2,1)S(1)}, bf16[256,768]{1,0:T(8,128)(2,1)S(1)}, u32[]{:S(2)}, u32[]{:S(2)}) collective-permute-start(bf16[256,768]{1,0:T(8,128)(2,1)S(1)} %conv.9.refs_5_), channel_id=1, source_target_pairs={{0,2},{1,5},{2,0},{3,7},{4,6},{5,1},{6,4},{7,3},{8,10},{9,13},{10,... | collective-permute-start | bytes 1179656 | tf_op jit(solution)/shard_map/ppermute | solution.py:645
  26.8 6.0 %collective-permute-start.9 = (bf16[32,16,128]{2,1,0:T(8,128)(2,1)S(1)}, bf16[32,16,128]{2,1,0:T(8,128)(2,1)S(1)}, u32[]{:S(2)}, u32[]{:S(2)}) collective-permute-start(bf16[32,16,128]{2,1,0:T(8,128)(2,1)S(1)} %unpack_pairs.1.turned_ref), channel_id=1, source_target_pairs={{0,1},{1,0},{2,3},{3,2},{4,5},{5,4},{6,7},{7,6},{8,9},{9,8},{10,11... | collective-permute-start | bytes 393224 | tf_op jit(solution)/shard_map/ppermute | solution.py:645
  28.8 15.2 %collective-permute-start.5 = (bf16[256,768]{1,0:T(8,128)(2,1)S(1)}, bf16[256,768]{1,0:T(8,128)(2,1)S(1)}, u32[]{:S(2)}, u32[]{:S(2)}) collective-permute-start(bf16[256,768]{1,0:T(8,128)(2,1)S(1)} %get-tuple-element.42), channel_id=1, source_target_pairs={{0,2},{1,5},{2,0},{3,7},{4,6},{5,1},{6,4},{7,3},{8,10},{9,13},{10,... | collective-permute-start | bytes 1179656 | tf_op jit(solution)/shard_map/ppermute | solution.py:645
  30.4 22.1 %collective-permute-start.6 = (bf16[256,768]{1,0:T(8,128)(2,1)S(1)}, bf16[256,768]{1,0:T(8,128)(2,1)S(1)}, u32[]{:S(2)}, u32[]{:S(2)}) collective-permute-start(bf16[256,768]{1,0:T(8,128)(2,1)S(1)} %get-tuple-element.43), channel_id=1, source_target_pairs={{0,2},{1,5},{2,0},{3,7},{4,6},{5,1},{6,4},{7,3},{8,10},{9,13},{10,... | collective-permute-start | bytes 1179656 | tf_op jit(solution)/shard_map/ppermute | solution.py:645
  32.9 19.6 %collective-permute-start.10 = (bf16[256,768]{1,0:T(8,128)(2,1)S(1)}, bf16[256,768]{1,0:T(8,128)(2,1)S(1)}, u32[]{:S(2)}, u32[]{:S(2)}) collective-permute-start(bf16[256,768]{1,0:T(8,128)(2,1)S(1)} %add_up.4), channel_id=1, source_target_pairs={{0,4},{1,3},{2,6},{3,1},{4,0},{5,7},{6,2},{7,5},{8,12},{9,11},{10,... | collective-permute-start | bytes 1179656 | tf_op jit(solution)/shard_map/ppermute | solution.py:645
  35.7 16.7 %collective-permute-start.12 = (bf16[256,768]{1,0:T(8,128)(2,1)S(1)}, bf16[256,768]{1,0:T(8,128)(2,1)S(1)}, u32[]{:S(2)}, u32[]{:S(2)}) collective-permute-start(bf16[256,768]{1,0:T(8,128)(2,1)S(1)} %add_up.5), channel_id=1, source_target_pairs={{0,4},{1,3},{2,6},{3,1},{4,0},{5,7},{6,2},{7,5},{8,12},{9,11},{10,... | collective-permute-start | bytes 1179656 | tf_op jit(solution)/shard_map/ppermute | solution.py:645
  54.7 4.9 %collective-permute-start.14 = (bf16[128,384]{1,0:T(8,128)(2,1)S(1)}, bf16[128,384]{1,0:T(8,128)(2,1)S(1)}, u32[]{:S(2)}, u32[]{:S(2)}) collective-permute-start(bf16[128,384]{1,0:T(8,128)(2,1)S(1)} %bundle.1.rest_0_.rest_3_), channel_id=1, source_target_pairs={{0,2},{1,3},{2,0},{3,1},{4,6},{5,7},{6,4},{7,5},{8,10},{9,11},{10,... | collective-permute-start | bytes 294920 | tf_op jit(solution)/shard_map/ppermute | solution.py:645
  56.2 6.7 %collective-permute-start.15 = (bf16[128,384]{1,0:T(8,128)(2,1)S(1)}, bf16[128,384]{1,0:T(8,128)(2,1)S(1)}, u32[]{:S(2)}, u32[]{:S(2)}) collective-permute-start(bf16[128,384]{1,0:T(8,128)(2,1)S(1)} %bundle.1.rest_0_.rest_3_), channel_id=1, source_target_pairs={{0,4},{1,5},{2,6},{3,7},{4,0},{5,1},{6,2},{7,3},{8,12},{9,13},{10,... | collective-permute-start | bytes 294920 | tf_op jit(solution)/shard_map/ppermute | solution.py:645
  56.8 6.1 %collective-permute-start.16 = (bf16[128,384]{1,0:T(8,128)(2,1)S(1)}, bf16[128,384]{1,0:T(8,128)(2,1)S(1)}, u32[]{:S(2)}, u32[]{:S(2)}) collective-permute-start(bf16[128,384]{1,0:T(8,128)(2,1)S(1)} %bundle.1.rest_0_.rest_3_), channel_id=1, source_target_pairs={{0,6},{1,7},{2,4},{3,5},{4,2},{5,3},{6,0},{7,1},{8,14},{9,15},{10,... | collective-permute-start | bytes 294920 | tf_op jit(solution)/shard_map/ppermute | solution.py:645
  58.2 7.9 %collective-permute-start.17 = (bf16[128,384]{1,0:T(8,128)(2,1)S(1)}, bf16[128,384]{1,0:T(8,128)(2,1)S(1)}, u32[]{:S(2)}, u32[]{:S(2)}) collective-permute-start(bf16[128,384]{1,0:T(8,128)(2,1)S(1)} %bundle.1.rest_0_.rest_3_), channel_id=1, source_target_pairs={{0,1},{1,0},{2,3},{3,2},{4,5},{5,4},{6,7},{7,6},{8,9},{9,8},{10,11... | collective-permute-start | bytes 294920 | tf_op jit(solution)/shard_map/ppermute | solution.py:645
  59.6 6.8 %collective-permute-start.18 = (bf16[128,384]{1,0:T(8,128)(2,1)S(1)}, bf16[128,384]{1,0:T(8,128)(2,1)S(1)}, u32[]{:S(2)}, u32[]{:S(2)}) collective-permute-start(bf16[128,384]{1,0:T(8,128)(2,1)S(1)} %collective-permute-done.14.rest_1_.rest_2_), channel_id=1, source_target_pairs={{0,1},{1,0},{2,3},{3,2},{4,5},{5,4},{6,7},{7,6},{8,9},{9,8},{10,11... | collective-permute-start | bytes 294920 | tf_op jit(solution)/shard_map/ppermute | solution.py:645
  63.0 5.3 %collective-permute-start.19 = (bf16[128,384]{1,0:T(8,128)(2,1)S(1)}, bf16[128,384]{1,0:T(8,128)(2,1)S(1)}, u32[]{:S(2)}, u32[]{:S(2)}) collective-permute-start(bf16[128,384]{1,0:T(8,128)(2,1)S(1)} %collective-permute-done.15.rest_2_.rest_1_), channel_id=1, source_target_pairs={{0,1},{1,0},{2,3},{3,2},{4,5},{5,4},{6,7},{7,6},{8,9},{9,8},{10,11... | collective-permute-start | bytes 294920 | tf_op jit(solution)/shard_map/ppermute | solution.py:645
  63.0 5.3 %collective-permute-start.20 = (bf16[128,384]{1,0:T(8,128)(2,1)S(1)}, bf16[128,384]{1,0:T(8,128)(2,1)S(1)}, u32[]{:S(2)}, u32[]{:S(2)}) collective-permute-start(bf16[128,384]{1,0:T(8,128)(2,1)S(1)} %collective-permute-done.16.rest_3_.rest_0_), channel_id=1, source_target_pairs={{0,1},{1,0},{2,3},{3,2},{4,5},{5,4},{6,7},{7,6},{8,9},{9,8},{10,11... | collective-permute-start | bytes 294920 | tf_op jit(solution)/shard_map/ppermute | solution.py:645
  64.7 6.4 %collective-permute-start.21 = (bf16[128,128]{1,0:T(8,128)(2,1)S(1)}, bf16[128,128]{1,0:T(8,128)(2,1)S(1)}, u32[]{:S(2)}, u32[]{:S(2)}) collective-permute-start(bf16[128,128]{1,0:T(8,128)(2,1)S(1)} %get-tuple-element.50.refs_3_), channel_id=1, source_target_pairs={{0,6},{1,7},{2,4},{3,5},{4,2},{5,3},{6,0},{7,1},{8,14},{9,15},{10,... | collective-permute-start | bytes 98312 | tf_op jit(solution)/shard_map/ppermute | solution.py:645
  66.1 5.0 %collective-permute-start.22 = (bf16[128,128]{1,0:T(8,128)(2,1)S(1)}, bf16[128,128]{1,0:T(8,128)(2,1)S(1)}, u32[]{:S(2)}, u32[]{:S(2)}) collective-permute-start(bf16[128,128]{1,0:T(8,128)(2,1)S(1)} %get-tuple-element.50.refs_3_), channel_id=1, source_target_pairs={{0,4},{1,5},{2,6},{3,7},{4,0},{5,1},{6,2},{7,3},{8,12},{9,13},{10,... | collective-permute-start | bytes 98312 | tf_op jit(solution)/shard_map/ppermute | solution.py:645
  71.2 8.0 %collective-permute-start.24 = (bf16[128,128]{1,0:T(8,128)(2,1)S(1)}, bf16[128,128]{1,0:T(8,128)(2,1)S(1)}, u32[]{:S(2)}, u32[]{:S(2)}) collective-permute-start(bf16[128,128]{1,0:T(8,128)(2,1)S(1)} %add_up.6.rest_8_.refs_3_), channel_id=1, source_target_pairs={{0,24},{8,16},{16,8},{24,0},{1,25},{9,17},{17,9},{25,1},{2,26},{10... | collective-permute-start | bytes 98312 | tf_op jit(solution)/shard_map/ppermute | solution.py:720
  74.8 4.8 %collective-permute-start.25 = (bf16[128,128]{1,0:T(8,128)(2,1)S(1)}, bf16[128,128]{1,0:T(8,128)(2,1)S(1)}, u32[]{:S(2)}, u32[]{:S(2)}) collective-permute-start(bf16[128,128]{1,0:T(8,128)(2,1)S(1)} %add_up.6.rest_8_.refs_3_), channel_id=1, source_target_pairs={{0,16},{8,24},{16,0},{24,8},{1,17},{9,25},{17,1},{25,9},{2,18},{10... | collective-permute-start | bytes 98312 | tf_op jit(solution)/shard_map/ppermute | solution.py:720
  74.8 4.8 %collective-permute-start.26 = (bf16[128,128]{1,0:T(8,128)(2,1)S(1)}, bf16[128,128]{1,0:T(8,128)(2,1)S(1)}, u32[]{:S(2)}, u32[]{:S(2)}) collective-permute-start(bf16[128,128]{1,0:T(8,128)(2,1)S(1)} %add_up.6.rest_8_.refs_3_), channel_id=1, source_target_pairs={{0,8},{8,0},{16,24},{24,16},{1,9},{9,1},{17,25},{25,17},{2,10},{10... | collective-permute-start | bytes 98312 | tf_op jit(solution)/shard_map/ppermute | solution.py:720
  (13 other events, 196.4 us)

commit v5 on v4

--- a/solution.py
+++ b/solution.py
@@ -9,6 +9,7 @@
 from jax.sharding import PartitionSpec as P
 
 PAIR_POOL = 16
+SPARE_ROWS = 32
 norm_eps = 1e-06
 logit_cap = 50.0
 MIB = 1 << 20
@@ -63,39 +64,6 @@
     return pairs
 
 
-def strip_kernel(margin, feat_hbm, out_ref, top, bottom, sems):
-    rows = feat_hbm.shape[0]
-    copies = [
-        pltpu.make_async_copy(feat_hbm.at[0:16, :], top, sems.at[0]),
-        pltpu.make_async_copy(feat_hbm.at[rows - 16 : rows, :], bottom, sems.at[1]),
-    ]
-    for c in copies:
-        c.start()
-    for c in copies:
-        c.wait()
-    first = top[...].astype(f32)[:margin]
-    last = bottom[...].astype(f32)[16 - margin :]
-    rest = jnp.zeros((16 - 2 * margin, first.shape[1]), f32)
-    out_ref[...] = jnp.concatenate([first, last, rest], axis=0).astype(bf16)
-
-
-def edge_strip(features, margin):
-    channels = features.shape[1]
-    return pl.pallas_call(
-        functools.partial(strip_kernel, margin),
-        name="edge_strip",
-        out_shape=array((16, channels), bf16),
-        in_specs=[anywhere()],
-        out_specs=whole_vmem(),
-        scratch_shapes=[
-            pltpu.VMEM((16, channels), bf16),
-            pltpu.VMEM((16, channels), bf16),
-            pltpu.SemaphoreType.DMA((2,)),
-        ],
-        compiler_params=pltpu.CompilerParams(vmem_limit_bytes=2 * MIB),
-    )(in_hbm(features))
-
-
 def pick_rows(rows):
     half = rows // 2
     target = lax.broadcasted_iota(jnp.int32, (rows, rows), 0)
@@ -104,47 +72,48 @@
     return jnp.where(source == wanted, 1.0, 0.0).astype(bf16)
 
 
-def gelu_rows(x, out_ref, at, chips, width):
-    v = x * lax.rsqrt(jnp.mean(x * x, axis=-1, keepdims=True) + norm_eps)
-    g = (0.5 * v) * (1.0 + lax.erf(v * math.sqrt(0.5)))
-    g = g.astype(bf16)
-    for q in range(chips):
-        out_ref[q, at, 0:width] = g[:, q * width : (q + 1) * width]
-
-
 def prep_kernel(chips, width, feat_hbm, pair_hbm, *rest):
     block_refs = rest[:chips]
-    feat, pair, wide, split, sems = rest[chips:]
+    feat, pair, split, sems = rest[chips:]
     rows = feat.shape[0]
     chip, _ = here()
     copy = pltpu.make_async_copy(feat_hbm, feat, sems.at[0])
     pair_copy = pltpu.make_async_copy(pair_hbm, pair, sems.at[1])
     copy.start()
     pair_copy.start()
-    split[:, :, width:] = jnp.zeros((chips, rows, split.shape[2] - width), bf16)
-    pick = pick_rows(rows)
     copy.wait()
-    wide[...] = jnp.dot(pick, feat[...], preferred_element_type=f32)
-    step = 32
-
-    def body(i, carry):
-        at = pl.ds(pl.multiple_of(i * step, step), step)
-        gelu_rows(wide[at, :], split, at, chips, width)
-        return carry
-
-    lax.fori_loop(0, rows // step, body, 0)
+    x = feat[...].astype(f32)
+    scale = lax.rsqrt(jnp.mean(x * x, axis=-1, keepdims=True) + norm_eps)
+    high = scale.astype(bf16)
+    middle = (scale - high.astype(f32)).astype(bf16)
+    low = (scale - high.astype(f32) - middle.astype(f32)).astype(bf16)
+    lane = lax.broadcasted_iota(jnp.int32, (rows, split.shape[2] - width), 1)
+    tail = jnp.where(
+        lane == 0,
+        high.astype(f32),
+        jnp.where(
+            lane == 1, middle.astype(f32), jnp.where(lane == 2, low.astype(f32), 0.0)
+        ),
+    ).astype(bf16)
+    for q in range(chips):
+        split[q, :, 0:width] = feat[:, q * width : (q + 1) * width]
+        split[q, :, width:] = tail
     pair_copy.wait()
     pairs, _, dim = pair.shape
     lanes = split.shape[2] // dim
-    extra = block_refs[0].shape[0] - rows - 16
+    extra = block_refs[0].shape[0] - rows
+    spare = dim * SPARE_ROWS // rows
     for k in range(chips):
-        block_refs[k][0:rows, :] = split[chip ^ k]
         at = pl.ds(pl.multiple_of((chip ^ k) * 2 * pairs, 16), 2 * pairs)
         piece = pair[:, at, :].reshape(2 * pairs * pairs, dim)
+        block_refs[k][0:rows, :] = split[chip ^ k]
+        for g in range(dim // spare):
+            block_refs[k][
+                g * SPARE_ROWS : (g + 1) * SPARE_ROWS, width + 8 : width + 8 + spare
+            ] = piece[:SPARE_ROWS, g * spare : (g + 1) * spare]
         for g in range(lanes):
-            part = piece[g * extra : (g + 1) * extra]
-            to = rows + 16
-            block_refs[k][to : to + part.shape[0], g * dim : (g + 1) * dim] = part
+            part = piece[SPARE_ROWS + g * extra : SPARE_ROWS + (g + 1) * extra]
+            block_refs[k][rows : rows + part.shape[0], g * dim : (g + 1) * dim] = part
 
 
 def prep(features, pair_input, chips):
@@ -152,48 +121,94 @@
     width = channels // chips
     padded = lane_pad(width)
     pairs, _, dim = pair_input.shape
-    extra = -(-2 * pairs * pairs // (16 * (padded // dim))) * 16
+    extra = -(-(2 * pairs * pairs - SPARE_ROWS) // (16 * (padded // dim))) * 16
     return pl.pallas_call(
         functools.partial(prep_kernel, chips, width),
         name="prep",
-        out_shape=[array((rows + 16 + extra, padded), bf16)] * chips,
+        out_shape=[array((rows + extra, padded), bf16)] * chips,
         in_specs=[anywhere()] * 2,
         out_specs=[whole_vmem()] * chips,
         scratch_shapes=[
             pltpu.VMEM((rows, channels), bf16),
             pltpu.VMEM(pair_input.shape, bf16),
-            pltpu.VMEM((rows, channels), f32),
             pltpu.VMEM((chips, rows, padded), bf16),
             pltpu.SemaphoreType.DMA((2,)),
         ],
-        compiler_params=pltpu.CompilerParams(vmem_limit_bytes=6 * MIB),
+        compiler_params=pltpu.CompilerParams(vmem_limit_bytes=10 * MIB),
     )(in_hbm(features), in_hbm(pair_input))
 
 
-def edges_kernel(chips, width, rows, strip_ref, *rest):
-    block_refs = rest[chips : 2 * chips]
-    split = rest[2 * chips]
-    chip, _ = here()
-    split[:, :, width:] = jnp.zeros((chips, 16, split.shape[2] - width), bf16)
-    gelu_rows(strip_ref[...].astype(f32), split, pl.ds(0, 16), chips, width)
+def gelu_of(block, width):
+    scale = block[:, width : width + 1] + block[:, width + 1 : width + 2]
+    scale = scale + block[:, width + 2 : width + 3]
+    v = block * scale
+    g = (0.5 * v) * (1.0 + lax.erf(v * math.sqrt(0.5)))
+    lane = lax.broadcasted_iota(jnp.int32, block.shape, 1)
+    return jnp.where(lane < width, g, 0.0)
+
+
+def edges_kernel(chips, width, rows, *refs):
+    message_refs = refs[:chips][::-1]
+    out_ref = refs[-1]
+    strips = []
+    for ref in message_refs:
+        for start, row in ((0, 0), (0, 1), (rows - 16, 14), (rows - 16, 15)):
+            strips.append(ref[start : start + 16, :].astype(f32)[row : row + 1])
+    prepared = gelu_of(jnp.concatenate(strips, axis=0), width)
     for k in range(chips):
-        block_refs[k][rows : rows + 16, :] = split[chip ^ k]
-
-
-def add_edges(blocks, strip, rows):
-    chips = len(blocks)
-    width = strip.shape[1] // chips
-    padded = blocks[0].shape[1]
+        out_ref[k, 0:4] = prepared[4 * k : 4 * k + 4]
+        out_ref[k, 4:8] = jnp.zeros((4, prepared.shape[1]), f32)
+
+
+def edge_rows(messages, width, rows, after):
+    chips = len(messages)
+    padded = messages[0].shape[1]
     return pl.pallas_call(
         functools.partial(edges_kernel, chips, width, rows),
-        name="add_edges",
-        out_shape=[array(b.shape, bf16) for b in blocks],
-        in_specs=[whole_vmem()] * (1 + chips),
-        out_specs=[whole_vmem()] * chips,
-        scratch_shapes=[pltpu.VMEM((chips, 16, padded), bf16)],
-        input_output_aliases={1 + k: k for k in range(chips)},
+        name="edge_rows",
+        out_shape=array((chips, 8, padded), f32),
+        in_specs=[whole_vmem()] * chips + [anywhere()] * len(after),
+        out_specs=whole_vmem(),
         compiler_params=pltpu.CompilerParams(vmem_limit_bytes=2 * MIB),
-    )(strip, *blocks)
+    )(*messages[::-1], *after)
+
+
+def activate_kernel(width, count, *refs):
+    message_refs, out_ref, wide = refs[:count], refs[-2], refs[-1]
+    _, core = here()
+    step = 32
+    rows = out_ref.shape[0]
+    pick = pick_rows(rows)
+    if count == 1:
+        wide[...] = jnp.dot(pick, message_refs[0][0:rows, :], preferred_element_type=f32)
+    else:
+
+        @pl.when(core == 0)
+        def _():
+            wide[...] = jnp.dot(pick, message_refs[0][0:rows, :], preferred_element_type=f32)
+
+        @pl.when(core != 0)
+        def _():
+            wide[...] = jnp.dot(pick, message_refs[1][0:rows, :], preferred_element_type=f32)
+
+    def body(i, carry):
+        at = pl.ds(pl.multiple_of(i * step, step), step)
+        out_ref[at, :] = gelu_of(wide[at, :], width).astype(bf16)
+        return carry
+
+    lax.fori_loop(0, out_ref.shape[0] // step, body, 0)
+
+
+def activate(messages, width, rows, after):
+    return pl.pallas_call(
+        functools.partial(activate_kernel, width, len(messages)),
+        name="activate",
+        out_shape=array((rows, messages[0].shape[1]), bf16),
+        in_specs=[whole_vmem()] * len(messages) + [anywhere()] * len(after),
+        out_specs=whole_vmem(),
+        scratch_shapes=[pltpu.VMEM((rows, messages[0].shape[1]), f32)],
+        compiler_params=pltpu.CompilerParams(vmem_limit_bytes=3 * MIB),
+    )(*messages, *after)
 
 
 def pack_kernel(taps, padded, own_hbm, peer_hbm, out_ref, sems):
@@ -241,30 +256,27 @@
     )(in_hbm(own), peer)
 
 
-def conv_kernel(chips, bits, taps, tile, wanted, first, outs, feat_hbm, *rest):
+def conv_kernel(chips, bits, taps, tile, wanted, first, outs, feat_hbm, edge_ref, *rest):
     count = len(wanted)
-    message_refs = rest[:chips][::-1]
-    weight_ref = rest[chips]
-    held, cols, feat, sem = rest[-4:]
-    out_refs = rest[-4 - outs : -4]
-    tall, padded = held.shape[1:]
-    rows = tall - 16
+    block_refs = rest[:count]
+    weight_ref = rest[count]
+    cols, feat, sem = rest[-3:]
+    out_refs = rest[-3 - outs : -3]
+    rows, padded = block_refs[0].shape
     half = rows // 2
     chip, core = here()
     if 0 in wanted:
         copy = pltpu.make_async_copy(feat_hbm, feat, sem)
         copy.start()
-    for k in range(chips):
-        held[k] = message_refs[k][0:tall, :]
     row = lax.broadcasted_iota(jnp.int32, (half, padded), 0)
     for j, k in enumerate(wanted):
         mask = jnp.where(core == 0, k, flipped_bits(k, bits))
         left = (chip ^ mask) - (1 - core)
         right = (chip ^ mask) + core
-        block = held[mask]
-        before = held[jnp.where(left >= 0, left ^ chip, 0), rows:tall, :].astype(f32)
+        block = block_refs[j][...]
+        before = edge_ref[jnp.where(left >= 0, left ^ chip, 0)]
         before = jnp.where(left >= 0, before, 0.0)
-        after = held[jnp.where(right < chips, right ^ chip, 0), rows:tall, :].astype(f32)
+        after = edge_ref[jnp.where(right < chips, right ^ chip, 0)]
         after = jnp.where(right < chips, after, 0.0)
         even = block[0:half].astype(f32)
         odd = block[half:rows].astype(f32)
@@ -311,13 +323,11 @@
                 out_refs[j * halves + h][:, n : n + tile] = got.astype(out_refs[j * halves].dtype)
 
 
-def conv(messages, features, weight, taps, wanted, dtypes, columns, after):
-    chips = len(messages)
+def conv(blocks, edges, features, weight, taps, wanted, dtypes, columns, after):
+    chips = edges.shape[0]
     bits = chips.bit_length() - 1
-    padded = messages[0].shape[1]
+    rows = features.shape[0]
     depth, model_dim = weight.shape
-    rows = features.shape[0]
-    tall = rows + 16
     count = len(wanted)
     first, last = columns
     span = model_dim // 2
@@ -328,16 +338,15 @@
         ),
         name="conv",
         out_shape=[array((rows, span), d) for d in dtypes for _ in range(halves)],
-        in_specs=[anywhere()] + [whole_vmem()] * (chips + 1) + [anywhere()] * len(after),
+        in_specs=[anywhere()] + [whole_vmem()] * (count + 2) + [anywhere()] * len(after),
         out_specs=[whole_vmem()] * (count * halves),
         scratch_shapes=[
-            pltpu.VMEM((chips, tall, padded), bf16),
             pltpu.VMEM((count * rows, depth), bf16),
             pltpu.VMEM(features.shape, bf16),
             pltpu.SemaphoreType.DMA,
         ],
         compiler_params=pltpu.CompilerParams(vmem_limit_bytes=(5 + 2 * count) * MIB),
-    )(in_hbm(features), *messages[::-1], weight, *after)
+    )(in_hbm(features), edges, *blocks, weight, *after)
     return [got[j * halves : (j + 1) * halves] for j in range(count)]
 
 
@@ -518,22 +527,33 @@
     )(scale, encoded, gain, query_weight, start, output_weight, *parts, *after)
 
 
-def unpack_kernel(chips, pairs, tall, *refs):
+def unpack_kernel(chips, pairs, rows, width, *refs):
     message_refs = refs[:chips][::-1]
     out_ref = refs[-1]
     dim = out_ref.shape[2]
     padded = message_refs[0].shape[1]
     for k in range(chips):
-        piece = message_refs[k][tall:, :]
-        piece = jnp.concatenate([piece[:, g : g + dim] for g in range(0, padded, dim)], axis=0)
+        spare = dim * SPARE_ROWS // rows
+        first = jnp.concatenate(
+            [
+                message_refs[k][
+                    g * SPARE_ROWS : (g + 1) * SPARE_ROWS, width + 8 : width + 8 + spare
+                ]
+                for g in range(dim // spare)
+            ],
+            axis=1,
+        )
+        piece = message_refs[k][rows:, :]
+        piece = [piece[:, g : g + dim] for g in range(0, padded, dim)]
+        piece = jnp.concatenate([first] + piece, axis=0)
         piece = piece[: 2 * pairs * pairs].reshape(pairs, 2 * pairs, dim)
         out_ref[k * pairs : (k + 1) * pairs] = piece
 
 
-def unpack_pairs(messages, pairs, dim, tall, after):
+def unpack_pairs(messages, pairs, dim, rows, width, after):
     chips = len(messages)
     return pl.pallas_call(
-        functools.partial(unpack_kernel, chips, pairs, tall),
+        functools.partial(unpack_kernel, chips, pairs, rows, width),
         name="unpack_pairs",
         out_shape=array((chips * pairs, 2 * pairs, dim), bf16),
         in_specs=[whole_vmem()] * chips + [anywhere()] * len(after),
@@ -644,12 +664,12 @@
         cores = mask if isinstance(mask, tuple) else (mask, mask)
         return lax.ppermute(value, GROUP, hop_pairs(chips, cores, flip))
 
-    strip = send(edge_strip(features, taps // 2), 0, 1)
     own_weight = conv_weight.reshape(-1, model_dim)
-    own_weight, strip = lax.optimization_barrier((own_weight, strip))
     peer_weight = send(own_weight, 0, 1)
 
-    blocks = add_edges(prep(features, pair_input[0], chips), strip, features.shape[0])
+    rows, channels = features.shape
+    width = channels // chips
+    blocks = prep(features, pair_input[0], chips)
     messages = [blocks[0]] + [None] * (chips - 1)
     for k in range(chips - 1, 0, -1):
         messages[k] = send(blocks[k], k)
@@ -660,15 +680,29 @@
     last = chips - 1
     rest = sorted(range(last), key=lambda k: (1 - (k & 1), -k))
 
+    prepared = {}
+
+    def active(k):
+        if k not in prepared:
+            sources = [messages[j] for j in dict.fromkeys(masks[k])]
+            after = [] if k == last else partial[last]
+            prepared[k] = activate(sources, width, rows, after)
+        return prepared[k]
+
+    edges = send(edge_rows(messages, width, rows, [active(last)]), 0, 1)
+
     def partials(ks, columns, after):
         dtypes = [bf16 if k & 1 else f32 for k in ks]
-        return dict(zip(ks, conv(messages, features, weight, taps, ks, dtypes, columns, after)))
+        got = conv(
+            [active(k) for k in ks], edges, features, weight, taps, ks, dtypes, columns, after
+        )
+        return dict(zip(ks, got))
 
     partial = partials([last], (0, model_dim // 2), [])
     partial[last] += partials([last], (model_dim // 2, model_dim), [cotangents[1]])[last]
     pairs, _, pair_dim = pair_input.shape[1:]
     turned = unpack_pairs(
-        messages, pairs, pair_dim, features.shape[0] + strip.shape[0], partial[last]
+        messages, pairs, pair_dim, rows, width, partial[last]
     )
     turned = (turned, send(turned, 0, 1))
     for ks in ([k for k in rest if k & 1], [k for k in rest if k and not k & 1], [0]):

time: 80.5 us -> 76.7 us (0.953)
  waiting for transfers between devices: 29.9 us -> 23 us
  Pallas kernels: 24.7 us -> 28.4 us
    ppermute x24, waiting for transfers between devices: 29.5 us -> 22.6 us  [send(): return lax.ppermute(value, GROUP, hop_pairs(chips, cores, flip))]
    pallas_call x3 -> x6, Pallas kernels: 1.06 us -> 6.52 us  [the longest x4 6.23 us: activate(): pl.pallas_call(functools.partial(activate_kernel, width, len(messages)),...]
    pallas_call x1, Pallas kernels: 3.31 us -> 1.84 us  [prep(): pl.pallas_call(functools.partial(prep_kernel, chips, width), name='prep',...]
  transfers between devices with their start and end apart: 27 -> 27, of which waited for: 11 -> 10; matrix products, arithmetic and copies ran while one was open for 0% -> 0% of each run, Pallas kernels for 28% -> 35%
where the time goes in v5:
time: 76.7 us; the launch traced here: 76.5 us
  Pallas kernels  28.4 us (37%)
  starting transfers between devices  24 us (31%)
  waiting for transfers between devices  23 us (30%)
  between operations  0.95 us (1%)
    ppermute x24, waiting for transfers between devices, send(): return lax.ppermute(value, GROUP, hop_pairs(chips, cores, flip))  22.6 us
    ppermute x24, starting transfers between devices, send(): return lax.ppermute(value, GROUP, hop_pairs(chips, cores, flip))  19.6 us
    pallas_call x5, Pallas kernels, conv(): pl.pallas_call(functools.partial(conv_kernel, chips, bits, taps, 256, wan...  8.87 us
    pallas_call x2, Pallas kernels, attend(): pl.pallas_call(functools.partial(attend_kernel, len(parts), heads, first,...  6.41 us
    pallas_call x4, Pallas kernels, activate(): pl.pallas_call(functools.partial(activate_kernel, width, len(messages)),...  6.23 us
    ppermute x3, starting transfers between devices, per_device(): lax.ppermute(grad, 'dp', [(w, w ^ k) for w in range(windows)])  4.45 us
    pallas_call x1, Pallas kernels, prep(): pl.pallas_call(functools.partial(prep_kernel, chips, width), name='prep',...  1.84 us
    pallas_call x1, Pallas kernels, pack_filter(): pl.pallas_call(functools.partial(pack_kernel, taps, padded), name='pack_f...  1.79 us
  transfers between devices with their start and end apart: 27, of which 10 were waited for; matrix products, arithmetic and copies ran while one was open for 0% of the time, Pallas kernels for 35%

profile of v5, /device:TPU:0, one launch (start us, length us, event | category | flops | bytes accessed | tf_op | source)
XLA Modules:
  0.0 76.5 jit_solution(5926031690847009097)
XLA Ops:
  1.1 1.8 %prep.1 = (bf16[288,384]{1,0:T(8,128)(2,1)S(1)}, bf16[288,384]{1,0:T(8,128)(2,1)S(1)}, bf16[288,384]{1,0:T(8,128)(2,1)S(1)}, bf16[288,384]{1,0:T(8,128)(2,1)S(1)}) custom-call(bf16[256,1408]{1,0:T(8,128)(2,1)} %bitcast.14, bf16[8,64,128]{2,1,0:T(8,128)(2,1)} %bitcast.10), custom_call_target="tpu_custom_call" | custom-call | tf_op jit(solution)/shard_map/prep/pallas_call | solution.py:125
  3.0 3.5 %collective-permute-start = (bf16[288,384]{1,0:T(8,128)(2,1)S(1)}, bf16[288,384]{1,0:T(8,128)(2,1)S(1)}, u32[]{:S(2)}, u32[]{:S(2)}) collective-permute-start(bf16[288,384]{1,0:T(8,128)(2,1)S(1)} %get-tuple-element.23), channel_id=1, source_target_pairs={{0,6},{1,7},{2,4},{3,5},{4,2},{5,3},{6,0},{7,1},{8,14},{9,15},{10,... | collective-permute-start | bytes 663560 | tf_op jit(solution)/shard_map/ppermute | solution.py:665
  7.2 1.8 %pack_filter.1.rest_1_ = bf16[1920,1536]{1,0:T(8,128)(2,1)S(1)} custom-call(bf16[880,1536]{1,0:T(8,128)(2,1)} %bitcast.21, bf16[880,1536]{1,0:T(8,128)(2,1)S(1)} %collective-permute-done.4.peer_hbm), custom_call_target="tpu_custom_call" | custom-call | tf_op jit(solution)/shard_map/pack_filter/pallas_call | solution.py:248
  9.1 3.8 %collective-permute-done.refs_0_ = bf16[288,384]{1,0:T(8,128)(2,1)S(1)} collective-permute-done((bf16[288,384]{1,0:T(8,128)(2,1)S(1)}, bf16[288,384]{1,0:T(8,128)(2,1)S(1)}, u32[]{:S(2)}, u32[]{:S(2)}) %collective-permute-start) | collective-permute-done | bytes 221216 | tf_op jit(solution)/shard_map/ppermute | solution.py:665
  12.8 1.5 %activate.4.refs_4_.rest_0_ = bf16[256,384]{1,0:T(8,128)(2,1)S(1)} custom-call(bf16[288,384]{1,0:T(8,128)(2,1)S(1)} %collective-permute-done.refs_0_), custom_call_target="tpu_custom_call" | custom-call | tf_op jit(solution)/shard_map/activate/pallas_call | solution.py:203
  14.4 3.0 %collective-permute-done.1.refs_1_.refs_0_ = bf16[288,384]{1,0:T(8,128)(2,1)S(1)} collective-permute-done((bf16[288,384]{1,0:T(8,128)(2,1)S(1)}, bf16[288,384]{1,0:T(8,128)(2,1)S(1)}, u32[]{:S(2)}, u32[]{:S(2)}) %collective-permute-start.1) | collective-permute-done | bytes 221216 | tf_op jit(solution)/shard_map/ppermute | solution.py:665
  20.1 1.6 %collective-permute-start.8 = (bf16[256,768]{1,0:T(8,128)(2,1)S(1)}, bf16[256,768]{1,0:T(8,128)(2,1)S(1)}, u32[]{:S(2)}, u32[]{:S(2)}) collective-permute-start(bf16[256,768]{1,0:T(8,128)(2,1)S(1)} %conv.5.refs_1_.refs_2_.refs_4_), channel_id=1, source_target_pairs={{0,2},{1,5},{2,0},{3,7},{4,6},{5,1},{6,4},{7,3},{8,10},{9,13},{10,... | collective-permute-start | bytes 1179656 | tf_op jit(solution)/shard_map/ppermute | solution.py:665
  23.5 1.5 %activate.6.rest_0_ = bf16[256,384]{1,0:T(8,128)(2,1)S(1)} custom-call(bf16[288,384]{1,0:T(8,128)(2,1)S(1)} %collective-permute-done.2.refs_2_.refs_0_.refs_1_, bf16[288,384]{1,0:T(8,128)(2,1)S(1)} %collective-permute-done.1.refs_1_.refs_0_, bf16[256,768]{1,0:T(8,128)(2,1)S(1)} %conv.5.refs_1_.refs_2_.refs_4_, bf16[256,768]{1,0:T(8,128)(2,1)S(1)} %conv.6.refs_2_.refs_3_.refs_5_), custom_call_target="tpu_custom_call" | custom-call | tf_op jit(solution)/shard_map/activate/pallas_call | solution.py:203
  25.1 1.8 %conv.8 = (bf16[256,768]{1,0:T(8,128)(2,1)S(1)}, bf16[256,768]{1,0:T(8,128)(2,1)S(1)}) custom-call(bf16[256,1408]{1,0:T(8,128)(2,1)} %bitcast.17, f32[4,8,384]{2,1,0:T(8,128)S(1)} %collective-permute-done.3.edge_ref, bf16[256,384]{1,0:T(8,128)(2,1)S(1)} %activate.6.rest_0_, bf16[1920,1536]{1,0:T(8,128)(2,1)S(1)} %pack_filter.1.rest_1_), custom_call_target="tpu_custom_call" | custom-call | tf_op jit(solution)/shard_map/conv/pallas_call | solution.py:335
  26.9 1.6 %collective-permute-start.6 = (bf16[256,768]{1,0:T(8,128)(2,1)S(1)}, bf16[256,768]{1,0:T(8,128)(2,1)S(1)}, u32[]{:S(2)}, u32[]{:S(2)}) collective-permute-start(bf16[256,768]{1,0:T(8,128)(2,1)S(1)} %get-tuple-element.31), channel_id=1, source_target_pairs={{0,2},{1,5},{2,0},{3,7},{4,6},{5,1},{6,4},{7,3},{8,10},{9,13},{10,... | collective-permute-start | bytes 1179656 | tf_op jit(solution)/shard_map/ppermute | solution.py:665
  29.0 1.7 %activate.7.rest_0_ = bf16[256,384]{1,0:T(8,128)(2,1)S(1)} custom-call(bf16[288,384]{1,0:T(8,128)(2,1)S(1)} %collective-permute-done.1.refs_1_.refs_0_, bf16[288,384]{1,0:T(8,128)(2,1)S(1)} %collective-permute-done.2.refs_2_.refs_0_.refs_1_, bf16[256,768]{1,0:T(8,128)(2,1)S(1)} %conv.5.refs_1_.refs_2_.refs_4_, bf16[256,768]{1,0:T(8,128)(2,1)S(1)} %conv.6.refs_2_.refs_3_.refs_5_), custom_call_target="tpu_custom_call" | custom-call | tf_op jit(solution)/shard_map/activate/pallas_call | solution.py:203
  30.7 1.8 %conv.9 = (f32[256,768]{1,0:T(8,128)S(1)}, f32[256,768]{1,0:T(8,128)S(1)}) custom-call(bf16[256,1408]{1,0:T(8,128)(2,1)} %bitcast.18, f32[4,8,384]{2,1,0:T(8,128)S(1)} %collective-permute-done.3.edge_ref, bf16[256,384]{1,0:T(8,128)(2,1)S(1)} %activate.7.rest_0_, bf16[1920,1536]{1,0:T(8,128)(2,1)S(1)} %pack_filter.1.rest_1_), custom_call_target="tpu_custom_call" | custom-call | tf_op jit(solution)/shard_map/conv/pallas_call | solution.py:335
  32.6 1.5 %collective-permute-start.10 = (bf16[256,768]{1,0:T(8,128)(2,1)S(1)}, bf16[256,768]{1,0:T(8,128)(2,1)S(1)}, u32[]{:S(2)}, u32[]{:S(2)}) collective-permute-start(bf16[256,768]{1,0:T(8,128)(2,1)S(1)} %add_up.4), channel_id=1, source_target_pairs={{0,4},{1,3},{2,6},{3,1},{4,0},{5,7},{6,2},{7,5},{8,12},{9,11},{10,... | collective-permute-start | bytes 1179656 | tf_op jit(solution)/shard_map/ppermute | solution.py:665
  34.8 1.5 %activate.5.rest_0_ = bf16[256,384]{1,0:T(8,128)(2,1)S(1)} custom-call(bf16[288,384]{1,0:T(8,128)(2,1)S(1)} %get-tuple-element.26.refs_3_.refs_0_, bf16[256,768]{1,0:T(8,128)(2,1)S(1)} %conv.5.refs_1_.refs_2_.refs_4_, bf16[256,768]{1,0:T(8,128)(2,1)S(1)} %conv.6.refs_2_.refs_3_.refs_5_), custom_call_target="tpu_custom_call" | custom-call | tf_op jit(solution)/shard_map/activate/pallas_call | solution.py:203
  36.4 3.2 %conv.7 = (f32[256,768]{1,0:T(8,128)S(1)}, f32[256,768]{1,0:T(8,128)S(1)}) custom-call(bf16[256,1408]{1,0:T(8,128)(2,1)} %bitcast.19, f32[4,8,384]{2,1,0:T(8,128)S(1)} %collective-permute-done.3.edge_ref, bf16[256,384]{1,0:T(8,128)(2,1)S(1)} %activate.5.rest_0_, bf16[1920,1536]{1,0:T(8,128)(2,1)S(1)} %pack_filter.1.rest_1_), custom_call_target="tpu_custom_call" | custom-call | tf_op jit(solution)/shard_map/conv/pallas_call | solution.py:335
  39.6 6.3 %collective-permute-done.7.rest_3_ = bf16[256,768]{1,0:T(8,128)(2,1)S(1)} collective-permute-done((bf16[256,768]{1,0:T(8,128)(2,1)S(1)}, bf16[256,768]{1,0:T(8,128)(2,1)S(1)}, u32[]{:S(2)}, u32[]{:S(2)}) %collective-permute-start.7) | collective-permute-done | bytes 393248 | tf_op jit(solution)/shard_map/ppermute | solution.py:665
  45.9 2.3 %collective-permute-done.12.rest_5_ = bf16[256,768]{1,0:T(8,128)(2,1)S(1)} collective-permute-done((bf16[256,768]{1,0:T(8,128)(2,1)S(1)}, bf16[256,768]{1,0:T(8,128)(2,1)S(1)}, u32[]{:S(2)}, u32[]{:S(2)}) %collective-permute-start.12) | collective-permute-done | bytes 393248 | tf_op jit(solution)/shard_map/ppermute | solution.py:665
  50.7 1.6 %collective-permute-start.14 = (bf16[128,384]{1,0:T(8,128)(2,1)S(1)}, bf16[128,384]{1,0:T(8,128)(2,1)S(1)}, u32[]{:S(2)}, u32[]{:S(2)}) collective-permute-start(bf16[128,384]{1,0:T(8,128)(2,1)S(1)} %bundle.1.rest_0_.rest_3_), channel_id=1, source_target_pairs={{0,2},{1,3},{2,0},{3,1},{4,6},{5,7},{6,4},{7,5},{8,10},{9,11},{10,... | collective-permute-start | bytes 294920 | tf_op jit(solution)/shard_map/ppermute | solution.py:665
  54.3 1.6 %collective-permute-done.14.rest_1_.rest_2_ = bf16[128,384]{1,0:T(8,128)(2,1)S(1)} collective-permute-done((bf16[128,384]{1,0:T(8,128)(2,1)S(1)}, bf16[128,384]{1,0:T(8,128)(2,1)S(1)}, u32[]{:S(2)}, u32[]{:S(2)}) %collective-permute-start.14) | collective-permute-done | bytes 98336 | tf_op jit(solution)/shard_map/ppermute | solution.py:665
  55.8 3.3 %collective-permute-done.15.rest_2_.rest_1_ = bf16[128,384]{1,0:T(8,128)(2,1)S(1)} collective-permute-done((bf16[128,384]{1,0:T(8,128)(2,1)S(1)}, bf16[128,384]{1,0:T(8,128)(2,1)S(1)}, u32[]{:S(2)}, u32[]{:S(2)}) %collective-permute-start.15) | collective-permute-done | bytes 98336 | tf_op jit(solution)/shard_map/ppermute | solution.py:665
  62.5 1.9 %collective-permute-start.23 = (bf16[128,128]{1,0:T(8,128)(2,1)S(1)}, bf16[128,128]{1,0:T(8,128)(2,1)S(1)}, u32[]{:S(2)}, u32[]{:S(2)}) collective-permute-start(bf16[128,128]{1,0:T(8,128)(2,1)S(1)} %get-tuple-element.38.refs_3_), channel_id=1, source_target_pairs={{0,2},{1,3},{2,0},{3,1},{4,6},{5,7},{6,4},{7,5},{8,10},{9,11},{10,... | collective-permute-start | bytes 98312 | tf_op jit(solution)/shard_map/ppermute | solution.py:665
  64.5 2.8 %attend.2 = (f32[128,1536]{1,0:T(8,128)S(1)}, f32[8,128]{1,0:T(8,128)S(1)}) custom-call(f32[8]{0:T(128)S(1)} %copy-done.7, bf16[128,1536]{1,0:T(8,128)(2,1)S(1)} %get-tuple-element.35.encoded_ref.start_ref, f32[1536]{0:T(1024)S(1)} %copy-done.5, bf16[1536,1024]{1,0:T(8,128)(2,1)S(1)} %copy-done, ...), custom_call_target="tpu_custom_call" | custom-call | tf_op jit(solution)/shard_map/attend/pallas_call | solution.py:514
  67.4 3.7 %collective-permute-start.24 = (bf16[128,128]{1,0:T(8,128)(2,1)S(1)}, bf16[128,128]{1,0:T(8,128)(2,1)S(1)}, u32[]{:S(2)}, u32[]{:S(2)}) collective-permute-start(bf16[128,128]{1,0:T(8,128)(2,1)S(1)} %add_up.6.rest_8_.refs_3_), channel_id=1, source_target_pairs={{0,24},{8,16},{16,8},{24,0},{1,25},{9,17},{17,9},{25,1},{2,26},{10... | collective-permute-start | bytes 98312 | tf_op jit(solution)/shard_map/ppermute | solution.py:754
  71.8 3.6 %attend.3 = (bf16[128,1536]{1,0:T(8,128)(2,1)}, f32[8,128]{1,0:T(8,128)S(1)}) custom-call(f32[8]{0:T(128)S(1)} %copy-done.7, bf16[128,1536]{1,0:T(8,128)(2,1)S(1)} %get-tuple-element.35.encoded_ref.start_ref, f32[1536]{0:T(1024)S(1)} %copy-done.5, bf16[1536,1024]{1,0:T(8,128)(2,1)S(1)} %copy-done, f32[128,1536]{1,0:T(8,128)S(1)} %get-tuple-element.37.start_ref, ...), custom_call_target="tpu_custom_call" | custom-call | tf_op jit(solution)/shard_map/attend/pallas_call | solution.py:514
  (73 shorter events, 16.9 us)
Async XLA Ops:
  0.6 6.5 %collective-permute-start.4 = (bf16[880,1536]{1,0:T(8,128)(2,1)}, bf16[880,1536]{1,0:T(8,128)(2,1)S(1)}, u32[]{:S(2)}, u32[]{:S(2)}) collective-permute-start(bf16[880,1536]{1,0:T(8,128)(2,1)} %bitcast.20), channel_id=1, source_target_pairs={{0,1},{1,0},{2,3},{3,2},{4,5},{5,4},{6,7},{7,6},{8,9},{9,8},{10,11... | collective-permute-start | bytes 8110088 | tf_op jit(solution)/shard_map/ppermute | solution.py:665
  3.0 9.9 %collective-permute-start = (bf16[288,384]{1,0:T(8,128)(2,1)S(1)}, bf16[288,384]{1,0:T(8,128)(2,1)S(1)}, u32[]{:S(2)}, u32[]{:S(2)}) collective-permute-start(bf16[288,384]{1,0:T(8,128)(2,1)S(1)} %get-tuple-element.23), channel_id=1, source_target_pairs={{0,6},{1,7},{2,4},{3,5},{4,2},{5,3},{6,0},{7,1},{8,14},{9,15},{10,... | collective-permute-start | bytes 663560 | tf_op jit(solution)/shard_map/ppermute | solution.py:665
  6.5 10.8 %collective-permute-start.1 = (bf16[288,384]{1,0:T(8,128)(2,1)S(1)}, bf16[288,384]{1,0:T(8,128)(2,1)S(1)}, u32[]{:S(2)}, u32[]{:S(2)}) collective-permute-start(bf16[288,384]{1,0:T(8,128)(2,1)S(1)} %get-tuple-element.24), channel_id=1, source_target_pairs={{0,4},{1,5},{2,6},{3,7},{4,0},{5,1},{6,2},{7,3},{8,12},{9,13},{10,... | collective-permute-start | bytes 663560 | tf_op jit(solution)/shard_map/ppermute | solution.py:665
  7.0 10.6 %collective-permute-start.2 = (bf16[288,384]{1,0:T(8,128)(2,1)S(1)}, bf16[288,384]{1,0:T(8,128)(2,1)S(1)}, u32[]{:S(2)}, u32[]{:S(2)}) collective-permute-start(bf16[288,384]{1,0:T(8,128)(2,1)S(1)} %get-tuple-element.25), channel_id=1, source_target_pairs={{0,2},{1,3},{2,0},{3,1},{4,6},{5,7},{6,4},{7,5},{8,10},{9,11},{10,... | collective-permute-start | bytes 663560 | tf_op jit(solution)/shard_map/ppermute | solution.py:665
  9.0 12.7 %collective-permute-start.5 = (bf16[8,64,128]{2,1,0:T(8,128)(2,1)S(1)}, bf16[8,64,128]{2,1,0:T(8,128)(2,1)S(1)}, u32[]{:S(2)}, u32[]{:S(2)}) collective-permute-start(bf16[8,64,128]{2,1,0:T(8,128)(2,1)S(1)} %bitcast.12), channel_id=1, source_target_pairs={{0,1},{1,0},{2,3},{3,2},{4,5},{5,4},{6,7},{7,6},{8,9},{9,8},{10,11... | collective-permute-start | bytes 393224 | tf_op jit(solution)/shard_map/ppermute | solution.py:665
  20.1 12.4 %collective-permute-start.8 = (bf16[256,768]{1,0:T(8,128)(2,1)S(1)}, bf16[256,768]{1,0:T(8,128)(2,1)S(1)}, u32[]{:S(2)}, u32[]{:S(2)}) collective-permute-start(bf16[256,768]{1,0:T(8,128)(2,1)S(1)} %conv.5.refs_1_.refs_2_.refs_4_), channel_id=1, source_target_pairs={{0,2},{1,5},{2,0},{3,7},{4,6},{5,1},{6,4},{7,3},{8,10},{9,13},{10,... | collective-permute-start | bytes 1179656 | tf_op jit(solution)/shard_map/ppermute | solution.py:665
  22.7 11.4 %collective-permute-start.11 = (bf16[256,768]{1,0:T(8,128)(2,1)S(1)}, bf16[256,768]{1,0:T(8,128)(2,1)S(1)}, u32[]{:S(2)}, u32[]{:S(2)}) collective-permute-start(bf16[256,768]{1,0:T(8,128)(2,1)S(1)} %conv.6.refs_2_.refs_3_.refs_5_), channel_id=1, source_target_pairs={{0,2},{1,5},{2,0},{3,7},{4,6},{5,1},{6,4},{7,3},{8,10},{9,13},{10,... | collective-permute-start | bytes 1179656 | tf_op jit(solution)/shard_map/ppermute | solution.py:665
  23.4 9.1 %collective-permute-start.9 = (bf16[32,16,128]{2,1,0:T(8,128)(2,1)S(1)}, bf16[32,16,128]{2,1,0:T(8,128)(2,1)S(1)}, u32[]{:S(2)}, u32[]{:S(2)}) collective-permute-start(bf16[32,16,128]{2,1,0:T(8,128)(2,1)S(1)} %unpack_pairs.1.turned_ref), channel_id=1, source_target_pairs={{0,1},{1,0},{2,3},{3,2},{4,5},{5,4},{6,7},{7,6},{8,9},{9,8},{10,11... | collective-permute-start | bytes 393224 | tf_op jit(solution)/shard_map/ppermute | solution.py:665
  26.9 12.8 %collective-permute-start.6 = (bf16[256,768]{1,0:T(8,128)(2,1)S(1)}, bf16[256,768]{1,0:T(8,128)(2,1)S(1)}, u32[]{:S(2)}, u32[]{:S(2)}) collective-permute-start(bf16[256,768]{1,0:T(8,128)(2,1)S(1)} %get-tuple-element.31), channel_id=1, source_target_pairs={{0,2},{1,5},{2,0},{3,7},{4,6},{5,1},{6,4},{7,3},{8,10},{9,13},{10,... | collective-permute-start | bytes 1179656 | tf_op jit(solution)/shard_map/ppermute | solution.py:665
  28.4 17.5 %collective-permute-start.7 = (bf16[256,768]{1,0:T(8,128)(2,1)S(1)}, bf16[256,768]{1,0:T(8,128)(2,1)S(1)}, u32[]{:S(2)}, u32[]{:S(2)}) collective-permute-start(bf16[256,768]{1,0:T(8,128)(2,1)S(1)} %get-tuple-element.32), channel_id=1, source_target_pairs={{0,2},{1,5},{2,0},{3,7},{4,6},{5,1},{6,4},{7,3},{8,10},{9,13},{10,... | collective-permute-start | bytes 1179656 | tf_op jit(solution)/shard_map/ppermute | solution.py:665
  32.6 13.3 %collective-permute-start.10 = (bf16[256,768]{1,0:T(8,128)(2,1)S(1)}, bf16[256,768]{1,0:T(8,128)(2,1)S(1)}, u32[]{:S(2)}, u32[]{:S(2)}) collective-permute-start(bf16[256,768]{1,0:T(8,128)(2,1)S(1)} %add_up.4), channel_id=1, source_target_pairs={{0,4},{1,3},{2,6},{3,1},{4,0},{5,7},{6,2},{7,5},{8,12},{9,11},{10,... | collective-permute-start | bytes 1179656 | tf_op jit(solution)/shard_map/ppermute | solution.py:665
  34.2 14.1 %collective-permute-start.12 = (bf16[256,768]{1,0:T(8,128)(2,1)S(1)}, bf16[256,768]{1,0:T(8,128)(2,1)S(1)}, u32[]{:S(2)}, u32[]{:S(2)}) collective-permute-start(bf16[256,768]{1,0:T(8,128)(2,1)S(1)} %add_up.5), channel_id=1, source_target_pairs={{0,4},{1,3},{2,6},{3,1},{4,0},{5,7},{6,2},{7,5},{8,12},{9,11},{10,... | collective-permute-start | bytes 1179656 | tf_op jit(solution)/shard_map/ppermute | solution.py:665
  50.7 5.1 %collective-permute-start.14 = (bf16[128,384]{1,0:T(8,128)(2,1)S(1)}, bf16[128,384]{1,0:T(8,128)(2,1)S(1)}, u32[]{:S(2)}, u32[]{:S(2)}) collective-permute-start(bf16[128,384]{1,0:T(8,128)(2,1)S(1)} %bundle.1.rest_0_.rest_3_), channel_id=1, source_target_pairs={{0,2},{1,3},{2,0},{3,1},{4,6},{5,7},{6,4},{7,5},{8,10},{9,11},{10,... | collective-permute-start | bytes 294920 | tf_op jit(solution)/shard_map/ppermute | solution.py:665
  52.3 6.9 %collective-permute-start.15 = (bf16[128,384]{1,0:T(8,128)(2,1)S(1)}, bf16[128,384]{1,0:T(8,128)(2,1)S(1)}, u32[]{:S(2)}, u32[]{:S(2)}) collective-permute-start(bf16[128,384]{1,0:T(8,128)(2,1)S(1)} %bundle.1.rest_0_.rest_3_), channel_id=1, source_target_pairs={{0,4},{1,5},{2,6},{3,7},{4,0},{5,1},{6,2},{7,3},{8,12},{9,13},{10,... | collective-permute-start | bytes 294920 | tf_op jit(solution)/shard_map/ppermute | solution.py:665
  52.9 6.3 %collective-permute-start.16 = (bf16[128,384]{1,0:T(8,128)(2,1)S(1)}, bf16[128,384]{1,0:T(8,128)(2,1)S(1)}, u32[]{:S(2)}, u32[]{:S(2)}) collective-permute-start(bf16[128,384]{1,0:T(8,128)(2,1)S(1)} %bundle.1.rest_0_.rest_3_), channel_id=1, source_target_pairs={{0,6},{1,7},{2,4},{3,5},{4,2},{5,3},{6,0},{7,1},{8,14},{9,15},{10,... | collective-permute-start | bytes 294920 | tf_op jit(solution)/shard_map/ppermute | solution.py:665
  54.3 8.0 %collective-permute-start.17 = (bf16[128,384]{1,0:T(8,128)(2,1)S(1)}, bf16[128,384]{1,0:T(8,128)(2,1)S(1)}, u32[]{:S(2)}, u32[]{:S(2)}) collective-permute-start(bf16[128,384]{1,0:T(8,128)(2,1)S(1)} %bundle.1.rest_0_.rest_3_), channel_id=1, source_target_pairs={{0,1},{1,0},{2,3},{3,2},{4,5},{5,4},{6,7},{7,6},{8,9},{9,8},{10,11... | collective-permute-start | bytes 294920 | tf_op jit(solution)/shard_map/ppermute | solution.py:665
  55.8 6.7 %collective-permute-start.18 = (bf16[128,384]{1,0:T(8,128)(2,1)S(1)}, bf16[128,384]{1,0:T(8,128)(2,1)S(1)}, u32[]{:S(2)}, u32[]{:S(2)}) collective-permute-start(bf16[128,384]{1,0:T(8,128)(2,1)S(1)} %collective-permute-done.14.rest_1_.rest_2_), channel_id=1, source_target_pairs={{0,1},{1,0},{2,3},{3,2},{4,5},{5,4},{6,7},{7,6},{8,9},{9,8},{10,11... | collective-permute-start | bytes 294920 | tf_op jit(solution)/shard_map/ppermute | solution.py:665
  59.1 5.3 %collective-permute-start.19 = (bf16[128,384]{1,0:T(8,128)(2,1)S(1)}, bf16[128,384]{1,0:T(8,128)(2,1)S(1)}, u32[]{:S(2)}, u32[]{:S(2)}) collective-permute-start(bf16[128,384]{1,0:T(8,128)(2,1)S(1)} %collective-permute-done.15.rest_2_.rest_1_), channel_id=1, source_target_pairs={{0,1},{1,0},{2,3},{3,2},{4,5},{5,4},{6,7},{7,6},{8,9},{9,8},{10,11... | collective-permute-start | bytes 294920 | tf_op jit(solution)/shard_map/ppermute | solution.py:665
  59.1 5.3 %collective-permute-start.20 = (bf16[128,384]{1,0:T(8,128)(2,1)S(1)}, bf16[128,384]{1,0:T(8,128)(2,1)S(1)}, u32[]{:S(2)}, u32[]{:S(2)}) collective-permute-start(bf16[128,384]{1,0:T(8,128)(2,1)S(1)} %collective-permute-done.16.rest_3_.rest_0_), channel_id=1, source_target_pairs={{0,1},{1,0},{2,3},{3,2},{4,5},{5,4},{6,7},{7,6},{8,9},{9,8},{10,11... | collective-permute-start | bytes 294920 | tf_op jit(solution)/shard_map/ppermute | solution.py:665
  60.9 6.4 %collective-permute-start.21 = (bf16[128,128]{1,0:T(8,128)(2,1)S(1)}, bf16[128,128]{1,0:T(8,128)(2,1)S(1)}, u32[]{:S(2)}, u32[]{:S(2)}) collective-permute-start(bf16[128,128]{1,0:T(8,128)(2,1)S(1)} %get-tuple-element.38.refs_3_), channel_id=1, source_target_pairs={{0,6},{1,7},{2,4},{3,5},{4,2},{5,3},{6,0},{7,1},{8,14},{9,15},{10,... | collective-permute-start | bytes 98312 | tf_op jit(solution)/shard_map/ppermute | solution.py:665
  62.3 5.0 %collective-permute-start.22 = (bf16[128,128]{1,0:T(8,128)(2,1)S(1)}, bf16[128,128]{1,0:T(8,128)(2,1)S(1)}, u32[]{:S(2)}, u32[]{:S(2)}) collective-permute-start(bf16[128,128]{1,0:T(8,128)(2,1)S(1)} %get-tuple-element.38.refs_3_), channel_id=1, source_target_pairs={{0,4},{1,5},{2,6},{3,7},{4,0},{5,1},{6,2},{7,3},{8,12},{9,13},{10,... | collective-permute-start | bytes 98312 | tf_op jit(solution)/shard_map/ppermute | solution.py:665
  62.5 4.8 %collective-permute-start.23 = (bf16[128,128]{1,0:T(8,128)(2,1)S(1)}, bf16[128,128]{1,0:T(8,128)(2,1)S(1)}, u32[]{:S(2)}, u32[]{:S(2)}) collective-permute-start(bf16[128,128]{1,0:T(8,128)(2,1)S(1)} %get-tuple-element.38.refs_3_), channel_id=1, source_target_pairs={{0,2},{1,3},{2,0},{3,1},{4,6},{5,7},{6,4},{7,5},{8,10},{9,11},{10,... | collective-permute-start | bytes 98312 | tf_op jit(solution)/shard_map/ppermute | solution.py:665
  67.4 8.0 %collective-permute-start.24 = (bf16[128,128]{1,0:T(8,128)(2,1)S(1)}, bf16[128,128]{1,0:T(8,128)(2,1)S(1)}, u32[]{:S(2)}, u32[]{:S(2)}) collective-permute-start(bf16[128,128]{1,0:T(8,128)(2,1)S(1)} %add_up.6.rest_8_.refs_3_), channel_id=1, source_target_pairs={{0,24},{8,16},{16,8},{24,0},{1,25},{9,17},{17,9},{25,1},{2,26},{10... | collective-permute-start | bytes 98312 | tf_op jit(solution)/shard_map/ppermute | solution.py:754
  71.0 4.8 %collective-permute-start.25 = (bf16[128,128]{1,0:T(8,128)(2,1)S(1)}, bf16[128,128]{1,0:T(8,128)(2,1)S(1)}, u32[]{:S(2)}, u32[]{:S(2)}) collective-permute-start(bf16[128,128]{1,0:T(8,128)(2,1)S(1)} %add_up.6.rest_8_.refs_3_), channel_id=1, source_target_pairs={{0,16},{8,24},{16,0},{24,8},{1,17},{9,25},{17,1},{25,9},{2,18},{10... | collective-permute-start | bytes 98312 | tf_op jit(solution)/shard_map/ppermute | solution.py:754
  (13 other events, 172.9 us)

commit v6 on v5

--- a/solution.py
+++ b/solution.py
@@ -77,27 +77,20 @@
     feat, pair, split, sems = rest[chips:]
     rows = feat.shape[0]
     chip, _ = here()
-    copy = pltpu.make_async_copy(feat_hbm, feat, sems.at[0])
-    pair_copy = pltpu.make_async_copy(pair_hbm, pair, sems.at[1])
-    copy.start()
+    chunks = sems.shape[0] - 1
+    step = rows // chunks
+
+    def copy(n):
+        at = pl.ds(n * step, step)
+        return pltpu.make_async_copy(feat_hbm.at[at, :], feat.at[at, :], sems.at[n])
+
+    pair_copy = pltpu.make_async_copy(pair_hbm, pair, sems.at[chunks])
+    for n in range(chunks):
+        copy(n).start()
     pair_copy.start()
-    copy.wait()
-    x = feat[...].astype(f32)
-    scale = lax.rsqrt(jnp.mean(x * x, axis=-1, keepdims=True) + norm_eps)
-    high = scale.astype(bf16)
-    middle = (scale - high.astype(f32)).astype(bf16)
-    low = (scale - high.astype(f32) - middle.astype(f32)).astype(bf16)
-    lane = lax.broadcasted_iota(jnp.int32, (rows, split.shape[2] - width), 1)
-    tail = jnp.where(
-        lane == 0,
-        high.astype(f32),
-        jnp.where(
-            lane == 1, middle.astype(f32), jnp.where(lane == 2, low.astype(f32), 0.0)
-        ),
-    ).astype(bf16)
-    for q in range(chips):
-        split[q, :, 0:width] = feat[:, q * width : (q + 1) * width]
-        split[q, :, width:] = tail
+    for n in range(chunks):
+        copy(n).wait()
+        fill_rows(chips, width, n * step, step, feat, split)
     pair_copy.wait()
     pairs, _, dim = pair.shape
     lanes = split.shape[2] // dim
@@ -114,6 +107,26 @@
         for g in range(lanes):
             part = piece[SPARE_ROWS + g * extra : SPARE_ROWS + (g + 1) * extra]
             block_refs[k][rows : rows + part.shape[0], g * dim : (g + 1) * dim] = part
+
+
+def fill_rows(chips, width, start, step, feat, split):
+    at = slice(start, start + step)
+    x = feat[at, :].astype(f32)
+    scale = lax.rsqrt(jnp.mean(x * x, axis=-1, keepdims=True) + norm_eps)
+    high = scale.astype(bf16)
+    middle = (scale - high.astype(f32)).astype(bf16)
+    low = (scale - high.astype(f32) - middle.astype(f32)).astype(bf16)
+    lane = lax.broadcasted_iota(jnp.int32, (step, split.shape[2] - width), 1)
+    tail = jnp.where(
+        lane == 0,
+        high.astype(f32),
+        jnp.where(
+            lane == 1, middle.astype(f32), jnp.where(lane == 2, low.astype(f32), 0.0)
+        ),
+    ).astype(bf16)
+    for q in range(chips):
+        split[q, at, 0:width] = feat[at, q * width : (q + 1) * width]
+        split[q, at, width:] = tail
 
 
 def prep(features, pair_input, chips):
@@ -256,7 +269,9 @@
     )(in_hbm(own), peer)
 
 
-def conv_kernel(chips, bits, taps, tile, wanted, first, outs, feat_hbm, edge_ref, *rest):
+def conv_kernel(
+    chips, bits, taps, tile, wanted, columns, outs, edged, feat_hbm, edge_ref, *rest
+):
     count = len(wanted)
     block_refs = rest[:count]
     weight_ref = rest[count]
@@ -274,10 +289,13 @@
         left = (chip ^ mask) - (1 - core)
         right = (chip ^ mask) + core
         block = block_refs[j][...]
-        before = edge_ref[jnp.where(left >= 0, left ^ chip, 0)]
-        before = jnp.where(left >= 0, before, 0.0)
-        after = edge_ref[jnp.where(right < chips, right ^ chip, 0)]
-        after = jnp.where(right < chips, after, 0.0)
+        if edged:
+            before = edge_ref[jnp.where(left >= 0, left ^ chip, 0)]
+            before = jnp.where(left >= 0, before, 0.0)
+            after = edge_ref[jnp.where(right < chips, right ^ chip, 0)]
+            after = jnp.where(right < chips, after, 0.0)
+        else:
+            before = after = jnp.zeros((8, padded), f32)
         even = block[0:half].astype(f32)
         odd = block[half:rows].astype(f32)
 
@@ -299,12 +317,10 @@
     pick = pick_rows(rows)
     if 0 in wanted:
         copy.wait()
-    halves = len(out_refs) // count
-    span = out_refs[0].shape[1]
     for j, k in enumerate(wanted):
-        for h in range(halves):
-            for n in range(0, span, tile):
-                at = first + h * span + n
+        for h, (first, last) in enumerate(columns):
+            out_ref = out_refs[j * len(columns) + h]
+            for at in range(first, last, tile):
                 got = jnp.dot(
                     cols[j * rows : (j + 1) * rows],
                     weight_ref[:, at : at + tile],
@@ -320,39 +336,83 @@
                             [skip, jnp.zeros((rows, tile - width), f32)], axis=1
                         )
                     got = got + skip
-                out_refs[j * halves + h][:, n : n + tile] = got.astype(out_refs[j * halves].dtype)
+                out_ref[:, at - first : at - first + tile] = got.astype(out_ref.dtype)
+
+
+def edge_terms_kernel(chips, taps, edge_ref, weight_ref, *rest):
+    out_ref, cols = rest[-2:]
+    padded = edge_ref.shape[2]
+    chip, core = here()
+    left = (chip ^ (chips - 1)) - (1 - core)
+    right = (chip ^ (chips - 1)) + core
+    before = edge_ref[jnp.where(left >= 0, left ^ chip, 0)]
+    before = jnp.where(left >= 0, before, 0.0)
+    after = edge_ref[jnp.where(right < chips, right ^ chip, 0)]
+    after = jnp.where(right < chips, after, 0.0)
+    none = jnp.zeros((1, padded), f32)
+    blank = jnp.zeros((12, padded), f32)
+    terms = {
+        0: (before[2:3], before[3:4], none, none),
+        1: (before[3:4], none, none, none),
+        3: (none, none, none, after[0:1]),
+        4: (none, none, after[0:1], after[1:2]),
+    }
+    for k in range(taps):
+        rows = terms.get(k, (none,) * 4)
+        cols[:, k * padded : (k + 1) * padded] = jnp.concatenate(
+            [*rows, blank], axis=0
+        ).astype(bf16)
+    span = out_ref.shape[1]
+    quarters = [
+        jnp.dot(cols[...], weight_ref[:, at : at + span], preferred_element_type=f32)[0:4]
+        for at in range(0, 4 * span, span)
+    ]
+    out_ref[...] = jnp.concatenate(quarters, axis=0).astype(bf16)
+
+
+def edge_terms(edges, weight, taps, after):
+    chips = edges.shape[0]
+    depth, model_dim = weight.shape
+    return pl.pallas_call(
+        functools.partial(edge_terms_kernel, chips, taps),
+        name="edge_terms",
+        out_shape=array((16, model_dim // 4), bf16),
+        in_specs=[whole_vmem()] * 2 + [anywhere()] * len(after),
+        out_specs=whole_vmem(),
+        scratch_shapes=[pltpu.VMEM((16, depth), bf16)],
+        compiler_params=pltpu.CompilerParams(vmem_limit_bytes=2 * MIB),
+    )(edges, weight, *after)
 
 
 def conv(blocks, edges, features, weight, taps, wanted, dtypes, columns, after):
-    chips = edges.shape[0]
+    chips = lax.axis_size("seq")
     bits = chips.bit_length() - 1
     rows = features.shape[0]
+    edged = edges is not None
     depth, model_dim = weight.shape
     count = len(wanted)
-    first, last = columns
-    span = model_dim // 2
-    halves = (last - first) // span
+    pieces = len(columns)
     got = pl.pallas_call(
         functools.partial(
-            conv_kernel, chips, bits, taps, 256, wanted, first, count * halves
+            conv_kernel, chips, bits, taps, 256, wanted, columns, count * pieces, edged
         ),
         name="conv",
-        out_shape=[array((rows, span), d) for d in dtypes for _ in range(halves)],
+        out_shape=[array((rows, b - a), d) for d in dtypes for a, b in columns],
         in_specs=[anywhere()] + [whole_vmem()] * (count + 2) + [anywhere()] * len(after),
-        out_specs=[whole_vmem()] * (count * halves),
+        out_specs=[whole_vmem()] * (count * pieces),
         scratch_shapes=[
             pltpu.VMEM((count * rows, depth), bf16),
             pltpu.VMEM(features.shape, bf16),
             pltpu.SemaphoreType.DMA,
         ],
         compiler_params=pltpu.CompilerParams(vmem_limit_bytes=(5 + 2 * count) * MIB),
-    )(in_hbm(features), edges, *blocks, weight, *after)
-    return [got[j * halves : (j + 1) * halves] for j in range(count)]
+    )(in_hbm(features), edges if edged else blocks[0], *blocks, weight, *after)
+    return [got[j * pieces : (j + 1) * pieces] for j in range(count)]
 
 
 def sum_kernel(count, *refs):
     out_ref = refs[-1]
-    out_ref[...] = tree_sum([r[...].astype(f32) for r in refs[:count][::-1]]).astype(out_ref.dtype)
+    out_ref[...] = tree_sum([r[...].astype(f32) for r in refs[:count]]).astype(out_ref.dtype)
 
 
 def add_up(terms, dtype, after=()):
@@ -363,48 +423,61 @@
         in_specs=[whole_vmem()] * len(terms) + [anywhere()] * len(after),
         out_specs=whole_vmem(),
         compiler_params=pltpu.CompilerParams(vmem_limit_bytes=4 * MIB),
-    )(*terms[::-1], *after)
-
-
-def encode_kernel(pieces, arrivals, pair_weight_ref, *rest):
+    )(*terms, *after)
+
+
+def encode_kernel(pieces, arrivals, pair_weight_ref, term_ref, *rest):
     own_refs = rest[:pieces]
     come_refs = rest[pieces : pieces + arrivals * pieces]
     encoded_ref, feats_ref = rest[-2:]
-    rows, span = own_refs[0].shape
+    rows = own_refs[0].shape[0]
     half = rows // 2
     pairs = half // PAIR_POOL
     at = lax.broadcasted_iota(jnp.int32, (pairs, half), 0)
     of = lax.broadcasted_iota(jnp.int32, (pairs, half), 1) // PAIR_POOL
     spread = jnp.where(at == of, 1.0 / PAIR_POOL, 0.0).astype(bf16)
     feats = jnp.zeros(feats_ref.shape, f32)
+    quarters = term_ref[...].astype(f32)
+    all_terms = jnp.concatenate([quarters[q : q + 4] for q in range(0, 16, 4)], axis=1)
+    first = 0
     for h in range(pieces):
+        last = first + own_refs[h].shape[1]
         total = own_refs[h][...]
         for a in range(arrivals):
             total = total + come_refs[a * pieces + h][...].astype(f32)
-        encoded = jnp.maximum(total[:half], total[half:]).astype(bf16)
-        encoded_ref[:, h * span : (h + 1) * span] = encoded
+        terms = all_terms[:, first:last]
+        row = lax.broadcasted_iota(jnp.int32, (half, last - first), 0)
+        even, odd = (
+            part
+            + jnp.where(row == 0, terms[i : i + 1], 0.0)
+            + jnp.where(row == half - 1, terms[i + 2 : i + 3], 0.0)
+            for i, part in enumerate((total[:half], total[half:]))
+        )
+        encoded = jnp.maximum(even, odd).astype(bf16)
+        encoded_ref[:, first:last] = encoded
         pooled = jnp.dot(spread, encoded, preferred_element_type=f32).astype(bf16)
         feats = feats + jnp.dot(
-            pooled, pair_weight_ref[h * span : (h + 1) * span, :], preferred_element_type=f32
+            pooled, pair_weight_ref[first:last, :], preferred_element_type=f32
         )
+        first = last
     feats_ref[...] = feats.astype(bf16).astype(f32)
 
 
-def encode(own, come, pair_weight, after):
-    rows, span = own[0].shape
+def encode(own, come, terms, pair_weight, after):
+    rows = own[0].shape[0]
     pieces = len(own)
     half = rows // 2
     return pl.pallas_call(
         functools.partial(encode_kernel, pieces, len(come)),
         name="encode",
         out_shape=[
-            array((half, span * pieces), bf16),
+            array((half, sum(v.shape[1] for v in own)), bf16),
             array((half // PAIR_POOL, pair_weight.shape[1]), f32),
         ],
-        in_specs=[whole_vmem()] * (1 + pieces * (1 + len(come))) + [anywhere()] * len(after),
+        in_specs=[whole_vmem()] * (2 + pieces * (1 + len(come))) + [anywhere()] * len(after),
         out_specs=[whole_vmem()] * 2,
         compiler_params=pltpu.CompilerParams(vmem_limit_bytes=8 * MIB),
-    )(pair_weight, *own, *sum(come, []), *after)
+    )(pair_weight, terms, *own, *sum(come, []), *after)
 
 
 def normalised(encoded_ref, gain_ref):
@@ -413,14 +486,28 @@
     return (wide * scale * gain_ref[...][None]).astype(bf16)
 
 
-def bundle_kernel(encoded_ref, gain_ref, weight_ref, mine_ref, other_ref, out_ref):
-    keyval = lax.dot_general(
+def keyval_kernel(encoded_ref, gain_ref, weight_ref, out_ref):
+    out_ref[...] = lax.dot_general(
         normalised(encoded_ref, gain_ref),
         weight_ref[...],
         (((1,), (1,)), ((), ())),
         preferred_element_type=f32,
-    )
-    rows, columns = keyval.shape
+    ).astype(bf16)
+
+
+def project_keyvals(encoded, gain, weight_t):
+    return pl.pallas_call(
+        keyval_kernel,
+        name="keyvals",
+        out_shape=array((encoded.shape[0], weight_t.shape[0]), bf16),
+        in_specs=[whole_vmem()] * 3,
+        out_specs=whole_vmem(),
+        compiler_params=pltpu.CompilerParams(vmem_limit_bytes=4 * MIB),
+    )(encoded, gain, weight_t)
+
+
+def bundle_kernel(keyval_ref, mine_ref, other_ref, out_ref):
+    rows, columns = keyval_ref.shape
     spare = out_ref.shape[1] - columns
     pieces = []
     for ref in (mine_ref, other_ref):
@@ -428,20 +515,19 @@
         pieces += [feats[:, g : g + spare] for g in range(0, feats.shape[1], spare)]
     used = sum(p.shape[0] for p in pieces)
     pieces.append(jnp.zeros((rows - used, spare), f32))
-    out_ref[...] = jnp.concatenate(
-        [keyval, jnp.concatenate(pieces, axis=0)], axis=1
-    ).astype(bf16)
-
-
-def bundle(encoded, gain, weight_t, mine, other):
+    out_ref[:, :columns] = keyval_ref[...]
+    out_ref[:, columns:] = jnp.concatenate(pieces, axis=0).astype(bf16)
+
+
+def bundle(keyval, mine, other):
     return pl.pallas_call(
         bundle_kernel,
         name="bundle",
-        out_shape=array((encoded.shape[0], lane_pad(weight_t.shape[0])), bf16),
-        in_specs=[whole_vmem()] * 5,
+        out_shape=array((keyval.shape[0], lane_pad(keyval.shape[1])), bf16),
+        in_specs=[whole_vmem()] * 3,
         out_specs=whole_vmem(),
         compiler_params=pltpu.CompilerParams(vmem_limit_bytes=4 * MIB),
-    )(encoded, gain, weight_t, mine, other)
+    )(keyval, mine, other)
 
 
 def attend_kernel(
@@ -565,7 +651,7 @@
 def pair_kernel(
     chips, columns_used, input_ref, cotangent_ref, other_cotangent_ref, flip_ref, turned_ref, other_ref, *rest
 ):
-    bundle_refs = rest[:chips][::-1]
+    bundle_refs = rest[:chips]
     out_ref, grad_ref, stacked, mirror, summed, flipped, cotangent = rest[-7:]
     rows, columns, dim = input_ref.shape
     parts = 2 * chips
@@ -634,7 +720,7 @@
         compiler_params=pltpu.CompilerParams(
             vmem_limit_bytes=6 * MIB if chips <= 4 else 32 * MIB
         ),
-    )(pair_input, *cotangents, flip_weight, *turned, *bundles[::-1])
+    )(pair_input, *cotangents, flip_weight, *turned, *bundles)
 
 
 def per_device(
@@ -664,12 +750,12 @@
         cores = mask if isinstance(mask, tuple) else (mask, mask)
         return lax.ppermute(value, GROUP, hop_pairs(chips, cores, flip))
 
+    rows, channels = features.shape
+    width = channels // chips
     own_weight = conv_weight.reshape(-1, model_dim)
     peer_weight = send(own_weight, 0, 1)
-
-    rows, channels = features.shape
-    width = channels // chips
     blocks = prep(features, pair_input[0], chips)
+
     messages = [blocks[0]] + [None] * (chips - 1)
     for k in range(chips - 1, 0, -1):
         messages[k] = send(blocks[k], k)
@@ -685,28 +771,31 @@
     def active(k):
         if k not in prepared:
             sources = [messages[j] for j in dict.fromkeys(masks[k])]
-            after = [] if k == last else partial[last]
+            after = [] if k == last else partial[last] if k & 1 else partial[1]
             prepared[k] = activate(sources, width, rows, after)
         return prepared[k]
 
-    edges = send(edge_rows(messages, width, rows, [active(last)]), 0, 1)
-
-    def partials(ks, columns, after):
+    def partials(ks, columns, edges, after):
         dtypes = [bf16 if k & 1 else f32 for k in ks]
         got = conv(
             [active(k) for k in ks], edges, features, weight, taps, ks, dtypes, columns, after
         )
         return dict(zip(ks, got))
 
-    partial = partials([last], (0, model_dim // 2), [])
-    partial[last] += partials([last], (model_dim // 2, model_dim), [cotangents[1]])[last]
+    columns = [(0, model_dim // 2), (model_dim // 2, model_dim)]
+    partial = partials([last], columns[:1], None, [])
+    partial[last] += partials([last], columns[1:], None, [cotangents[1]])[last]
+    edges = send(edge_rows(messages, width, rows, partial[last]), 0, 1)
+    arrivals = [messages[k] for k in range(1, last)]
+    partial[last] = [lax.optimization_barrier((v, *arrivals))[0] for v in partial[last]]
     pairs, _, pair_dim = pair_input.shape[1:]
     turned = unpack_pairs(
         messages, pairs, pair_dim, rows, width, partial[last]
     )
     turned = (turned, send(turned, 0, 1))
     for ks in ([k for k in rest if k & 1], [k for k in rest if k and not k & 1], [0]):
-        partial.update(partials(ks, (0, model_dim), []))
+        partial.update(partials(ks, columns, edges, [turned[1]]))
+    terms = send(edge_terms(edges, weight, taps, partial[last ^ 1]), last)
     arrived = []
     for b in range(bits):
         bit = 1 << b
@@ -721,9 +810,10 @@
                     add_up([p, v], dtype, [turned[1]]) for p, v in zip(partial[k], values)
                 ]
 
-    encoded, feats = encode(partial[0], arrived, pair_weight, [])
-    own_bundle = bundle(encoded, norm_gain, keyval_weight.T, feats, send(feats, 0, 1))
-    bundles = [own_bundle] + [send(own_bundle, k) for k in range(chips - 1, 0, -1)][::-1]
+    encoded, feats = encode(partial[0], arrived, terms, pair_weight, [])
+    keyval = project_keyvals(encoded, norm_gain, keyval_weight.T)
+    own_bundle = bundle(keyval, feats, send(feats, 0, 1))
+    bundles = [own_bundle] + [send(own_bundle, k) for k in range(1, chips)]
     pair_out, grad = pair_update(
         pair_input[0], cotangents, flip_weight, turned, bundles, keyval_weight.shape[1]
     )

time: 76.7 us -> 74.6 us (0.973)
  waiting for transfers between devices: 23 us -> 16.4 us
  starting transfers between devices: 24 us -> 27.4 us
  Pallas kernels: 28.4 us -> 29.6 us
    ppermute x24 -> x25, waiting for transfers between devices: 22.6 us -> 16 us  [send(): return lax.ppermute(value, GROUP, hop_pairs(chips, cores, flip))]
    ppermute x24 -> x25, starting transfers between devices: 19.6 us -> 23 us  [send(): return lax.ppermute(value, GROUP, hop_pairs(chips, cores, flip))]
    pallas_call x1 -> x3, Pallas kernels: 0.52 us -> 1.57 us  [the longest x1 0.89 us: edge_terms(): pl.pallas_call(functools.partial(edge_terms_kernel, chips, taps), name='e...]
  transfers between devices with their start and end apart: 27 -> 28, of which waited for: 10 -> 9; matrix products, arithmetic and copies ran while one was open for 0% -> 0% of each run, Pallas kernels for 35% -> 38%
where the time goes in v6:
time: 74.6 us; the launch traced here: 74.4 us
  Pallas kernels  29.6 us (40%)
  starting transfers between devices  27.4 us (37%)
  waiting for transfers between devices  16.4 us (22%)
  between operations  0.95 us (1%)
    ppermute x25, starting transfers between devices, send(): return lax.ppermute(value, GROUP, hop_pairs(chips, cores, flip))  23 us
    ppermute x25, waiting for transfers between devices, send(): return lax.ppermute(value, GROUP, hop_pairs(chips, cores, flip))  16 us
    pallas_call x5, Pallas kernels, conv(): pl.pallas_call(functools.partial(conv_kernel, chips, bits, taps, 256, wan...  8.87 us
    pallas_call x2, Pallas kernels, attend(): pl.pallas_call(functools.partial(attend_kernel, len(parts), heads, first,...  6.44 us
    pallas_call x4, Pallas kernels, activate(): pl.pallas_call(functools.partial(activate_kernel, width, len(messages)),...  6.23 us
    ppermute x3, starting transfers between devices, per_device(): lax.ppermute(grad, 'dp', [(w, w ^ k) for w in range(windows)])  4.45 us
    pallas_call x1, Pallas kernels, prep(): pl.pallas_call(functools.partial(prep_kernel, chips, width), name='prep',...  1.84 us
    pallas_call x1, Pallas kernels, pack_filter(): pl.pallas_call(functools.partial(pack_kernel, taps, padded), name='pack_f...  1.79 us
  transfers between devices with their start and end apart: 28, of which 9 were waited for; matrix products, arithmetic and copies ran while one was open for 0% of the time, Pallas kernels for 38%

profile of v6, /device:TPU:0, one launch (start us, length us, event | category | flops | bytes accessed | tf_op | source)
XLA Modules:
  0.0 74.4 jit_solution(5427416549884873138)
XLA Ops:
  1.1 1.8 %prep.1 = (bf16[288,384]{1,0:T(8,128)(2,1)S(1)}, bf16[288,384]{1,0:T(8,128)(2,1)S(1)}, bf16[288,384]{1,0:T(8,128)(2,1)S(1)}, bf16[288,384]{1,0:T(8,128)(2,1)S(1)}) custom-call(bf16[256,1408]{1,0:T(8,128)(2,1)} %bitcast.14, bf16[8,64,128]{2,1,0:T(8,128)(2,1)} %bitcast.10), custom_call_target="tpu_custom_call" | custom-call | tf_op jit(solution)/shard_map/prep/pallas_call | solution.py:138
  3.0 3.5 %collective-permute-start = (bf16[288,384]{1,0:T(8,128)(2,1)S(1)}, bf16[288,384]{1,0:T(8,128)(2,1)S(1)}, u32[]{:S(2)}, u32[]{:S(2)}) collective-permute-start(bf16[288,384]{1,0:T(8,128)(2,1)S(1)} %get-tuple-element.25), channel_id=1, source_target_pairs={{0,6},{1,7},{2,4},{3,5},{4,2},{5,3},{6,0},{7,1},{8,14},{9,15},{10,... | collective-permute-start | bytes 663560 | tf_op jit(solution)/shard_map/ppermute | solution.py:751
  7.2 1.8 %pack_filter.1.rest_1_.weight_ref = bf16[1920,1536]{1,0:T(8,128)(2,1)S(1)} custom-call(bf16[880,1536]{1,0:T(8,128)(2,1)} %bitcast.21, bf16[880,1536]{1,0:T(8,128)(2,1)S(1)} %collective-permute-done.3.peer_hbm), custom_call_target="tpu_custom_call" | custom-call | tf_op jit(solution)/shard_map/pack_filter/pallas_call | solution.py:261
  9.1 3.8 %collective-permute-done.refs_0_ = bf16[288,384]{1,0:T(8,128)(2,1)S(1)} collective-permute-done((bf16[288,384]{1,0:T(8,128)(2,1)S(1)}, bf16[288,384]{1,0:T(8,128)(2,1)S(1)}, u32[]{:S(2)}, u32[]{:S(2)}) %collective-permute-start) | collective-permute-done | bytes 221216 | tf_op jit(solution)/shard_map/ppermute | solution.py:751
  12.8 1.5 %activate.4.edge_ref.rest_0_ = bf16[256,384]{1,0:T(8,128)(2,1)S(1)} custom-call(bf16[288,384]{1,0:T(8,128)(2,1)S(1)} %collective-permute-done.refs_0_), custom_call_target="tpu_custom_call" | custom-call | tf_op jit(solution)/shard_map/activate/pallas_call | solution.py:216
  15.4 2.0 %collective-permute-done.1.refs_1_.refs_0_ = bf16[288,384]{1,0:T(8,128)(2,1)S(1)} collective-permute-done((bf16[288,384]{1,0:T(8,128)(2,1)S(1)}, bf16[288,384]{1,0:T(8,128)(2,1)S(1)}, u32[]{:S(2)}, u32[]{:S(2)}) %collective-permute-start.1) | collective-permute-done | bytes 221216 | tf_op jit(solution)/shard_map/ppermute | solution.py:751
  17.6 1.5 %collective-permute-start.10 = (bf16[256,768]{1,0:T(8,128)(2,1)S(1)}, bf16[256,768]{1,0:T(8,128)(2,1)S(1)}, u32[]{:S(2)}, u32[]{:S(2)}) collective-permute-start(bf16[256,768]{1,0:T(8,128)(2,1)S(1)} %conv.5.refs_4_.refs_2_), channel_id=1, source_target_pairs={{0,2},{1,5},{2,0},{3,7},{4,6},{5,1},{6,4},{7,3},{8,10},{9,13},{10,... | collective-permute-start | bytes 1179656 | tf_op jit(solution)/shard_map/ppermute | solution.py:751
  21.7 1.5 %activate.5.rest_0_ = bf16[256,384]{1,0:T(8,128)(2,1)S(1)} custom-call(bf16[288,384]{1,0:T(8,128)(2,1)S(1)} %collective-permute-done.2.refs_2_.refs_0_.refs_1_, bf16[288,384]{1,0:T(8,128)(2,1)S(1)} %collective-permute-done.1.refs_1_.refs_0_, bf16[256,768]{1,0:T(8,128)(2,1)S(1)} %conv.5.refs_4_.refs_2_, bf16[256,768]{1,0:T(8,128)(2,1)S(1)} %conv.6.refs_5_.refs_3_), custom_call_target="tpu_custom_call" | custom-call | tf_op jit(solution)/shard_map/activate/pallas_call | solution.py:216
  23.3 1.8 %conv.7 = (bf16[256,768]{1,0:T(8,128)(2,1)S(1)}, bf16[256,768]{1,0:T(8,128)(2,1)S(1)}) custom-call(bf16[256,1408]{1,0:T(8,128)(2,1)} %bitcast.17, f32[4,8,384]{2,1,0:T(8,128)S(1)} %collective-permute-done.5.edge_ref, bf16[256,384]{1,0:T(8,128)(2,1)S(1)} %activate.5.rest_0_, bf16[1920,1536]{1,0:T(8,128)(2,1)S(1)} %pack_filter.1.rest_1_.weight_ref, ...), custom_call_target="tpu_custom_call" | custom-call | tf_op jit(solution)/shard_map/conv/pallas_call | solution.py:395
  25.1 1.6 %collective-permute-start.8 = (bf16[256,768]{1,0:T(8,128)(2,1)S(1)}, bf16[256,768]{1,0:T(8,128)(2,1)S(1)}, u32[]{:S(2)}, u32[]{:S(2)}) collective-permute-start(bf16[256,768]{1,0:T(8,128)(2,1)S(1)} %get-tuple-element.33.refs_2_.refs_1_), channel_id=1, source_target_pairs={{0,2},{1,5},{2,0},{3,7},{4,6},{5,1},{6,4},{7,3},{8,10},{9,13},{10,... | collective-permute-start | bytes 1179656 | tf_op jit(solution)/shard_map/ppermute | solution.py:751
  27.2 1.7 %activate.6.rest_0_ = bf16[256,384]{1,0:T(8,128)(2,1)S(1)} custom-call(bf16[288,384]{1,0:T(8,128)(2,1)S(1)} %collective-permute-done.1.refs_1_.refs_0_, bf16[288,384]{1,0:T(8,128)(2,1)S(1)} %collective-permute-done.2.refs_2_.refs_0_.refs_1_, bf16[256,768]{1,0:T(8,128)(2,1)S(1)} %get-tuple-element.33.refs_2_.refs_1_, ...), custom_call_target="tpu_custom_call" | custom-call | tf_op jit(solution)/shard_map/activate/pallas_call | solution.py:216
  28.9 1.8 %conv.8 = (f32[256,768]{1,0:T(8,128)S(1)}, f32[256,768]{1,0:T(8,128)S(1)}) custom-call(bf16[256,1408]{1,0:T(8,128)(2,1)} %bitcast.18, f32[4,8,384]{2,1,0:T(8,128)S(1)} %collective-permute-done.5.edge_ref, bf16[256,384]{1,0:T(8,128)(2,1)S(1)} %activate.6.rest_0_, bf16[1920,1536]{1,0:T(8,128)(2,1)S(1)} %pack_filter.1.rest_1_.weight_ref, ...), custom_call_target="tpu_custom_call" | custom-call | tf_op jit(solution)/shard_map/conv/pallas_call | solution.py:395
  33.9 1.6 %collective-permute-start.7 = (bf16[16,384]{1,0:T(8,128)(2,1)S(1)}, bf16[16,384]{1,0:T(8,128)(2,1)S(1)}, u32[]{:S(2)}, u32[]{:S(2)}) collective-permute-start(bf16[16,384]{1,0:T(8,128)(2,1)S(1)} %edge_terms.1), channel_id=1, source_target_pairs={{0,6},{1,7},{2,4},{3,5},{4,2},{5,3},{6,0},{7,1},{8,14},{9,15},{10,... | collective-permute-start | bytes 36872 | tf_op jit(solution)/shard_map/ppermute | solution.py:751
  35.5 1.5 %activate.7.rest_0_ = bf16[256,384]{1,0:T(8,128)(2,1)S(1)} custom-call(bf16[288,384]{1,0:T(8,128)(2,1)S(1)} %get-tuple-element.28.refs_3_.refs_0_, bf16[256,768]{1,0:T(8,128)(2,1)S(1)} %get-tuple-element.33.refs_2_.refs_1_, bf16[256,768]{1,0:T(8,128)(2,1)S(1)} %get-tuple-element.34.refs_3_.refs_2_), custom_call_target="tpu_custom_call" | custom-call | tf_op jit(solution)/shard_map/activate/pallas_call | solution.py:216
  37.0 3.2 %conv.9 = (f32[256,768]{1,0:T(8,128)S(1)}, f32[256,768]{1,0:T(8,128)S(1)}) custom-call(bf16[256,1408]{1,0:T(8,128)(2,1)} %bitcast.19, f32[4,8,384]{2,1,0:T(8,128)S(1)} %collective-permute-done.5.edge_ref, bf16[256,384]{1,0:T(8,128)(2,1)S(1)} %activate.7.rest_0_, bf16[1920,1536]{1,0:T(8,128)(2,1)S(1)} %pack_filter.1.rest_1_.weight_ref, ...), custom_call_target="tpu_custom_call" | custom-call | tf_op jit(solution)/shard_map/conv/pallas_call | solution.py:395
  40.3 3.9 %collective-permute-done.7.term_ref = bf16[16,384]{1,0:T(8,128)(2,1)S(1)} collective-permute-done((bf16[16,384]{1,0:T(8,128)(2,1)S(1)}, bf16[16,384]{1,0:T(8,128)(2,1)S(1)}, u32[]{:S(2)}, u32[]{:S(2)}) %collective-permute-start.7) | collective-permute-done | bytes 12320 | tf_op jit(solution)/shard_map/ppermute | solution.py:751
  45.9 2.1 %collective-permute-start.14 = (f32[8,256]{1,0:T(8,128)S(1)}, f32[8,256]{1,0:T(8,128)S(1)}, u32[]{:S(2)}, u32[]{:S(2)}) collective-permute-start(f32[8,256]{1,0:T(8,128)S(1)} %get-tuple-element.40.mine_ref), channel_id=1, source_target_pairs={{0,1},{1,0},{2,3},{3,2},{4,5},{5,4},{6,7},{7,6},{8,9},{9,8},{10,11... | collective-permute-start | bytes 24584 | tf_op jit(solution)/shard_map/ppermute | solution.py:751
  49.0 1.5 %collective-permute-start.17 = (bf16[128,384]{1,0:T(8,128)(2,1)S(1)}, bf16[128,384]{1,0:T(8,128)(2,1)S(1)}, u32[]{:S(2)}, u32[]{:S(2)}) collective-permute-start(bf16[128,384]{1,0:T(8,128)(2,1)S(1)} %bundle.1.rest_0_), channel_id=1, source_target_pairs={{0,6},{1,7},{2,4},{3,5},{4,2},{5,3},{6,0},{7,1},{8,14},{9,15},{10,... | collective-permute-start | bytes 294920 | tf_op jit(solution)/shard_map/ppermute | solution.py:751
  52.5 3.0 %collective-permute-done.17.rest_3_ = bf16[128,384]{1,0:T(8,128)(2,1)S(1)} collective-permute-done((bf16[128,384]{1,0:T(8,128)(2,1)S(1)}, bf16[128,384]{1,0:T(8,128)(2,1)S(1)}, u32[]{:S(2)}, u32[]{:S(2)}) %collective-permute-start.17) | collective-permute-done | bytes 98336 | tf_op jit(solution)/shard_map/ppermute | solution.py:751
  55.5 1.5 %collective-permute-done.16.rest_2_ = bf16[128,384]{1,0:T(8,128)(2,1)S(1)} collective-permute-done((bf16[128,384]{1,0:T(8,128)(2,1)S(1)}, bf16[128,384]{1,0:T(8,128)(2,1)S(1)}, u32[]{:S(2)}, u32[]{:S(2)}) %collective-permute-start.16) | collective-permute-done | bytes 98336 | tf_op jit(solution)/shard_map/ppermute | solution.py:751
  58.8 1.5 %collective-permute-start.24 = (bf16[128,128]{1,0:T(8,128)(2,1)S(1)}, bf16[128,128]{1,0:T(8,128)(2,1)S(1)}, u32[]{:S(2)}, u32[]{:S(2)}) collective-permute-start(bf16[128,128]{1,0:T(8,128)(2,1)S(1)} %get-tuple-element.42.refs_0_), channel_id=1, source_target_pairs={{0,6},{1,7},{2,4},{3,5},{4,2},{5,3},{6,0},{7,1},{8,14},{9,15},{10,... | collective-permute-start | bytes 98312 | tf_op jit(solution)/shard_map/ppermute | solution.py:751
  62.4 2.8 %attend.2 = (f32[128,1536]{1,0:T(8,128)S(1)}, f32[8,128]{1,0:T(8,128)S(1)}) custom-call(f32[8]{0:T(128)S(1)} %copy-done.7, bf16[128,1536]{1,0:T(8,128)(2,1)S(1)} %get-tuple-element.39.encoded_ref.start_ref, f32[1536]{0:T(1024)S(1)} %copy-done.5, bf16[1536,1024]{1,0:T(8,128)(2,1)S(1)} %copy-done, ...), custom_call_target="tpu_custom_call" | custom-call | tf_op jit(solution)/shard_map/attend/pallas_call | solution.py:600
  65.3 3.7 %collective-permute-start.27 = (bf16[128,128]{1,0:T(8,128)(2,1)S(1)}, bf16[128,128]{1,0:T(8,128)(2,1)S(1)}, u32[]{:S(2)}, u32[]{:S(2)}) collective-permute-start(bf16[128,128]{1,0:T(8,128)(2,1)S(1)} %add_up.6.rest_8_.refs_0_), channel_id=1, source_target_pairs={{0,24},{8,16},{16,8},{24,0},{1,25},{9,17},{17,9},{25,1},{2,26},{10... | collective-permute-start | bytes 98312 | tf_op jit(solution)/shard_map/ppermute | solution.py:844
  69.7 3.6 %attend.3 = (bf16[128,1536]{1,0:T(8,128)(2,1)}, f32[8,128]{1,0:T(8,128)S(1)}) custom-call(f32[8]{0:T(128)S(1)} %copy-done.7, bf16[128,1536]{1,0:T(8,128)(2,1)S(1)} %get-tuple-element.39.encoded_ref.start_ref, f32[1536]{0:T(1024)S(1)} %copy-done.5, bf16[1536,1024]{1,0:T(8,128)(2,1)S(1)} %copy-done, f32[128,1536]{1,0:T(8,128)S(1)} %get-tuple-element.41.start_ref, ...), custom_call_target="tpu_custom_call" | custom-call | tf_op jit(solution)/shard_map/attend/pallas_call | solution.py:600
  (77 shorter events, 19.0 us)
Async XLA Ops:
  0.6 6.5 %collective-permute-start.3 = (bf16[880,1536]{1,0:T(8,128)(2,1)}, bf16[880,1536]{1,0:T(8,128)(2,1)S(1)}, u32[]{:S(2)}, u32[]{:S(2)}) collective-permute-start(bf16[880,1536]{1,0:T(8,128)(2,1)} %bitcast.20), channel_id=1, source_target_pairs={{0,1},{1,0},{2,3},{3,2},{4,5},{5,4},{6,7},{7,6},{8,9},{9,8},{10,11... | collective-permute-start | bytes 8110088 | tf_op jit(solution)/shard_map/ppermute | solution.py:751
  3.0 9.9 %collective-permute-start = (bf16[288,384]{1,0:T(8,128)(2,1)S(1)}, bf16[288,384]{1,0:T(8,128)(2,1)S(1)}, u32[]{:S(2)}, u32[]{:S(2)}) collective-permute-start(bf16[288,384]{1,0:T(8,128)(2,1)S(1)} %get-tuple-element.25), channel_id=1, source_target_pairs={{0,6},{1,7},{2,4},{3,5},{4,2},{5,3},{6,0},{7,1},{8,14},{9,15},{10,... | collective-permute-start | bytes 663560 | tf_op jit(solution)/shard_map/ppermute | solution.py:751
  6.5 10.8 %collective-permute-start.1 = (bf16[288,384]{1,0:T(8,128)(2,1)S(1)}, bf16[288,384]{1,0:T(8,128)(2,1)S(1)}, u32[]{:S(2)}, u32[]{:S(2)}) collective-permute-start(bf16[288,384]{1,0:T(8,128)(2,1)S(1)} %get-tuple-element.26), channel_id=1, source_target_pairs={{0,4},{1,5},{2,6},{3,7},{4,0},{5,1},{6,2},{7,3},{8,12},{9,13},{10,... | collective-permute-start | bytes 663560 | tf_op jit(solution)/shard_map/ppermute | solution.py:751
  7.0 10.6 %collective-permute-start.2 = (bf16[288,384]{1,0:T(8,128)(2,1)S(1)}, bf16[288,384]{1,0:T(8,128)(2,1)S(1)}, u32[]{:S(2)}, u32[]{:S(2)}) collective-permute-start(bf16[288,384]{1,0:T(8,128)(2,1)S(1)} %get-tuple-element.27), channel_id=1, source_target_pairs={{0,2},{1,3},{2,0},{3,1},{4,6},{5,7},{6,4},{7,5},{8,10},{9,11},{10,... | collective-permute-start | bytes 663560 | tf_op jit(solution)/shard_map/ppermute | solution.py:751
  9.0 10.2 %collective-permute-start.4 = (bf16[8,64,128]{2,1,0:T(8,128)(2,1)S(1)}, bf16[8,64,128]{2,1,0:T(8,128)(2,1)S(1)}, u32[]{:S(2)}, u32[]{:S(2)}) collective-permute-start(bf16[8,64,128]{2,1,0:T(8,128)(2,1)S(1)} %bitcast.12), channel_id=1, source_target_pairs={{0,1},{1,0},{2,3},{3,2},{4,5},{5,4},{6,7},{7,6},{8,9},{9,8},{10,11... | collective-permute-start | bytes 393224 | tf_op jit(solution)/shard_map/ppermute | solution.py:751
  17.6 13.1 %collective-permute-start.10 = (bf16[256,768]{1,0:T(8,128)(2,1)S(1)}, bf16[256,768]{1,0:T(8,128)(2,1)S(1)}, u32[]{:S(2)}, u32[]{:S(2)}) collective-permute-start(bf16[256,768]{1,0:T(8,128)(2,1)S(1)} %conv.5.refs_4_.refs_2_), channel_id=1, source_target_pairs={{0,2},{1,5},{2,0},{3,7},{4,6},{5,1},{6,4},{7,3},{8,10},{9,13},{10,... | collective-permute-start | bytes 1179656 | tf_op jit(solution)/shard_map/ppermute | solution.py:751
  20.2 12.1 %collective-permute-start.12 = (bf16[256,768]{1,0:T(8,128)(2,1)S(1)}, bf16[256,768]{1,0:T(8,128)(2,1)S(1)}, u32[]{:S(2)}, u32[]{:S(2)}) collective-permute-start(bf16[256,768]{1,0:T(8,128)(2,1)S(1)} %conv.6.refs_5_.refs_3_), channel_id=1, source_target_pairs={{0,2},{1,5},{2,0},{3,7},{4,6},{5,1},{6,4},{7,3},{8,10},{9,13},{10,... | collective-permute-start | bytes 1179656 | tf_op jit(solution)/shard_map/ppermute | solution.py:751
  25.1 19.2 %collective-permute-start.8 = (bf16[256,768]{1,0:T(8,128)(2,1)S(1)}, bf16[256,768]{1,0:T(8,128)(2,1)S(1)}, u32[]{:S(2)}, u32[]{:S(2)}) collective-permute-start(bf16[256,768]{1,0:T(8,128)(2,1)S(1)} %get-tuple-element.33.refs_2_.refs_1_), channel_id=1, source_target_pairs={{0,2},{1,5},{2,0},{3,7},{4,6},{5,1},{6,4},{7,3},{8,10},{9,13},{10,... | collective-permute-start | bytes 1179656 | tf_op jit(solution)/shard_map/ppermute | solution.py:751
  26.6 17.6 %collective-permute-start.9 = (bf16[256,768]{1,0:T(8,128)(2,1)S(1)}, bf16[256,768]{1,0:T(8,128)(2,1)S(1)}, u32[]{:S(2)}, u32[]{:S(2)}) collective-permute-start(bf16[256,768]{1,0:T(8,128)(2,1)S(1)} %get-tuple-element.34.refs_3_.refs_2_), channel_id=1, source_target_pairs={{0,2},{1,5},{2,0},{3,7},{4,6},{5,1},{6,4},{7,3},{8,10},{9,13},{10,... | collective-permute-start | bytes 1179656 | tf_op jit(solution)/shard_map/ppermute | solution.py:751
  30.8 13.5 %collective-permute-start.11 = (bf16[256,768]{1,0:T(8,128)(2,1)S(1)}, bf16[256,768]{1,0:T(8,128)(2,1)S(1)}, u32[]{:S(2)}, u32[]{:S(2)}) collective-permute-start(bf16[256,768]{1,0:T(8,128)(2,1)S(1)} %add_up.4), channel_id=1, source_target_pairs={{0,4},{1,3},{2,6},{3,1},{4,0},{5,7},{6,2},{7,5},{8,12},{9,11},{10,... | collective-permute-start | bytes 1179656 | tf_op jit(solution)/shard_map/ppermute | solution.py:751
  32.3 13.1 %collective-permute-start.13 = (bf16[256,768]{1,0:T(8,128)(2,1)S(1)}, bf16[256,768]{1,0:T(8,128)(2,1)S(1)}, u32[]{:S(2)}, u32[]{:S(2)}) collective-permute-start(bf16[256,768]{1,0:T(8,128)(2,1)S(1)} %add_up.5), channel_id=1, source_target_pairs={{0,4},{1,3},{2,6},{3,1},{4,0},{5,7},{6,2},{7,5},{8,12},{9,11},{10,... | collective-permute-start | bytes 1179656 | tf_op jit(solution)/shard_map/ppermute | solution.py:751
  33.9 10.3 %collective-permute-start.7 = (bf16[16,384]{1,0:T(8,128)(2,1)S(1)}, bf16[16,384]{1,0:T(8,128)(2,1)S(1)}, u32[]{:S(2)}, u32[]{:S(2)}) collective-permute-start(bf16[16,384]{1,0:T(8,128)(2,1)S(1)} %edge_terms.1), channel_id=1, source_target_pairs={{0,6},{1,7},{2,4},{3,5},{4,2},{5,3},{6,0},{7,1},{8,14},{9,15},{10,... | collective-permute-start | bytes 36872 | tf_op jit(solution)/shard_map/ppermute | solution.py:751
  49.0 6.5 %collective-permute-start.17 = (bf16[128,384]{1,0:T(8,128)(2,1)S(1)}, bf16[128,384]{1,0:T(8,128)(2,1)S(1)}, u32[]{:S(2)}, u32[]{:S(2)}) collective-permute-start(bf16[128,384]{1,0:T(8,128)(2,1)S(1)} %bundle.1.rest_0_), channel_id=1, source_target_pairs={{0,6},{1,7},{2,4},{3,5},{4,2},{5,3},{6,0},{7,1},{8,14},{9,15},{10,... | collective-permute-start | bytes 294920 | tf_op jit(solution)/shard_map/ppermute | solution.py:751
  50.5 6.5 %collective-permute-start.16 = (bf16[128,384]{1,0:T(8,128)(2,1)S(1)}, bf16[128,384]{1,0:T(8,128)(2,1)S(1)}, u32[]{:S(2)}, u32[]{:S(2)}) collective-permute-start(bf16[128,384]{1,0:T(8,128)(2,1)S(1)} %bundle.1.rest_0_), channel_id=1, source_target_pairs={{0,4},{1,5},{2,6},{3,7},{4,0},{5,1},{6,2},{7,3},{8,12},{9,13},{10,... | collective-permute-start | bytes 294920 | tf_op jit(solution)/shard_map/ppermute | solution.py:751
  51.1 5.9 %collective-permute-start.15 = (bf16[128,384]{1,0:T(8,128)(2,1)S(1)}, bf16[128,384]{1,0:T(8,128)(2,1)S(1)}, u32[]{:S(2)}, u32[]{:S(2)}) collective-permute-start(bf16[128,384]{1,0:T(8,128)(2,1)S(1)} %bundle.1.rest_0_), channel_id=1, source_target_pairs={{0,2},{1,3},{2,0},{3,1},{4,6},{5,7},{6,4},{7,5},{8,10},{9,11},{10,... | collective-permute-start | bytes 294920 | tf_op jit(solution)/shard_map/ppermute | solution.py:751
  52.5 7.9 %collective-permute-start.18 = (bf16[128,384]{1,0:T(8,128)(2,1)S(1)}, bf16[128,384]{1,0:T(8,128)(2,1)S(1)}, u32[]{:S(2)}, u32[]{:S(2)}) collective-permute-start(bf16[128,384]{1,0:T(8,128)(2,1)S(1)} %bundle.1.rest_0_), channel_id=1, source_target_pairs={{0,1},{1,0},{2,3},{3,2},{4,5},{5,4},{6,7},{7,6},{8,9},{9,8},{10,11... | collective-permute-start | bytes 294920 | tf_op jit(solution)/shard_map/ppermute | solution.py:751
  55.5 5.4 %collective-permute-start.21 = (bf16[128,384]{1,0:T(8,128)(2,1)S(1)}, bf16[128,384]{1,0:T(8,128)(2,1)S(1)}, u32[]{:S(2)}, u32[]{:S(2)}) collective-permute-start(bf16[128,384]{1,0:T(8,128)(2,1)S(1)} %collective-permute-done.17.rest_3_), channel_id=1, source_target_pairs={{0,1},{1,0},{2,3},{3,2},{4,5},{5,4},{6,7},{7,6},{8,9},{9,8},{10,11... | collective-permute-start | bytes 294920 | tf_op jit(solution)/shard_map/ppermute | solution.py:751
  57.1 5.3 %collective-permute-start.20 = (bf16[128,384]{1,0:T(8,128)(2,1)S(1)}, bf16[128,384]{1,0:T(8,128)(2,1)S(1)}, u32[]{:S(2)}, u32[]{:S(2)}) collective-permute-start(bf16[128,384]{1,0:T(8,128)(2,1)S(1)} %collective-permute-done.16.rest_2_), channel_id=1, source_target_pairs={{0,1},{1,0},{2,3},{3,2},{4,5},{5,4},{6,7},{7,6},{8,9},{9,8},{10,11... | collective-permute-start | bytes 294920 | tf_op jit(solution)/shard_map/ppermute | solution.py:751
  57.1 5.3 %collective-permute-start.19 = (bf16[128,384]{1,0:T(8,128)(2,1)S(1)}, bf16[128,384]{1,0:T(8,128)(2,1)S(1)}, u32[]{:S(2)}, u32[]{:S(2)}) collective-permute-start(bf16[128,384]{1,0:T(8,128)(2,1)S(1)} %collective-permute-done.15.rest_1_), channel_id=1, source_target_pairs={{0,1},{1,0},{2,3},{3,2},{4,5},{5,4},{6,7},{7,6},{8,9},{9,8},{10,11... | collective-permute-start | bytes 294920 | tf_op jit(solution)/shard_map/ppermute | solution.py:751
  58.8 6.4 %collective-permute-start.24 = (bf16[128,128]{1,0:T(8,128)(2,1)S(1)}, bf16[128,128]{1,0:T(8,128)(2,1)S(1)}, u32[]{:S(2)}, u32[]{:S(2)}) collective-permute-start(bf16[128,128]{1,0:T(8,128)(2,1)S(1)} %get-tuple-element.42.refs_0_), channel_id=1, source_target_pairs={{0,6},{1,7},{2,4},{3,5},{4,2},{5,3},{6,0},{7,1},{8,14},{9,15},{10,... | collective-permute-start | bytes 98312 | tf_op jit(solution)/shard_map/ppermute | solution.py:751
  60.4 4.9 %collective-permute-start.23 = (bf16[128,128]{1,0:T(8,128)(2,1)S(1)}, bf16[128,128]{1,0:T(8,128)(2,1)S(1)}, u32[]{:S(2)}, u32[]{:S(2)}) collective-permute-start(bf16[128,128]{1,0:T(8,128)(2,1)S(1)} %get-tuple-element.42.refs_0_), channel_id=1, source_target_pairs={{0,4},{1,5},{2,6},{3,7},{4,0},{5,1},{6,2},{7,3},{8,12},{9,13},{10,... | collective-permute-start | bytes 98312 | tf_op jit(solution)/shard_map/ppermute | solution.py:751
  65.3 8.1 %collective-permute-start.27 = (bf16[128,128]{1,0:T(8,128)(2,1)S(1)}, bf16[128,128]{1,0:T(8,128)(2,1)S(1)}, u32[]{:S(2)}, u32[]{:S(2)}) collective-permute-start(bf16[128,128]{1,0:T(8,128)(2,1)S(1)} %add_up.6.rest_8_.refs_0_), channel_id=1, source_target_pairs={{0,24},{8,16},{16,8},{24,0},{1,25},{9,17},{17,9},{25,1},{2,26},{10... | collective-permute-start | bytes 98312 | tf_op jit(solution)/shard_map/ppermute | solution.py:844
  69.0 4.8 %collective-permute-start.26 = (bf16[128,128]{1,0:T(8,128)(2,1)S(1)}, bf16[128,128]{1,0:T(8,128)(2,1)S(1)}, u32[]{:S(2)}, u32[]{:S(2)}) collective-permute-start(bf16[128,128]{1,0:T(8,128)(2,1)S(1)} %add_up.6.rest_8_.refs_0_), channel_id=1, source_target_pairs={{0,16},{8,24},{16,0},{24,8},{1,17},{9,25},{17,1},{25,9},{2,18},{10... | collective-permute-start | bytes 98312 | tf_op jit(solution)/shard_map/ppermute | solution.py:844
  69.0 4.8 %collective-permute-start.25 = (bf16[128,128]{1,0:T(8,128)(2,1)S(1)}, bf16[128,128]{1,0:T(8,128)(2,1)S(1)}, u32[]{:S(2)}, u32[]{:S(2)}) collective-permute-start(bf16[128,128]{1,0:T(8,128)(2,1)S(1)} %add_up.6.rest_8_.refs_0_), channel_id=1, source_target_pairs={{0,8},{8,0},{16,24},{24,16},{1,9},{9,1},{17,25},{25,17},{2,10},{10... | collective-permute-start | bytes 98312 | tf_op jit(solution)/shard_map/ppermute | solution.py:844
  (14 other events, 158.1 us)

commit v7 on v6

--- a/solution.py
+++ b/solution.py
@@ -410,14 +410,16 @@
     return [got[j * pieces : (j + 1) * pieces] for j in range(count)]
 
 
-def sum_kernel(count, *refs):
+def sum_kernel(count, backwards, *refs):
     out_ref = refs[-1]
-    out_ref[...] = tree_sum([r[...].astype(f32) for r in refs[:count]]).astype(out_ref.dtype)
-
-
-def add_up(terms, dtype, after=()):
-    return pl.pallas_call(
-        functools.partial(sum_kernel, len(terms)),
+    terms = [r[...].astype(f32) for r in refs[:count]]
+    out_ref[...] = tree_sum(terms[::-1] if backwards else terms).astype(out_ref.dtype)
+
+
+def add_up(terms, dtype, after=(), backwards=False):
+    terms = terms[::-1] if backwards else terms
+    return pl.pallas_call(
+        functools.partial(sum_kernel, len(terms), backwards),
         name="add_up",
         out_shape=array(terms[0].shape, dtype),
         in_specs=[whole_vmem()] * len(terms) + [anywhere()] * len(after),
@@ -768,23 +770,21 @@
 
     prepared = {}
 
-    def active(k):
+    def active(k, wait):
         if k not in prepared:
             sources = [messages[j] for j in dict.fromkeys(masks[k])]
-            after = [] if k == last else partial[last] if k & 1 else partial[1]
-            prepared[k] = activate(sources, width, rows, after)
+            prepared[k] = activate(sources, width, rows, wait)
         return prepared[k]
 
-    def partials(ks, columns, edges, after):
+    def partials(ks, columns, edges, after, wait):
         dtypes = [bf16 if k & 1 else f32 for k in ks]
-        got = conv(
-            [active(k) for k in ks], edges, features, weight, taps, ks, dtypes, columns, after
-        )
+        blocks = [active(k, wait) for k in ks]
+        got = conv(blocks, edges, features, weight, taps, ks, dtypes, columns, after)
         return dict(zip(ks, got))
 
     columns = [(0, model_dim // 2), (model_dim // 2, model_dim)]
-    partial = partials([last], columns[:1], None, [])
-    partial[last] += partials([last], columns[1:], None, [cotangents[1]])[last]
+    partial = partials([last], columns[:1], None, [], [])
+    partial[last] += partials([last], columns[1:], None, [cotangents[1]], [])[last]
     edges = send(edge_rows(messages, width, rows, partial[last]), 0, 1)
     arrivals = [messages[k] for k in range(1, last)]
     partial[last] = [lax.optimization_barrier((v, *arrivals))[0] for v in partial[last]]
@@ -793,9 +793,13 @@
         messages, pairs, pair_dim, rows, width, partial[last]
     )
     turned = (turned, send(turned, 0, 1))
-    for ks in ([k for k in rest if k & 1], [k for k in rest if k and not k & 1], [0]):
-        partial.update(partials(ks, columns, edges, [turned[1]]))
-    terms = send(edge_terms(edges, weight, taps, partial[last ^ 1]), last)
+    odd = [k for k in rest if k & 1]
+    even = [k for k in rest if k and not k & 1]
+    partial.update(partials(odd, columns, edges, [turned[1]], partial[last]))
+    own_terms = edge_terms(edges, weight, taps, partial[1])
+    terms = send(own_terms, last)
+    for ks in (even, [0]):
+        partial.update(partials(ks, columns, edges, [turned[1]], [own_terms]))
     arrived = []
     for b in range(bits):
         bit = 1 << b
@@ -838,15 +842,11 @@
     first_half, done = attend_heads(encoded, 0, halfway, f32, [])
     grad = add_up([grad] + [send(grad, k) for k in range(1, chips)], bf16, [done])
     block_out, done = attend_heads(first_half, halfway, heads, bf16, [grad])
-    grad = add_up(
-        [grad]
-        + [
-            lax.ppermute(grad, "dp", [(w, w ^ k) for w in range(windows)])
-            for k in range(1, windows)
-        ],
-        f32,
-        [done],
-    )
+    planes = [
+        lax.ppermute(grad, "dp", [(w, w ^ k) for w in range(windows)])
+        for k in range(windows - 1, 0, -1)
+    ]
+    grad = add_up([grad] + planes[::-1], f32, [done], backwards=True)
     return (block_out[None], pair_out[None], grad)
 
 

time: 74.6 us -> 74 us (level)
  transfers between devices with their start and end apart: 28 -> 28, of which waited for: 9 -> 11; matrix products, arithmetic and copies ran while one was open for 0% -> 0% of each run, Pallas kernels for 38% -> 38%
where the time goes in v7:
time: 74 us; the launch traced here: 73.8 us
  Pallas kernels  29.6 us (40%)
  starting transfers between devices  26.8 us (36%)
  waiting for transfers between devices  16.4 us (22%)
  between operations  0.95 us (1%)
    ppermute x25, starting transfers between devices, send(): return lax.ppermute(value, GROUP, hop_pairs(chips, cores, flip))  22.4 us
    ppermute x25, waiting for transfers between devices, send(): return lax.ppermute(value, GROUP, hop_pairs(chips, cores, flip))  16 us
    pallas_call x5, Pallas kernels, conv(): pl.pallas_call(functools.partial(conv_kernel, chips, bits, taps, 256, wan...  8.88 us
    pallas_call x2, Pallas kernels, attend(): pl.pallas_call(functools.partial(attend_kernel, len(parts), heads, first,...  6.43 us
    pallas_call x4, Pallas kernels, activate(): pl.pallas_call(functools.partial(activate_kernel, width, len(messages)),...  6.25 us
    ppermute x3, starting transfers between devices, per_device(): lax.ppermute(grad, 'dp', [(w, w ^ k) for w in range(windows)])  4.45 us
    pallas_call x1, Pallas kernels, prep(): pl.pallas_call(functools.partial(prep_kernel, chips, width), name='prep',...  1.84 us
    pallas_call x1, Pallas kernels, pack_filter(): pl.pallas_call(functools.partial(pack_kernel, taps, padded), name='pack_f...  1.79 us
  transfers between devices with their start and end apart: 28, of which 11 were waited for; matrix products, arithmetic and copies ran while one was open for 0% of the time, Pallas kernels for 38%

profile of v7, /device:TPU:0, one launch (start us, length us, event | category | flops | bytes accessed | tf_op | source)
XLA Modules:
  0.0 73.8 jit_solution(18184105592637385948)
XLA Ops:
  1.1 1.8 %prep.1 = (bf16[288,384]{1,0:T(8,128)(2,1)S(1)}, bf16[288,384]{1,0:T(8,128)(2,1)S(1)}, bf16[288,384]{1,0:T(8,128)(2,1)S(1)}, bf16[288,384]{1,0:T(8,128)(2,1)S(1)}) custom-call(bf16[256,1408]{1,0:T(8,128)(2,1)} %bitcast.14, bf16[8,64,128]{2,1,0:T(8,128)(2,1)} %bitcast.10), custom_call_target="tpu_custom_call" | custom-call | tf_op jit(solution)/shard_map/prep/pallas_call | solution.py:138
  3.0 3.5 %collective-permute-start = (bf16[288,384]{1,0:T(8,128)(2,1)S(1)}, bf16[288,384]{1,0:T(8,128)(2,1)S(1)}, u32[]{:S(2)}, u32[]{:S(2)}) collective-permute-start(bf16[288,384]{1,0:T(8,128)(2,1)S(1)} %get-tuple-element.25), channel_id=1, source_target_pairs={{0,6},{1,7},{2,4},{3,5},{4,2},{5,3},{6,0},{7,1},{8,14},{9,15},{10,... | collective-permute-start | bytes 663560 | tf_op jit(solution)/shard_map/ppermute | solution.py:753
  7.2 1.8 %pack_filter.1.rest_1_.weight_ref = bf16[1920,1536]{1,0:T(8,128)(2,1)S(1)} custom-call(bf16[880,1536]{1,0:T(8,128)(2,1)} %bitcast.21, bf16[880,1536]{1,0:T(8,128)(2,1)S(1)} %collective-permute-done.3.peer_hbm), custom_call_target="tpu_custom_call" | custom-call | tf_op jit(solution)/shard_map/pack_filter/pallas_call | solution.py:261
  9.1 3.8 %collective-permute-done.refs_0_ = bf16[288,384]{1,0:T(8,128)(2,1)S(1)} collective-permute-done((bf16[288,384]{1,0:T(8,128)(2,1)S(1)}, bf16[288,384]{1,0:T(8,128)(2,1)S(1)}, u32[]{:S(2)}, u32[]{:S(2)}) %collective-permute-start) | collective-permute-done | bytes 221216 | tf_op jit(solution)/shard_map/ppermute | solution.py:753
  12.8 1.5 %activate.4.edge_ref.rest_0_ = bf16[256,384]{1,0:T(8,128)(2,1)S(1)} custom-call(bf16[288,384]{1,0:T(8,128)(2,1)S(1)} %collective-permute-done.refs_0_), custom_call_target="tpu_custom_call" | custom-call | tf_op jit(solution)/shard_map/activate/pallas_call | solution.py:216
  15.4 2.0 %collective-permute-done.1.refs_1_.refs_0_ = bf16[288,384]{1,0:T(8,128)(2,1)S(1)} collective-permute-done((bf16[288,384]{1,0:T(8,128)(2,1)S(1)}, bf16[288,384]{1,0:T(8,128)(2,1)S(1)}, u32[]{:S(2)}, u32[]{:S(2)}) %collective-permute-start.1) | collective-permute-done | bytes 221216 | tf_op jit(solution)/shard_map/ppermute | solution.py:753
  17.6 1.5 %collective-permute-start.10 = (bf16[256,768]{1,0:T(8,128)(2,1)S(1)}, bf16[256,768]{1,0:T(8,128)(2,1)S(1)}, u32[]{:S(2)}, u32[]{:S(2)}) collective-permute-start(bf16[256,768]{1,0:T(8,128)(2,1)S(1)} %conv.5.refs_4_.refs_2_), channel_id=1, source_target_pairs={{0,2},{1,5},{2,0},{3,7},{4,6},{5,1},{6,4},{7,3},{8,10},{9,13},{10,... | collective-permute-start | bytes 1179656 | tf_op jit(solution)/shard_map/ppermute | solution.py:753
  21.7 1.5 %activate.5.rest_0_ = bf16[256,384]{1,0:T(8,128)(2,1)S(1)} custom-call(bf16[288,384]{1,0:T(8,128)(2,1)S(1)} %collective-permute-done.2.refs_2_.refs_0_.refs_1_, bf16[288,384]{1,0:T(8,128)(2,1)S(1)} %collective-permute-done.1.refs_1_.refs_0_, bf16[256,768]{1,0:T(8,128)(2,1)S(1)} %conv.5.refs_4_.refs_2_, bf16[256,768]{1,0:T(8,128)(2,1)S(1)} %conv.6.refs_5_.refs_3_), custom_call_target="tpu_custom_call" | custom-call | tf_op jit(solution)/shard_map/activate/pallas_call | solution.py:216
  23.3 1.8 %conv.7 = (bf16[256,768]{1,0:T(8,128)(2,1)S(1)}, bf16[256,768]{1,0:T(8,128)(2,1)S(1)}) custom-call(bf16[256,1408]{1,0:T(8,128)(2,1)} %bitcast.17, f32[4,8,384]{2,1,0:T(8,128)S(1)} %collective-permute-done.5.edge_ref, bf16[256,384]{1,0:T(8,128)(2,1)S(1)} %activate.5.rest_0_, bf16[1920,1536]{1,0:T(8,128)(2,1)S(1)} %pack_filter.1.rest_1_.weight_ref, ...), custom_call_target="tpu_custom_call" | custom-call | tf_op jit(solution)/shard_map/conv/pallas_call | solution.py:395
  25.1 1.6 %collective-permute-start.8 = (bf16[256,768]{1,0:T(8,128)(2,1)S(1)}, bf16[256,768]{1,0:T(8,128)(2,1)S(1)}, u32[]{:S(2)}, u32[]{:S(2)}) collective-permute-start(bf16[256,768]{1,0:T(8,128)(2,1)S(1)} %get-tuple-element.33.rest_0_), channel_id=1, source_target_pairs={{0,2},{1,5},{2,0},{3,7},{4,6},{5,1},{6,4},{7,3},{8,10},{9,13},{10,... | collective-permute-start | bytes 1179656 | tf_op jit(solution)/shard_map/ppermute | solution.py:753
  28.1 1.7 %activate.7.rest_0_ = bf16[256,384]{1,0:T(8,128)(2,1)S(1)} custom-call(bf16[288,384]{1,0:T(8,128)(2,1)S(1)} %collective-permute-done.1.refs_1_.refs_0_, bf16[288,384]{1,0:T(8,128)(2,1)S(1)} %collective-permute-done.2.refs_2_.refs_0_.refs_1_, bf16[16,384]{1,0:T(8,128)(2,1)S(1)} %edge_terms.1.refs_1_.refs_2_), custom_call_target="tpu_custom_call" | custom-call | tf_op jit(solution)/shard_map/activate/pallas_call | solution.py:216
  29.8 1.8 %conv.9 = (f32[256,768]{1,0:T(8,128)S(1)}, f32[256,768]{1,0:T(8,128)S(1)}) custom-call(bf16[256,1408]{1,0:T(8,128)(2,1)} %bitcast.18, f32[4,8,384]{2,1,0:T(8,128)S(1)} %collective-permute-done.5.edge_ref, bf16[256,384]{1,0:T(8,128)(2,1)S(1)} %activate.7.rest_0_, bf16[1920,1536]{1,0:T(8,128)(2,1)S(1)} %pack_filter.1.rest_1_.weight_ref, ...), custom_call_target="tpu_custom_call" | custom-call | tf_op jit(solution)/shard_map/conv/pallas_call | solution.py:395
  33.9 1.5 %collective-permute-start.7 = (bf16[16,384]{1,0:T(8,128)(2,1)S(1)}, bf16[16,384]{1,0:T(8,128)(2,1)S(1)}, u32[]{:S(2)}, u32[]{:S(2)}) collective-permute-start(bf16[16,384]{1,0:T(8,128)(2,1)S(1)} %edge_terms.1.refs_1_.refs_2_), channel_id=1, source_target_pairs={{0,6},{1,7},{2,4},{3,5},{4,2},{5,3},{6,0},{7,1},{8,14},{9,15},{10,... | collective-permute-start | bytes 36872 | tf_op jit(solution)/shard_map/ppermute | solution.py:753
  35.5 1.5 %activate.6.rest_0_ = bf16[256,384]{1,0:T(8,128)(2,1)S(1)} custom-call(bf16[288,384]{1,0:T(8,128)(2,1)S(1)} %get-tuple-element.28.refs_3_.refs_0_, bf16[16,384]{1,0:T(8,128)(2,1)S(1)} %edge_terms.1.refs_1_.refs_2_), custom_call_target="tpu_custom_call" | custom-call | tf_op jit(solution)/shard_map/activate/pallas_call | solution.py:216
  37.0 3.2 %conv.8 = (f32[256,768]{1,0:T(8,128)S(1)}, f32[256,768]{1,0:T(8,128)S(1)}) custom-call(bf16[256,1408]{1,0:T(8,128)(2,1)} %bitcast.19, f32[4,8,384]{2,1,0:T(8,128)S(1)} %collective-permute-done.5.edge_ref, bf16[256,384]{1,0:T(8,128)(2,1)S(1)} %activate.6.rest_0_, bf16[1920,1536]{1,0:T(8,128)(2,1)S(1)} %pack_filter.1.rest_1_.weight_ref, ...), custom_call_target="tpu_custom_call" | custom-call | tf_op jit(solution)/shard_map/conv/pallas_call | solution.py:395
  40.3 3.1 %collective-permute-done.7.term_ref = bf16[16,384]{1,0:T(8,128)(2,1)S(1)} collective-permute-done((bf16[16,384]{1,0:T(8,128)(2,1)S(1)}, bf16[16,384]{1,0:T(8,128)(2,1)S(1)}, u32[]{:S(2)}, u32[]{:S(2)}) %collective-permute-start.7) | collective-permute-done | bytes 12320 | tf_op jit(solution)/shard_map/ppermute | solution.py:753
  43.4 2.0 %collective-permute-done.13.rest_5_ = bf16[256,768]{1,0:T(8,128)(2,1)S(1)} collective-permute-done((bf16[256,768]{1,0:T(8,128)(2,1)S(1)}, bf16[256,768]{1,0:T(8,128)(2,1)S(1)}, u32[]{:S(2)}, u32[]{:S(2)}) %collective-permute-start.13) | collective-permute-done | bytes 393248 | tf_op jit(solution)/shard_map/ppermute | solution.py:753
  45.9 2.1 %collective-permute-start.14 = (f32[8,256]{1,0:T(8,128)S(1)}, f32[8,256]{1,0:T(8,128)S(1)}, u32[]{:S(2)}, u32[]{:S(2)}) collective-permute-start(f32[8,256]{1,0:T(8,128)S(1)} %get-tuple-element.40.mine_ref), channel_id=1, source_target_pairs={{0,1},{1,0},{2,3},{3,2},{4,5},{5,4},{6,7},{7,6},{8,9},{9,8},{10,11... | collective-permute-start | bytes 24584 | tf_op jit(solution)/shard_map/ppermute | solution.py:753
  52.5 2.1 %collective-permute-done.15.rest_1_ = bf16[128,384]{1,0:T(8,128)(2,1)S(1)} collective-permute-done((bf16[128,384]{1,0:T(8,128)(2,1)S(1)}, bf16[128,384]{1,0:T(8,128)(2,1)S(1)}, u32[]{:S(2)}, u32[]{:S(2)}) %collective-permute-start.15) | collective-permute-done | bytes 98336 | tf_op jit(solution)/shard_map/ppermute | solution.py:753
  57.9 1.8 %collective-permute-start.22 = (bf16[128,128]{1,0:T(8,128)(2,1)S(1)}, bf16[128,128]{1,0:T(8,128)(2,1)S(1)}, u32[]{:S(2)}, u32[]{:S(2)}) collective-permute-start(bf16[128,128]{1,0:T(8,128)(2,1)S(1)} %get-tuple-element.42.refs_0_), channel_id=1, source_target_pairs={{0,2},{1,3},{2,0},{3,1},{4,6},{5,7},{6,4},{7,5},{8,10},{9,11},{10,... | collective-permute-start | bytes 98312 | tf_op jit(solution)/shard_map/ppermute | solution.py:753
  59.8 1.5 %collective-permute-start.24 = (bf16[128,128]{1,0:T(8,128)(2,1)S(1)}, bf16[128,128]{1,0:T(8,128)(2,1)S(1)}, u32[]{:S(2)}, u32[]{:S(2)}) collective-permute-start(bf16[128,128]{1,0:T(8,128)(2,1)S(1)} %get-tuple-element.42.refs_0_), channel_id=1, source_target_pairs={{0,6},{1,7},{2,4},{3,5},{4,2},{5,3},{6,0},{7,1},{8,14},{9,15},{10,... | collective-permute-start | bytes 98312 | tf_op jit(solution)/shard_map/ppermute | solution.py:753
  61.4 2.8 %attend.2 = (f32[128,1536]{1,0:T(8,128)S(1)}, f32[8,128]{1,0:T(8,128)S(1)}) custom-call(f32[8]{0:T(128)S(1)} %copy-done.7, bf16[128,1536]{1,0:T(8,128)(2,1)S(1)} %get-tuple-element.39.encoded_ref.start_ref, f32[1536]{0:T(1024)S(1)} %copy-done.5, bf16[1536,1024]{1,0:T(8,128)(2,1)S(1)} %copy-done, ...), custom_call_target="tpu_custom_call" | custom-call | tf_op jit(solution)/shard_map/attend/pallas_call | solution.py:602
  64.7 3.7 %collective-permute-start.25 = (bf16[128,128]{1,0:T(8,128)(2,1)S(1)}, bf16[128,128]{1,0:T(8,128)(2,1)S(1)}, u32[]{:S(2)}, u32[]{:S(2)}) collective-permute-start(bf16[128,128]{1,0:T(8,128)(2,1)S(1)} %add_up.6.rest_8_.refs_3_), channel_id=1, source_target_pairs={{0,24},{8,16},{16,8},{24,0},{1,25},{9,17},{17,9},{25,1},{2,26},{10... | collective-permute-start | bytes 98312 | tf_op jit(solution)/shard_map/ppermute | solution.py:846
  69.1 3.6 %attend.3 = (bf16[128,1536]{1,0:T(8,128)(2,1)}, f32[8,128]{1,0:T(8,128)S(1)}) custom-call(f32[8]{0:T(128)S(1)} %copy-done.7, bf16[128,1536]{1,0:T(8,128)(2,1)S(1)} %get-tuple-element.39.encoded_ref.start_ref, f32[1536]{0:T(1024)S(1)} %copy-done.5, bf16[1536,1024]{1,0:T(8,128)(2,1)S(1)} %copy-done, f32[128,1536]{1,0:T(8,128)S(1)} %get-tuple-element.41.start_ref, ...), custom_call_target="tpu_custom_call" | custom-call | tf_op jit(solution)/shard_map/attend/pallas_call | solution.py:602
  (77 shorter events, 19.5 us)
Async XLA Ops:
  0.6 6.5 %collective-permute-start.3 = (bf16[880,1536]{1,0:T(8,128)(2,1)}, bf16[880,1536]{1,0:T(8,128)(2,1)S(1)}, u32[]{:S(2)}, u32[]{:S(2)}) collective-permute-start(bf16[880,1536]{1,0:T(8,128)(2,1)} %bitcast.20), channel_id=1, source_target_pairs={{0,1},{1,0},{2,3},{3,2},{4,5},{5,4},{6,7},{7,6},{8,9},{9,8},{10,11... | collective-permute-start | bytes 8110088 | tf_op jit(solution)/shard_map/ppermute | solution.py:753
  3.0 9.9 %collective-permute-start = (bf16[288,384]{1,0:T(8,128)(2,1)S(1)}, bf16[288,384]{1,0:T(8,128)(2,1)S(1)}, u32[]{:S(2)}, u32[]{:S(2)}) collective-permute-start(bf16[288,384]{1,0:T(8,128)(2,1)S(1)} %get-tuple-element.25), channel_id=1, source_target_pairs={{0,6},{1,7},{2,4},{3,5},{4,2},{5,3},{6,0},{7,1},{8,14},{9,15},{10,... | collective-permute-start | bytes 663560 | tf_op jit(solution)/shard_map/ppermute | solution.py:753
  6.5 10.8 %collective-permute-start.1 = (bf16[288,384]{1,0:T(8,128)(2,1)S(1)}, bf16[288,384]{1,0:T(8,128)(2,1)S(1)}, u32[]{:S(2)}, u32[]{:S(2)}) collective-permute-start(bf16[288,384]{1,0:T(8,128)(2,1)S(1)} %get-tuple-element.26), channel_id=1, source_target_pairs={{0,4},{1,5},{2,6},{3,7},{4,0},{5,1},{6,2},{7,3},{8,12},{9,13},{10,... | collective-permute-start | bytes 663560 | tf_op jit(solution)/shard_map/ppermute | solution.py:753
  7.0 10.6 %collective-permute-start.2 = (bf16[288,384]{1,0:T(8,128)(2,1)S(1)}, bf16[288,384]{1,0:T(8,128)(2,1)S(1)}, u32[]{:S(2)}, u32[]{:S(2)}) collective-permute-start(bf16[288,384]{1,0:T(8,128)(2,1)S(1)} %get-tuple-element.27), channel_id=1, source_target_pairs={{0,2},{1,3},{2,0},{3,1},{4,6},{5,7},{6,4},{7,5},{8,10},{9,11},{10,... | collective-permute-start | bytes 663560 | tf_op jit(solution)/shard_map/ppermute | solution.py:753
  9.0 10.2 %collective-permute-start.4 = (bf16[8,64,128]{2,1,0:T(8,128)(2,1)S(1)}, bf16[8,64,128]{2,1,0:T(8,128)(2,1)S(1)}, u32[]{:S(2)}, u32[]{:S(2)}) collective-permute-start(bf16[8,64,128]{2,1,0:T(8,128)(2,1)S(1)} %bitcast.12), channel_id=1, source_target_pairs={{0,1},{1,0},{2,3},{3,2},{4,5},{5,4},{6,7},{7,6},{8,9},{9,8},{10,11... | collective-permute-start | bytes 393224 | tf_op jit(solution)/shard_map/ppermute | solution.py:753
  17.6 14.0 %collective-permute-start.10 = (bf16[256,768]{1,0:T(8,128)(2,1)S(1)}, bf16[256,768]{1,0:T(8,128)(2,1)S(1)}, u32[]{:S(2)}, u32[]{:S(2)}) collective-permute-start(bf16[256,768]{1,0:T(8,128)(2,1)S(1)} %conv.5.refs_4_.refs_2_), channel_id=1, source_target_pairs={{0,2},{1,5},{2,0},{3,7},{4,6},{5,1},{6,4},{7,3},{8,10},{9,13},{10,... | collective-permute-start | bytes 1179656 | tf_op jit(solution)/shard_map/ppermute | solution.py:753
  20.2 13.0 %collective-permute-start.12 = (bf16[256,768]{1,0:T(8,128)(2,1)S(1)}, bf16[256,768]{1,0:T(8,128)(2,1)S(1)}, u32[]{:S(2)}, u32[]{:S(2)}) collective-permute-start(bf16[256,768]{1,0:T(8,128)(2,1)S(1)} %conv.6.refs_5_.refs_3_), channel_id=1, source_target_pairs={{0,2},{1,5},{2,0},{3,7},{4,6},{5,1},{6,4},{7,3},{8,10},{9,13},{10,... | collective-permute-start | bytes 1179656 | tf_op jit(solution)/shard_map/ppermute | solution.py:753
  25.1 18.3 %collective-permute-start.8 = (bf16[256,768]{1,0:T(8,128)(2,1)S(1)}, bf16[256,768]{1,0:T(8,128)(2,1)S(1)}, u32[]{:S(2)}, u32[]{:S(2)}) collective-permute-start(bf16[256,768]{1,0:T(8,128)(2,1)S(1)} %get-tuple-element.33.rest_0_), channel_id=1, source_target_pairs={{0,2},{1,5},{2,0},{3,7},{4,6},{5,1},{6,4},{7,3},{8,10},{9,13},{10,... | collective-permute-start | bytes 1179656 | tf_op jit(solution)/shard_map/ppermute | solution.py:753
  26.6 16.7 %collective-permute-start.9 = (bf16[256,768]{1,0:T(8,128)(2,1)S(1)}, bf16[256,768]{1,0:T(8,128)(2,1)S(1)}, u32[]{:S(2)}, u32[]{:S(2)}) collective-permute-start(bf16[256,768]{1,0:T(8,128)(2,1)S(1)} %get-tuple-element.34.rest_1_), channel_id=1, source_target_pairs={{0,2},{1,5},{2,0},{3,7},{4,6},{5,1},{6,4},{7,3},{8,10},{9,13},{10,... | collective-permute-start | bytes 1179656 | tf_op jit(solution)/shard_map/ppermute | solution.py:753
  31.7 11.7 %collective-permute-start.11 = (bf16[256,768]{1,0:T(8,128)(2,1)S(1)}, bf16[256,768]{1,0:T(8,128)(2,1)S(1)}, u32[]{:S(2)}, u32[]{:S(2)}) collective-permute-start(bf16[256,768]{1,0:T(8,128)(2,1)S(1)} %add_up.4), channel_id=1, source_target_pairs={{0,4},{1,3},{2,6},{3,1},{4,0},{5,7},{6,2},{7,5},{8,12},{9,11},{10,... | collective-permute-start | bytes 1179656 | tf_op jit(solution)/shard_map/ppermute | solution.py:753
  33.3 12.1 %collective-permute-start.13 = (bf16[256,768]{1,0:T(8,128)(2,1)S(1)}, bf16[256,768]{1,0:T(8,128)(2,1)S(1)}, u32[]{:S(2)}, u32[]{:S(2)}) collective-permute-start(bf16[256,768]{1,0:T(8,128)(2,1)S(1)} %add_up.5), channel_id=1, source_target_pairs={{0,4},{1,3},{2,6},{3,1},{4,0},{5,7},{6,2},{7,5},{8,12},{9,11},{10,... | collective-permute-start | bytes 1179656 | tf_op jit(solution)/shard_map/ppermute | solution.py:753
  33.9 9.4 %collective-permute-start.7 = (bf16[16,384]{1,0:T(8,128)(2,1)S(1)}, bf16[16,384]{1,0:T(8,128)(2,1)S(1)}, u32[]{:S(2)}, u32[]{:S(2)}) collective-permute-start(bf16[16,384]{1,0:T(8,128)(2,1)S(1)} %edge_terms.1.refs_1_.refs_2_), channel_id=1, source_target_pairs={{0,6},{1,7},{2,4},{3,5},{4,2},{5,3},{6,0},{7,1},{8,14},{9,15},{10,... | collective-permute-start | bytes 36872 | tf_op jit(solution)/shard_map/ppermute | solution.py:753
  49.0 5.6 %collective-permute-start.15 = (bf16[128,384]{1,0:T(8,128)(2,1)S(1)}, bf16[128,384]{1,0:T(8,128)(2,1)S(1)}, u32[]{:S(2)}, u32[]{:S(2)}) collective-permute-start(bf16[128,384]{1,0:T(8,128)(2,1)S(1)} %bundle.1.rest_0_), channel_id=1, source_target_pairs={{0,2},{1,3},{2,0},{3,1},{4,6},{5,7},{6,4},{7,5},{8,10},{9,11},{10,... | collective-permute-start | bytes 294920 | tf_op jit(solution)/shard_map/ppermute | solution.py:753
  49.7 5.8 %collective-permute-start.16 = (bf16[128,384]{1,0:T(8,128)(2,1)S(1)}, bf16[128,384]{1,0:T(8,128)(2,1)S(1)}, u32[]{:S(2)}, u32[]{:S(2)}) collective-permute-start(bf16[128,384]{1,0:T(8,128)(2,1)S(1)} %bundle.1.rest_0_), channel_id=1, source_target_pairs={{0,4},{1,5},{2,6},{3,7},{4,0},{5,1},{6,2},{7,3},{8,12},{9,13},{10,... | collective-permute-start | bytes 294920 | tf_op jit(solution)/shard_map/ppermute | solution.py:753
  51.1 5.5 %collective-permute-start.17 = (bf16[128,384]{1,0:T(8,128)(2,1)S(1)}, bf16[128,384]{1,0:T(8,128)(2,1)S(1)}, u32[]{:S(2)}, u32[]{:S(2)}) collective-permute-start(bf16[128,384]{1,0:T(8,128)(2,1)S(1)} %bundle.1.rest_0_), channel_id=1, source_target_pairs={{0,6},{1,7},{2,4},{3,5},{4,2},{5,3},{6,0},{7,1},{8,14},{9,15},{10,... | collective-permute-start | bytes 294920 | tf_op jit(solution)/shard_map/ppermute | solution.py:753
  52.5 7.2 %collective-permute-start.18 = (bf16[128,384]{1,0:T(8,128)(2,1)S(1)}, bf16[128,384]{1,0:T(8,128)(2,1)S(1)}, u32[]{:S(2)}, u32[]{:S(2)}) collective-permute-start(bf16[128,384]{1,0:T(8,128)(2,1)S(1)} %bundle.1.rest_0_), channel_id=1, source_target_pairs={{0,1},{1,0},{2,3},{3,2},{4,5},{5,4},{6,7},{7,6},{8,9},{9,8},{10,11... | collective-permute-start | bytes 294920 | tf_op jit(solution)/shard_map/ppermute | solution.py:753
  54.6 5.3 %collective-permute-start.19 = (bf16[128,384]{1,0:T(8,128)(2,1)S(1)}, bf16[128,384]{1,0:T(8,128)(2,1)S(1)}, u32[]{:S(2)}, u32[]{:S(2)}) collective-permute-start(bf16[128,384]{1,0:T(8,128)(2,1)S(1)} %collective-permute-done.15.rest_1_), channel_id=1, source_target_pairs={{0,1},{1,0},{2,3},{3,2},{4,5},{5,4},{6,7},{7,6},{8,9},{9,8},{10,11... | collective-permute-start | bytes 294920 | tf_op jit(solution)/shard_map/ppermute | solution.py:753
  55.5 5.9 %collective-permute-start.20 = (bf16[128,384]{1,0:T(8,128)(2,1)S(1)}, bf16[128,384]{1,0:T(8,128)(2,1)S(1)}, u32[]{:S(2)}, u32[]{:S(2)}) collective-permute-start(bf16[128,384]{1,0:T(8,128)(2,1)S(1)} %collective-permute-done.16.rest_2_), channel_id=1, source_target_pairs={{0,1},{1,0},{2,3},{3,2},{4,5},{5,4},{6,7},{7,6},{8,9},{9,8},{10,11... | collective-permute-start | bytes 294920 | tf_op jit(solution)/shard_map/ppermute | solution.py:753
  56.6 4.8 %collective-permute-start.21 = (bf16[128,384]{1,0:T(8,128)(2,1)S(1)}, bf16[128,384]{1,0:T(8,128)(2,1)S(1)}, u32[]{:S(2)}, u32[]{:S(2)}) collective-permute-start(bf16[128,384]{1,0:T(8,128)(2,1)S(1)} %collective-permute-done.17.rest_3_), channel_id=1, source_target_pairs={{0,1},{1,0},{2,3},{3,2},{4,5},{5,4},{6,7},{7,6},{8,9},{9,8},{10,11... | collective-permute-start | bytes 294920 | tf_op jit(solution)/shard_map/ppermute | solution.py:753
  57.9 6.4 %collective-permute-start.22 = (bf16[128,128]{1,0:T(8,128)(2,1)S(1)}, bf16[128,128]{1,0:T(8,128)(2,1)S(1)}, u32[]{:S(2)}, u32[]{:S(2)}) collective-permute-start(bf16[128,128]{1,0:T(8,128)(2,1)S(1)} %get-tuple-element.42.refs_0_), channel_id=1, source_target_pairs={{0,2},{1,3},{2,0},{3,1},{4,6},{5,7},{6,4},{7,5},{8,10},{9,11},{10,... | collective-permute-start | bytes 98312 | tf_op jit(solution)/shard_map/ppermute | solution.py:753
  59.8 4.8 %collective-permute-start.24 = (bf16[128,128]{1,0:T(8,128)(2,1)S(1)}, bf16[128,128]{1,0:T(8,128)(2,1)S(1)}, u32[]{:S(2)}, u32[]{:S(2)}) collective-permute-start(bf16[128,128]{1,0:T(8,128)(2,1)S(1)} %get-tuple-element.42.refs_0_), channel_id=1, source_target_pairs={{0,6},{1,7},{2,4},{3,5},{4,2},{5,3},{6,0},{7,1},{8,14},{9,15},{10,... | collective-permute-start | bytes 98312 | tf_op jit(solution)/shard_map/ppermute | solution.py:753
  64.7 8.0 %collective-permute-start.25 = (bf16[128,128]{1,0:T(8,128)(2,1)S(1)}, bf16[128,128]{1,0:T(8,128)(2,1)S(1)}, u32[]{:S(2)}, u32[]{:S(2)}) collective-permute-start(bf16[128,128]{1,0:T(8,128)(2,1)S(1)} %add_up.6.rest_8_.refs_3_), channel_id=1, source_target_pairs={{0,24},{8,16},{16,8},{24,0},{1,25},{9,17},{17,9},{25,1},{2,26},{10... | collective-permute-start | bytes 98312 | tf_op jit(solution)/shard_map/ppermute | solution.py:846
  68.3 4.8 %collective-permute-start.26 = (bf16[128,128]{1,0:T(8,128)(2,1)S(1)}, bf16[128,128]{1,0:T(8,128)(2,1)S(1)}, u32[]{:S(2)}, u32[]{:S(2)}) collective-permute-start(bf16[128,128]{1,0:T(8,128)(2,1)S(1)} %add_up.6.rest_8_.refs_3_), channel_id=1, source_target_pairs={{0,16},{8,24},{16,0},{24,8},{1,17},{9,25},{17,1},{25,9},{2,18},{10... | collective-permute-start | bytes 98312 | tf_op jit(solution)/shard_map/ppermute | solution.py:846
  68.3 4.8 %collective-permute-start.27 = (bf16[128,128]{1,0:T(8,128)(2,1)S(1)}, bf16[128,128]{1,0:T(8,128)(2,1)S(1)}, u32[]{:S(2)}, u32[]{:S(2)}) collective-permute-start(bf16[128,128]{1,0:T(8,128)(2,1)S(1)} %add_up.6.rest_8_.refs_3_), channel_id=1, source_target_pairs={{0,8},{8,0},{16,24},{24,16},{1,9},{9,1},{17,25},{25,17},{2,10},{10... | collective-permute-start | bytes 98312 | tf_op jit(solution)/shard_map/ppermute | solution.py:846
  (14 other events, 153.0 us)

commit v8 on v7

--- a/solution.py
+++ b/solution.py
@@ -840,7 +840,8 @@
 
     halfway = heads // 2
     first_half, done = attend_heads(encoded, 0, halfway, f32, [])
-    grad = add_up([grad] + [send(grad, k) for k in range(1, chips)], bf16, [done])
+    others = [send(grad, k) for k in range(chips - 1, 0, -1)][::-1]
+    grad = add_up([grad] + others, bf16, [done], backwards=True)
     block_out, done = attend_heads(first_half, halfway, heads, bf16, [grad])
     planes = [
         lax.ppermute(grad, "dp", [(w, w ^ k) for w in range(windows)])

time: 74 us -> 74.4 us (level)
  no operation moved by 1% of the time
where the time goes in v8:
time: 74.4 us; the launch traced here: 74.2 us
  Pallas kernels  29.6 us (40%)
  starting transfers between devices  26.8 us (36%)
  waiting for transfers between devices  16.8 us (23%)
  between operations  0.95 us (1%)
    ppermute x25, starting transfers between devices, send(): return lax.ppermute(value, GROUP, hop_pairs(chips, cores, flip))  22.4 us
    ppermute x25, waiting for transfers between devices, send(): return lax.ppermute(value, GROUP, hop_pairs(chips, cores, flip))  16.4 us
    pallas_call x5, Pallas kernels, conv(): pl.pallas_call(functools.partial(conv_kernel, chips, bits, taps, 256, wan...  8.88 us
    pallas_call x2, Pallas kernels, attend(): pl.pallas_call(functools.partial(attend_kernel, len(parts), heads, first,...  6.43 us
    pallas_call x4, Pallas kernels, activate(): pl.pallas_call(functools.partial(activate_kernel, width, len(messages)),...  6.25 us
    ppermute x3, starting transfers between devices, per_device(): lax.ppermute(grad, 'dp', [(w, w ^ k) for w in range(windows)])  4.45 us
    pallas_call x1, Pallas kernels, prep(): pl.pallas_call(functools.partial(prep_kernel, chips, width), name='prep',...  1.84 us
    pallas_call x1, Pallas kernels, pack_filter(): pl.pallas_call(functools.partial(pack_kernel, taps, padded), name='pack_f...  1.79 us
  transfers between devices with their start and end apart: 28, of which 11 were waited for; matrix products, arithmetic and copies ran while one was open for 0% of the time, Pallas kernels for 38%

profile of v8, /device:TPU:0, one launch (start us, length us, event | category | flops | bytes accessed | tf_op | source)
XLA Modules:
  0.0 74.2 jit_solution(9559605280474819315)
XLA Ops:
  1.1 1.8 %prep.1 = (bf16[288,384]{1,0:T(8,128)(2,1)S(1)}, bf16[288,384]{1,0:T(8,128)(2,1)S(1)}, bf16[288,384]{1,0:T(8,128)(2,1)S(1)}, bf16[288,384]{1,0:T(8,128)(2,1)S(1)}) custom-call(bf16[256,1408]{1,0:T(8,128)(2,1)} %bitcast.14, bf16[8,64,128]{2,1,0:T(8,128)(2,1)} %bitcast.10), custom_call_target="tpu_custom_call" | custom-call | tf_op jit(solution)/shard_map/prep/pallas_call | solution.py:138
  3.0 3.5 %collective-permute-start = (bf16[288,384]{1,0:T(8,128)(2,1)S(1)}, bf16[288,384]{1,0:T(8,128)(2,1)S(1)}, u32[]{:S(2)}, u32[]{:S(2)}) collective-permute-start(bf16[288,384]{1,0:T(8,128)(2,1)S(1)} %get-tuple-element.25), channel_id=1, source_target_pairs={{0,6},{1,7},{2,4},{3,5},{4,2},{5,3},{6,0},{7,1},{8,14},{9,15},{10,... | collective-permute-start | bytes 663560 | tf_op jit(solution)/shard_map/ppermute | solution.py:753
  7.2 1.8 %pack_filter.1.rest_1_.weight_ref = bf16[1920,1536]{1,0:T(8,128)(2,1)S(1)} custom-call(bf16[880,1536]{1,0:T(8,128)(2,1)} %bitcast.21, bf16[880,1536]{1,0:T(8,128)(2,1)S(1)} %collective-permute-done.3.peer_hbm), custom_call_target="tpu_custom_call" | custom-call | tf_op jit(solution)/shard_map/pack_filter/pallas_call | solution.py:261
  9.1 3.8 %collective-permute-done.refs_0_ = bf16[288,384]{1,0:T(8,128)(2,1)S(1)} collective-permute-done((bf16[288,384]{1,0:T(8,128)(2,1)S(1)}, bf16[288,384]{1,0:T(8,128)(2,1)S(1)}, u32[]{:S(2)}, u32[]{:S(2)}) %collective-permute-start) | collective-permute-done | bytes 221216 | tf_op jit(solution)/shard_map/ppermute | solution.py:753
  12.8 1.5 %activate.4.edge_ref.rest_0_ = bf16[256,384]{1,0:T(8,128)(2,1)S(1)} custom-call(bf16[288,384]{1,0:T(8,128)(2,1)S(1)} %collective-permute-done.refs_0_), custom_call_target="tpu_custom_call" | custom-call | tf_op jit(solution)/shard_map/activate/pallas_call | solution.py:216
  15.4 2.0 %collective-permute-done.1.refs_1_.refs_0_ = bf16[288,384]{1,0:T(8,128)(2,1)S(1)} collective-permute-done((bf16[288,384]{1,0:T(8,128)(2,1)S(1)}, bf16[288,384]{1,0:T(8,128)(2,1)S(1)}, u32[]{:S(2)}, u32[]{:S(2)}) %collective-permute-start.1) | collective-permute-done | bytes 221216 | tf_op jit(solution)/shard_map/ppermute | solution.py:753
  17.6 1.5 %collective-permute-start.10 = (bf16[256,768]{1,0:T(8,128)(2,1)S(1)}, bf16[256,768]{1,0:T(8,128)(2,1)S(1)}, u32[]{:S(2)}, u32[]{:S(2)}) collective-permute-start(bf16[256,768]{1,0:T(8,128)(2,1)S(1)} %conv.5.refs_4_.refs_2_), channel_id=1, source_target_pairs={{0,2},{1,5},{2,0},{3,7},{4,6},{5,1},{6,4},{7,3},{8,10},{9,13},{10,... | collective-permute-start | bytes 1179656 | tf_op jit(solution)/shard_map/ppermute | solution.py:753
  21.7 1.5 %activate.5.rest_0_ = bf16[256,384]{1,0:T(8,128)(2,1)S(1)} custom-call(bf16[288,384]{1,0:T(8,128)(2,1)S(1)} %collective-permute-done.2.refs_2_.refs_0_.refs_1_, bf16[288,384]{1,0:T(8,128)(2,1)S(1)} %collective-permute-done.1.refs_1_.refs_0_, bf16[256,768]{1,0:T(8,128)(2,1)S(1)} %conv.5.refs_4_.refs_2_, bf16[256,768]{1,0:T(8,128)(2,1)S(1)} %conv.6.refs_5_.refs_3_), custom_call_target="tpu_custom_call" | custom-call | tf_op jit(solution)/shard_map/activate/pallas_call | solution.py:216
  23.3 1.8 %conv.7 = (bf16[256,768]{1,0:T(8,128)(2,1)S(1)}, bf16[256,768]{1,0:T(8,128)(2,1)S(1)}) custom-call(bf16[256,1408]{1,0:T(8,128)(2,1)} %bitcast.17, f32[4,8,384]{2,1,0:T(8,128)S(1)} %collective-permute-done.5.edge_ref, bf16[256,384]{1,0:T(8,128)(2,1)S(1)} %activate.5.rest_0_, bf16[1920,1536]{1,0:T(8,128)(2,1)S(1)} %pack_filter.1.rest_1_.weight_ref, ...), custom_call_target="tpu_custom_call" | custom-call | tf_op jit(solution)/shard_map/conv/pallas_call | solution.py:395
  25.1 1.6 %collective-permute-start.8 = (bf16[256,768]{1,0:T(8,128)(2,1)S(1)}, bf16[256,768]{1,0:T(8,128)(2,1)S(1)}, u32[]{:S(2)}, u32[]{:S(2)}) collective-permute-start(bf16[256,768]{1,0:T(8,128)(2,1)S(1)} %get-tuple-element.33.rest_0_), channel_id=1, source_target_pairs={{0,2},{1,5},{2,0},{3,7},{4,6},{5,1},{6,4},{7,3},{8,10},{9,13},{10,... | collective-permute-start | bytes 1179656 | tf_op jit(solution)/shard_map/ppermute | solution.py:753
  28.1 1.7 %activate.7.rest_0_ = bf16[256,384]{1,0:T(8,128)(2,1)S(1)} custom-call(bf16[288,384]{1,0:T(8,128)(2,1)S(1)} %collective-permute-done.1.refs_1_.refs_0_, bf16[288,384]{1,0:T(8,128)(2,1)S(1)} %collective-permute-done.2.refs_2_.refs_0_.refs_1_, bf16[16,384]{1,0:T(8,128)(2,1)S(1)} %edge_terms.1.refs_1_.refs_2_), custom_call_target="tpu_custom_call" | custom-call | tf_op jit(solution)/shard_map/activate/pallas_call | solution.py:216
  29.8 1.8 %conv.9 = (f32[256,768]{1,0:T(8,128)S(1)}, f32[256,768]{1,0:T(8,128)S(1)}) custom-call(bf16[256,1408]{1,0:T(8,128)(2,1)} %bitcast.18, f32[4,8,384]{2,1,0:T(8,128)S(1)} %collective-permute-done.5.edge_ref, bf16[256,384]{1,0:T(8,128)(2,1)S(1)} %activate.7.rest_0_, bf16[1920,1536]{1,0:T(8,128)(2,1)S(1)} %pack_filter.1.rest_1_.weight_ref, ...), custom_call_target="tpu_custom_call" | custom-call | tf_op jit(solution)/shard_map/conv/pallas_call | solution.py:395
  31.7 1.5 %collective-permute-start.11 = (bf16[256,768]{1,0:T(8,128)(2,1)S(1)}, bf16[256,768]{1,0:T(8,128)(2,1)S(1)}, u32[]{:S(2)}, u32[]{:S(2)}) collective-permute-start(bf16[256,768]{1,0:T(8,128)(2,1)S(1)} %add_up.4), channel_id=1, source_target_pairs={{0,4},{1,3},{2,6},{3,1},{4,0},{5,7},{6,2},{7,5},{8,12},{9,11},{10,... | collective-permute-start | bytes 1179656 | tf_op jit(solution)/shard_map/ppermute | solution.py:753
  33.9 1.5 %collective-permute-start.7 = (bf16[16,384]{1,0:T(8,128)(2,1)S(1)}, bf16[16,384]{1,0:T(8,128)(2,1)S(1)}, u32[]{:S(2)}, u32[]{:S(2)}) collective-permute-start(bf16[16,384]{1,0:T(8,128)(2,1)S(1)} %edge_terms.1.refs_1_.refs_2_), channel_id=1, source_target_pairs={{0,6},{1,7},{2,4},{3,5},{4,2},{5,3},{6,0},{7,1},{8,14},{9,15},{10,... | collective-permute-start | bytes 36872 | tf_op jit(solution)/shard_map/ppermute | solution.py:753
  35.5 1.5 %activate.6.rest_0_ = bf16[256,384]{1,0:T(8,128)(2,1)S(1)} custom-call(bf16[288,384]{1,0:T(8,128)(2,1)S(1)} %get-tuple-element.28.refs_3_.refs_0_, bf16[16,384]{1,0:T(8,128)(2,1)S(1)} %edge_terms.1.refs_1_.refs_2_), custom_call_target="tpu_custom_call" | custom-call | tf_op jit(solution)/shard_map/activate/pallas_call | solution.py:216
  37.0 3.2 %conv.8 = (f32[256,768]{1,0:T(8,128)S(1)}, f32[256,768]{1,0:T(8,128)S(1)}) custom-call(bf16[256,1408]{1,0:T(8,128)(2,1)} %bitcast.19, f32[4,8,384]{2,1,0:T(8,128)S(1)} %collective-permute-done.5.edge_ref, bf16[256,384]{1,0:T(8,128)(2,1)S(1)} %activate.6.rest_0_, bf16[1920,1536]{1,0:T(8,128)(2,1)S(1)} %pack_filter.1.rest_1_.weight_ref, ...), custom_call_target="tpu_custom_call" | custom-call | tf_op jit(solution)/shard_map/conv/pallas_call | solution.py:395
  40.3 3.1 %collective-permute-done.7.term_ref = bf16[16,384]{1,0:T(8,128)(2,1)S(1)} collective-permute-done((bf16[16,384]{1,0:T(8,128)(2,1)S(1)}, bf16[16,384]{1,0:T(8,128)(2,1)S(1)}, u32[]{:S(2)}, u32[]{:S(2)}) %collective-permute-start.7) | collective-permute-done | bytes 12320 | tf_op jit(solution)/shard_map/ppermute | solution.py:753
  43.4 2.0 %collective-permute-done.13.rest_5_ = bf16[256,768]{1,0:T(8,128)(2,1)S(1)} collective-permute-done((bf16[256,768]{1,0:T(8,128)(2,1)S(1)}, bf16[256,768]{1,0:T(8,128)(2,1)S(1)}, u32[]{:S(2)}, u32[]{:S(2)}) %collective-permute-start.13) | collective-permute-done | bytes 393248 | tf_op jit(solution)/shard_map/ppermute | solution.py:753
  45.9 2.1 %collective-permute-start.14 = (f32[8,256]{1,0:T(8,128)S(1)}, f32[8,256]{1,0:T(8,128)S(1)}, u32[]{:S(2)}, u32[]{:S(2)}) collective-permute-start(f32[8,256]{1,0:T(8,128)S(1)} %get-tuple-element.40.mine_ref), channel_id=1, source_target_pairs={{0,1},{1,0},{2,3},{3,2},{4,5},{5,4},{6,7},{7,6},{8,9},{9,8},{10,11... | collective-permute-start | bytes 24584 | tf_op jit(solution)/shard_map/ppermute | solution.py:753
  52.5 2.1 %collective-permute-done.15.rest_1_ = bf16[128,384]{1,0:T(8,128)(2,1)S(1)} collective-permute-done((bf16[128,384]{1,0:T(8,128)(2,1)S(1)}, bf16[128,384]{1,0:T(8,128)(2,1)S(1)}, u32[]{:S(2)}, u32[]{:S(2)}) %collective-permute-start.15) | collective-permute-done | bytes 98336 | tf_op jit(solution)/shard_map/ppermute | solution.py:753
  59.3 1.9 %collective-permute-start.23 = (bf16[128,128]{1,0:T(8,128)(2,1)S(1)}, bf16[128,128]{1,0:T(8,128)(2,1)S(1)}, u32[]{:S(2)}, u32[]{:S(2)}) collective-permute-start(bf16[128,128]{1,0:T(8,128)(2,1)S(1)} %get-tuple-element.42.refs_3_), channel_id=1, source_target_pairs={{0,4},{1,5},{2,6},{3,7},{4,0},{5,1},{6,2},{7,3},{8,12},{9,13},{10,... | collective-permute-start | bytes 98312 | tf_op jit(solution)/shard_map/ppermute | solution.py:753
  61.4 2.8 %attend.2 = (f32[128,1536]{1,0:T(8,128)S(1)}, f32[8,128]{1,0:T(8,128)S(1)}) custom-call(f32[8]{0:T(128)S(1)} %copy-done.7, bf16[128,1536]{1,0:T(8,128)(2,1)S(1)} %get-tuple-element.39.encoded_ref.start_ref, f32[1536]{0:T(1024)S(1)} %copy-done.5, bf16[1536,1024]{1,0:T(8,128)(2,1)S(1)} %copy-done, ...), custom_call_target="tpu_custom_call" | custom-call | tf_op jit(solution)/shard_map/attend/pallas_call | solution.py:602
  65.1 3.7 %collective-permute-start.25 = (bf16[128,128]{1,0:T(8,128)(2,1)S(1)}, bf16[128,128]{1,0:T(8,128)(2,1)S(1)}, u32[]{:S(2)}, u32[]{:S(2)}) collective-permute-start(bf16[128,128]{1,0:T(8,128)(2,1)S(1)} %add_up.6.rest_8_.refs_3_), channel_id=1, source_target_pairs={{0,24},{8,16},{16,8},{24,0},{1,25},{9,17},{17,9},{25,1},{2,26},{10... | collective-permute-start | bytes 98312 | tf_op jit(solution)/shard_map/ppermute | solution.py:847
  69.5 3.6 %attend.3 = (bf16[128,1536]{1,0:T(8,128)(2,1)}, f32[8,128]{1,0:T(8,128)S(1)}) custom-call(f32[8]{0:T(128)S(1)} %copy-done.7, bf16[128,1536]{1,0:T(8,128)(2,1)S(1)} %get-tuple-element.39.encoded_ref.start_ref, f32[1536]{0:T(1024)S(1)} %copy-done.5, bf16[1536,1024]{1,0:T(8,128)(2,1)S(1)} %copy-done, f32[128,1536]{1,0:T(8,128)S(1)} %get-tuple-element.41.start_ref, ...), custom_call_target="tpu_custom_call" | custom-call | tf_op jit(solution)/shard_map/attend/pallas_call | solution.py:602
  (77 shorter events, 19.9 us)
Async XLA Ops:
  0.6 6.5 %collective-permute-start.3 = (bf16[880,1536]{1,0:T(8,128)(2,1)}, bf16[880,1536]{1,0:T(8,128)(2,1)S(1)}, u32[]{:S(2)}, u32[]{:S(2)}) collective-permute-start(bf16[880,1536]{1,0:T(8,128)(2,1)} %bitcast.20), channel_id=1, source_target_pairs={{0,1},{1,0},{2,3},{3,2},{4,5},{5,4},{6,7},{7,6},{8,9},{9,8},{10,11... | collective-permute-start | bytes 8110088 | tf_op jit(solution)/shard_map/ppermute | solution.py:753
  3.0 9.9 %collective-permute-start = (bf16[288,384]{1,0:T(8,128)(2,1)S(1)}, bf16[288,384]{1,0:T(8,128)(2,1)S(1)}, u32[]{:S(2)}, u32[]{:S(2)}) collective-permute-start(bf16[288,384]{1,0:T(8,128)(2,1)S(1)} %get-tuple-element.25), channel_id=1, source_target_pairs={{0,6},{1,7},{2,4},{3,5},{4,2},{5,3},{6,0},{7,1},{8,14},{9,15},{10,... | collective-permute-start | bytes 663560 | tf_op jit(solution)/shard_map/ppermute | solution.py:753
  6.5 10.8 %collective-permute-start.1 = (bf16[288,384]{1,0:T(8,128)(2,1)S(1)}, bf16[288,384]{1,0:T(8,128)(2,1)S(1)}, u32[]{:S(2)}, u32[]{:S(2)}) collective-permute-start(bf16[288,384]{1,0:T(8,128)(2,1)S(1)} %get-tuple-element.26), channel_id=1, source_target_pairs={{0,4},{1,5},{2,6},{3,7},{4,0},{5,1},{6,2},{7,3},{8,12},{9,13},{10,... | collective-permute-start | bytes 663560 | tf_op jit(solution)/shard_map/ppermute | solution.py:753
  7.0 10.6 %collective-permute-start.2 = (bf16[288,384]{1,0:T(8,128)(2,1)S(1)}, bf16[288,384]{1,0:T(8,128)(2,1)S(1)}, u32[]{:S(2)}, u32[]{:S(2)}) collective-permute-start(bf16[288,384]{1,0:T(8,128)(2,1)S(1)} %get-tuple-element.27), channel_id=1, source_target_pairs={{0,2},{1,3},{2,0},{3,1},{4,6},{5,7},{6,4},{7,5},{8,10},{9,11},{10,... | collective-permute-start | bytes 663560 | tf_op jit(solution)/shard_map/ppermute | solution.py:753
  9.0 10.2 %collective-permute-start.4 = (bf16[8,64,128]{2,1,0:T(8,128)(2,1)S(1)}, bf16[8,64,128]{2,1,0:T(8,128)(2,1)S(1)}, u32[]{:S(2)}, u32[]{:S(2)}) collective-permute-start(bf16[8,64,128]{2,1,0:T(8,128)(2,1)S(1)} %bitcast.12), channel_id=1, source_target_pairs={{0,1},{1,0},{2,3},{3,2},{4,5},{5,4},{6,7},{7,6},{8,9},{9,8},{10,11... | collective-permute-start | bytes 393224 | tf_op jit(solution)/shard_map/ppermute | solution.py:753
  17.6 14.0 %collective-permute-start.10 = (bf16[256,768]{1,0:T(8,128)(2,1)S(1)}, bf16[256,768]{1,0:T(8,128)(2,1)S(1)}, u32[]{:S(2)}, u32[]{:S(2)}) collective-permute-start(bf16[256,768]{1,0:T(8,128)(2,1)S(1)} %conv.5.refs_4_.refs_2_), channel_id=1, source_target_pairs={{0,2},{1,5},{2,0},{3,7},{4,6},{5,1},{6,4},{7,3},{8,10},{9,13},{10,... | collective-permute-start | bytes 1179656 | tf_op jit(solution)/shard_map/ppermute | solution.py:753
  20.2 13.0 %collective-permute-start.12 = (bf16[256,768]{1,0:T(8,128)(2,1)S(1)}, bf16[256,768]{1,0:T(8,128)(2,1)S(1)}, u32[]{:S(2)}, u32[]{:S(2)}) collective-permute-start(bf16[256,768]{1,0:T(8,128)(2,1)S(1)} %conv.6.refs_5_.refs_3_), channel_id=1, source_target_pairs={{0,2},{1,5},{2,0},{3,7},{4,6},{5,1},{6,4},{7,3},{8,10},{9,13},{10,... | collective-permute-start | bytes 1179656 | tf_op jit(solution)/shard_map/ppermute | solution.py:753
  25.1 18.3 %collective-permute-start.8 = (bf16[256,768]{1,0:T(8,128)(2,1)S(1)}, bf16[256,768]{1,0:T(8,128)(2,1)S(1)}, u32[]{:S(2)}, u32[]{:S(2)}) collective-permute-start(bf16[256,768]{1,0:T(8,128)(2,1)S(1)} %get-tuple-element.33.rest_0_), channel_id=1, source_target_pairs={{0,2},{1,5},{2,0},{3,7},{4,6},{5,1},{6,4},{7,3},{8,10},{9,13},{10,... | collective-permute-start | bytes 1179656 | tf_op jit(solution)/shard_map/ppermute | solution.py:753
  26.6 16.7 %collective-permute-start.9 = (bf16[256,768]{1,0:T(8,128)(2,1)S(1)}, bf16[256,768]{1,0:T(8,128)(2,1)S(1)}, u32[]{:S(2)}, u32[]{:S(2)}) collective-permute-start(bf16[256,768]{1,0:T(8,128)(2,1)S(1)} %get-tuple-element.34.rest_1_), channel_id=1, source_target_pairs={{0,2},{1,5},{2,0},{3,7},{4,6},{5,1},{6,4},{7,3},{8,10},{9,13},{10,... | collective-permute-start | bytes 1179656 | tf_op jit(solution)/shard_map/ppermute | solution.py:753
  31.7 11.7 %collective-permute-start.11 = (bf16[256,768]{1,0:T(8,128)(2,1)S(1)}, bf16[256,768]{1,0:T(8,128)(2,1)S(1)}, u32[]{:S(2)}, u32[]{:S(2)}) collective-permute-start(bf16[256,768]{1,0:T(8,128)(2,1)S(1)} %add_up.4), channel_id=1, source_target_pairs={{0,4},{1,3},{2,6},{3,1},{4,0},{5,7},{6,2},{7,5},{8,12},{9,11},{10,... | collective-permute-start | bytes 1179656 | tf_op jit(solution)/shard_map/ppermute | solution.py:753
  33.3 12.1 %collective-permute-start.13 = (bf16[256,768]{1,0:T(8,128)(2,1)S(1)}, bf16[256,768]{1,0:T(8,128)(2,1)S(1)}, u32[]{:S(2)}, u32[]{:S(2)}) collective-permute-start(bf16[256,768]{1,0:T(8,128)(2,1)S(1)} %add_up.5), channel_id=1, source_target_pairs={{0,4},{1,3},{2,6},{3,1},{4,0},{5,7},{6,2},{7,5},{8,12},{9,11},{10,... | collective-permute-start | bytes 1179656 | tf_op jit(solution)/shard_map/ppermute | solution.py:753
  33.9 9.4 %collective-permute-start.7 = (bf16[16,384]{1,0:T(8,128)(2,1)S(1)}, bf16[16,384]{1,0:T(8,128)(2,1)S(1)}, u32[]{:S(2)}, u32[]{:S(2)}) collective-permute-start(bf16[16,384]{1,0:T(8,128)(2,1)S(1)} %edge_terms.1.refs_1_.refs_2_), channel_id=1, source_target_pairs={{0,6},{1,7},{2,4},{3,5},{4,2},{5,3},{6,0},{7,1},{8,14},{9,15},{10,... | collective-permute-start | bytes 36872 | tf_op jit(solution)/shard_map/ppermute | solution.py:753
  49.0 5.6 %collective-permute-start.15 = (bf16[128,384]{1,0:T(8,128)(2,1)S(1)}, bf16[128,384]{1,0:T(8,128)(2,1)S(1)}, u32[]{:S(2)}, u32[]{:S(2)}) collective-permute-start(bf16[128,384]{1,0:T(8,128)(2,1)S(1)} %bundle.1.rest_0_), channel_id=1, source_target_pairs={{0,2},{1,3},{2,0},{3,1},{4,6},{5,7},{6,4},{7,5},{8,10},{9,11},{10,... | collective-permute-start | bytes 294920 | tf_op jit(solution)/shard_map/ppermute | solution.py:753
  49.7 5.8 %collective-permute-start.16 = (bf16[128,384]{1,0:T(8,128)(2,1)S(1)}, bf16[128,384]{1,0:T(8,128)(2,1)S(1)}, u32[]{:S(2)}, u32[]{:S(2)}) collective-permute-start(bf16[128,384]{1,0:T(8,128)(2,1)S(1)} %bundle.1.rest_0_), channel_id=1, source_target_pairs={{0,4},{1,5},{2,6},{3,7},{4,0},{5,1},{6,2},{7,3},{8,12},{9,13},{10,... | collective-permute-start | bytes 294920 | tf_op jit(solution)/shard_map/ppermute | solution.py:753
  51.1 5.5 %collective-permute-start.17 = (bf16[128,384]{1,0:T(8,128)(2,1)S(1)}, bf16[128,384]{1,0:T(8,128)(2,1)S(1)}, u32[]{:S(2)}, u32[]{:S(2)}) collective-permute-start(bf16[128,384]{1,0:T(8,128)(2,1)S(1)} %bundle.1.rest_0_), channel_id=1, source_target_pairs={{0,6},{1,7},{2,4},{3,5},{4,2},{5,3},{6,0},{7,1},{8,14},{9,15},{10,... | collective-permute-start | bytes 294920 | tf_op jit(solution)/shard_map/ppermute | solution.py:753
  52.5 6.8 %collective-permute-start.18 = (bf16[128,384]{1,0:T(8,128)(2,1)S(1)}, bf16[128,384]{1,0:T(8,128)(2,1)S(1)}, u32[]{:S(2)}, u32[]{:S(2)}) collective-permute-start(bf16[128,384]{1,0:T(8,128)(2,1)S(1)} %bundle.1.rest_0_), channel_id=1, source_target_pairs={{0,1},{1,0},{2,3},{3,2},{4,5},{5,4},{6,7},{7,6},{8,9},{9,8},{10,11... | collective-permute-start | bytes 294920 | tf_op jit(solution)/shard_map/ppermute | solution.py:753
  54.6 6.6 %collective-permute-start.19 = (bf16[128,384]{1,0:T(8,128)(2,1)S(1)}, bf16[128,384]{1,0:T(8,128)(2,1)S(1)}, u32[]{:S(2)}, u32[]{:S(2)}) collective-permute-start(bf16[128,384]{1,0:T(8,128)(2,1)S(1)} %collective-permute-done.15.rest_1_), channel_id=1, source_target_pairs={{0,1},{1,0},{2,3},{3,2},{4,5},{5,4},{6,7},{7,6},{8,9},{9,8},{10,11... | collective-permute-start | bytes 294920 | tf_op jit(solution)/shard_map/ppermute | solution.py:753
  55.5 5.9 %collective-permute-start.20 = (bf16[128,384]{1,0:T(8,128)(2,1)S(1)}, bf16[128,384]{1,0:T(8,128)(2,1)S(1)}, u32[]{:S(2)}, u32[]{:S(2)}) collective-permute-start(bf16[128,384]{1,0:T(8,128)(2,1)S(1)} %collective-permute-done.16.rest_2_), channel_id=1, source_target_pairs={{0,1},{1,0},{2,3},{3,2},{4,5},{5,4},{6,7},{7,6},{8,9},{9,8},{10,11... | collective-permute-start | bytes 294920 | tf_op jit(solution)/shard_map/ppermute | solution.py:753
  56.6 4.8 %collective-permute-start.21 = (bf16[128,384]{1,0:T(8,128)(2,1)S(1)}, bf16[128,384]{1,0:T(8,128)(2,1)S(1)}, u32[]{:S(2)}, u32[]{:S(2)}) collective-permute-start(bf16[128,384]{1,0:T(8,128)(2,1)S(1)} %collective-permute-done.17.rest_3_), channel_id=1, source_target_pairs={{0,1},{1,0},{2,3},{3,2},{4,5},{5,4},{6,7},{7,6},{8,9},{9,8},{10,11... | collective-permute-start | bytes 294920 | tf_op jit(solution)/shard_map/ppermute | solution.py:753
  57.9 6.4 %collective-permute-start.22 = (bf16[128,128]{1,0:T(8,128)(2,1)S(1)}, bf16[128,128]{1,0:T(8,128)(2,1)S(1)}, u32[]{:S(2)}, u32[]{:S(2)}) collective-permute-start(bf16[128,128]{1,0:T(8,128)(2,1)S(1)} %get-tuple-element.42.refs_3_), channel_id=1, source_target_pairs={{0,6},{1,7},{2,4},{3,5},{4,2},{5,3},{6,0},{7,1},{8,14},{9,15},{10,... | collective-permute-start | bytes 98312 | tf_op jit(solution)/shard_map/ppermute | solution.py:753
  59.3 5.0 %collective-permute-start.23 = (bf16[128,128]{1,0:T(8,128)(2,1)S(1)}, bf16[128,128]{1,0:T(8,128)(2,1)S(1)}, u32[]{:S(2)}, u32[]{:S(2)}) collective-permute-start(bf16[128,128]{1,0:T(8,128)(2,1)S(1)} %get-tuple-element.42.refs_3_), channel_id=1, source_target_pairs={{0,4},{1,5},{2,6},{3,7},{4,0},{5,1},{6,2},{7,3},{8,12},{9,13},{10,... | collective-permute-start | bytes 98312 | tf_op jit(solution)/shard_map/ppermute | solution.py:753
  65.1 8.0 %collective-permute-start.25 = (bf16[128,128]{1,0:T(8,128)(2,1)S(1)}, bf16[128,128]{1,0:T(8,128)(2,1)S(1)}, u32[]{:S(2)}, u32[]{:S(2)}) collective-permute-start(bf16[128,128]{1,0:T(8,128)(2,1)S(1)} %add_up.6.rest_8_.refs_3_), channel_id=1, source_target_pairs={{0,24},{8,16},{16,8},{24,0},{1,25},{9,17},{17,9},{25,1},{2,26},{10... | collective-permute-start | bytes 98312 | tf_op jit(solution)/shard_map/ppermute | solution.py:847
  68.7 4.8 %collective-permute-start.26 = (bf16[128,128]{1,0:T(8,128)(2,1)S(1)}, bf16[128,128]{1,0:T(8,128)(2,1)S(1)}, u32[]{:S(2)}, u32[]{:S(2)}) collective-permute-start(bf16[128,128]{1,0:T(8,128)(2,1)S(1)} %add_up.6.rest_8_.refs_3_), channel_id=1, source_target_pairs={{0,16},{8,24},{16,0},{24,8},{1,17},{9,25},{17,1},{25,9},{2,18},{10... | collective-permute-start | bytes 98312 | tf_op jit(solution)/shard_map/ppermute | solution.py:847
  68.7 4.8 %collective-permute-start.27 = (bf16[128,128]{1,0:T(8,128)(2,1)S(1)}, bf16[128,128]{1,0:T(8,128)(2,1)S(1)}, u32[]{:S(2)}, u32[]{:S(2)}) collective-permute-start(bf16[128,128]{1,0:T(8,128)(2,1)S(1)} %add_up.6.rest_8_.refs_3_), channel_id=1, source_target_pairs={{0,8},{8,0},{16,24},{24,16},{1,9},{9,1},{17,25},{25,17},{2,10},{10... | collective-permute-start | bytes 98312 | tf_op jit(solution)/shard_map/ppermute | solution.py:847
  (14 other events, 152.3 us)

commit v9 on v7

--- a/solution.py
+++ b/solution.py
@@ -394,7 +394,7 @@
     pieces = len(columns)
     got = pl.pallas_call(
         functools.partial(
-            conv_kernel, chips, bits, taps, 256, wanted, columns, count * pieces, edged
+            conv_kernel, chips, bits, taps, 768, wanted, columns, count * pieces, edged
         ),
         name="conv",
         out_shape=[array((rows, b - a), d) for d in dtypes for a, b in columns],

time: 74 us -> 74 us (level)
  no operation moved by 1% of the time
where the time goes in v9:
time: 74 us; the launch traced here: 73.8 us
  Pallas kernels  29.6 us (40%)
  starting transfers between devices  26.9 us (36%)
  waiting for transfers between devices  16.4 us (22%)
  between operations  0.95 us (1%)
    ppermute x25, starting transfers between devices, send(): return lax.ppermute(value, GROUP, hop_pairs(chips, cores, flip))  22.4 us
    ppermute x25, waiting for transfers between devices, send(): return lax.ppermute(value, GROUP, hop_pairs(chips, cores, flip))  16 us
    pallas_call x5, Pallas kernels, conv(): pl.pallas_call(functools.partial(conv_kernel, chips, bits, taps, 768, wan...  8.86 us
    pallas_call x2, Pallas kernels, attend(): pl.pallas_call(functools.partial(attend_kernel, len(parts), heads, first,...  6.43 us
    pallas_call x4, Pallas kernels, activate(): pl.pallas_call(functools.partial(activate_kernel, width, len(messages)),...  6.24 us
    ppermute x3, starting transfers between devices, per_device(): lax.ppermute(grad, 'dp', [(w, w ^ k) for w in range(windows)])  4.45 us
    pallas_call x1, Pallas kernels, prep(): pl.pallas_call(functools.partial(prep_kernel, chips, width), name='prep',...  1.84 us
    pallas_call x1, Pallas kernels, pack_filter(): pl.pallas_call(functools.partial(pack_kernel, taps, padded), name='pack_f...  1.79 us
  transfers between devices with their start and end apart: 28, of which 11 were waited for; matrix products, arithmetic and copies ran while one was open for 0% of the time, Pallas kernels for 38%

profile of v9, /device:TPU:0, one launch (start us, length us, event | category | flops | bytes accessed | tf_op | source)
XLA Modules:
  0.0 73.8 jit_solution(16394726589233039989)
XLA Ops:
  1.1 1.8 %prep.1 = (bf16[288,384]{1,0:T(8,128)(2,1)S(1)}, bf16[288,384]{1,0:T(8,128)(2,1)S(1)}, bf16[288,384]{1,0:T(8,128)(2,1)S(1)}, bf16[288,384]{1,0:T(8,128)(2,1)S(1)}) custom-call(bf16[256,1408]{1,0:T(8,128)(2,1)} %bitcast.14, bf16[8,64,128]{2,1,0:T(8,128)(2,1)} %bitcast.10), custom_call_target="tpu_custom_call" | custom-call | tf_op jit(solution)/shard_map/prep/pallas_call | solution.py:138
  3.0 3.5 %collective-permute-start = (bf16[288,384]{1,0:T(8,128)(2,1)S(1)}, bf16[288,384]{1,0:T(8,128)(2,1)S(1)}, u32[]{:S(2)}, u32[]{:S(2)}) collective-permute-start(bf16[288,384]{1,0:T(8,128)(2,1)S(1)} %get-tuple-element.25), channel_id=1, source_target_pairs={{0,6},{1,7},{2,4},{3,5},{4,2},{5,3},{6,0},{7,1},{8,14},{9,15},{10,... | collective-permute-start | bytes 663560 | tf_op jit(solution)/shard_map/ppermute | solution.py:753
  7.2 1.8 %pack_filter.1.rest_1_.weight_ref = bf16[1920,1536]{1,0:T(8,128)(2,1)S(1)} custom-call(bf16[880,1536]{1,0:T(8,128)(2,1)} %bitcast.21, bf16[880,1536]{1,0:T(8,128)(2,1)S(1)} %collective-permute-done.3.peer_hbm), custom_call_target="tpu_custom_call" | custom-call | tf_op jit(solution)/shard_map/pack_filter/pallas_call | solution.py:261
  9.1 3.8 %collective-permute-done.refs_0_ = bf16[288,384]{1,0:T(8,128)(2,1)S(1)} collective-permute-done((bf16[288,384]{1,0:T(8,128)(2,1)S(1)}, bf16[288,384]{1,0:T(8,128)(2,1)S(1)}, u32[]{:S(2)}, u32[]{:S(2)}) %collective-permute-start) | collective-permute-done | bytes 221216 | tf_op jit(solution)/shard_map/ppermute | solution.py:753
  12.8 1.5 %activate.4.edge_ref.rest_0_ = bf16[256,384]{1,0:T(8,128)(2,1)S(1)} custom-call(bf16[288,384]{1,0:T(8,128)(2,1)S(1)} %collective-permute-done.refs_0_), custom_call_target="tpu_custom_call" | custom-call | tf_op jit(solution)/shard_map/activate/pallas_call | solution.py:216
  15.4 2.0 %collective-permute-done.1.refs_1_.refs_0_ = bf16[288,384]{1,0:T(8,128)(2,1)S(1)} collective-permute-done((bf16[288,384]{1,0:T(8,128)(2,1)S(1)}, bf16[288,384]{1,0:T(8,128)(2,1)S(1)}, u32[]{:S(2)}, u32[]{:S(2)}) %collective-permute-start.1) | collective-permute-done | bytes 221216 | tf_op jit(solution)/shard_map/ppermute | solution.py:753
  17.6 1.5 %collective-permute-start.10 = (bf16[256,768]{1,0:T(8,128)(2,1)S(1)}, bf16[256,768]{1,0:T(8,128)(2,1)S(1)}, u32[]{:S(2)}, u32[]{:S(2)}) collective-permute-start(bf16[256,768]{1,0:T(8,128)(2,1)S(1)} %conv.5.refs_4_.refs_2_), channel_id=1, source_target_pairs={{0,2},{1,5},{2,0},{3,7},{4,6},{5,1},{6,4},{7,3},{8,10},{9,13},{10,... | collective-permute-start | bytes 1179656 | tf_op jit(solution)/shard_map/ppermute | solution.py:753
  21.7 1.5 %activate.5.rest_0_ = bf16[256,384]{1,0:T(8,128)(2,1)S(1)} custom-call(bf16[288,384]{1,0:T(8,128)(2,1)S(1)} %collective-permute-done.2.refs_2_.refs_0_.refs_1_, bf16[288,384]{1,0:T(8,128)(2,1)S(1)} %collective-permute-done.1.refs_1_.refs_0_, bf16[256,768]{1,0:T(8,128)(2,1)S(1)} %conv.5.refs_4_.refs_2_, bf16[256,768]{1,0:T(8,128)(2,1)S(1)} %conv.6.refs_5_.refs_3_), custom_call_target="tpu_custom_call" | custom-call | tf_op jit(solution)/shard_map/activate/pallas_call | solution.py:216
  23.2 1.8 %conv.7 = (bf16[256,768]{1,0:T(8,128)(2,1)S(1)}, bf16[256,768]{1,0:T(8,128)(2,1)S(1)}) custom-call(bf16[256,1408]{1,0:T(8,128)(2,1)} %bitcast.17, f32[4,8,384]{2,1,0:T(8,128)S(1)} %collective-permute-done.5.edge_ref, bf16[256,384]{1,0:T(8,128)(2,1)S(1)} %activate.5.rest_0_, bf16[1920,1536]{1,0:T(8,128)(2,1)S(1)} %pack_filter.1.rest_1_.weight_ref, ...), custom_call_target="tpu_custom_call" | custom-call | tf_op jit(solution)/shard_map/conv/pallas_call | solution.py:395
  25.1 1.6 %collective-permute-start.8 = (bf16[256,768]{1,0:T(8,128)(2,1)S(1)}, bf16[256,768]{1,0:T(8,128)(2,1)S(1)}, u32[]{:S(2)}, u32[]{:S(2)}) collective-permute-start(bf16[256,768]{1,0:T(8,128)(2,1)S(1)} %get-tuple-element.33.rest_0_), channel_id=1, source_target_pairs={{0,2},{1,5},{2,0},{3,7},{4,6},{5,1},{6,4},{7,3},{8,10},{9,13},{10,... | collective-permute-start | bytes 1179656 | tf_op jit(solution)/shard_map/ppermute | solution.py:753
  28.1 1.7 %activate.7.rest_0_ = bf16[256,384]{1,0:T(8,128)(2,1)S(1)} custom-call(bf16[288,384]{1,0:T(8,128)(2,1)S(1)} %collective-permute-done.1.refs_1_.refs_0_, bf16[288,384]{1,0:T(8,128)(2,1)S(1)} %collective-permute-done.2.refs_2_.refs_0_.refs_1_, bf16[16,384]{1,0:T(8,128)(2,1)S(1)} %edge_terms.1.refs_1_.refs_2_), custom_call_target="tpu_custom_call" | custom-call | tf_op jit(solution)/shard_map/activate/pallas_call | solution.py:216
  29.8 1.8 %conv.9 = (f32[256,768]{1,0:T(8,128)S(1)}, f32[256,768]{1,0:T(8,128)S(1)}) custom-call(bf16[256,1408]{1,0:T(8,128)(2,1)} %bitcast.18, f32[4,8,384]{2,1,0:T(8,128)S(1)} %collective-permute-done.5.edge_ref, bf16[256,384]{1,0:T(8,128)(2,1)S(1)} %activate.7.rest_0_, bf16[1920,1536]{1,0:T(8,128)(2,1)S(1)} %pack_filter.1.rest_1_.weight_ref, ...), custom_call_target="tpu_custom_call" | custom-call | tf_op jit(solution)/shard_map/conv/pallas_call | solution.py:395
  33.9 1.5 %collective-permute-start.7 = (bf16[16,384]{1,0:T(8,128)(2,1)S(1)}, bf16[16,384]{1,0:T(8,128)(2,1)S(1)}, u32[]{:S(2)}, u32[]{:S(2)}) collective-permute-start(bf16[16,384]{1,0:T(8,128)(2,1)S(1)} %edge_terms.1.refs_1_.refs_2_), channel_id=1, source_target_pairs={{0,6},{1,7},{2,4},{3,5},{4,2},{5,3},{6,0},{7,1},{8,14},{9,15},{10,... | collective-permute-start | bytes 36872 | tf_op jit(solution)/shard_map/ppermute | solution.py:753
  35.5 1.5 %activate.6.rest_0_ = bf16[256,384]{1,0:T(8,128)(2,1)S(1)} custom-call(bf16[288,384]{1,0:T(8,128)(2,1)S(1)} %get-tuple-element.28.refs_3_.refs_0_, bf16[16,384]{1,0:T(8,128)(2,1)S(1)} %edge_terms.1.refs_1_.refs_2_), custom_call_target="tpu_custom_call" | custom-call | tf_op jit(solution)/shard_map/activate/pallas_call | solution.py:216
  37.0 3.2 %conv.8 = (f32[256,768]{1,0:T(8,128)S(1)}, f32[256,768]{1,0:T(8,128)S(1)}) custom-call(bf16[256,1408]{1,0:T(8,128)(2,1)} %bitcast.19, f32[4,8,384]{2,1,0:T(8,128)S(1)} %collective-permute-done.5.edge_ref, bf16[256,384]{1,0:T(8,128)(2,1)S(1)} %activate.6.rest_0_, bf16[1920,1536]{1,0:T(8,128)(2,1)S(1)} %pack_filter.1.rest_1_.weight_ref, ...), custom_call_target="tpu_custom_call" | custom-call | tf_op jit(solution)/shard_map/conv/pallas_call | solution.py:395
  40.3 3.1 %collective-permute-done.7.term_ref = bf16[16,384]{1,0:T(8,128)(2,1)S(1)} collective-permute-done((bf16[16,384]{1,0:T(8,128)(2,1)S(1)}, bf16[16,384]{1,0:T(8,128)(2,1)S(1)}, u32[]{:S(2)}, u32[]{:S(2)}) %collective-permute-start.7) | collective-permute-done | bytes 12320 | tf_op jit(solution)/shard_map/ppermute | solution.py:753
  43.4 2.0 %collective-permute-done.13.rest_5_ = bf16[256,768]{1,0:T(8,128)(2,1)S(1)} collective-permute-done((bf16[256,768]{1,0:T(8,128)(2,1)S(1)}, bf16[256,768]{1,0:T(8,128)(2,1)S(1)}, u32[]{:S(2)}, u32[]{:S(2)}) %collective-permute-start.13) | collective-permute-done | bytes 393248 | tf_op jit(solution)/shard_map/ppermute | solution.py:753
  45.9 2.1 %collective-permute-start.14 = (f32[8,256]{1,0:T(8,128)S(1)}, f32[8,256]{1,0:T(8,128)S(1)}, u32[]{:S(2)}, u32[]{:S(2)}) collective-permute-start(f32[8,256]{1,0:T(8,128)S(1)} %get-tuple-element.40.mine_ref), channel_id=1, source_target_pairs={{0,1},{1,0},{2,3},{3,2},{4,5},{5,4},{6,7},{7,6},{8,9},{9,8},{10,11... | collective-permute-start | bytes 24584 | tf_op jit(solution)/shard_map/ppermute | solution.py:753
  52.5 2.1 %collective-permute-done.15.rest_1_ = bf16[128,384]{1,0:T(8,128)(2,1)S(1)} collective-permute-done((bf16[128,384]{1,0:T(8,128)(2,1)S(1)}, bf16[128,384]{1,0:T(8,128)(2,1)S(1)}, u32[]{:S(2)}, u32[]{:S(2)}) %collective-permute-start.15) | collective-permute-done | bytes 98336 | tf_op jit(solution)/shard_map/ppermute | solution.py:753
  57.9 1.8 %collective-permute-start.22 = (bf16[128,128]{1,0:T(8,128)(2,1)S(1)}, bf16[128,128]{1,0:T(8,128)(2,1)S(1)}, u32[]{:S(2)}, u32[]{:S(2)}) collective-permute-start(bf16[128,128]{1,0:T(8,128)(2,1)S(1)} %get-tuple-element.42.refs_0_), channel_id=1, source_target_pairs={{0,2},{1,3},{2,0},{3,1},{4,6},{5,7},{6,4},{7,5},{8,10},{9,11},{10,... | collective-permute-start | bytes 98312 | tf_op jit(solution)/shard_map/ppermute | solution.py:753
  59.8 1.5 %collective-permute-start.24 = (bf16[128,128]{1,0:T(8,128)(2,1)S(1)}, bf16[128,128]{1,0:T(8,128)(2,1)S(1)}, u32[]{:S(2)}, u32[]{:S(2)}) collective-permute-start(bf16[128,128]{1,0:T(8,128)(2,1)S(1)} %get-tuple-element.42.refs_0_), channel_id=1, source_target_pairs={{0,6},{1,7},{2,4},{3,5},{4,2},{5,3},{6,0},{7,1},{8,14},{9,15},{10,... | collective-permute-start | bytes 98312 | tf_op jit(solution)/shard_map/ppermute | solution.py:753
  61.4 2.8 %attend.2 = (f32[128,1536]{1,0:T(8,128)S(1)}, f32[8,128]{1,0:T(8,128)S(1)}) custom-call(f32[8]{0:T(128)S(1)} %copy-done.7, bf16[128,1536]{1,0:T(8,128)(2,1)S(1)} %get-tuple-element.39.encoded_ref.start_ref, f32[1536]{0:T(1024)S(1)} %copy-done.5, bf16[1536,1024]{1,0:T(8,128)(2,1)S(1)} %copy-done, ...), custom_call_target="tpu_custom_call" | custom-call | tf_op jit(solution)/shard_map/attend/pallas_call | solution.py:602
  64.7 3.7 %collective-permute-start.25 = (bf16[128,128]{1,0:T(8,128)(2,1)S(1)}, bf16[128,128]{1,0:T(8,128)(2,1)S(1)}, u32[]{:S(2)}, u32[]{:S(2)}) collective-permute-start(bf16[128,128]{1,0:T(8,128)(2,1)S(1)} %add_up.6.rest_8_.refs_3_), channel_id=1, source_target_pairs={{0,24},{8,16},{16,8},{24,0},{1,25},{9,17},{17,9},{25,1},{2,26},{10... | collective-permute-start | bytes 98312 | tf_op jit(solution)/shard_map/ppermute | solution.py:846
  69.1 3.6 %attend.3 = (bf16[128,1536]{1,0:T(8,128)(2,1)}, f32[8,128]{1,0:T(8,128)S(1)}) custom-call(f32[8]{0:T(128)S(1)} %copy-done.7, bf16[128,1536]{1,0:T(8,128)(2,1)S(1)} %get-tuple-element.39.encoded_ref.start_ref, f32[1536]{0:T(1024)S(1)} %copy-done.5, bf16[1536,1024]{1,0:T(8,128)(2,1)S(1)} %copy-done, f32[128,1536]{1,0:T(8,128)S(1)} %get-tuple-element.41.start_ref, ...), custom_call_target="tpu_custom_call" | custom-call | tf_op jit(solution)/shard_map/attend/pallas_call | solution.py:602
  (77 shorter events, 19.5 us)
Async XLA Ops:
  0.6 6.5 %collective-permute-start.3 = (bf16[880,1536]{1,0:T(8,128)(2,1)}, bf16[880,1536]{1,0:T(8,128)(2,1)S(1)}, u32[]{:S(2)}, u32[]{:S(2)}) collective-permute-start(bf16[880,1536]{1,0:T(8,128)(2,1)} %bitcast.20), channel_id=1, source_target_pairs={{0,1},{1,0},{2,3},{3,2},{4,5},{5,4},{6,7},{7,6},{8,9},{9,8},{10,11... | collective-permute-start | bytes 8110088 | tf_op jit(solution)/shard_map/ppermute | solution.py:753
  3.0 9.9 %collective-permute-start = (bf16[288,384]{1,0:T(8,128)(2,1)S(1)}, bf16[288,384]{1,0:T(8,128)(2,1)S(1)}, u32[]{:S(2)}, u32[]{:S(2)}) collective-permute-start(bf16[288,384]{1,0:T(8,128)(2,1)S(1)} %get-tuple-element.25), channel_id=1, source_target_pairs={{0,6},{1,7},{2,4},{3,5},{4,2},{5,3},{6,0},{7,1},{8,14},{9,15},{10,... | collective-permute-start | bytes 663560 | tf_op jit(solution)/shard_map/ppermute | solution.py:753
  6.5 10.8 %collective-permute-start.1 = (bf16[288,384]{1,0:T(8,128)(2,1)S(1)}, bf16[288,384]{1,0:T(8,128)(2,1)S(1)}, u32[]{:S(2)}, u32[]{:S(2)}) collective-permute-start(bf16[288,384]{1,0:T(8,128)(2,1)S(1)} %get-tuple-element.26), channel_id=1, source_target_pairs={{0,4},{1,5},{2,6},{3,7},{4,0},{5,1},{6,2},{7,3},{8,12},{9,13},{10,... | collective-permute-start | bytes 663560 | tf_op jit(solution)/shard_map/ppermute | solution.py:753
  7.0 10.6 %collective-permute-start.2 = (bf16[288,384]{1,0:T(8,128)(2,1)S(1)}, bf16[288,384]{1,0:T(8,128)(2,1)S(1)}, u32[]{:S(2)}, u32[]{:S(2)}) collective-permute-start(bf16[288,384]{1,0:T(8,128)(2,1)S(1)} %get-tuple-element.27), channel_id=1, source_target_pairs={{0,2},{1,3},{2,0},{3,1},{4,6},{5,7},{6,4},{7,5},{8,10},{9,11},{10,... | collective-permute-start | bytes 663560 | tf_op jit(solution)/shard_map/ppermute | solution.py:753
  9.0 10.2 %collective-permute-start.4 = (bf16[8,64,128]{2,1,0:T(8,128)(2,1)S(1)}, bf16[8,64,128]{2,1,0:T(8,128)(2,1)S(1)}, u32[]{:S(2)}, u32[]{:S(2)}) collective-permute-start(bf16[8,64,128]{2,1,0:T(8,128)(2,1)S(1)} %bitcast.12), channel_id=1, source_target_pairs={{0,1},{1,0},{2,3},{3,2},{4,5},{5,4},{6,7},{7,6},{8,9},{9,8},{10,11... | collective-permute-start | bytes 393224 | tf_op jit(solution)/shard_map/ppermute | solution.py:753
  17.6 14.0 %collective-permute-start.10 = (bf16[256,768]{1,0:T(8,128)(2,1)S(1)}, bf16[256,768]{1,0:T(8,128)(2,1)S(1)}, u32[]{:S(2)}, u32[]{:S(2)}) collective-permute-start(bf16[256,768]{1,0:T(8,128)(2,1)S(1)} %conv.5.refs_4_.refs_2_), channel_id=1, source_target_pairs={{0,2},{1,5},{2,0},{3,7},{4,6},{5,1},{6,4},{7,3},{8,10},{9,13},{10,... | collective-permute-start | bytes 1179656 | tf_op jit(solution)/shard_map/ppermute | solution.py:753
  20.2 13.0 %collective-permute-start.12 = (bf16[256,768]{1,0:T(8,128)(2,1)S(1)}, bf16[256,768]{1,0:T(8,128)(2,1)S(1)}, u32[]{:S(2)}, u32[]{:S(2)}) collective-permute-start(bf16[256,768]{1,0:T(8,128)(2,1)S(1)} %conv.6.refs_5_.refs_3_), channel_id=1, source_target_pairs={{0,2},{1,5},{2,0},{3,7},{4,6},{5,1},{6,4},{7,3},{8,10},{9,13},{10,... | collective-permute-start | bytes 1179656 | tf_op jit(solution)/shard_map/ppermute | solution.py:753
  25.1 18.3 %collective-permute-start.8 = (bf16[256,768]{1,0:T(8,128)(2,1)S(1)}, bf16[256,768]{1,0:T(8,128)(2,1)S(1)}, u32[]{:S(2)}, u32[]{:S(2)}) collective-permute-start(bf16[256,768]{1,0:T(8,128)(2,1)S(1)} %get-tuple-element.33.rest_0_), channel_id=1, source_target_pairs={{0,2},{1,5},{2,0},{3,7},{4,6},{5,1},{6,4},{7,3},{8,10},{9,13},{10,... | collective-permute-start | bytes 1179656 | tf_op jit(solution)/shard_map/ppermute | solution.py:753
  26.6 16.8 %collective-permute-start.9 = (bf16[256,768]{1,0:T(8,128)(2,1)S(1)}, bf16[256,768]{1,0:T(8,128)(2,1)S(1)}, u32[]{:S(2)}, u32[]{:S(2)}) collective-permute-start(bf16[256,768]{1,0:T(8,128)(2,1)S(1)} %get-tuple-element.34.rest_1_), channel_id=1, source_target_pairs={{0,2},{1,5},{2,0},{3,7},{4,6},{5,1},{6,4},{7,3},{8,10},{9,13},{10,... | collective-permute-start | bytes 1179656 | tf_op jit(solution)/shard_map/ppermute | solution.py:753
  31.7 11.7 %collective-permute-start.11 = (bf16[256,768]{1,0:T(8,128)(2,1)S(1)}, bf16[256,768]{1,0:T(8,128)(2,1)S(1)}, u32[]{:S(2)}, u32[]{:S(2)}) collective-permute-start(bf16[256,768]{1,0:T(8,128)(2,1)S(1)} %add_up.4), channel_id=1, source_target_pairs={{0,4},{1,3},{2,6},{3,1},{4,0},{5,7},{6,2},{7,5},{8,12},{9,11},{10,... | collective-permute-start | bytes 1179656 | tf_op jit(solution)/shard_map/ppermute | solution.py:753
  33.2 12.1 %collective-permute-start.13 = (bf16[256,768]{1,0:T(8,128)(2,1)S(1)}, bf16[256,768]{1,0:T(8,128)(2,1)S(1)}, u32[]{:S(2)}, u32[]{:S(2)}) collective-permute-start(bf16[256,768]{1,0:T(8,128)(2,1)S(1)} %add_up.5), channel_id=1, source_target_pairs={{0,4},{1,3},{2,6},{3,1},{4,0},{5,7},{6,2},{7,5},{8,12},{9,11},{10,... | collective-permute-start | bytes 1179656 | tf_op jit(solution)/shard_map/ppermute | solution.py:753
  33.9 9.5 %collective-permute-start.7 = (bf16[16,384]{1,0:T(8,128)(2,1)S(1)}, bf16[16,384]{1,0:T(8,128)(2,1)S(1)}, u32[]{:S(2)}, u32[]{:S(2)}) collective-permute-start(bf16[16,384]{1,0:T(8,128)(2,1)S(1)} %edge_terms.1.refs_1_.refs_2_), channel_id=1, source_target_pairs={{0,6},{1,7},{2,4},{3,5},{4,2},{5,3},{6,0},{7,1},{8,14},{9,15},{10,... | collective-permute-start | bytes 36872 | tf_op jit(solution)/shard_map/ppermute | solution.py:753
  49.0 5.6 %collective-permute-start.15 = (bf16[128,384]{1,0:T(8,128)(2,1)S(1)}, bf16[128,384]{1,0:T(8,128)(2,1)S(1)}, u32[]{:S(2)}, u32[]{:S(2)}) collective-permute-start(bf16[128,384]{1,0:T(8,128)(2,1)S(1)} %bundle.1.rest_0_), channel_id=1, source_target_pairs={{0,2},{1,3},{2,0},{3,1},{4,6},{5,7},{6,4},{7,5},{8,10},{9,11},{10,... | collective-permute-start | bytes 294920 | tf_op jit(solution)/shard_map/ppermute | solution.py:753
  49.7 5.8 %collective-permute-start.16 = (bf16[128,384]{1,0:T(8,128)(2,1)S(1)}, bf16[128,384]{1,0:T(8,128)(2,1)S(1)}, u32[]{:S(2)}, u32[]{:S(2)}) collective-permute-start(bf16[128,384]{1,0:T(8,128)(2,1)S(1)} %bundle.1.rest_0_), channel_id=1, source_target_pairs={{0,4},{1,5},{2,6},{3,7},{4,0},{5,1},{6,2},{7,3},{8,12},{9,13},{10,... | collective-permute-start | bytes 294920 | tf_op jit(solution)/shard_map/ppermute | solution.py:753
  51.1 5.5 %collective-permute-start.17 = (bf16[128,384]{1,0:T(8,128)(2,1)S(1)}, bf16[128,384]{1,0:T(8,128)(2,1)S(1)}, u32[]{:S(2)}, u32[]{:S(2)}) collective-permute-start(bf16[128,384]{1,0:T(8,128)(2,1)S(1)} %bundle.1.rest_0_), channel_id=1, source_target_pairs={{0,6},{1,7},{2,4},{3,5},{4,2},{5,3},{6,0},{7,1},{8,14},{9,15},{10,... | collective-permute-start | bytes 294920 | tf_op jit(solution)/shard_map/ppermute | solution.py:753
  52.5 7.2 %collective-permute-start.18 = (bf16[128,384]{1,0:T(8,128)(2,1)S(1)}, bf16[128,384]{1,0:T(8,128)(2,1)S(1)}, u32[]{:S(2)}, u32[]{:S(2)}) collective-permute-start(bf16[128,384]{1,0:T(8,128)(2,1)S(1)} %bundle.1.rest_0_), channel_id=1, source_target_pairs={{0,1},{1,0},{2,3},{3,2},{4,5},{5,4},{6,7},{7,6},{8,9},{9,8},{10,11... | collective-permute-start | bytes 294920 | tf_op jit(solution)/shard_map/ppermute | solution.py:753
  54.6 5.3 %collective-permute-start.19 = (bf16[128,384]{1,0:T(8,128)(2,1)S(1)}, bf16[128,384]{1,0:T(8,128)(2,1)S(1)}, u32[]{:S(2)}, u32[]{:S(2)}) collective-permute-start(bf16[128,384]{1,0:T(8,128)(2,1)S(1)} %collective-permute-done.15.rest_1_), channel_id=1, source_target_pairs={{0,1},{1,0},{2,3},{3,2},{4,5},{5,4},{6,7},{7,6},{8,9},{9,8},{10,11... | collective-permute-start | bytes 294920 | tf_op jit(solution)/shard_map/ppermute | solution.py:753
  55.5 5.9 %collective-permute-start.20 = (bf16[128,384]{1,0:T(8,128)(2,1)S(1)}, bf16[128,384]{1,0:T(8,128)(2,1)S(1)}, u32[]{:S(2)}, u32[]{:S(2)}) collective-permute-start(bf16[128,384]{1,0:T(8,128)(2,1)S(1)} %collective-permute-done.16.rest_2_), channel_id=1, source_target_pairs={{0,1},{1,0},{2,3},{3,2},{4,5},{5,4},{6,7},{7,6},{8,9},{9,8},{10,11... | collective-permute-start | bytes 294920 | tf_op jit(solution)/shard_map/ppermute | solution.py:753
  56.6 4.8 %collective-permute-start.21 = (bf16[128,384]{1,0:T(8,128)(2,1)S(1)}, bf16[128,384]{1,0:T(8,128)(2,1)S(1)}, u32[]{:S(2)}, u32[]{:S(2)}) collective-permute-start(bf16[128,384]{1,0:T(8,128)(2,1)S(1)} %collective-permute-done.17.rest_3_), channel_id=1, source_target_pairs={{0,1},{1,0},{2,3},{3,2},{4,5},{5,4},{6,7},{7,6},{8,9},{9,8},{10,11... | collective-permute-start | bytes 294920 | tf_op jit(solution)/shard_map/ppermute | solution.py:753
  57.9 6.4 %collective-permute-start.22 = (bf16[128,128]{1,0:T(8,128)(2,1)S(1)}, bf16[128,128]{1,0:T(8,128)(2,1)S(1)}, u32[]{:S(2)}, u32[]{:S(2)}) collective-permute-start(bf16[128,128]{1,0:T(8,128)(2,1)S(1)} %get-tuple-element.42.refs_0_), channel_id=1, source_target_pairs={{0,2},{1,3},{2,0},{3,1},{4,6},{5,7},{6,4},{7,5},{8,10},{9,11},{10,... | collective-permute-start | bytes 98312 | tf_op jit(solution)/shard_map/ppermute | solution.py:753
  59.8 4.8 %collective-permute-start.24 = (bf16[128,128]{1,0:T(8,128)(2,1)S(1)}, bf16[128,128]{1,0:T(8,128)(2,1)S(1)}, u32[]{:S(2)}, u32[]{:S(2)}) collective-permute-start(bf16[128,128]{1,0:T(8,128)(2,1)S(1)} %get-tuple-element.42.refs_0_), channel_id=1, source_target_pairs={{0,6},{1,7},{2,4},{3,5},{4,2},{5,3},{6,0},{7,1},{8,14},{9,15},{10,... | collective-permute-start | bytes 98312 | tf_op jit(solution)/shard_map/ppermute | solution.py:753
  64.7 8.0 %collective-permute-start.25 = (bf16[128,128]{1,0:T(8,128)(2,1)S(1)}, bf16[128,128]{1,0:T(8,128)(2,1)S(1)}, u32[]{:S(2)}, u32[]{:S(2)}) collective-permute-start(bf16[128,128]{1,0:T(8,128)(2,1)S(1)} %add_up.6.rest_8_.refs_3_), channel_id=1, source_target_pairs={{0,24},{8,16},{16,8},{24,0},{1,25},{9,17},{17,9},{25,1},{2,26},{10... | collective-permute-start | bytes 98312 | tf_op jit(solution)/shard_map/ppermute | solution.py:846
  68.3 4.8 %collective-permute-start.26 = (bf16[128,128]{1,0:T(8,128)(2,1)S(1)}, bf16[128,128]{1,0:T(8,128)(2,1)S(1)}, u32[]{:S(2)}, u32[]{:S(2)}) collective-permute-start(bf16[128,128]{1,0:T(8,128)(2,1)S(1)} %add_up.6.rest_8_.refs_3_), channel_id=1, source_target_pairs={{0,16},{8,24},{16,0},{24,8},{1,17},{9,25},{17,1},{25,9},{2,18},{10... | collective-permute-start | bytes 98312 | tf_op jit(solution)/shard_map/ppermute | solution.py:846
  68.3 4.8 %collective-permute-start.27 = (bf16[128,128]{1,0:T(8,128)(2,1)S(1)}, bf16[128,128]{1,0:T(8,128)(2,1)S(1)}, u32[]{:S(2)}, u32[]{:S(2)}) collective-permute-start(bf16[128,128]{1,0:T(8,128)(2,1)S(1)} %add_up.6.rest_8_.refs_3_), channel_id=1, source_target_pairs={{0,8},{8,0},{16,24},{24,16},{1,9},{9,1},{17,25},{25,17},{2,10},{10... | collective-permute-start | bytes 98312 | tf_op jit(solution)/shard_map/ppermute | solution.py:846
  (14 other events, 153.0 us)
